TPU v7x, 512 devices: a whole 4x8x8 slice. The times are simulated.
512 devices in a mesh: gx: 32 (over x, y), gy: 16 (over z, core).
Axes of the slice: x: 4, y: 8, z: 8, core: 2. Of those that a mesh axis runs over, the one named last changes fastest.
Arguments:
- tokens: bfloat16 [131072, 512], P(('gx', 'gy')), may hold values from -8 to 8
- w_qkv: bfloat16 [512, 1536], replicated, may hold values from -0.25 to 0.25
- w_out: bfloat16 [512, 512], replicated, may hold values from -0.25 to 0.25
Outputs:
- mixed: bfloat16 [131072, 512], P(('gx', 'gy'))
All inputs are finite; a program needn't handle non-finite values.
Results may differ from a plain program's by a relative error of at most 0.0063.
Values may be sent and summed in bfloat16 or wider, within the bound.
No kernel may reach another device: no remote copies, remote signals or barrier semaphores. Data moves between devices by JAX's collectives and lax.ppermute only.
A program may use at most 64 MiB of HBM per device.

v0:
```python
import jax
import jax.numpy as jnp
from jax import lax
from jax.sharding import PartitionSpec as P

HEADS = 8
BLOCK = 64


def padded_2(block, sides, width):
    for axis, dim in sides:
        count = lax.axis_size(axis)
        forward = [(i, i + 1) for i in range(count - 1)]
        backward = [(target, source) for source, target in forward]
        low = lax.ppermute(
            lax.slice_in_dim(block, block.shape[dim] - width, None, axis=dim), axis, forward
        )
        high = lax.ppermute(lax.slice_in_dim(block, 0, width, axis=dim), axis, backward)
        block = jnp.concatenate([low, block, high], axis=dim)
    return block


def swapped(block, axis, stride):
    count = lax.axis_size(axis)
    route = []
    for low in range(count):
        high = low | 1 << stride
        if high != low and high < count:
            route += [(low, high), (high, low)]
    return lax.ppermute(block, axis, route)


def pool_rows(values):
    shape = values.shape
    paired = values.reshape(shape[:-2] + (shape[-2] // 2, 2, shape[-1])).astype(jnp.float32)
    return lax.optimization_barrier(
        ((paired[..., 0, :] + paired[..., 1, :]) * 0.5).astype(jnp.bfloat16)
    )


def attend_groups(grouped_q, key_blocks, scale, mask):
    groups, key_rows, channels = key_blocks.shape
    model_width = channels // 2
    heads = grouped_q.shape[2]
    head_size = grouped_q.shape[3]
    keys = key_blocks[:, :, :model_width].reshape(groups, key_rows, heads, head_size)
    values = key_blocks[:, :, model_width:].reshape(groups, key_rows, heads, head_size)
    scores = (
        jnp.einsum("grhd,gkhd->grhk", grouped_q, keys, preferred_element_type=jnp.float32) * scale
    )
    weights = jnp.exp(scores)
    if mask is not None:
        weights = weights * mask[:, None, None, :]
    totals = jnp.sum(weights, axis=-1)
    numerator = jnp.einsum(
        "grhk,gkhd->grhd", weights.astype(jnp.bfloat16), values, preferred_element_type=jnp.float32
    )
    rows = groups * grouped_q.shape[1]
    return (numerator.reshape(rows, heads, head_size), totals.reshape(rows, heads))


def per_device(tokens, w_qkv, w_out):
    tok_rows = tokens.shape[0]
    model_width = w_out.shape[0]
    head_size = model_width // HEADS
    block_rows = BLOCK
    block_count = tok_rows // block_rows
    scale = head_size ** (-0.5)
    projected = jnp.dot(tokens, w_qkv, preferred_element_type=jnp.float32)
    queries = projected[:, :model_width].astype(jnp.bfloat16)
    keyvals = projected[:, model_width:].astype(jnp.bfloat16)
    channels = keyvals.shape[1]
    place_index = lax.axis_index(("gx", "gy"))
    device_count = lax.axis_size(("gx", "gy"))
    padded = padded_2(keyvals, ((("gx", "gy"), 0),), block_rows)
    padded_blocks = padded.reshape(block_count + 2, block_rows, channels)
    block_q = queries.reshape(block_count, block_rows, HEADS, head_size)
    block_ids = jnp.arange(block_count)[:, None]
    ones_mask = jnp.ones((block_count, block_rows), jnp.float32)
    first_off = (block_ids == 0) & (place_index == 0)
    last_off = (block_ids == block_count - 1) & (place_index == device_count - 1)
    shift_masks = [jnp.where(first_off, 0.0, ones_mask), None, jnp.where(last_off, 0.0, ones_mask)]
    numerator = jnp.zeros((tok_rows, HEADS, head_size), jnp.float32)
    totals = jnp.zeros((tok_rows, HEADS), jnp.float32)
    for shift in range(3):
        part_num, part_tot = attend_groups(
            block_q, padded_blocks[shift : shift + block_count], scale, shift_masks[shift]
        )
        numerator = numerator + part_num
        totals = totals + part_tot
    current = keyvals
    current = pool_rows(current)
    groups = block_count >> 1
    sibling = current.reshape(groups // 2, 2, block_rows, channels)[:, ::-1].reshape(
        groups, block_rows, channels
    )
    grouped_q = queries.reshape(groups, block_rows << 1, HEADS, head_size)
    part_num, part_tot = attend_groups(grouped_q, sibling, scale, None)
    numerator = numerator + part_num
    totals = totals + part_tot
    top_block = pool_rows(current)
    far_blocks = []
    level_bits = device_count.bit_length() - 1
    own_block = top_block
    for bit_num in range(level_bits):
        sibling = swapped(own_block, ("gx", "gy"), bit_num)
        far_blocks.append(sibling)
        if bit_num + 1 < level_bits:
            on_left = jnp.bitwise_and(jnp.right_shift(place_index, bit_num), 1) == 0
            joined = jnp.where(
                on_left,
                jnp.concatenate([own_block, sibling], axis=0),
                jnp.concatenate([sibling, own_block], axis=0),
            )
            own_block = pool_rows(joined)
    far_keys = jnp.concatenate(far_blocks, axis=0)
    far_count = far_keys.shape[0]
    far_k = far_keys[:, :model_width].reshape(far_count, HEADS, head_size)
    far_v = far_keys[:, model_width:].reshape(far_count, HEADS, head_size)
    head_q = queries.reshape(tok_rows, HEADS, head_size)
    far_scores = (
        jnp.einsum("thd,khd->thk", head_q, far_k, preferred_element_type=jnp.float32) * scale
    )
    far_weights = jnp.exp(far_scores)
    far_tot = jnp.sum(far_weights, axis=-1)
    far_num = jnp.einsum(
        "thk,khd->thd", far_weights.astype(jnp.bfloat16), far_v, preferred_element_type=jnp.float32
    )
    numerator = numerator + far_num
    totals = totals + far_tot
    attended = (numerator / totals[:, :, None]).reshape(tok_rows, model_width).astype(jnp.bfloat16)
    return jnp.dot(attended, w_out, preferred_element_type=jnp.float32).astype(jnp.bfloat16)


def solution(mesh):
    return jax.shard_map(
        per_device,
        mesh=mesh,
        in_specs=(P(("gx", "gy"), None), P(), P()),
        out_specs=P(("gx", "gy"), None),
        check_vma=False,
    )
```

profile of v0, /device:TPU:6, one launch (start us, length us, event | category | flops | bytes accessed | tf_op | source)
XLA Modules:
  0.0 139.0 jit_solution(1559512676078699478)
XLA Ops:
  3.7 13.5 %collective-permute-start.1 = (bf16[64,1024]{1,0:T(8,128)(2,1)}, bf16[64,1024]{1,0:T(8,128)(2,1)}, u32[]{:S(2)}, u32[]{:S(2)}) collective-permute-start(bf16[64,1024]{1,0:T(8,128)(2,1)} %get-tuple-element.9), channel_id=1, source_target_pairs={{1,0},{2,1},{3,2},{4,3},{5,4},{6,5},{7,6},{8,7},{9,8},{10,9},{11,1... | collective-permute-start | bytes 393224 | tf_op jit(solution)/shard_map/ppermute | solution.py:18
  17.2 1.9 %collective-permute-start = (bf16[64,1024]{1,0:T(8,128)(2,1)}, bf16[64,1024]{1,0:T(8,128)(2,1)}, u32[]{:S(2)}, u32[]{:S(2)}) collective-permute-start(bf16[64,1024]{1,0:T(8,128)(2,1)} %get-tuple-element.10), channel_id=1, source_target_pairs={{0,1},{1,2},{2,3},{3,4},{4,5},{5,6},{6,7},{7,8},{8,9},{9,10},{10,1... | collective-permute-start | bytes 393224 | tf_op jit(solution)/shard_map/ppermute | solution.py:15
  20.3 2.8 %reshape.222 = f32[128,2,1024]{2,1,0:T(2,128)} reshape(f32[256,1024]{1,0:T(8,128)} %get-tuple-element.12) | data formatting | bytes 2097152 | tf_op jit(solution)/shard_map/convert_element_type | solution.py:35
  23.1 2.4 %fusion.71 = (f32[128,1,1024]{2,1,0:T(1,128)S(1)}, f32[128,1,1024]{2,1,0:T(1,128)S(1)}) fusion(f32[128,2,1024]{2,1,0:T(2,128)} %reshape.222), kind=kLoop, calls=%fused_computation.119 | loop fusion | bytes 2097152 | tf_op jit(solution)/shard_map/slice | solution.py:37
  28.7 1.9 %collective-permute-start.2 = (bf16[64,1024]{1,0:T(8,128)(2,1)S(1)}, bf16[64,1024]{1,0:T(8,128)(2,1)}, u32[]{:S(2)}, u32[]{:S(2)}) collective-permute-start(bf16[64,1024]{1,0:T(8,128)(2,1)S(1)} %fusion.59), channel_id=1, source_target_pairs={{0,1},{1,0},{2,3},{3,2},{4,5},{5,4},{6,7},{7,6},{8,9},{9,8},{10,11... | collective-permute-start | bytes 393224 | tf_op jit(solution)/shard_map/ppermute | solution.py:30
  36.9 2.2 %fusion.90 = (f32[2,128,8]{1,2,0:T(8,128)}, bf16[2,128,8,64]{1,3,2,0:T(8,128)(2,1)S(1)}) fusion(bf16[2,128,8,64]{3,2,1,0:T(8,128)(2,1)} %reshape.232, bf16[2,64,8,64]{3,2,1,0:T(8,128)(2,1)} %reshape.215), kind=kOutput, calls=%fused_computation.138 | convolution fusion | flops 17168384 | bytes 663552 | tf_op jit(solution)/shard_map/grhd,gkhd->grhk/dot_general | solution.py:49
  43.8 1.9 %collective-permute-start.3 = (bf16[64,1024]{1,0:T(8,128)(2,1)S(1)}, bf16[64,1024]{1,0:T(8,128)(2,1)}, u32[]{:S(2)}, u32[]{:S(2)}) collective-permute-start(bf16[64,1024]{1,0:T(8,128)(2,1)S(1)} %fusion.60), channel_id=1, source_target_pairs={{0,2},{2,0},{1,3},{3,1},{4,6},{6,4},{5,7},{7,5},{8,10},{10,8},{9,1... | collective-permute-start | bytes 393224 | tf_op jit(solution)/shard_map/ppermute | solution.py:30
  48.3 2.1 %fusion.88 = (f32[4,64,8]{1,2,0:T(8,128)}, bf16[4,64,8,64]{1,3,2,0:T(8,128)(2,1)S(1)}) fusion(f32[4]{0:T(128)S(1)} %and_select_fusion.1, bf16[4,64,8,64]{3,2,1,0:T(8,128)(2,1)S(1)} %copy-done.8, bf16[4,64,8,64]{3,2,1,0:T(8,128)(2,1)} %reshape.206), kind=kOutput, calls=%fused_computation.136 | convolution fusion | flops 17299456 | bytes 794640 | tf_op jit(solution)/shard_map/grhd,gkhd->grhk/dot_general | solution.py:49
  52.7 2.1 %reshape.211 = bf16[4,64,8,64]{3,2,1,0:T(8,128)(2,1)} reshape(bf16[4,64,512]{2,1,0:T(8,128)(2,1)} %get-tuple-element.13) | data formatting | bytes 524288 | tf_op jit(solution)/shard_map/reshape | solution.py:46
  58.4 1.9 %collective-permute-start.4 = (bf16[64,1024]{1,0:T(8,128)(2,1)S(1)}, bf16[64,1024]{1,0:T(8,128)(2,1)S(1)}, u32[]{:S(2)}, u32[]{:S(2)}) collective-permute-start(bf16[64,1024]{1,0:T(8,128)(2,1)S(1)} %fusion.61), channel_id=1, source_target_pairs={{0,4},{4,0},{1,5},{5,1},{2,6},{6,2},{3,7},{7,3},{8,12},{12,8},{9,1... | collective-permute-start | bytes 393224 | tf_op jit(solution)/shard_map/ppermute | solution.py:30
  63.2 6.7 %collective-permute-done.4 = bf16[64,1024]{1,0:T(8,128)(2,1)S(1)} collective-permute-done((bf16[64,1024]{1,0:T(8,128)(2,1)S(1)}, bf16[64,1024]{1,0:T(8,128)(2,1)S(1)}, u32[]{:S(2)}, u32[]{:S(2)}) %collective-permute-start.4) | collective-permute-done | bytes 131104 | tf_op jit(solution)/shard_map/ppermute | solution.py:30
  72.7 3.3 %collective-permute-start.5 = (bf16[64,1024]{1,0:T(8,128)(2,1)S(1)}, bf16[64,1024]{1,0:T(8,128)(2,1)S(1)}, u32[]{:S(2)}, u32[]{:S(2)}) collective-permute-start(bf16[64,1024]{1,0:T(8,128)(2,1)S(1)} %fusion.62), channel_id=1, source_target_pairs={{0,8},{8,0},{1,9},{9,1},{2,10},{10,2},{3,11},{11,3},{4,12},{12,4},... | collective-permute-start | bytes 393224 | tf_op jit(solution)/shard_map/ppermute | solution.py:30
  77.3 7.5 %collective-permute-done.5 = bf16[64,1024]{1,0:T(8,128)(2,1)S(1)} collective-permute-done((bf16[64,1024]{1,0:T(8,128)(2,1)S(1)}, bf16[64,1024]{1,0:T(8,128)(2,1)S(1)}, u32[]{:S(2)}, u32[]{:S(2)}) %collective-permute-start.5) | collective-permute-done | bytes 131104 | tf_op jit(solution)/shard_map/ppermute | solution.py:30
  85.6 1.9 %collective-permute-start.6 = (bf16[64,1024]{1,0:T(8,128)(2,1)S(1)}, bf16[64,1024]{1,0:T(8,128)(2,1)S(1)}, u32[]{:S(2)}, u32[]{:S(2)}) collective-permute-start(bf16[64,1024]{1,0:T(8,128)(2,1)S(1)} %fusion.63), channel_id=1, source_target_pairs={{0,16},{16,0},{1,17},{17,1},{2,18},{18,2},{3,19},{19,3},{4,20},{20... | collective-permute-start | bytes 393224 | tf_op jit(solution)/shard_map/ppermute | solution.py:30
  87.6 5.2 %collective-permute-done.6 = bf16[64,1024]{1,0:T(8,128)(2,1)S(1)} collective-permute-done((bf16[64,1024]{1,0:T(8,128)(2,1)S(1)}, bf16[64,1024]{1,0:T(8,128)(2,1)S(1)}, u32[]{:S(2)}, u32[]{:S(2)}) %collective-permute-start.6) | collective-permute-done | bytes 131104 | tf_op jit(solution)/shard_map/ppermute | solution.py:30
  93.7 2.6 %collective-permute-start.7 = (bf16[64,1024]{1,0:T(8,128)(2,1)S(1)}, bf16[64,1024]{1,0:T(8,128)(2,1)S(1)}, u32[]{:S(2)}, u32[]{:S(2)}) collective-permute-start(bf16[64,1024]{1,0:T(8,128)(2,1)S(1)} %fusion.64), channel_id=1, source_target_pairs={{0,32},{32,0},{1,33},{33,1},{2,34},{34,2},{3,35},{35,3},{4,36},{36... | collective-permute-start | bytes 393224 | tf_op jit(solution)/shard_map/ppermute | solution.py:30
  99.6 2.7 %add.99 = f32[256,8,64]{0,2,1:T(8,128)} reshape(f32[4,64,8,64]{1,0,3,2:T(4,128)} %copy.422) | data formatting | bytes 1048576 | tf_op jit(solution)/shard_map/add | solution.py:89
  104.7 6.8 %collective-permute-start.8 = (bf16[64,1024]{1,0:T(8,128)(2,1)S(1)}, bf16[64,1024]{1,0:T(8,128)(2,1)S(1)}, u32[]{:S(2)}, u32[]{:S(2)}) collective-permute-start(bf16[64,1024]{1,0:T(8,128)(2,1)S(1)} %fusion.65), channel_id=1, source_target_pairs={{0,64},{64,0},{1,65},{65,1},{2,66},{66,2},{3,67},{67,3},{4,68},{68... | collective-permute-start | bytes 393224 | tf_op jit(solution)/shard_map/ppermute | solution.py:30
  112.8 4.4 %collective-permute-done.8 = bf16[64,1024]{1,0:T(8,128)(2,1)S(1)} collective-permute-done((bf16[64,1024]{1,0:T(8,128)(2,1)S(1)}, bf16[64,1024]{1,0:T(8,128)(2,1)S(1)}, u32[]{:S(2)}, u32[]{:S(2)}) %collective-permute-start.8) | collective-permute-done | bytes 131104 | tf_op jit(solution)/shard_map/ppermute | solution.py:30
  118.1 3.1 %collective-permute-start.9 = (bf16[64,1024]{1,0:T(8,128)(2,1)S(1)}, bf16[64,1024]{1,0:T(8,128)(2,1)S(1)}, u32[]{:S(2)}, u32[]{:S(2)}) collective-permute-start(bf16[64,1024]{1,0:T(8,128)(2,1)S(1)} %fusion.66), channel_id=1, source_target_pairs={{0,128},{128,0},{1,129},{129,1},{2,130},{130,2},{3,131},{131,3},{4... | collective-permute-start | bytes 393224 | tf_op jit(solution)/shard_map/ppermute | solution.py:30
  122.5 2.5 %collective-permute-done.9 = bf16[64,1024]{1,0:T(8,128)(2,1)S(1)} collective-permute-done((bf16[64,1024]{1,0:T(8,128)(2,1)S(1)}, bf16[64,1024]{1,0:T(8,128)(2,1)S(1)}, u32[]{:S(2)}, u32[]{:S(2)}) %collective-permute-start.9) | collective-permute-done | bytes 131104 | tf_op jit(solution)/shard_map/ppermute | solution.py:30
  125.8 4.6 %collective-permute-start.10 = (bf16[64,1024]{1,0:T(8,128)(2,1)S(1)}, bf16[64,1024]{1,0:T(8,128)(2,1)S(1)}, u32[]{:S(2)}, u32[]{:S(2)}) collective-permute-start(bf16[64,1024]{1,0:T(8,128)(2,1)S(1)} %fusion.67), channel_id=1, source_target_pairs={{0,256},{256,0},{1,257},{257,1},{2,258},{258,2},{3,259},{259,3},{4... | collective-permute-start | bytes 393224 | tf_op jit(solution)/shard_map/ppermute | solution.py:30
  130.5 3.7 %collective-permute-done.10 = bf16[64,1024]{1,0:T(8,128)(2,1)S(1)} collective-permute-done((bf16[64,1024]{1,0:T(8,128)(2,1)S(1)}, bf16[64,1024]{1,0:T(8,128)(2,1)S(1)}, u32[]{:S(2)}, u32[]{:S(2)}) %collective-permute-start.10) | collective-permute-done | bytes 131104 | tf_op jit(solution)/shard_map/ppermute | solution.py:30
  134.9 2.0 %bitcast_reduce_fusion = (f32[256,8]{0,1:T(8,128)S(1)}, f32[8,576,256]{2,1,0:T(8,128)S(1)}) fusion(bf16[576,8,64]{0,2,1:T(8,128)(2,1)S(1)} %bitcast.96, bf16[256,8,64]{0,2,1:T(8,128)(2,1)} %bitcast.103), kind=kOutput, calls=%fused_computation | convolution fusion | flops 153352192 | bytes 5578752 | tf_op jit(solution)/shard_map/thd,khd->thk/dot_general | solution.py:122
  (126 shorter events, 48.6 us)
Async XLA Ops:
  3.7 42.1 %collective-permute-start.1 = (bf16[64,1024]{1,0:T(8,128)(2,1)}, bf16[64,1024]{1,0:T(8,128)(2,1)}, u32[]{:S(2)}, u32[]{:S(2)}) collective-permute-start(bf16[64,1024]{1,0:T(8,128)(2,1)} %get-tuple-element.9), channel_id=1, source_target_pairs={{1,0},{2,1},{3,2},{4,3},{5,4},{6,5},{7,6},{8,7},{9,8},{10,9},{11,1... | collective-permute-start | bytes 393224 | tf_op jit(solution)/shard_map/ppermute | solution.py:18
  17.2 28.6 %collective-permute-start = (bf16[64,1024]{1,0:T(8,128)(2,1)}, bf16[64,1024]{1,0:T(8,128)(2,1)}, u32[]{:S(2)}, u32[]{:S(2)}) collective-permute-start(bf16[64,1024]{1,0:T(8,128)(2,1)} %get-tuple-element.10), channel_id=1, source_target_pairs={{0,1},{1,2},{2,3},{3,4},{4,5},{5,6},{6,7},{7,8},{8,9},{9,10},{10,1... | collective-permute-start | bytes 393224 | tf_op jit(solution)/shard_map/ppermute | solution.py:15
  28.7 13.3 %collective-permute-start.2 = (bf16[64,1024]{1,0:T(8,128)(2,1)S(1)}, bf16[64,1024]{1,0:T(8,128)(2,1)}, u32[]{:S(2)}, u32[]{:S(2)}) collective-permute-start(bf16[64,1024]{1,0:T(8,128)(2,1)S(1)} %fusion.59), channel_id=1, source_target_pairs={{0,1},{1,0},{2,3},{3,2},{4,5},{5,4},{6,7},{7,6},{8,9},{9,8},{10,11... | collective-permute-start | bytes 393224 | tf_op jit(solution)/shard_map/ppermute | solution.py:30
  35.9 3.3 %copy-start.7 = (bf16[4,64,8,64]{3,2,1,0:T(8,128)(2,1)S(1)}, bf16[4,64,8,64]{3,2,1,0:T(8,128)(2,1)}, u32[]{:S(2)}) copy-start(bf16[4,64,8,64]{3,2,1,0:T(8,128)(2,1)} %reshape.207) | copy-start | bytes 786436
  36.9 2.2 %copy-start.11 = (bf16[4,64,8,64]{3,2,1,0:T(8,128)(2,1)S(1)}, bf16[4,64,8,64]{3,2,1,0:T(8,128)(2,1)}, u32[]{:S(2)}) copy-start(bf16[4,64,8,64]{3,2,1,0:T(8,128)(2,1)} %reshape.209) | copy-start | bytes 786436
  43.8 10.9 %collective-permute-start.3 = (bf16[64,1024]{1,0:T(8,128)(2,1)S(1)}, bf16[64,1024]{1,0:T(8,128)(2,1)}, u32[]{:S(2)}, u32[]{:S(2)}) collective-permute-start(bf16[64,1024]{1,0:T(8,128)(2,1)S(1)} %fusion.60), channel_id=1, source_target_pairs={{0,2},{2,0},{1,3},{3,1},{4,6},{6,4},{5,7},{7,5},{8,10},{10,8},{9,1... | collective-permute-start | bytes 393224 | tf_op jit(solution)/shard_map/ppermute | solution.py:30
  57.9 2.5 %copy-start.9 = (bf16[4,64,8,64]{3,2,1,0:T(8,128)(2,1)S(1)}, bf16[4,64,8,64]{3,2,1,0:T(8,128)(2,1)}, u32[]{:S(2)}) copy-start(bf16[4,64,8,64]{3,2,1,0:T(8,128)(2,1)} %reshape.207) | copy-start | bytes 786436
  57.9 2.5 %copy-start.10 = (bf16[4,64,8,64]{3,2,1,0:T(8,128)(2,1)S(1)}, bf16[4,64,8,64]{3,2,1,0:T(8,128)(2,1)}, u32[]{:S(2)}) copy-start(bf16[4,64,8,64]{3,2,1,0:T(8,128)(2,1)} %reshape.211) | copy-start | bytes 786436
  58.4 11.5 %collective-permute-start.4 = (bf16[64,1024]{1,0:T(8,128)(2,1)S(1)}, bf16[64,1024]{1,0:T(8,128)(2,1)S(1)}, u32[]{:S(2)}, u32[]{:S(2)}) collective-permute-start(bf16[64,1024]{1,0:T(8,128)(2,1)S(1)} %fusion.61), channel_id=1, source_target_pairs={{0,4},{4,0},{1,5},{5,1},{2,6},{6,2},{3,7},{7,3},{8,12},{12,8},{9,1... | collective-permute-start | bytes 393224 | tf_op jit(solution)/shard_map/ppermute | solution.py:30
  72.1 3.8 %copy-start.5 = (bf16[4,64,512]{1,2,0:T(8,128)(2,1)S(1)}, bf16[4,64,512]{1,2,0:T(8,128)(2,1)}, u32[]{:S(2)}) copy-start(bf16[4,64,512]{1,2,0:T(8,128)(2,1)} %copy.418) | copy-start | bytes 786436
  72.2 3.8 %copy-start.14 = (bf16[4,64,8,64]{1,3,2,0:T(8,128)(2,1)S(1)}, bf16[4,64,8,64]{1,3,2,0:T(8,128)(2,1)}, u32[]{:S(2)}) copy-start(bf16[4,64,8,64]{1,3,2,0:T(8,128)(2,1)} %get-tuple-element.44) | copy-start | bytes 786436
  72.7 12.0 %collective-permute-start.5 = (bf16[64,1024]{1,0:T(8,128)(2,1)S(1)}, bf16[64,1024]{1,0:T(8,128)(2,1)S(1)}, u32[]{:S(2)}, u32[]{:S(2)}) collective-permute-start(bf16[64,1024]{1,0:T(8,128)(2,1)S(1)} %fusion.62), channel_id=1, source_target_pairs={{0,8},{8,0},{1,9},{9,1},{2,10},{10,2},{3,11},{11,3},{4,12},{12,4},... | collective-permute-start | bytes 393224 | tf_op jit(solution)/shard_map/ppermute | solution.py:30
  84.8 2.8 %copy-start.15 = (f32[4,64,8]{1,2,0:T(8,128)S(1)}, f32[4,64,8]{1,2,0:T(8,128)}, u32[]{:S(2)}) copy-start(f32[4,64,8]{1,2,0:T(8,128)} %get-tuple-element.47) | copy-start | bytes 24580
  84.8 2.8 %copy-start.16 = (f32[4,64,8]{1,2,0:T(8,128)S(1)}, f32[4,64,8]{1,2,0:T(8,128)}, u32[]{:S(2)}) copy-start(f32[4,64,8]{1,2,0:T(8,128)} %get-tuple-element.45) | copy-start | bytes 24580
  84.8 2.8 %copy-start.17 = (f32[4,64,8]{1,2,0:T(8,128)S(1)}, f32[4,64,8]{1,2,0:T(8,128)}, u32[]{:S(2)}) copy-start(f32[4,64,8]{1,2,0:T(8,128)} %get-tuple-element.43) | copy-start | bytes 24580
  85.6 7.2 %collective-permute-start.6 = (bf16[64,1024]{1,0:T(8,128)(2,1)S(1)}, bf16[64,1024]{1,0:T(8,128)(2,1)S(1)}, u32[]{:S(2)}, u32[]{:S(2)}) collective-permute-start(bf16[64,1024]{1,0:T(8,128)(2,1)S(1)} %fusion.63), channel_id=1, source_target_pairs={{0,16},{16,0},{1,17},{17,1},{2,18},{18,2},{3,19},{19,3},{4,20},{20... | collective-permute-start | bytes 393224 | tf_op jit(solution)/shard_map/ppermute | solution.py:30
  93.2 4.7 %copy-start.1 = (f32[4,64,8,64]{1,3,2,0:T(8,128)S(1)}, f32[4,64,8,64]{1,3,2,0:T(8,128)}, u32[]{:S(2)}) copy-start(f32[4,64,8,64]{1,3,2,0:T(8,128)} %fusion.2) | copy-start | bytes 1572868
  93.7 10.1 %collective-permute-start.7 = (bf16[64,1024]{1,0:T(8,128)(2,1)S(1)}, bf16[64,1024]{1,0:T(8,128)(2,1)S(1)}, u32[]{:S(2)}, u32[]{:S(2)}) collective-permute-start(bf16[64,1024]{1,0:T(8,128)(2,1)S(1)} %fusion.64), channel_id=1, source_target_pairs={{0,32},{32,0},{1,33},{33,1},{2,34},{34,2},{3,35},{35,3},{4,36},{36... | collective-permute-start | bytes 393224 | tf_op jit(solution)/shard_map/ppermute | solution.py:30
  104.7 12.5 %collective-permute-start.8 = (bf16[64,1024]{1,0:T(8,128)(2,1)S(1)}, bf16[64,1024]{1,0:T(8,128)(2,1)S(1)}, u32[]{:S(2)}, u32[]{:S(2)}) collective-permute-start(bf16[64,1024]{1,0:T(8,128)(2,1)S(1)} %fusion.65), channel_id=1, source_target_pairs={{0,64},{64,0},{1,65},{65,1},{2,66},{66,2},{3,67},{67,3},{4,68},{68... | collective-permute-start | bytes 393224 | tf_op jit(solution)/shard_map/ppermute | solution.py:30
  118.1 6.9 %collective-permute-start.9 = (bf16[64,1024]{1,0:T(8,128)(2,1)S(1)}, bf16[64,1024]{1,0:T(8,128)(2,1)S(1)}, u32[]{:S(2)}, u32[]{:S(2)}) collective-permute-start(bf16[64,1024]{1,0:T(8,128)(2,1)S(1)} %fusion.66), channel_id=1, source_target_pairs={{0,128},{128,0},{1,129},{129,1},{2,130},{130,2},{3,131},{131,3},{4... | collective-permute-start | bytes 393224 | tf_op jit(solution)/shard_map/ppermute | solution.py:30
  125.3 5.2 %copy-start.6 = (bf16[576,1024]{1,0:T(8,128)(2,1)S(1)}, bf16[576,1024]{1,0:T(8,128)(2,1)}, u32[]{:S(2)}) copy-start(bf16[576,1024]{1,0:T(8,128)(2,1)} %constant_dynamic-update-slice_fusion.3) | copy-start | bytes 3538948
  125.8 8.4 %collective-permute-start.10 = (bf16[64,1024]{1,0:T(8,128)(2,1)S(1)}, bf16[64,1024]{1,0:T(8,128)(2,1)S(1)}, u32[]{:S(2)}, u32[]{:S(2)}) collective-permute-start(bf16[64,1024]{1,0:T(8,128)(2,1)S(1)} %fusion.67), channel_id=1, source_target_pairs={{0,256},{256,0},{1,257},{257,1},{2,258},{258,2},{3,259},{259,3},{4... | collective-permute-start | bytes 393224 | tf_op jit(solution)/shard_map/ppermute | solution.py:30
  134.9 2.1 %copy-start.2 = (f32[256,8,64]{0,2,1:T(8,128)S(1)}, f32[256,8,64]{0,2,1:T(8,128)}, u32[]{:S(2)}) copy-start(f32[256,8,64]{0,2,1:T(8,128)} %add.99) | copy-start | bytes 1572868
  134.9 2.1 %copy-start.3 = (f32[2,8,8,8,128]{4,3,2,1,0:T(8,128)S(1)}, f32[2,8,8,8,128]{4,3,2,1,0:T(8,128)}, u32[]{:S(2)}) copy-start(f32[2,8,8,8,128]{4,3,2,1,0:T(8,128)} %convolution_bitcast_fusion) | copy-start | bytes 1572868
  (6 other events, 8.1 us)
where the time goes:
time: 141 us; the launch traced here: 139 us
  starting transfers between devices  43.5 us (31%)
  local copies, waits for them, and re-layouts  41.4 us (29%)
  waiting for transfers between devices  29.9 us (21%)
  matrix products  16.3 us (12%)
  other arithmetic  7.14 us (5%)
    ppermute x9, waiting for transfers between devices, swapped(): return lax.ppermute(block, axis, route)  29.9 us
    ppermute x9, starting transfers between devices, swapped(): return lax.ppermute(block, axis, route)  28.1 us
    ppermute x1, starting transfers between devices, padded_2(): lax.ppermute(lax.slice_in_dim(block, 0, width, axis=dim), axis, backward)  13.5 us
    convert_element_type x10, local copies, waits for them, and re-layouts, pool_rows(): values.reshape(shape[:-2] + (shape[-2] // 2, 2, shape[-1]))  8.49 us
    unnamed x46, local copies, waits for them, and re-layouts  8.28 us
    dot_general x4, matrix products, attend_groups(): jnp.einsum('grhd,gkhd->grhk', grouped_q, keys, preferred_element_type=jnp...  8.02 us
    slice x10, local copies, waits for them, and re-layouts, pool_rows(): paired[..., 0, :] + paired[..., 1, :]  7.38 us
    reshape x4, local copies, waits for them, and re-layouts, attend_groups(): key_blocks[:, :, :model_width].reshape(groups, key_rows, heads, head_size)  5.11 us
  transfers between devices with their start and end apart: 11, of which 6 were waited for; matrix products, arithmetic and copies ran while one was open for 32% of the time, Pallas kernels for 0%

commit v1 on v0

v1 whole, which is shorter than its diff:
```python
import functools

import jax
import jax.numpy as jnp
import numpy as np
from jax import lax
from jax.experimental import pallas as pl
from jax.experimental.pallas import tpu as pltpu
from jax.sharding import PartitionSpec as P

HEADS = 8
BLOCK = 64
AXES = ("gx", "gy")
ROUNDS = (
    ("core", 0, "ag"),
    ("z1", 1, "ag"),
    ("z2", 2, "ag"),
    ("z4", 3, "pp"),
    ("y1", 4, "pp"),
    ("y2", 5, "ag"),
    ("y4", 6, "pp"),
    ("x1", 7, "ag"),
    ("x2", 8, "ag"),
)
FAR8 = (6, 7, 4, 5, 2, 3, 0, 1)
FAR4 = (3, 2, 1, 0)


def partners(bit, count):
    route = []
    for index in range(count):
        if bit == 3:
            z = index >> 1 & 7
            route.append(index & ~14 | FAR8[z] << 1)
        elif bit == 6:
            y = index >> 4 & 7
            route.append(index & ~112 | FAR8[y] << 4)
        elif bit == 8:
            x = index >> 7 & 3
            route.append(index & ~384 | FAR4[x] << 7)
        else:
            route.append(index ^ 1 << bit)
    return route


def vmem(count):
    return [pl.BlockSpec(memory_space=pltpu.VMEM)] * count


SMEM = pl.BlockSpec(memory_space=pltpu.SMEM)


def call(kernel, outs, in_specs, *args, flops=0, scratch=()):
    return pl.pallas_call(
        kernel,
        out_shape=outs,
        in_specs=in_specs,
        out_specs=jax.tree.map(lambda _: pl.BlockSpec(memory_space=pltpu.VMEM), outs),
        scratch_shapes=list(scratch),
        compiler_params=pltpu.CompilerParams(vmem_limit_bytes=24 * 2**20),
        cost_estimate=pl.CostEstimate(flops=flops, bytes_accessed=2**20, transcendentals=0),
    )(*args)


def pool_matrix(rows):
    r = lax.broadcasted_iota(jnp.int32, (rows, 2 * rows), 0)
    c = lax.broadcasted_iota(jnp.int32, (rows, 2 * rows), 1)
    return jnp.where(c >> 1 == r, 0.5, 0.0).astype(jnp.bfloat16)


def pooled(block):
    return jnp.dot(
        pool_matrix(block.shape[0] // 2), block, preferred_element_type=jnp.float32
    ).astype(jnp.bfloat16)


def project_kernel(place, x_ref, w_hbm, kv_ref, near_ref, other_ref, w_buf, sems):
    model = x_ref.shape[1]
    width = w_buf.shape[2]
    steps = w_buf.shape[0]
    copies = []
    for step in range(steps):
        columns = pl.ds(model + step * width, width)
        copy = pltpu.make_async_copy(w_hbm.at[:, columns], w_buf.at[step], sems.at[step])
        copy.start()
        copies.append(copy)
    core = place[0]
    x = x_ref[...]
    for step in range(steps):
        copies[step].wait()
        lanes = slice(step * width, (step + 1) * width)
        part = jnp.dot(x, w_buf[step], preferred_element_type=jnp.float32).astype(jnp.bfloat16)
        kv_ref[:, lanes] = part
        near_ref[BLOCK:, lanes] = pooled(pooled(part))
    last = x_ref.shape[0] - BLOCK
    low = pl.multiple_of(core * last, BLOCK)
    high = pl.multiple_of((1 - core) * last, BLOCK)
    near_ref[:BLOCK, :] = kv_ref[pl.ds(high, BLOCK), :]
    other_ref[...] = kv_ref[pl.ds(low, BLOCK), :]


def pool_kernel(*refs):
    ins, out_ref = refs[:-1], refs[-1]
    half = BLOCK // len(ins)
    for num, ref in enumerate(ins):
        rows = ref.shape[0]
        block = ref[...]
        if len(ins) == 1:
            out_ref[...] = pooled(block)
        else:
            out_ref[num * half : (num + 1) * half, :] = pooled(block)


def pool_near_kernel(near_ref, out_ref):
    out_ref[: BLOCK // 2, :] = pooled(near_ref[BLOCK : 2 * BLOCK, :])
    out_ref[BLOCK // 2 :, :] = pooled(near_ref[3 * BLOCK :, :])


def attend_pair(q, keys, values, ones):
    rows = q.shape[0]
    lane = lax.broadcasted_iota(jnp.int32, q.shape, 1)
    first = lane < 64
    zero = jnp.zeros_like(q)
    both = jnp.concatenate([jnp.where(first, q, zero), jnp.where(first, zero, q)], axis=0)
    scores = lax.dot_general(
        both, keys, (((1,), (1,)), ((), ())), preferred_element_type=jnp.float32
    )
    weights = jnp.exp(scores).astype(jnp.bfloat16)
    sums = jnp.dot(
        weights, jnp.concatenate([values, ones], axis=1), preferred_element_type=jnp.float32
    )
    num = jnp.where(first, sums[:rows, :128], sums[rows:, :128])
    tot = jnp.where(first, sums[:rows, 128:], sums[rows:, 128:])
    return num, tot


def local_kernel(place, x_ref, w_ref, kv_ref, near_ref, other_ref, q_ref, num_ref, tot_ref, pad, l1):
    rows, model = x_ref.shape
    blocks = rows // BLOCK
    q_ref[...] = (
        jnp.dot(x_ref[...], w_ref[...], preferred_element_type=jnp.float32)
        .astype(jnp.bfloat16) * jnp.bfloat16(0.125)
    )
    core = place[0]
    sib_halo = near_ref[pl.ds(pl.multiple_of((1 - core) * 2 * BLOCK, BLOCK), BLOCK), :]
    other = other_ref[...]
    is_first = core == 0
    pad[:BLOCK, :] = jnp.where(is_first, other, sib_halo)
    pad[BLOCK : BLOCK + rows, :] = kv_ref[...]
    pad[BLOCK + rows :, :] = jnp.where(is_first, sib_halo, other)
    l1[...] = pooled(kv_ref[...])
    key_row = lax.broadcasted_iota(jnp.int32, (4 * BLOCK, 128), 0)
    for i in range(blocks):
        ones = jnp.ones((4 * BLOCK, 128), jnp.float32)
        if i == 0:
            ones = jnp.where((key_row < BLOCK) & (place[1] == 1), 0.0, ones)
        if i == blocks - 1:
            ones = jnp.where((key_row >= 2 * BLOCK) & (key_row < 3 * BLOCK) & (place[2] == 1), 0.0, ones)
        ones = ones.astype(jnp.bfloat16)
        sib = (i >> 1) ^ 1
        here = slice(i * BLOCK, (i + 1) * BLOCK)
        for lanes in range(0, model, 128):
            kl = slice(lanes, lanes + 128)
            vl = slice(model + lanes, model + lanes + 128)
            keys = jnp.concatenate(
                [pad[i * BLOCK : (i + 3) * BLOCK, kl], l1[sib * BLOCK : (sib + 1) * BLOCK, kl]], axis=0
            )
            values = jnp.concatenate(
                [pad[i * BLOCK : (i + 3) * BLOCK, vl], l1[sib * BLOCK : (sib + 1) * BLOCK, vl]], axis=0
            )
            num, tot = attend_pair(q_ref[here, kl], keys, values, ones)
            num_ref[here, kl] = num
            tot_ref[here, kl] = tot


def sibling_rows(place, kinds, refs):
    rows = []
    for (kind, bit), ref in zip(kinds, refs):
        if kind == "near":
            start = (1 - place[0]) * 2 * BLOCK + BLOCK
        elif kind == "ag":
            start = (1 - place[3 + bit]) * BLOCK
        else:
            start = None
        rows.append((ref, start))
    return rows


def far_sums(place, kinds, refs, q_ref, lanes, model):
    keys, values = [], []
    for ref, start in sibling_rows(place, kinds, refs):
        at = slice(None) if start is None else pl.ds(pl.multiple_of(start, BLOCK), BLOCK)
        keys.append(ref[at, lanes : lanes + 128])
        values.append(ref[at, model + lanes : model + lanes + 128])
    keys = jnp.concatenate(keys, axis=0)
    values = jnp.concatenate(values, axis=0)
    ones = jnp.ones(values.shape, jnp.bfloat16)
    return attend_pair(q_ref[:, lanes : lanes + 128], keys, values, ones)


def far_kernel(kinds, place, q_ref, num_in, tot_in, *refs):
    num_ref, tot_ref = refs[-2:]
    model = q_ref.shape[1]
    for lanes in range(0, model, 128):
        at = slice(lanes, lanes + 128)
        num, tot = far_sums(place, kinds, refs[:-2], q_ref, lanes, model)
        num_ref[:, at] = num_in[:, at] + num
        tot_ref[:, at] = tot_in[:, at] + tot


def final_kernel(kinds, place, q_ref, num_in, tot_in, w_ref, *refs):
    out_ref, att = refs[-2:]
    model = q_ref.shape[1]
    for lanes in range(0, model, 128):
        at = slice(lanes, lanes + 128)
        num, tot = far_sums(place, kinds, refs[:-2], q_ref, lanes, model)
        att[:, at] = ((num_in[:, at] + num) / (tot_in[:, at] + tot)).astype(jnp.bfloat16)
    out_ref[...] = jnp.dot(att[...], w_ref[...], preferred_element_type=jnp.float32).astype(
        jnp.bfloat16
    )


def per_device(tokens, w_qkv, w_out):
    rows, model = tokens.shape
    index = lax.axis_index(AXES)
    count = lax.axis_size(AXES)
    bits = count.bit_length() - 1
    place = jnp.stack(
        [index & 1, (index == 0).astype(jnp.int32), (index == count - 1).astype(jnp.int32)]
        + [(index >> bit) & 1 for bit in range(bits)]
    ).astype(jnp.int32)
    bf16 = lambda *shape: jax.ShapeDtypeStruct(shape, jnp.bfloat16)
    f32 = lambda *shape: jax.ShapeDtypeStruct(shape, jnp.float32)
    steps = 4
    width = 2 * model // steps
    kv, near, other = call(
        project_kernel,
        (bf16(rows, 2 * model), bf16(2 * BLOCK, 2 * model), bf16(BLOCK, 2 * model)),
        [SMEM, *vmem(1), pl.BlockSpec(memory_space=pl.ANY)],
        place, tokens, w_qkv,
        flops=4 * rows * model * model,
        scratch=(pltpu.VMEM((steps, model, width), jnp.bfloat16), pltpu.SemaphoreType.DMA((steps,))),
    )
    pairs = [[i, i ^ 1] for i in range(0, count, 2)]
    near_all = lax.all_gather(near, AXES, axis_index_groups=pairs, tiled=True)
    swap = [(i, i + 1) for i in range(1, count - 1, 2)]
    swap += [(j, i) for i, j in swap]
    other_halo = lax.ppermute(other, AXES, swap)

    own = call(pool_near_kernel, bf16(BLOCK, 2 * model), vmem(1), near_all)
    found = [(("near", 0), near_all)]
    for _, bit, mode in ROUNDS[1:bits]:
        to = partners(bit, count)
        if mode == "ag":
            groups = [[i, to[i]] for i in range(count) if not i >> bit & 1]
            got = lax.all_gather(own, AXES, axis_index_groups=groups, tiled=True)
            ins = (got,)
        else:
            got = lax.ppermute(own, AXES, list(enumerate(to)))
            ins = (own, got)
        found.append(((mode, bit), got))
        if bit < bits - 1:
            own = call(pool_kernel, bf16(BLOCK, 2 * model), vmem(len(ins)), *ins)

    w_q = w_qkv[:, :model]
    q, num, tot = call(
        local_kernel,
        (bf16(rows, model), f32(rows, model), f32(rows, model)),
        [SMEM, *vmem(5)],
        place, tokens, w_q, kv, near_all, other_halo,
        flops=10**9,
        scratch=(
            pltpu.VMEM((rows + 2 * BLOCK, 2 * model), jnp.bfloat16),
            pltpu.VMEM((rows // 2, 2 * model), jnp.bfloat16),
        ),
    )
    for part in (found[0:4], found[4:8]):
        kinds = tuple(kind for kind, _ in part)
        num, tot = call(
            functools.partial(far_kernel, kinds),
            (f32(rows, model), f32(rows, model)),
            [SMEM, *vmem(3 + len(part))],
            place, q, num, tot, *[got for _, got in part],
            flops=10**9,
        )
    part = found[8:]
    return call(
        functools.partial(final_kernel, tuple(kind for kind, _ in part)),
        bf16(rows, model),
        [SMEM, *vmem(4 + len(part))],
        place, q, num, tot, w_out, *[got for _, got in part],
        flops=10**9,
        scratch=(pltpu.VMEM((rows, model), jnp.bfloat16),),
    )


def solution(mesh):
    return jax.shard_map(
        per_device,
        mesh=mesh,
        in_specs=(P(AXES, None), P(), P()),
        out_specs=P(AXES, None),
        check_vma=False,
    )
```

time: 141 us -> 84.9 us (0.60)
  the two profiles are of different devices: /device:TPU:6 before, /device:TPU:8 now
where the time goes in v1:
time: 84.9 us; the launch traced here: 84.6 us
  blocking collectives  40.8 us (48%)
  starting transfers between devices  22.9 us (27%)
  Pallas kernels  11 us (13%)
  waiting for transfers between devices  6.21 us (7%)
  local copies, waits for them, and re-layouts  3.53 us (4%)
    all_gather x5, blocking collectives, per_device(): got = lax.all_gather(own, AXES, axis_index_groups=groups, tiled=True)  38.6 us
    ppermute x3, starting transfers between devices, per_device(): got = lax.ppermute(own, AXES, list(enumerate(to)))  18.2 us
    pallas_call x13, Pallas kernels, call(): pl.pallas_call(kernel, out_shape=outs, in_specs=in_specs, out_specs=jax.t...  11 us
    ppermute x3, waiting for transfers between devices, per_device(): got = lax.ppermute(own, AXES, list(enumerate(to)))  6.2 us
    ppermute x1, starting transfers between devices, per_device(): other_halo = lax.ppermute(other, AXES, swap)  4.62 us
    unnamed x8, local copies, waits for them, and re-layouts  2.36 us
    all_gather x1, blocking collectives, per_device(): near_all = lax.all_gather(near, AXES, axis_index_groups=pairs, tiled=True)  2.18 us
  transfers between devices with their start and end apart: 4, of which 2 were waited for; matrix products, arithmetic and copies ran while one was open for 1% of the time, Pallas kernels for 4%

profile of v1, /device:TPU:8, one launch (start us, length us, event | category | flops | bytes accessed | tf_op | source)
XLA Modules:
  0.0 84.6 jit_solution(17262085206622521046)
XLA Ops:
  0.1 1.4 %copy-done = bf16[512,1536]{1,0:T(8,128)(2,1)S(1)} copy-done((bf16[512,1536]{1,0:T(8,128)(2,1)S(1)}, bf16[512,1536]{1,0:T(8,128)(2,1)}, u32[]{:S(2)}) %copy-start) | copy-done | bytes 1572888
  1.5 0.9 %copy-done.1 = bf16[256,512]{1,0:T(8,128)(2,1)S(1)} copy-done((bf16[256,512]{1,0:T(8,128)(2,1)S(1)}, bf16[256,512]{1,0:T(8,128)(2,1)}, u32[]{:S(2)}) %copy-start.1) | copy-done | bytes 262168
  2.5 2.9 %shard_map.37 = (bf16[256,1024]{1,0:T(8,128)(2,1)S(1)}, bf16[128,1024]{1,0:T(8,128)(2,1)S(1)}, bf16[64,1024]{1,0:T(8,128)(2,1)S(1)}) custom-call(s32[12]{0:T(128)S(1)} %stack.59.place, bf16[256,512]{1,0:T(8,128)(2,1)S(1)} %copy-done.1, bf16[512,1536]{1,0:T(8,128)(2,1)S(1)} %copy-done), custom_call_target="tpu_custom_call" | custom-call | flops 268435456 | bytes 1048576 | tf_op jit(solution)/shard_map/pallas_call | solution.py:54
  5.4 2.2 %all_gather.18.near_ref.refs_0_ = bf16[256,1024]{1,0:T(8,128)(2,1)S(1)} all-gather(bf16[128,1024]{1,0:T(8,128)(2,1)S(1)} %get-tuple-element.16), channel_id=1, replica_groups={{0,1},{2,3},{4,5},{6,7},{8,9},{10,11},{12,13},{14,15},{16,17},{18,19},{..., dimensions={0}, use_global_device_ids=true | all-gather | bytes 786432 | tf_op jit(solution)/shard_map/all_gather | solution.py:245
  7.7 6.8 %all_gather.19.refs_0_.refs_1_ = bf16[128,1024]{1,0:T(8,128)(2,1)S(1)} all-gather(bf16[64,1024]{1,0:T(8,128)(2,1)S(1)} %shard_map.39), channel_id=1, replica_groups={{0,2},{1,3},{4,6},{5,7},{8,10},{9,11},{12,14},{13,15},{16,18},{17,19},{..., dimensions={0}, use_global_device_ids=true | all-gather | bytes 393216 | tf_op jit(solution)/shard_map/all_gather | solution.py:256
  14.6 0.2 shard_map.40
  14.7 10.9 %all_gather.20.refs_0_.refs_2_ = bf16[128,1024]{1,0:T(8,128)(2,1)S(1)} all-gather(bf16[64,1024]{1,0:T(8,128)(2,1)S(1)} %shard_map.40), channel_id=1, replica_groups={{0,4},{1,5},{2,6},{3,7},{8,12},{9,13},{10,14},{11,15},{16,20},{17,21},{..., dimensions={0}, use_global_device_ids=true | all-gather | bytes 393216 | tf_op jit(solution)/shard_map/all_gather | solution.py:256
  25.7 0.2 shard_map.41.refs_0_
  25.8 5.9 %collective-permute-start.1 = (bf16[64,1024]{1,0:T(8,128)(2,1)S(1)}, bf16[64,1024]{1,0:T(8,128)(2,1)S(1)}, u32[]{:S(2)}, u32[]{:S(2)}) collective-permute-start(bf16[64,1024]{1,0:T(8,128)(2,1)S(1)} %shard_map.41.refs_0_), channel_id=1, source_target_pairs={{0,12},{1,13},{2,14},{3,15},{4,8},{5,9},{6,10},{7,11},{8,4},{9,5},... | collective-permute-start | bytes 393224 | tf_op jit(solution)/shard_map/ppermute | solution.py:259
  31.8 3.0 %collective-permute-done.1.refs_3_.refs_1_ = bf16[64,1024]{1,0:T(8,128)(2,1)S(1)} collective-permute-done((bf16[64,1024]{1,0:T(8,128)(2,1)S(1)}, bf16[64,1024]{1,0:T(8,128)(2,1)S(1)}, u32[]{:S(2)}, u32[]{:S(2)}) %collective-permute-start.1) | collective-permute-done | bytes 131104 | tf_op jit(solution)/shard_map/ppermute | solution.py:259
  35.0 5.8 %collective-permute-start.2 = (bf16[64,1024]{1,0:T(8,128)(2,1)S(1)}, bf16[64,1024]{1,0:T(8,128)(2,1)S(1)}, u32[]{:S(2)}, u32[]{:S(2)}) collective-permute-start(bf16[64,1024]{1,0:T(8,128)(2,1)S(1)} %shard_map.43.refs_0_), channel_id=1, source_target_pairs={{0,16},{1,17},{2,18},{3,19},{4,20},{5,21},{6,22},{7,23},{8,24},{9,... | collective-permute-start | bytes 393224 | tf_op jit(solution)/shard_map/ppermute | solution.py:259
  40.8 4.6 %collective-permute-start = (bf16[64,1024]{1,0:T(8,128)(2,1)S(1)}, bf16[64,1024]{1,0:T(8,128)(2,1)S(1)}, u32[]{:S(2)}, u32[]{:S(2)}) collective-permute-start(bf16[64,1024]{1,0:T(8,128)(2,1)S(1)} %get-tuple-element.17), channel_id=1, source_target_pairs={{1,2},{3,4},{5,6},{7,8},{9,10},{11,12},{13,14},{15,16},{17,18},{19... | collective-permute-start | bytes 393224 | tf_op jit(solution)/shard_map/ppermute | solution.py:248
  45.4 1.1 %slice.3.w_ref = bf16[512,512]{1,0:T(8,128)(2,1)S(1)} slice(bf16[512,1536]{1,0:T(8,128)(2,1)} %w_hbm.1), slice={[0:512], [0:512]} | slice | bytes 1048576 | tf_op jit(solution)/shard_map/slice | solution.py:265
  46.7 7.9 %all_gather.21.refs_0_.refs_1_ = bf16[128,1024]{1,0:T(8,128)(2,1)S(1)} all-gather(bf16[64,1024]{1,0:T(8,128)(2,1)S(1)} %shard_map.44), channel_id=1, replica_groups={{0,32},{1,33},{2,34},{3,35},{4,36},{5,37},{6,38},{7,39},{8,40},{9,41},{..., dimensions={0}, use_global_device_ids=true | all-gather | bytes 393216 | tf_op jit(solution)/shard_map/all_gather | solution.py:256
  54.6 0.2 shard_map.45.refs_0_
  54.8 6.5 %collective-permute-start.3 = (bf16[64,1024]{1,0:T(8,128)(2,1)S(1)}, bf16[64,1024]{1,0:T(8,128)(2,1)S(1)}, u32[]{:S(2)}, u32[]{:S(2)}) collective-permute-start(bf16[64,1024]{1,0:T(8,128)(2,1)S(1)} %shard_map.45.refs_0_), channel_id=1, source_target_pairs={{0,96},{1,97},{2,98},{3,99},{4,100},{5,101},{6,102},{7,103},{8,104... | collective-permute-start | bytes 393224 | tf_op jit(solution)/shard_map/ppermute | solution.py:259
  61.3 1.7 %shard_map.38 = (bf16[256,512]{1,0:T(8,128)(2,1)S(1)}, f32[256,512]{1,0:T(8,128)S(1)}, f32[256,512]{1,0:T(8,128)S(1)}) custom-call(s32[12]{0:T(128)S(1)} %stack.59.place, bf16[256,512]{1,0:T(8,128)(2,1)S(1)} %copy-done.2, bf16[512,512]{1,0:T(8,128)(2,1)S(1)} %slice.3.w_ref, bf16[256,1024]{1,0:T(8,128)(2,1)S(1)} %get-tuple-element.15.kv_ref, ...), custom_call_target="tpu_custom_call" | custom-call | flops 1000000000 | bytes 1048576 | tf_op jit(solution)/shard_map/pallas_call | solution.py:54
  63.0 1.4 %shard_map.42 = (f32[256,512]{1,0:T(8,128)S(1)}, f32[256,512]{1,0:T(8,128)S(1)}) custom-call(s32[12]{0:T(128)S(1)} %stack.59.place, bf16[256,512]{1,0:T(8,128)(2,1)S(1)} %get-tuple-element.18.q_ref, f32[256,512]{1,0:T(8,128)S(1)} %get-tuple-element.19.num_in, f32[256,512]{1,0:T(8,128)S(1)} %get-tuple-element.20.tot_in, ...), custom_call_target="tpu_custom_call" | custom-call | flops 1000000000 | bytes 1048576 | tf_op jit(solution)/shard_map/pallas_call | solution.py:54
  64.4 3.2 %collective-permute-done.3.refs_1_.refs_2_ = bf16[64,1024]{1,0:T(8,128)(2,1)S(1)} collective-permute-done((bf16[64,1024]{1,0:T(8,128)(2,1)S(1)}, bf16[64,1024]{1,0:T(8,128)(2,1)S(1)}, u32[]{:S(2)}, u32[]{:S(2)}) %collective-permute-start.3) | collective-permute-done | bytes 131104 | tf_op jit(solution)/shard_map/ppermute | solution.py:259
  67.7 6.1 %all_gather.22.refs_3_.refs_0_ = bf16[128,1024]{1,0:T(8,128)(2,1)S(1)} all-gather(bf16[64,1024]{1,0:T(8,128)(2,1)S(1)} %shard_map.46), channel_id=1, replica_groups={{0,128},{1,129},{2,130},{3,131},{4,132},{5,133},{6,134},{7,135},{8,136}..., dimensions={0}, use_global_device_ids=true | all-gather | bytes 393216 | tf_op jit(solution)/shard_map/all_gather | solution.py:256
  73.9 0.2 shard_map.48
  74.0 6.9 %all_gather.23.refs_0_ = bf16[128,1024]{1,0:T(8,128)(2,1)S(1)} all-gather(bf16[64,1024]{1,0:T(8,128)(2,1)S(1)} %shard_map.48), channel_id=1, replica_groups={{0,384},{1,385},{2,386},{3,387},{4,388},{5,389},{6,390},{7,391},{8,392}..., dimensions={0}, use_global_device_ids=true | all-gather | bytes 393216 | tf_op jit(solution)/shard_map/all_gather | solution.py:256
  80.9 1.4 %shard_map.47 = (f32[256,512]{1,0:T(8,128)S(1)}, f32[256,512]{1,0:T(8,128)S(1)}) custom-call(s32[12]{0:T(128)S(1)} %stack.59.place, bf16[256,512]{1,0:T(8,128)(2,1)S(1)} %get-tuple-element.18.q_ref, f32[256,512]{1,0:T(8,128)S(1)} %get-tuple-element.21.num_in, f32[256,512]{1,0:T(8,128)S(1)} %get-tuple-element.22.tot_in, ...), custom_call_target="tpu_custom_call" | custom-call | flops 1000000000 | bytes 1048576 | tf_op jit(solution)/shard_map/pallas_call | solution.py:54
  82.3 2.3 %shard_map.49 = bf16[256,512]{1,0:T(8,128)(2,1)} custom-call(s32[12]{0:T(128)S(1)} %stack.59.place, bf16[256,512]{1,0:T(8,128)(2,1)S(1)} %get-tuple-element.18.q_ref, f32[256,512]{1,0:T(8,128)S(1)} %get-tuple-element.23.num_in, f32[256,512]{1,0:T(8,128)S(1)} %get-tuple-element.24.tot_in, bf16[512,512]{1,0:T(8,128)(2,1)S(1)} %copy-done.3, ...), custom_call_target="tpu_custom_call" | custom-call | flops 1000000000 | bytes 1048576 | tf_op jit(solution)/shard_map/pallas_call | solution.py:54
  (13 shorter events, 0.8 us)
Async XLA Ops:
  0.1 1.4 %copy-start = (bf16[512,1536]{1,0:T(8,128)(2,1)S(1)}, bf16[512,1536]{1,0:T(8,128)(2,1)}, u32[]{:S(2)}) copy-start(bf16[512,1536]{1,0:T(8,128)(2,1)} %w_hbm.1) | copy-start | bytes 4718596
  1.5 0.9 %copy-start.1 = (bf16[256,512]{1,0:T(8,128)(2,1)S(1)}, bf16[256,512]{1,0:T(8,128)(2,1)}, u32[]{:S(2)}) copy-start(bf16[256,512]{1,0:T(8,128)(2,1)} %x_ref.3) | copy-start | bytes 786436
  25.7 35.6 %copy-start.2 = (bf16[256,512]{1,0:T(8,128)(2,1)S(1)}, bf16[256,512]{1,0:T(8,128)(2,1)}, u32[]{:S(2)}) copy-start(bf16[256,512]{1,0:T(8,128)(2,1)} %x_ref.3) | copy-start | bytes 786436
  25.8 9.0 %collective-permute-start.1 = (bf16[64,1024]{1,0:T(8,128)(2,1)S(1)}, bf16[64,1024]{1,0:T(8,128)(2,1)S(1)}, u32[]{:S(2)}, u32[]{:S(2)}) collective-permute-start(bf16[64,1024]{1,0:T(8,128)(2,1)S(1)} %shard_map.41.refs_0_), channel_id=1, source_target_pairs={{0,12},{1,13},{2,14},{3,15},{4,8},{5,9},{6,10},{7,11},{8,4},{9,5},... | collective-permute-start | bytes 393224 | tf_op jit(solution)/shard_map/ppermute | solution.py:259
  35.0 11.5 %collective-permute-start.2 = (bf16[64,1024]{1,0:T(8,128)(2,1)S(1)}, bf16[64,1024]{1,0:T(8,128)(2,1)S(1)}, u32[]{:S(2)}, u32[]{:S(2)}) collective-permute-start(bf16[64,1024]{1,0:T(8,128)(2,1)S(1)} %shard_map.43.refs_0_), channel_id=1, source_target_pairs={{0,16},{1,17},{2,18},{3,19},{4,20},{5,21},{6,22},{7,23},{8,24},{9,... | collective-permute-start | bytes 393224 | tf_op jit(solution)/shard_map/ppermute | solution.py:259
  40.8 20.5 %collective-permute-start = (bf16[64,1024]{1,0:T(8,128)(2,1)S(1)}, bf16[64,1024]{1,0:T(8,128)(2,1)S(1)}, u32[]{:S(2)}, u32[]{:S(2)}) collective-permute-start(bf16[64,1024]{1,0:T(8,128)(2,1)S(1)} %get-tuple-element.17), channel_id=1, source_target_pairs={{1,2},{3,4},{5,6},{7,8},{9,10},{11,12},{13,14},{15,16},{17,18},{19... | collective-permute-start | bytes 393224 | tf_op jit(solution)/shard_map/ppermute | solution.py:248
  54.8 12.8 %collective-permute-start.3 = (bf16[64,1024]{1,0:T(8,128)(2,1)S(1)}, bf16[64,1024]{1,0:T(8,128)(2,1)S(1)}, u32[]{:S(2)}, u32[]{:S(2)}) collective-permute-start(bf16[64,1024]{1,0:T(8,128)(2,1)S(1)} %shard_map.45.refs_0_), channel_id=1, source_target_pairs={{0,96},{1,97},{2,98},{3,99},{4,100},{5,101},{6,102},{7,103},{8,104... | collective-permute-start | bytes 393224 | tf_op jit(solution)/shard_map/ppermute | solution.py:259
  80.9 1.4 %copy-start.3 = (bf16[512,512]{1,0:T(8,128)(2,1)S(1)}, bf16[512,512]{1,0:T(8,128)(2,1)}, u32[]{:S(2)}) copy-start(bf16[512,512]{1,0:T(8,128)(2,1)} %w_ref.1) | copy-start | bytes 1572868

commit v2 on v1

--- a/solution.py
+++ b/solution.py
@@ -11,17 +11,7 @@
 HEADS = 8
 BLOCK = 64
 AXES = ("gx", "gy")
-ROUNDS = (
-    ("core", 0, "ag"),
-    ("z1", 1, "ag"),
-    ("z2", 2, "ag"),
-    ("z4", 3, "pp"),
-    ("y1", 4, "pp"),
-    ("y2", 5, "ag"),
-    ("y4", 6, "pp"),
-    ("x1", 7, "ag"),
-    ("x2", 8, "ag"),
-)
+ROUNDS = ((4, "ag"), (5, "ag"), (6, "pp"), (7, "pp"), (8, "pp"))
 FAR8 = (6, 7, 4, 5, 2, 3, 0, 1)
 FAR4 = (3, 2, 1, 0)
 
@@ -50,14 +40,14 @@
 SMEM = pl.BlockSpec(memory_space=pltpu.SMEM)
 
 
-def call(kernel, outs, in_specs, *args, flops=0, scratch=()):
+def call(kernel, outs, in_specs, *args, flops=0, scratch=(), limit=24):
     return pl.pallas_call(
         kernel,
         out_shape=outs,
         in_specs=in_specs,
         out_specs=jax.tree.map(lambda _: pl.BlockSpec(memory_space=pltpu.VMEM), outs),
         scratch_shapes=list(scratch),
-        compiler_params=pltpu.CompilerParams(vmem_limit_bytes=24 * 2**20),
+        compiler_params=pltpu.CompilerParams(vmem_limit_bytes=limit * 2**20),
         cost_estimate=pl.CostEstimate(flops=flops, bytes_accessed=2**20, transcendentals=0),
     )(*args)
 
@@ -74,10 +64,14 @@
     ).astype(jnp.bfloat16)
 
 
-def project_kernel(place, x_ref, w_hbm, kv_ref, near_ref, other_ref, w_buf, sems):
-    model = x_ref.shape[1]
+def project_kernel(
+    place, x_hbm, w_hbm, kv_ref, near_ref, other_ref, l3_ref, l6_ref, x_buf, w_buf, sems
+):
+    model = x_buf.shape[1]
     width = w_buf.shape[2]
     steps = w_buf.shape[0]
+    x_copy = pltpu.make_async_copy(x_hbm, x_buf, sems.at[steps])
+    x_copy.start()
     copies = []
     for step in range(steps):
         columns = pl.ds(model + step * width, width)
@@ -85,35 +79,50 @@
         copy.start()
         copies.append(copy)
     core = place[0]
-    x = x_ref[...]
+    x_copy.wait()
+    x = x_buf[...]
+    pieces = []
     for step in range(steps):
         copies[step].wait()
         lanes = slice(step * width, (step + 1) * width)
         part = jnp.dot(x, w_buf[step], preferred_element_type=jnp.float32).astype(jnp.bfloat16)
         kv_ref[:, lanes] = part
-        near_ref[BLOCK:, lanes] = pooled(pooled(part))
-    last = x_ref.shape[0] - BLOCK
+        level_2 = pooled(pooled(part))
+        near_ref[BLOCK:, lanes] = level_2
+        level_3 = pooled(level_2)
+        l3_ref[:, lanes] = level_3
+        level_5 = pooled(pooled(level_3)).astype(jnp.float32)
+        pieces += [level_5[:, at : at + 128] for at in range(0, width, 128)]
+    level_6 = pooled(jnp.concatenate(pieces, axis=0).astype(jnp.bfloat16))
+    size = level_6.shape[0]
+    for copy in range(l6_ref.shape[0] // size):
+        l6_ref[copy * size : (copy + 1) * size, :] = level_6
+    last = x_buf.shape[0] - BLOCK
     low = pl.multiple_of(core * last, BLOCK)
     high = pl.multiple_of((1 - core) * last, BLOCK)
     near_ref[:BLOCK, :] = kv_ref[pl.ds(high, BLOCK), :]
     other_ref[...] = kv_ref[pl.ds(low, BLOCK), :]
 
 
+def unpack_kernel(in_ref, out_ref):
+    total = in_ref.shape[0]
+    tiles = out_ref.shape[1] // 128
+    each = 4
+    row = lax.broadcasted_iota(jnp.int32, (BLOCK, total), 0)
+    column = lax.broadcasted_iota(jnp.int32, (BLOCK, total), 1)
+    source = (row >> 2) * (each * tiles) + (row & 3)
+    for tile in range(tiles):
+        pick = jnp.where(column == source + each * tile, 1.0, 0.0).astype(jnp.bfloat16)
+        out_ref[:, tile * 128 : (tile + 1) * 128] = jnp.dot(
+            pick, in_ref[...], preferred_element_type=jnp.float32
+        ).astype(jnp.bfloat16)
+
+
 def pool_kernel(*refs):
     ins, out_ref = refs[:-1], refs[-1]
     half = BLOCK // len(ins)
     for num, ref in enumerate(ins):
-        rows = ref.shape[0]
-        block = ref[...]
-        if len(ins) == 1:
-            out_ref[...] = pooled(block)
-        else:
-            out_ref[num * half : (num + 1) * half, :] = pooled(block)
-
-
-def pool_near_kernel(near_ref, out_ref):
-    out_ref[: BLOCK // 2, :] = pooled(near_ref[BLOCK : 2 * BLOCK, :])
-    out_ref[BLOCK // 2 :, :] = pooled(near_ref[3 * BLOCK :, :])
+        out_ref[num * half : (num + 1) * half, :] = pooled(ref[...])
 
 
 def attend_pair(q, keys, values, ones):
@@ -173,37 +182,42 @@
             tot_ref[here, kl] = tot
 
 
-def sibling_rows(place, kinds, refs):
-    rows = []
-    for (kind, bit), ref in zip(kinds, refs):
+def sibling_blocks(place, kinds, refs):
+    blocks = []
+    for kind, ref in zip(kinds, refs):
         if kind == "near":
             start = (1 - place[0]) * 2 * BLOCK + BLOCK
-        elif kind == "ag":
-            start = (1 - place[3 + bit]) * BLOCK
+            blocks.append(ref[pl.ds(pl.multiple_of(start, BLOCK), BLOCK), :])
+        elif kind == "low":
+            chip = place[3]
+            for shift in range(3):
+                rows = BLOCK << shift
+                start = ((chip >> shift) ^ 1) * rows
+                block = ref[pl.ds(pl.multiple_of(start, BLOCK), rows), :]
+                for _ in range(shift):
+                    block = pooled(block)
+                blocks.append(block)
+        elif kind == "pp":
+            blocks.append(ref[...])
         else:
-            start = None
-        rows.append((ref, start))
-    return rows
-
-
-def far_sums(place, kinds, refs, q_ref, lanes, model):
-    keys, values = [], []
-    for ref, start in sibling_rows(place, kinds, refs):
-        at = slice(None) if start is None else pl.ds(pl.multiple_of(start, BLOCK), BLOCK)
-        keys.append(ref[at, lanes : lanes + 128])
-        values.append(ref[at, model + lanes : model + lanes + 128])
-    keys = jnp.concatenate(keys, axis=0)
-    values = jnp.concatenate(values, axis=0)
-    ones = jnp.ones(values.shape, jnp.bfloat16)
-    return attend_pair(q_ref[:, lanes : lanes + 128], keys, values, ones)
+            start = (1 - place[kind]) * BLOCK
+            blocks.append(ref[pl.ds(pl.multiple_of(start, BLOCK), BLOCK), :])
+    return jnp.concatenate(blocks, axis=0)
+
+
+def far_sums(far, q, lanes, model):
+    keys = far[:, lanes : lanes + 128]
+    values = far[:, model + lanes : model + lanes + 128]
+    return attend_pair(q, keys, values, jnp.ones(values.shape, jnp.bfloat16))
 
 
 def far_kernel(kinds, place, q_ref, num_in, tot_in, *refs):
     num_ref, tot_ref = refs[-2:]
     model = q_ref.shape[1]
+    far = sibling_blocks(place, kinds, refs[:-2])
     for lanes in range(0, model, 128):
         at = slice(lanes, lanes + 128)
-        num, tot = far_sums(place, kinds, refs[:-2], q_ref, lanes, model)
+        num, tot = far_sums(far, q_ref[:, at], lanes, model)
         num_ref[:, at] = num_in[:, at] + num
         tot_ref[:, at] = tot_in[:, at] + tot
 
@@ -211,9 +225,10 @@
 def final_kernel(kinds, place, q_ref, num_in, tot_in, w_ref, *refs):
     out_ref, att = refs[-2:]
     model = q_ref.shape[1]
+    far = sibling_blocks(place, kinds, refs[:-2])
     for lanes in range(0, model, 128):
         at = slice(lanes, lanes + 128)
-        num, tot = far_sums(place, kinds, refs[:-2], q_ref, lanes, model)
+        num, tot = far_sums(far, q_ref[:, at], lanes, model)
         att[:, at] = ((num_in[:, at] + num) / (tot_in[:, at] + tot)).astype(jnp.bfloat16)
     out_ref[...] = jnp.dot(att[...], w_ref[...], preferred_element_type=jnp.float32).astype(
         jnp.bfloat16
@@ -223,42 +238,60 @@
 def per_device(tokens, w_qkv, w_out):
     rows, model = tokens.shape
     index = lax.axis_index(AXES)
+    inner = lax.axis_index("gy")
     count = lax.axis_size(AXES)
+    members = lax.axis_size("gy")
     bits = count.bit_length() - 1
     place = jnp.stack(
-        [index & 1, (index == 0).astype(jnp.int32), (index == count - 1).astype(jnp.int32)]
-        + [(index >> bit) & 1 for bit in range(bits)]
+        [index & 1, (index == 0).astype(jnp.int32), (index == count - 1).astype(jnp.int32), inner >> 1]
+        + [(index >> bit) & 1 for bit in range(4, bits)]
     ).astype(jnp.int32)
     bf16 = lambda *shape: jax.ShapeDtypeStruct(shape, jnp.bfloat16)
     f32 = lambda *shape: jax.ShapeDtypeStruct(shape, jnp.float32)
+    anywhere = pl.BlockSpec(memory_space=pl.ANY)
     steps = 4
     width = 2 * model // steps
-    kv, near, other = call(
+    packed = 4 * 2 * model // 128
+    kv, near, other, level_3, level_6 = call(
         project_kernel,
-        (bf16(rows, 2 * model), bf16(2 * BLOCK, 2 * model), bf16(BLOCK, 2 * model)),
-        [SMEM, *vmem(1), pl.BlockSpec(memory_space=pl.ANY)],
+        (
+            bf16(rows, 2 * model),
+            bf16(2 * BLOCK, 2 * model),
+            bf16(BLOCK, 2 * model),
+            bf16(BLOCK // 2, 2 * model),
+            bf16(members * packed, 128),
+        ),
+        [SMEM, anywhere, anywhere],
         place, tokens, w_qkv,
         flops=4 * rows * model * model,
-        scratch=(pltpu.VMEM((steps, model, width), jnp.bfloat16), pltpu.SemaphoreType.DMA((steps,))),
-    )
+        scratch=(
+            pltpu.VMEM((rows, model), jnp.bfloat16),
+            pltpu.VMEM((steps, model, width), jnp.bfloat16),
+            pltpu.SemaphoreType.DMA((steps + 1,)),
+        ),
+        limit=56,
+    )
+    low = lax.all_gather(level_3, "gy", tiled=True)
     pairs = [[i, i ^ 1] for i in range(0, count, 2)]
     near_all = lax.all_gather(near, AXES, axis_index_groups=pairs, tiled=True)
+    spread = lax.all_to_all(level_6, "gy", 0, 0, tiled=True)
     swap = [(i, i + 1) for i in range(1, count - 1, 2)]
     swap += [(j, i) for i, j in swap]
     other_halo = lax.ppermute(other, AXES, swap)
 
-    own = call(pool_near_kernel, bf16(BLOCK, 2 * model), vmem(1), near_all)
-    found = [(("near", 0), near_all)]
-    for _, bit, mode in ROUNDS[1:bits]:
+    own = call(unpack_kernel, bf16(BLOCK, 2 * model), vmem(1), spread)
+    found = []
+    for bit, mode in ROUNDS:
         to = partners(bit, count)
         if mode == "ag":
             groups = [[i, to[i]] for i in range(count) if not i >> bit & 1]
             got = lax.all_gather(own, AXES, axis_index_groups=groups, tiled=True)
             ins = (got,)
+            found.append((bit, got))
         else:
             got = lax.ppermute(own, AXES, list(enumerate(to)))
             ins = (own, got)
-        found.append(((mode, bit), got))
+            found.append(("pp", got))
         if bit < bits - 1:
             own = call(pool_kernel, bf16(BLOCK, 2 * model), vmem(len(ins)), *ins)
 
@@ -274,16 +307,15 @@
             pltpu.VMEM((rows // 2, 2 * model), jnp.bfloat16),
         ),
     )
-    for part in (found[0:4], found[4:8]):
-        kinds = tuple(kind for kind, _ in part)
+    for part in (found[:3], [("near", near_all), ("low", low)]):
         num, tot = call(
-            functools.partial(far_kernel, kinds),
+            functools.partial(far_kernel, tuple(kind for kind, _ in part)),
             (f32(rows, model), f32(rows, model)),
             [SMEM, *vmem(3 + len(part))],
             place, q, num, tot, *[got for _, got in part],
             flops=10**9,
         )
-    part = found[8:]
+    part = found[3:]
     return call(
         functools.partial(final_kernel, tuple(kind for kind, _ in part)),
         bf16(rows, model),

time: 84.9 us -> 89.5 us (1.054)
  the two profiles are of different devices: /device:TPU:8 before, /device:TPU:16 now
where the time goes in v2:
time: 89.5 us; the launch traced here: 89.1 us
  blocking collectives  35.7 us (40%)
  starting transfers between devices  17.7 us (20%)
  Pallas kernels  14.4 us (16%)
  between operations  13.6 us (15%)
  waiting for transfers between devices  4.68 us (5%)
  local copies, waits for them, and re-layouts  2.92 us (3%)
    all_to_all x1, blocking collectives, per_device(): spread = lax.all_to_all(level_6, 'gy', 0, 0, tiled=True)  19.3 us
    ppermute x3, starting transfers between devices, per_device(): got = lax.ppermute(own, AXES, list(enumerate(to)))  15.8 us
    pallas_call x10, Pallas kernels, call(): pl.pallas_call(kernel, out_shape=outs, in_specs=in_specs, out_specs=jax.t...  14.4 us
    all_gather x2, blocking collectives, per_device(): got = lax.all_gather(own, AXES, axis_index_groups=groups, tiled=True)  14.2 us
    ppermute x3, waiting for transfers between devices, per_device(): got = lax.ppermute(own, AXES, list(enumerate(to)))  4.64 us
    all_gather x1, blocking collectives, per_device(): near_all = lax.all_gather(near, AXES, axis_index_groups=pairs, tiled=True)  2.18 us
    ppermute x1, starting transfers between devices, per_device(): other_halo = lax.ppermute(other, AXES, swap)  1.92 us
  transfers between devices with their start and end apart: 5, of which 2 were waited for; matrix products, arithmetic and copies ran while one was open for 1% of the time, Pallas kernels for 7%

profile of v2, /device:TPU:16, one launch (start us, length us, event | category | flops | bytes accessed | tf_op | source)
XLA Modules:
  0.0 89.1 jit_solution(5800384838976528807)
XLA Ops:
  6.5 0.6 stack.47.place
  7.1 6.2 %shard_map.37 = (bf16[256,1024]{1,0:T(8,128)(2,1)}, bf16[128,1024]{1,0:T(8,128)(2,1)}, bf16[64,1024]{1,0:T(8,128)(2,1)}, bf16[32,1024]{1,0:T(8,128)(2,1)}, bf16[512,128]{1,0:T(8,128)(2,1)}) custom-call(s32[9]{0:T(128)} %stack.47.place, bf16[256,512]{1,0:T(8,128)(2,1)} %x_ref.1, bf16[512,1536]{1,0:T(8,128)(2,1)} %w_hbm.1), custom_call_target="tpu_custom_call" | custom-call | flops 268435456 | bytes 1048576 | tf_op jit(solution)/shard_map/pallas_call | solution.py:44
  13.4 19.3 %all_to_all.11 = bf16[16,32,128]{2,1,0:T(8,128)(2,1)S(1)} all-to-all(bf16[16,32,128]{2,1,0:T(8,128)(2,1)} %bitcast.12), channel_id=1, replica_groups=mesh['gx'=32,'gy'=16] {'gy'}, dimensions={0} | all-to-all | bytes 262144 | tf_op jit(solution)/shard_map/all_to_all | solution.py:277
  32.7 0.3 shard_map.39
  33.0 6.9 %all_gather.13.refs_0_ = bf16[128,1024]{1,0:T(8,128)(2,1)S(1)} all-gather(bf16[64,1024]{1,0:T(8,128)(2,1)S(1)} %shard_map.39), channel_id=1, replica_groups={{0,16},{1,17},{2,18},{3,19},{4,20},{5,21},{6,22},{7,23},{8,24},{9,25},{..., dimensions={0}, use_global_device_ids=true | all-gather | bytes 393216 | tf_op jit(solution)/shard_map/all_gather | solution.py:288
  39.9 0.2 shard_map.40
  40.1 7.3 %all_gather.14.refs_0_.refs_1_ = bf16[128,1024]{1,0:T(8,128)(2,1)S(1)} all-gather(bf16[64,1024]{1,0:T(8,128)(2,1)S(1)} %shard_map.40), channel_id=1, replica_groups={{0,32},{1,33},{2,34},{3,35},{4,36},{5,37},{6,38},{7,39},{8,40},{9,41},{..., dimensions={0}, use_global_device_ids=true | all-gather | bytes 393216 | tf_op jit(solution)/shard_map/all_gather | solution.py:288
  47.4 0.2 shard_map.41.refs_0_
  47.6 8.4 %collective-permute-start.1 = (bf16[64,1024]{1,0:T(8,128)(2,1)S(1)}, bf16[64,1024]{1,0:T(8,128)(2,1)S(1)}, u32[]{:S(2)}, u32[]{:S(2)}) collective-permute-start(bf16[64,1024]{1,0:T(8,128)(2,1)S(1)} %shard_map.41.refs_0_), channel_id=1, source_target_pairs={{0,96},{1,97},{2,98},{3,99},{4,100},{5,101},{6,102},{7,103},{8,104... | collective-permute-start | bytes 393224 | tf_op jit(solution)/shard_map/ppermute | solution.py:292
  56.0 1.9 %collective-permute-start = (bf16[64,1024]{1,0:T(8,128)(2,1)S(1)}, bf16[64,1024]{1,0:T(8,128)(2,1)S(1)}, u32[]{:S(2)}, u32[]{:S(2)}) collective-permute-start(bf16[64,1024]{1,0:T(8,128)(2,1)S(1)} %copy-done.6), channel_id=1, source_target_pairs={{1,2},{3,4},{5,6},{7,8},{9,10},{11,12},{13,14},{15,16},{17,18},{19... | collective-permute-start | bytes 393224 | tf_op jit(solution)/shard_map/ppermute | solution.py:280
  57.9 4.5 %collective-permute-done.1.refs_2_.refs_1_ = bf16[64,1024]{1,0:T(8,128)(2,1)S(1)} collective-permute-done((bf16[64,1024]{1,0:T(8,128)(2,1)S(1)}, bf16[64,1024]{1,0:T(8,128)(2,1)S(1)}, u32[]{:S(2)}, u32[]{:S(2)}) %collective-permute-start.1) | collective-permute-done | bytes 131104 | tf_op jit(solution)/shard_map/ppermute | solution.py:292
  62.5 0.2 shard_map.44.refs_0_
  62.6 3.4 %collective-permute-start.2 = (bf16[64,1024]{1,0:T(8,128)(2,1)S(1)}, bf16[64,1024]{1,0:T(8,128)(2,1)S(1)}, u32[]{:S(2)}, u32[]{:S(2)}) collective-permute-start(bf16[64,1024]{1,0:T(8,128)(2,1)S(1)} %shard_map.44.refs_0_), channel_id=1, source_target_pairs={{0,128},{1,129},{2,130},{3,131},{4,132},{5,133},{6,134},{7,135},{8... | collective-permute-start | bytes 393224 | tf_op jit(solution)/shard_map/ppermute | solution.py:292
  66.1 2.2 %all_gather.12.near_ref.refs_0_ = bf16[256,1024]{1,0:T(8,128)(2,1)S(1)} all-gather(bf16[128,1024]{1,0:T(8,128)(2,1)S(1)} %copy-done.5), channel_id=1, replica_groups={{0,1},{2,3},{4,5},{6,7},{8,9},{10,11},{12,13},{14,15},{16,17},{18,19},{..., dimensions={0}, use_global_device_ids=true | all-gather | bytes 786432 | tf_op jit(solution)/shard_map/all_gather | solution.py:276
  68.2 1.1 %slice.3.w_ref = bf16[512,512]{1,0:T(8,128)(2,1)S(1)} slice(bf16[512,1536]{1,0:T(8,128)(2,1)} %w_hbm.1), slice={[0:512], [0:512]} | slice | bytes 1048576 | tf_op jit(solution)/shard_map/slice | solution.py:298
  69.4 1.7 %shard_map.38 = (bf16[256,512]{1,0:T(8,128)(2,1)S(1)}, f32[256,512]{1,0:T(8,128)S(1)}, f32[256,512]{1,0:T(8,128)S(1)}) custom-call(s32[9]{0:T(128)S(1)} %copy-done.1, bf16[256,512]{1,0:T(8,128)(2,1)S(1)} %copy-done, bf16[512,512]{1,0:T(8,128)(2,1)S(1)} %slice.3.w_ref, bf16[256,1024]{1,0:T(8,128)(2,1)S(1)} %copy-done.4, ...), custom_call_target="tpu_custom_call" | custom-call | flops 1000000000 | bytes 1048576 | tf_op jit(solution)/shard_map/pallas_call | solution.py:44
  71.1 0.2 shard_map.45
  71.3 4.0 %collective-permute-start.3 = (bf16[64,1024]{1,0:T(8,128)(2,1)S(1)}, bf16[64,1024]{1,0:T(8,128)(2,1)S(1)}, u32[]{:S(2)}, u32[]{:S(2)}) collective-permute-start(bf16[64,1024]{1,0:T(8,128)(2,1)S(1)} %shard_map.45), channel_id=1, source_target_pairs={{0,384},{1,385},{2,386},{3,387},{4,388},{5,389},{6,390},{7,391},{8... | collective-permute-start | bytes 393224 | tf_op jit(solution)/shard_map/ppermute | solution.py:292
  75.3 1.5 %shard_map.42 = (f32[256,512]{1,0:T(8,128)S(1)}, f32[256,512]{1,0:T(8,128)S(1)}) custom-call(s32[9]{0:T(128)S(1)} %copy-done.1, bf16[256,512]{1,0:T(8,128)(2,1)S(1)} %get-tuple-element.20.q_ref, f32[256,512]{1,0:T(8,128)S(1)} %get-tuple-element.21.num_in, f32[256,512]{1,0:T(8,128)S(1)} %get-tuple-element.22.tot_in, ...), custom_call_target="tpu_custom_call" | custom-call | flops 1000000000 | bytes 1048576 | tf_op jit(solution)/shard_map/pallas_call | solution.py:44
  76.8 0.0 all-gather.2.cloned.1.call-done.refs_1_
  76.8 1.2 %copy-done.2 = bf16[512,1024]{1,0:T(8,128)(2,1)S(1)} copy-done((bf16[512,1024]{1,0:T(8,128)(2,1)S(1)}, bf16[512,1024]{1,0:T(8,128)(2,1)}, u32[]{:S(2)}) %copy-start.2) | copy-done | bytes 1048600
  78.0 1.7 %shard_map.43 = (f32[256,512]{1,0:T(8,128)S(1)}, f32[256,512]{1,0:T(8,128)S(1)}) custom-call(s32[9]{0:T(128)S(1)} %copy-done.1, bf16[256,512]{1,0:T(8,128)(2,1)S(1)} %get-tuple-element.20.q_ref, f32[256,512]{1,0:T(8,128)S(1)} %get-tuple-element.24.num_in, f32[256,512]{1,0:T(8,128)S(1)} %get-tuple-element.25.tot_in, ...), custom_call_target="tpu_custom_call" | custom-call | flops 1000000000 | bytes 1048576 | tf_op jit(solution)/shard_map/pallas_call | solution.py:44
  79.8 0.1 collective-permute-done.3.refs_1_
  79.9 2.3 %shard_map.46 = bf16[256,512]{1,0:T(8,128)(2,1)} custom-call(s32[9]{0:T(128)S(1)} %copy-done.1, bf16[256,512]{1,0:T(8,128)(2,1)S(1)} %get-tuple-element.20.q_ref, f32[256,512]{1,0:T(8,128)S(1)} %get-tuple-element.27.num_in, f32[256,512]{1,0:T(8,128)S(1)} %get-tuple-element.28.tot_in, bf16[512,512]{1,0:T(8,128)(2,1)S(1)} %copy-done.3, ...), custom_call_target="tpu_custom_call" | custom-call | flops 1000000000 | bytes 1048576 | tf_op jit(solution)/shard_map/pallas_call | solution.py:44
  (17 shorter events, 0.1 us)
Async XLA Ops:
  6.5 70.3 %all-gather.2.cloned.1.call-start = ((), (), s32[]{:S(2)}) async-start(), calls=%async_computation.1 | async-start | bytes 1114112 | tf_op jit(solution)/shard_map/all_gather | solution.py:274
  13.3 42.7 %copy-start.6 = (bf16[64,1024]{1,0:T(8,128)(2,1)S(1)}, bf16[64,1024]{1,0:T(8,128)(2,1)}, u32[]{:S(2)}) copy-start(bf16[64,1024]{1,0:T(8,128)(2,1)} %get-tuple-element.19) | copy-start | bytes 393220
  13.3 52.7 %copy-start.5 = (bf16[128,1024]{1,0:T(8,128)(2,1)S(1)}, bf16[128,1024]{1,0:T(8,128)(2,1)}, u32[]{:S(2)}) copy-start(bf16[128,1024]{1,0:T(8,128)(2,1)} %get-tuple-element.18) | copy-start | bytes 786436
  40.1 29.3 %copy-start = (bf16[256,512]{1,0:T(8,128)(2,1)S(1)}, bf16[256,512]{1,0:T(8,128)(2,1)}, u32[]{:S(2)}) copy-start(bf16[256,512]{1,0:T(8,128)(2,1)} %x_ref.1) | copy-start | bytes 786436
  40.1 29.3 %copy-start.1 = (s32[9]{0:T(128)S(1)}, s32[9]{0:T(128)}, u32[]{:S(2)}) copy-start(s32[9]{0:T(128)} %stack.47.place) | copy-start | bytes 112
  40.1 29.3 %copy-start.4 = (bf16[256,1024]{1,0:T(8,128)(2,1)S(1)}, bf16[256,1024]{1,0:T(8,128)(2,1)}, u32[]{:S(2)}) copy-start(bf16[256,1024]{1,0:T(8,128)(2,1)} %get-tuple-element.17.kv_ref) | copy-start | bytes 1572868
  47.6 14.9 %collective-permute-start.1 = (bf16[64,1024]{1,0:T(8,128)(2,1)S(1)}, bf16[64,1024]{1,0:T(8,128)(2,1)S(1)}, u32[]{:S(2)}, u32[]{:S(2)}) collective-permute-start(bf16[64,1024]{1,0:T(8,128)(2,1)S(1)} %shard_map.41.refs_0_), channel_id=1, source_target_pairs={{0,96},{1,97},{2,98},{3,99},{4,100},{5,101},{6,102},{7,103},{8,104... | collective-permute-start | bytes 393224 | tf_op jit(solution)/shard_map/ppermute | solution.py:292
  56.0 13.3 %collective-permute-start = (bf16[64,1024]{1,0:T(8,128)(2,1)S(1)}, bf16[64,1024]{1,0:T(8,128)(2,1)S(1)}, u32[]{:S(2)}, u32[]{:S(2)}) collective-permute-start(bf16[64,1024]{1,0:T(8,128)(2,1)S(1)} %copy-done.6), channel_id=1, source_target_pairs={{1,2},{3,4},{5,6},{7,8},{9,10},{11,12},{13,14},{15,16},{17,18},{19... | collective-permute-start | bytes 393224 | tf_op jit(solution)/shard_map/ppermute | solution.py:280
  62.6 8.4 %collective-permute-start.2 = (bf16[64,1024]{1,0:T(8,128)(2,1)S(1)}, bf16[64,1024]{1,0:T(8,128)(2,1)S(1)}, u32[]{:S(2)}, u32[]{:S(2)}) collective-permute-start(bf16[64,1024]{1,0:T(8,128)(2,1)S(1)} %shard_map.44.refs_0_), channel_id=1, source_target_pairs={{0,128},{1,129},{2,130},{3,131},{4,132},{5,133},{6,134},{7,135},{8... | collective-permute-start | bytes 393224 | tf_op jit(solution)/shard_map/ppermute | solution.py:292
  71.3 8.6 %collective-permute-start.3 = (bf16[64,1024]{1,0:T(8,128)(2,1)S(1)}, bf16[64,1024]{1,0:T(8,128)(2,1)S(1)}, u32[]{:S(2)}, u32[]{:S(2)}) collective-permute-start(bf16[64,1024]{1,0:T(8,128)(2,1)S(1)} %shard_map.45), channel_id=1, source_target_pairs={{0,384},{1,385},{2,386},{3,387},{4,388},{5,389},{6,390},{7,391},{8... | collective-permute-start | bytes 393224 | tf_op jit(solution)/shard_map/ppermute | solution.py:292
  76.8 1.2 %copy-start.2 = (bf16[512,1024]{1,0:T(8,128)(2,1)S(1)}, bf16[512,1024]{1,0:T(8,128)(2,1)}, u32[]{:S(2)}) copy-start(bf16[512,1024]{1,0:T(8,128)(2,1)} %all-gather.2.cloned.1.call-done.refs_1_) | copy-start | bytes 3145732
  78.0 1.9 %copy-start.3 = (bf16[512,512]{1,0:T(8,128)(2,1)S(1)}, bf16[512,512]{1,0:T(8,128)(2,1)}, u32[]{:S(2)}) copy-start(bf16[512,512]{1,0:T(8,128)(2,1)} %w_ref.1) | copy-start | bytes 1572868
Sparse Core Ops, SparseCore 0:
  13.5 46.4 all-gather.1

commit v3 on v2

--- a/solution.py
+++ b/solution.py
@@ -11,7 +11,6 @@
 HEADS = 8
 BLOCK = 64
 AXES = ("gx", "gy")
-ROUNDS = ((4, "ag"), (5, "ag"), (6, "pp"), (7, "pp"), (8, "pp"))
 FAR8 = (6, 7, 4, 5, 2, 3, 0, 1)
 FAR4 = (3, 2, 1, 0)
 
@@ -40,16 +39,21 @@
 SMEM = pl.BlockSpec(memory_space=pltpu.SMEM)
 
 
-def call(kernel, outs, in_specs, *args, flops=0, scratch=(), limit=24):
+def call(kernel, outs, in_specs, *args, flops=0, scratch=(), limit=24, after=()):
+    count = len(args)
+
+    def body(*refs):
+        kernel(*refs[:count], *refs[count + len(after) :])
+
     return pl.pallas_call(
-        kernel,
+        body,
         out_shape=outs,
-        in_specs=in_specs,
+        in_specs=list(in_specs) + [pl.BlockSpec(memory_space=pl.ANY)] * len(after),
         out_specs=jax.tree.map(lambda _: pl.BlockSpec(memory_space=pltpu.VMEM), outs),
         scratch_shapes=list(scratch),
         compiler_params=pltpu.CompilerParams(vmem_limit_bytes=limit * 2**20),
         cost_estimate=pl.CostEstimate(flops=flops, bytes_accessed=2**20, transcendentals=0),
-    )(*args)
+    )(*args, *after)
 
 
 def pool_matrix(rows):
@@ -65,9 +69,9 @@
 
 
 def project_kernel(
-    place, x_hbm, w_hbm, kv_ref, near_ref, other_ref, l3_ref, l6_ref, x_buf, w_buf, sems
+    place, x_hbm, w_hbm, kv_ref, near_ref, other_ref, packed_ref, x_buf, w_buf, part_buf, sems
 ):
-    model = x_buf.shape[1]
+    rows, model = x_buf.shape
     width = w_buf.shape[2]
     steps = w_buf.shape[0]
     x_copy = pltpu.make_async_copy(x_hbm, x_buf, sems.at[steps])
@@ -78,7 +82,6 @@
         copy = pltpu.make_async_copy(w_hbm.at[:, columns], w_buf.at[step], sems.at[step])
         copy.start()
         copies.append(copy)
-    core = place[0]
     x_copy.wait()
     x = x_buf[...]
     pieces = []
@@ -87,17 +90,26 @@
         lanes = slice(step * width, (step + 1) * width)
         part = jnp.dot(x, w_buf[step], preferred_element_type=jnp.float32).astype(jnp.bfloat16)
         kv_ref[:, lanes] = part
-        level_2 = pooled(pooled(part))
-        near_ref[BLOCK:, lanes] = level_2
-        level_3 = pooled(level_2)
-        l3_ref[:, lanes] = level_3
-        level_5 = pooled(pooled(level_3)).astype(jnp.float32)
-        pieces += [level_5[:, at : at + 128] for at in range(0, width, 128)]
-    level_6 = pooled(jnp.concatenate(pieces, axis=0).astype(jnp.bfloat16))
-    size = level_6.shape[0]
-    for copy in range(l6_ref.shape[0] // size):
-        l6_ref[copy * size : (copy + 1) * size, :] = level_6
-    last = x_buf.shape[0] - BLOCK
+        wide = part.astype(jnp.float32)
+        for at in range(0, width, 128):
+            tile = (step * width + at) // 128
+            part_buf[tile] = wide[:, at : at + 128]
+            size = rows
+            while size > 8:
+                size //= 2
+                even = part_buf[tile, pl.ds(0, size, stride=2), :]
+                odd = part_buf[tile, pl.ds(1, size, stride=2), :]
+                level = ((even + odd) * 0.5).astype(jnp.bfloat16)
+                if size == BLOCK:
+                    near_ref[BLOCK:, tile * 128 : (tile + 1) * 128] = level
+                part_buf[tile, :size, :] = level.astype(jnp.float32)
+            pieces.append(level.astype(jnp.float32))
+    packed = pooled(pooled(jnp.concatenate(pieces, axis=0).astype(jnp.bfloat16)))
+    size = packed.shape[0]
+    for copy in range(packed_ref.shape[0] // size):
+        packed_ref[copy * size : (copy + 1) * size, :] = packed
+    core = place[0]
+    last = rows - BLOCK
     low = pl.multiple_of(core * last, BLOCK)
     high = pl.multiple_of((1 - core) * last, BLOCK)
     near_ref[:BLOCK, :] = kv_ref[pl.ds(high, BLOCK), :]
@@ -107,15 +119,19 @@
 def unpack_kernel(in_ref, out_ref):
     total = in_ref.shape[0]
     tiles = out_ref.shape[1] // 128
-    each = 4
     row = lax.broadcasted_iota(jnp.int32, (BLOCK, total), 0)
     column = lax.broadcasted_iota(jnp.int32, (BLOCK, total), 1)
-    source = (row >> 2) * (each * tiles) + (row & 3)
+    source = (row >> 1) * (2 * tiles) + (row & 1)
     for tile in range(tiles):
-        pick = jnp.where(column == source + each * tile, 1.0, 0.0).astype(jnp.bfloat16)
+        pick = jnp.where(column == source + 2 * tile, 1.0, 0.0).astype(jnp.bfloat16)
         out_ref[:, tile * 128 : (tile + 1) * 128] = jnp.dot(
             pick, in_ref[...], preferred_element_type=jnp.float32
         ).astype(jnp.bfloat16)
+
+
+def pool_near_kernel(near_ref, out_ref):
+    out_ref[: BLOCK // 2, :] = pooled(near_ref[BLOCK : 2 * BLOCK, :])
+    out_ref[BLOCK // 2 :, :] = pooled(near_ref[3 * BLOCK :, :])
 
 
 def pool_kernel(*refs):
@@ -143,13 +159,13 @@
     return num, tot
 
 
-def local_kernel(place, x_ref, w_ref, kv_ref, near_ref, other_ref, q_ref, num_ref, tot_ref, pad, l1):
+def local_kernel(
+    place, x_ref, w_hbm, kv_ref, near_ref, other_ref, q_ref, num_ref, tot_ref, pad, l1, w_ref, sem
+):
     rows, model = x_ref.shape
     blocks = rows // BLOCK
-    q_ref[...] = (
-        jnp.dot(x_ref[...], w_ref[...], preferred_element_type=jnp.float32)
-        .astype(jnp.bfloat16) * jnp.bfloat16(0.125)
-    )
+    copy = pltpu.make_async_copy(w_hbm.at[:, pl.ds(0, model)], w_ref, sem)
+    copy.start()
     core = place[0]
     sib_halo = near_ref[pl.ds(pl.multiple_of((1 - core) * 2 * BLOCK, BLOCK), BLOCK), :]
     other = other_ref[...]
@@ -158,6 +174,11 @@
     pad[BLOCK : BLOCK + rows, :] = kv_ref[...]
     pad[BLOCK + rows :, :] = jnp.where(is_first, sib_halo, other)
     l1[...] = pooled(kv_ref[...])
+    copy.wait()
+    q_ref[...] = (
+        jnp.dot(x_ref[...], w_ref[...], preferred_element_type=jnp.float32)
+        .astype(jnp.bfloat16) * jnp.bfloat16(0.125)
+    )
     key_row = lax.broadcasted_iota(jnp.int32, (4 * BLOCK, 128), 0)
     for i in range(blocks):
         ones = jnp.ones((4 * BLOCK, 128), jnp.float32)
@@ -188,20 +209,8 @@
         if kind == "near":
             start = (1 - place[0]) * 2 * BLOCK + BLOCK
             blocks.append(ref[pl.ds(pl.multiple_of(start, BLOCK), BLOCK), :])
-        elif kind == "low":
-            chip = place[3]
-            for shift in range(3):
-                rows = BLOCK << shift
-                start = ((chip >> shift) ^ 1) * rows
-                block = ref[pl.ds(pl.multiple_of(start, BLOCK), rows), :]
-                for _ in range(shift):
-                    block = pooled(block)
-                blocks.append(block)
-        elif kind == "pp":
+        else:
             blocks.append(ref[...])
-        else:
-            start = (1 - place[kind]) * BLOCK
-            blocks.append(ref[pl.ds(pl.multiple_of(start, BLOCK), BLOCK), :])
     return jnp.concatenate(blocks, axis=0)
 
 
@@ -238,89 +247,98 @@
 def per_device(tokens, w_qkv, w_out):
     rows, model = tokens.shape
     index = lax.axis_index(AXES)
-    inner = lax.axis_index("gy")
     count = lax.axis_size(AXES)
-    members = lax.axis_size("gy")
-    bits = count.bit_length() - 1
     place = jnp.stack(
-        [index & 1, (index == 0).astype(jnp.int32), (index == count - 1).astype(jnp.int32), inner >> 1]
-        + [(index >> bit) & 1 for bit in range(4, bits)]
+        [index & 1, (index == 0).astype(jnp.int32), (index == count - 1).astype(jnp.int32)]
     ).astype(jnp.int32)
     bf16 = lambda *shape: jax.ShapeDtypeStruct(shape, jnp.bfloat16)
     f32 = lambda *shape: jax.ShapeDtypeStruct(shape, jnp.float32)
     anywhere = pl.BlockSpec(memory_space=pl.ANY)
-    steps = 4
+    steps = 2
     width = 2 * model // steps
-    packed = 4 * 2 * model // 128
-    kv, near, other, level_3, level_6 = call(
+    members = 32
+    packed = 2 * 2 * model // 128
+    block = bf16(BLOCK, 2 * model)
+    kv, near, other, level_7 = call(
         project_kernel,
-        (
-            bf16(rows, 2 * model),
-            bf16(2 * BLOCK, 2 * model),
-            bf16(BLOCK, 2 * model),
-            bf16(BLOCK // 2, 2 * model),
-            bf16(members * packed, 128),
-        ),
+        (bf16(rows, 2 * model), bf16(2 * BLOCK, 2 * model), block, bf16(members * packed, 128)),
         [SMEM, anywhere, anywhere],
         place, tokens, w_qkv,
         flops=4 * rows * model * model,
         scratch=(
             pltpu.VMEM((rows, model), jnp.bfloat16),
             pltpu.VMEM((steps, model, width), jnp.bfloat16),
+            pltpu.VMEM((2 * model // 128, rows, 128), jnp.float32),
             pltpu.SemaphoreType.DMA((steps + 1,)),
         ),
         limit=56,
     )
-    low = lax.all_gather(level_3, "gy", tiled=True)
     pairs = [[i, i ^ 1] for i in range(0, count, 2)]
     near_all = lax.all_gather(near, AXES, axis_index_groups=pairs, tiled=True)
-    spread = lax.all_to_all(level_6, "gy", 0, 0, tiled=True)
     swap = [(i, i + 1) for i in range(1, count - 1, 2)]
     swap += [(j, i) for i, j in swap]
     other_halo = lax.ppermute(other, AXES, swap)
 
-    own = call(unpack_kernel, bf16(BLOCK, 2 * model), vmem(1), spread)
-    found = []
-    for bit, mode in ROUNDS:
-        to = partners(bit, count)
-        if mode == "ag":
-            groups = [[i, to[i]] for i in range(count) if not i >> bit & 1]
-            got = lax.all_gather(own, AXES, axis_index_groups=groups, tiled=True)
-            ins = (got,)
-            found.append((bit, got))
-        else:
-            got = lax.ppermute(own, AXES, list(enumerate(to)))
-            ins = (own, got)
-            found.append(("pp", got))
-        if bit < bits - 1:
-            own = call(pool_kernel, bf16(BLOCK, 2 * model), vmem(len(ins)), *ins)
-
-    w_q = w_qkv[:, :model]
-    q, num, tot = call(
-        local_kernel,
-        (bf16(rows, model), f32(rows, model), f32(rows, model)),
-        [SMEM, *vmem(5)],
-        place, tokens, w_q, kv, near_all, other_halo,
-        flops=10**9,
-        scratch=(
-            pltpu.VMEM((rows + 2 * BLOCK, 2 * model), jnp.bfloat16),
-            pltpu.VMEM((rows // 2, 2 * model), jnp.bfloat16),
-        ),
-    )
-    for part in (found[:3], [("near", near_all), ("low", low)]):
-        num, tot = call(
+    def exchange(own, bit):
+        return lax.ppermute(own, AXES, list(enumerate(partners(bit, count))))
+
+    def pool(own, got, *after):
+        return call(pool_kernel, block, vmem(2), own, got, after=after)
+
+    def far(num, tot, *part, after=()):
+        return call(
             functools.partial(far_kernel, tuple(kind for kind, _ in part)),
             (f32(rows, model), f32(rows, model)),
             [SMEM, *vmem(3 + len(part))],
             place, q, num, tot, *[got for _, got in part],
             flops=10**9,
+            after=after,
         )
-    part = found[3:]
+
+    own_3 = call(pool_near_kernel, block, vmem(1), near_all)
+    sib_3 = exchange(own_3, 1)
+    level_7, _ = lax.optimization_barrier((level_7, own_3))
+    teams = [list(range(i, i + members)) for i in range(0, count, members)]
+    spread = lax.all_to_all(level_7, AXES, 0, 0, axis_index_groups=teams, tiled=True)
+    own_7 = call(unpack_kernel, block, vmem(1), spread)
+    sib_7 = exchange(own_7, 5)
+    own_4 = pool(own_3, sib_3, own_7)
+    sib_4 = exchange(own_4, 2)
+    q, num, tot = call(
+        local_kernel,
+        (bf16(rows, model), f32(rows, model), f32(rows, model)),
+        [SMEM, *vmem(1), anywhere, *vmem(3)],
+        place, tokens, w_qkv, kv, near_all, other_halo,
+        flops=10**9,
+        scratch=(
+            pltpu.VMEM((rows + 2 * BLOCK, 2 * model), jnp.bfloat16),
+            pltpu.VMEM((rows // 2, 2 * model), jnp.bfloat16),
+            pltpu.VMEM((model, model), jnp.bfloat16),
+            pltpu.SemaphoreType.DMA(()),
+        ),
+        after=(own_4,),
+    )
+    own_8 = pool(own_7, sib_7, q)
+    sib_8 = exchange(own_8, 6)
+    own_5 = pool(own_4, sib_4, own_8)
+    sib_5 = exchange(own_5, 3)
+    num, tot = far(
+        num, tot, ("near", near_all), ("pp", sib_3), ("pp", sib_4), ("pp", sib_7), after=(own_5,)
+    )
+    own_9 = pool(own_8, sib_8, num)
+    sib_9 = exchange(own_9, 7)
+    own_6 = pool(own_5, sib_5, own_9)
+    sib_6 = exchange(own_6, 4)
+    own_10 = pool(own_9, sib_9, own_6)
+    sib_10 = exchange(own_10, 8)
+    num, tot = far(
+        num, tot, ("pp", sib_5), ("pp", sib_6), ("pp", sib_8), ("pp", sib_9), after=(own_10,)
+    )
     return call(
-        functools.partial(final_kernel, tuple(kind for kind, _ in part)),
+        functools.partial(final_kernel, ("pp",)),
         bf16(rows, model),
-        [SMEM, *vmem(4 + len(part))],
-        place, q, num, tot, w_out, *[got for _, got in part],
+        [SMEM, *vmem(5)],
+        place, q, num, tot, w_out, sib_10,
         flops=10**9,
         scratch=(pltpu.VMEM((rows, model), jnp.bfloat16),),
     )

time: 89.5 us -> 69.4 us (0.78)
  the two profiles are of different devices: /device:TPU:16 before, /device:TPU:6 now
where the time goes in v3:
time: 69.4 us; the launch traced here: 68.1 us
  starting transfers between devices  44.6 us (64%)
  Pallas kernels  12 us (17%)
  waiting for transfers between devices  8.05 us (12%)
  blocking collectives  2.52 us (4%)
    ppermute x8, starting transfers between devices, exchange(): return lax.ppermute(own, AXES, list(enumerate(partners(bit, count))))  25.7 us
    pallas_call x13, Pallas kernels, call(): pl.pallas_call(body, out_shape=outs, in_specs=list(in_specs) + [pl.BlockS...  12 us
    all_to_all x1, starting transfers between devices, per_device(): lax.all_to_all(level_7, AXES, 0, 0, axis_index_groups=teams, tiled=True)  11.7 us
    ppermute x8, waiting for transfers between devices, exchange(): return lax.ppermute(own, AXES, list(enumerate(partners(bit, count))))  8.05 us
    ppermute x1, starting transfers between devices, per_device(): other_halo = lax.ppermute(other, AXES, swap)  7.18 us
    all_gather x1, blocking collectives, per_device(): near_all = lax.all_gather(near, AXES, axis_index_groups=pairs, tiled=True)  2.52 us
  transfers between devices with their start and end apart: 10, of which 6 were waited for; matrix products, arithmetic and copies ran while one was open for 0% of the time, Pallas kernels for 9%

profile of v3, /device:TPU:6, one launch (start us, length us, event | category | flops | bytes accessed | tf_op | source)
XLA Modules:
  0.0 68.1 jit_solution(4716780034078269012)
XLA Ops:
  0.0 0.6 pad_add_fusion.refs_0_
  0.6 3.6 %shard_map.37 = (bf16[256,1024]{1,0:T(8,128)(2,1)}, bf16[128,1024]{1,0:T(8,128)(2,1)}, bf16[64,1024]{1,0:T(8,128)(2,1)}, bf16[512,128]{1,0:T(8,128)(2,1)}) custom-call(s32[3]{0:T(128)} %pad_add_fusion.refs_0_, bf16[256,512]{1,0:T(8,128)(2,1)} %refs_1_.3, bf16[512,1536]{1,0:T(8,128)(2,1)} %refs_2_.3), custom_call_target="tpu_custom_call" | custom-call | flops 268435456 | bytes 1048576 | tf_op jit(solution)/shard_map/pallas_call | solution.py:48
  4.2 2.5 %all_gather.3.refs_0_.refs_4_ = bf16[256,1024]{1,0:T(8,128)(2,1)S(1)} all-gather(bf16[128,1024]{1,0:T(8,128)(2,1)} %get-tuple-element.18), channel_id=1, replica_groups={{0,1},{2,3},{4,5},{6,7},{8,9},{10,11},{12,13},{14,15},{16,17},{18,19},{..., dimensions={0}, use_global_device_ids=true | all-gather | bytes 786432 | tf_op jit(solution)/shard_map/all_gather | solution.py:277
  6.9 11.7 %all-to-all-start = ((bf16[32,16,128]{2,1,0:T(8,128)(2,1)}), bf16[32,16,128]{2,1,0:T(8,128)(2,1)S(1)}, u32[]{:S(2)}, u32[]{:S(2)}) async-start(bf16[32,16,128]{2,1,0:T(8,128)(2,1)} %bitcast.6), calls=%async_computation | async-start | bytes 262144 | tf_op jit(solution)/shard_map/all_to_all | solution.py:302
  18.7 3.7 %collective-permute-start.1 = (bf16[64,1024]{1,0:T(8,128)(2,1)S(1)}, bf16[64,1024]{1,0:T(8,128)(2,1)S(1)}, u32[]{:S(2)}, u32[]{:S(2)}) collective-permute-start(bf16[64,1024]{1,0:T(8,128)(2,1)S(1)} %shard_map.38.refs_0_), channel_id=1, source_target_pairs={{0,2},{1,3},{2,0},{3,1},{4,6},{5,7},{6,4},{7,5},{8,10},{9,11},{10,... | collective-permute-start | bytes 393224 | tf_op jit(solution)/shard_map/ppermute | solution.py:283
  22.4 7.2 %collective-permute-start = (bf16[64,1024]{1,0:T(8,128)(2,1)}, bf16[64,1024]{1,0:T(8,128)(2,1)S(1)}, u32[]{:S(2)}, u32[]{:S(2)}) collective-permute-start(bf16[64,1024]{1,0:T(8,128)(2,1)} %get-tuple-element.19), channel_id=1, source_target_pairs={{1,2},{3,4},{5,6},{7,8},{9,10},{11,12},{13,14},{15,16},{17,18},{19... | collective-permute-start | bytes 393224 | tf_op jit(solution)/shard_map/ppermute | solution.py:280
  29.6 0.3 shard_map.39.refs_2_.refs_0_
  29.9 2.7 %collective-permute-start.3 = (bf16[64,1024]{1,0:T(8,128)(2,1)S(1)}, bf16[64,1024]{1,0:T(8,128)(2,1)S(1)}, u32[]{:S(2)}, u32[]{:S(2)}) collective-permute-start(bf16[64,1024]{1,0:T(8,128)(2,1)S(1)} %shard_map.39.refs_2_.refs_0_), channel_id=1, source_target_pairs={{0,32},{1,33},{2,34},{3,35},{4,36},{5,37},{6,38},{7,39},{8,40},{9,... | collective-permute-start | bytes 393224 | tf_op jit(solution)/shard_map/ppermute | solution.py:283
  32.8 2.9 %collective-permute-start.2 = (bf16[64,1024]{1,0:T(8,128)(2,1)S(1)}, bf16[64,1024]{1,0:T(8,128)(2,1)S(1)}, u32[]{:S(2)}, u32[]{:S(2)}) collective-permute-start(bf16[64,1024]{1,0:T(8,128)(2,1)S(1)} %shard_map.40.refs_6_.refs_0_), channel_id=1, source_target_pairs={{0,4},{1,5},{2,6},{3,7},{4,0},{5,1},{6,2},{7,3},{8,12},{9,13},{10,... | collective-permute-start | bytes 393224 | tf_op jit(solution)/shard_map/ppermute | solution.py:283
  35.8 1.9 %shard_map.41 = (bf16[256,512]{1,0:T(8,128)(2,1)S(1)}, f32[256,512]{1,0:T(8,128)S(1)}, f32[256,512]{1,0:T(8,128)S(1)}) custom-call(s32[3]{0:T(128)S(1)} %copy-done.2, bf16[256,512]{1,0:T(8,128)(2,1)S(1)} %copy-done.1, bf16[512,1536]{1,0:T(8,128)(2,1)S(1)} %copy-done, bf16[256,1024]{1,0:T(8,128)(2,1)S(1)} %copy-done.4, ...), custom_call_target="tpu_custom_call" | custom-call | flops 1000000000 | bytes 1048576 | tf_op jit(solution)/shard_map/pallas_call | solution.py:48
  37.7 1.4 %collective-permute-done.3.refs_1_.refs_7_ = bf16[64,1024]{1,0:T(8,128)(2,1)S(1)} collective-permute-done((bf16[64,1024]{1,0:T(8,128)(2,1)S(1)}, bf16[64,1024]{1,0:T(8,128)(2,1)S(1)}, u32[]{:S(2)}, u32[]{:S(2)}) %collective-permute-start.3) | collective-permute-done | bytes 131104 | tf_op jit(solution)/shard_map/ppermute | solution.py:283
  39.3 4.0 %collective-permute-start.5 = (bf16[64,1024]{1,0:T(8,128)(2,1)S(1)}, bf16[64,1024]{1,0:T(8,128)(2,1)S(1)}, u32[]{:S(2)}, u32[]{:S(2)}) collective-permute-start(bf16[64,1024]{1,0:T(8,128)(2,1)S(1)} %shard_map.42.refs_2_.refs_0_), channel_id=1, source_target_pairs={{0,96},{1,97},{2,98},{3,99},{4,100},{5,101},{6,102},{7,103},{8,104... | collective-permute-start | bytes 393224 | tf_op jit(solution)/shard_map/ppermute | solution.py:283
  43.3 0.2 collective-permute-done.2.refs_1_.refs_6_
  43.7 2.7 %collective-permute-start.4 = (bf16[64,1024]{1,0:T(8,128)(2,1)S(1)}, bf16[64,1024]{1,0:T(8,128)(2,1)S(1)}, u32[]{:S(2)}, u32[]{:S(2)}) collective-permute-start(bf16[64,1024]{1,0:T(8,128)(2,1)S(1)} %shard_map.43.refs_8_.refs_0_), channel_id=1, source_target_pairs={{0,12},{1,13},{2,14},{3,15},{4,8},{5,9},{6,10},{7,11},{8,4},{9,5},... | collective-permute-start | bytes 393224 | tf_op jit(solution)/shard_map/ppermute | solution.py:283
  46.4 1.4 %shard_map.44 = (f32[256,512]{1,0:T(8,128)S(1)}, f32[256,512]{1,0:T(8,128)S(1)}) custom-call(s32[3]{0:T(128)S(1)} %copy-done.2, bf16[256,512]{1,0:T(8,128)(2,1)S(1)} %get-tuple-element.22.refs_2_.refs_1_, f32[256,512]{1,0:T(8,128)S(1)} %get-tuple-element.23.refs_2_, f32[256,512]{1,0:T(8,128)S(1)} %get-tuple-element.24.refs_3_, ...), custom_call_target="tpu_custom_call" | custom-call | flops 1000000000 | bytes 1048576 | tf_op jit(solution)/shard_map/pallas_call | solution.py:48
  47.8 0.5 collective-permute-done.5.refs_1_.refs_6_
  48.4 2.7 %collective-permute-start.7 = (bf16[64,1024]{1,0:T(8,128)(2,1)S(1)}, bf16[64,1024]{1,0:T(8,128)(2,1)S(1)}, u32[]{:S(2)}, u32[]{:S(2)}) collective-permute-start(bf16[64,1024]{1,0:T(8,128)(2,1)S(1)} %shard_map.45.refs_2_.refs_0_), channel_id=1, source_target_pairs={{0,128},{1,129},{2,130},{3,131},{4,132},{5,133},{6,134},{7,135},{8... | collective-permute-start | bytes 393224 | tf_op jit(solution)/shard_map/ppermute | solution.py:283
  51.2 1.8 %collective-permute-done.4.refs_1_.refs_4_ = bf16[64,1024]{1,0:T(8,128)(2,1)S(1)} collective-permute-done((bf16[64,1024]{1,0:T(8,128)(2,1)S(1)}, bf16[64,1024]{1,0:T(8,128)(2,1)S(1)}, u32[]{:S(2)}, u32[]{:S(2)}) %collective-permute-start.4) | collective-permute-done | bytes 131104 | tf_op jit(solution)/shard_map/ppermute | solution.py:283
  53.2 4.3 %collective-permute-start.6 = (bf16[64,1024]{1,0:T(8,128)(2,1)S(1)}, bf16[64,1024]{1,0:T(8,128)(2,1)S(1)}, u32[]{:S(2)}, u32[]{:S(2)}) collective-permute-start(bf16[64,1024]{1,0:T(8,128)(2,1)S(1)} %shard_map.46.refs_2_), channel_id=1, source_target_pairs={{0,16},{1,17},{2,18},{3,19},{4,20},{5,21},{6,22},{7,23},{8,24},{9,... | collective-permute-start | bytes 393224 | tf_op jit(solution)/shard_map/ppermute | solution.py:283
  57.7 2.6 %collective-permute-start.8 = (bf16[64,1024]{1,0:T(8,128)(2,1)S(1)}, bf16[64,1024]{1,0:T(8,128)(2,1)S(1)}, u32[]{:S(2)}, u32[]{:S(2)}) collective-permute-start(bf16[64,1024]{1,0:T(8,128)(2,1)S(1)} %shard_map.47.refs_8_), channel_id=1, source_target_pairs={{0,384},{1,385},{2,386},{3,387},{4,388},{5,389},{6,390},{7,391},{8... | collective-permute-start | bytes 393224 | tf_op jit(solution)/shard_map/ppermute | solution.py:283
  60.3 0.2 collective-permute-done.6.refs_5_
  60.5 1.4 %shard_map.48 = (f32[256,512]{1,0:T(8,128)S(1)}, f32[256,512]{1,0:T(8,128)S(1)}) custom-call(s32[3]{0:T(128)S(1)} %copy-done.2, bf16[256,512]{1,0:T(8,128)(2,1)S(1)} %get-tuple-element.22.refs_2_.refs_1_, f32[256,512]{1,0:T(8,128)S(1)} %get-tuple-element.25.refs_2_, f32[256,512]{1,0:T(8,128)S(1)} %get-tuple-element.26.refs_3_, ...), custom_call_target="tpu_custom_call" | custom-call | flops 1000000000 | bytes 1048576 | tf_op jit(solution)/shard_map/pallas_call | solution.py:48
  61.8 3.9 %collective-permute-done.8.refs_5_ = bf16[64,1024]{1,0:T(8,128)(2,1)S(1)} collective-permute-done((bf16[64,1024]{1,0:T(8,128)(2,1)S(1)}, bf16[64,1024]{1,0:T(8,128)(2,1)S(1)}, u32[]{:S(2)}, u32[]{:S(2)}) %collective-permute-start.8) | collective-permute-done | bytes 131104 | tf_op jit(solution)/shard_map/ppermute | solution.py:283
  65.8 2.3 %shard_map.49 = bf16[256,512]{1,0:T(8,128)(2,1)} custom-call(s32[3]{0:T(128)S(1)} %copy-done.2, bf16[256,512]{1,0:T(8,128)(2,1)S(1)} %get-tuple-element.22.refs_2_.refs_1_, f32[256,512]{1,0:T(8,128)S(1)} %get-tuple-element.27.refs_2_, f32[256,512]{1,0:T(8,128)S(1)} %get-tuple-element.28.refs_3_, bf16[512,512]{1,0:T(8,128)(2,1)S(1)} %copy-done.3, ...), custom_call_target="tpu_custom_call" | custom-call | flops 1000000000 | bytes 1048576 | tf_op jit(solution)/shard_map/pallas_call | solution.py:48
  (21 shorter events, 1.2 us)
Async XLA Ops:
  4.2 31.6 %copy-start = (bf16[512,1536]{1,0:T(8,128)(2,1)S(1)}, bf16[512,1536]{1,0:T(8,128)(2,1)}, u32[]{:S(2)}) copy-start(bf16[512,1536]{1,0:T(8,128)(2,1)} %refs_2_.3) | copy-start | bytes 4718596
  4.2 31.6 %copy-start.1 = (bf16[256,512]{1,0:T(8,128)(2,1)S(1)}, bf16[256,512]{1,0:T(8,128)(2,1)}, u32[]{:S(2)}) copy-start(bf16[256,512]{1,0:T(8,128)(2,1)} %refs_1_.3) | copy-start | bytes 786436
  4.2 31.6 %copy-start.2 = (s32[3]{0:T(128)S(1)}, s32[3]{0:T(128)}, u32[]{:S(2)}) copy-start(s32[3]{0:T(128)} %pad_add_fusion.refs_0_) | copy-start | bytes 40
  4.2 31.6 %copy-start.4 = (bf16[256,1024]{1,0:T(8,128)(2,1)S(1)}, bf16[256,1024]{1,0:T(8,128)(2,1)}, u32[]{:S(2)}) copy-start(bf16[256,1024]{1,0:T(8,128)(2,1)} %get-tuple-element.17.refs_3_) | copy-start | bytes 1572868
  6.9 22.6 %all-to-all-start = ((bf16[32,16,128]{2,1,0:T(8,128)(2,1)}), bf16[32,16,128]{2,1,0:T(8,128)(2,1)S(1)}, u32[]{:S(2)}, u32[]{:S(2)}) async-start(bf16[32,16,128]{2,1,0:T(8,128)(2,1)} %bitcast.6), calls=%async_computation | async-start | bytes 262144 | tf_op jit(solution)/shard_map/all_to_all | solution.py:302
  18.7 14.0 %collective-permute-start.1 = (bf16[64,1024]{1,0:T(8,128)(2,1)S(1)}, bf16[64,1024]{1,0:T(8,128)(2,1)S(1)}, u32[]{:S(2)}, u32[]{:S(2)}) collective-permute-start(bf16[64,1024]{1,0:T(8,128)(2,1)S(1)} %shard_map.38.refs_0_), channel_id=1, source_target_pairs={{0,2},{1,3},{2,0},{3,1},{4,6},{5,7},{6,4},{7,5},{8,10},{9,11},{10,... | collective-permute-start | bytes 393224 | tf_op jit(solution)/shard_map/ppermute | solution.py:283
  22.4 13.4 %collective-permute-start = (bf16[64,1024]{1,0:T(8,128)(2,1)}, bf16[64,1024]{1,0:T(8,128)(2,1)S(1)}, u32[]{:S(2)}, u32[]{:S(2)}) collective-permute-start(bf16[64,1024]{1,0:T(8,128)(2,1)} %get-tuple-element.19), channel_id=1, source_target_pairs={{1,2},{3,4},{5,6},{7,8},{9,10},{11,12},{13,14},{15,16},{17,18},{19... | collective-permute-start | bytes 393224 | tf_op jit(solution)/shard_map/ppermute | solution.py:280
  29.9 9.3 %collective-permute-start.3 = (bf16[64,1024]{1,0:T(8,128)(2,1)S(1)}, bf16[64,1024]{1,0:T(8,128)(2,1)S(1)}, u32[]{:S(2)}, u32[]{:S(2)}) collective-permute-start(bf16[64,1024]{1,0:T(8,128)(2,1)S(1)} %shard_map.39.refs_2_.refs_0_), channel_id=1, source_target_pairs={{0,32},{1,33},{2,34},{3,35},{4,36},{5,37},{6,38},{7,39},{8,40},{9,... | collective-permute-start | bytes 393224 | tf_op jit(solution)/shard_map/ppermute | solution.py:283
  32.8 10.7 %collective-permute-start.2 = (bf16[64,1024]{1,0:T(8,128)(2,1)S(1)}, bf16[64,1024]{1,0:T(8,128)(2,1)S(1)}, u32[]{:S(2)}, u32[]{:S(2)}) collective-permute-start(bf16[64,1024]{1,0:T(8,128)(2,1)S(1)} %shard_map.40.refs_6_.refs_0_), channel_id=1, source_target_pairs={{0,4},{1,5},{2,6},{3,7},{4,0},{5,1},{6,2},{7,3},{8,12},{9,13},{10,... | collective-permute-start | bytes 393224 | tf_op jit(solution)/shard_map/ppermute | solution.py:283
  39.3 9.0 %collective-permute-start.5 = (bf16[64,1024]{1,0:T(8,128)(2,1)S(1)}, bf16[64,1024]{1,0:T(8,128)(2,1)S(1)}, u32[]{:S(2)}, u32[]{:S(2)}) collective-permute-start(bf16[64,1024]{1,0:T(8,128)(2,1)S(1)} %shard_map.42.refs_2_.refs_0_), channel_id=1, source_target_pairs={{0,96},{1,97},{2,98},{3,99},{4,100},{5,101},{6,102},{7,103},{8,104... | collective-permute-start | bytes 393224 | tf_op jit(solution)/shard_map/ppermute | solution.py:283
  43.7 9.3 %collective-permute-start.4 = (bf16[64,1024]{1,0:T(8,128)(2,1)S(1)}, bf16[64,1024]{1,0:T(8,128)(2,1)S(1)}, u32[]{:S(2)}, u32[]{:S(2)}) collective-permute-start(bf16[64,1024]{1,0:T(8,128)(2,1)S(1)} %shard_map.43.refs_8_.refs_0_), channel_id=1, source_target_pairs={{0,12},{1,13},{2,14},{3,15},{4,8},{5,9},{6,10},{7,11},{8,4},{9,5},... | collective-permute-start | bytes 393224 | tf_op jit(solution)/shard_map/ppermute | solution.py:283
  48.4 9.1 %collective-permute-start.7 = (bf16[64,1024]{1,0:T(8,128)(2,1)S(1)}, bf16[64,1024]{1,0:T(8,128)(2,1)S(1)}, u32[]{:S(2)}, u32[]{:S(2)}) collective-permute-start(bf16[64,1024]{1,0:T(8,128)(2,1)S(1)} %shard_map.45.refs_2_.refs_0_), channel_id=1, source_target_pairs={{0,128},{1,129},{2,130},{3,131},{4,132},{5,133},{6,134},{7,135},{8... | collective-permute-start | bytes 393224 | tf_op jit(solution)/shard_map/ppermute | solution.py:283
  53.2 7.3 %collective-permute-start.6 = (bf16[64,1024]{1,0:T(8,128)(2,1)S(1)}, bf16[64,1024]{1,0:T(8,128)(2,1)S(1)}, u32[]{:S(2)}, u32[]{:S(2)}) collective-permute-start(bf16[64,1024]{1,0:T(8,128)(2,1)S(1)} %shard_map.46.refs_2_), channel_id=1, source_target_pairs={{0,16},{1,17},{2,18},{3,19},{4,20},{5,21},{6,22},{7,23},{8,24},{9,... | collective-permute-start | bytes 393224 | tf_op jit(solution)/shard_map/ppermute | solution.py:283
  57.7 8.1 %collective-permute-start.8 = (bf16[64,1024]{1,0:T(8,128)(2,1)S(1)}, bf16[64,1024]{1,0:T(8,128)(2,1)S(1)}, u32[]{:S(2)}, u32[]{:S(2)}) collective-permute-start(bf16[64,1024]{1,0:T(8,128)(2,1)S(1)} %shard_map.47.refs_8_), channel_id=1, source_target_pairs={{0,384},{1,385},{2,386},{3,387},{4,388},{5,389},{6,390},{7,391},{8... | collective-permute-start | bytes 393224 | tf_op jit(solution)/shard_map/ppermute | solution.py:283
  60.5 5.3 %copy-start.3 = (bf16[512,512]{1,0:T(8,128)(2,1)S(1)}, bf16[512,512]{1,0:T(8,128)(2,1)}, u32[]{:S(2)}) copy-start(bf16[512,512]{1,0:T(8,128)(2,1)} %refs_4_.1) | copy-start | bytes 1572868

commit v4 on v3

--- a/solution.py
+++ b/solution.py
@@ -104,11 +104,11 @@
                     near_ref[BLOCK:, tile * 128 : (tile + 1) * 128] = level
                 part_buf[tile, :size, :] = level.astype(jnp.float32)
             pieces.append(level.astype(jnp.float32))
-    packed = pooled(pooled(jnp.concatenate(pieces, axis=0).astype(jnp.bfloat16)))
+    packed = pooled(jnp.concatenate(pieces, axis=0).astype(jnp.bfloat16))
     size = packed.shape[0]
     for copy in range(packed_ref.shape[0] // size):
         packed_ref[copy * size : (copy + 1) * size, :] = packed
-    core = place[0]
+    core = place[0] & 1
     last = rows - BLOCK
     low = pl.multiple_of(core * last, BLOCK)
     high = pl.multiple_of((1 - core) * last, BLOCK)
@@ -116,22 +116,27 @@
     other_ref[...] = kv_ref[pl.ds(low, BLOCK), :]
 
 
-def unpack_kernel(in_ref, out_ref):
-    total = in_ref.shape[0]
-    tiles = out_ref.shape[1] // 128
-    row = lax.broadcasted_iota(jnp.int32, (BLOCK, total), 0)
-    column = lax.broadcasted_iota(jnp.int32, (BLOCK, total), 1)
-    source = (row >> 1) * (2 * tiles) + (row & 1)
+def unpack_kernel(place, in_ref, own_6_ref, own_7_ref):
+    half = in_ref.shape[0] // 2
+    tiles = own_6_ref.shape[1] // 128
+    row = lax.broadcasted_iota(jnp.int32, (BLOCK, half), 0)
+    column = lax.broadcasted_iota(jnp.int32, (BLOCK, half), 1)
+    source = (row >> 2) * (4 * tiles) + (row & 3)
+    upper = (place[0] >> 4) & 1
     for tile in range(tiles):
-        pick = jnp.where(column == source + 2 * tile, 1.0, 0.0).astype(jnp.bfloat16)
-        out_ref[:, tile * 128 : (tile + 1) * 128] = jnp.dot(
-            pick, in_ref[...], preferred_element_type=jnp.float32
-        ).astype(jnp.bfloat16)
-
-
-def pool_near_kernel(near_ref, out_ref):
-    out_ref[: BLOCK // 2, :] = pooled(near_ref[BLOCK : 2 * BLOCK, :])
-    out_ref[BLOCK // 2 :, :] = pooled(near_ref[3 * BLOCK :, :])
+        lanes = slice(tile * 128, (tile + 1) * 128)
+        pick = jnp.where(column == source + 4 * tile, 1.0, 0.0).astype(jnp.bfloat16)
+        parts = [
+            jnp.dot(pick, in_ref[at : at + half, :], preferred_element_type=jnp.float32)
+            for at in (0, half)
+        ]
+        own_6_ref[:, lanes] = jnp.where(upper == 1, parts[1], parts[0]).astype(jnp.bfloat16)
+        own_7_ref[:, lanes] = pooled(jnp.concatenate(parts, axis=0).astype(jnp.bfloat16))
+
+
+def pool_near_kernel(near_ref, sib_ref, out_ref):
+    out_ref[: BLOCK // 2, :] = pooled(near_ref[BLOCK:, :])
+    out_ref[BLOCK // 2 :, :] = pooled(sib_ref[BLOCK:, :])
 
 
 def pool_kernel(*refs):
@@ -160,14 +165,14 @@
 
 
 def local_kernel(
-    place, x_ref, w_hbm, kv_ref, near_ref, other_ref, q_ref, num_ref, tot_ref, pad, l1, w_ref, sem
+    count, place, x_ref, w_hbm, kv_ref, near_ref, other_ref, q_ref, num_ref, tot_ref, pad, l1, w_ref, sem
 ):
     rows, model = x_ref.shape
     blocks = rows // BLOCK
     copy = pltpu.make_async_copy(w_hbm.at[:, pl.ds(0, model)], w_ref, sem)
     copy.start()
-    core = place[0]
-    sib_halo = near_ref[pl.ds(pl.multiple_of((1 - core) * 2 * BLOCK, BLOCK), BLOCK), :]
+    core = place[0] & 1
+    sib_halo = near_ref[:BLOCK, :]
     other = other_ref[...]
     is_first = core == 0
     pad[:BLOCK, :] = jnp.where(is_first, other, sib_halo)
@@ -183,9 +188,9 @@
     for i in range(blocks):
         ones = jnp.ones((4 * BLOCK, 128), jnp.float32)
         if i == 0:
-            ones = jnp.where((key_row < BLOCK) & (place[1] == 1), 0.0, ones)
+            ones = jnp.where((key_row < BLOCK) & (place[0] == 0), 0.0, ones)
         if i == blocks - 1:
-            ones = jnp.where((key_row >= 2 * BLOCK) & (key_row < 3 * BLOCK) & (place[2] == 1), 0.0, ones)
+            ones = jnp.where((key_row >= 2 * BLOCK) & (key_row < 3 * BLOCK) & (place[0] == count - 1), 0.0, ones)
         ones = ones.astype(jnp.bfloat16)
         sib = (i >> 1) ^ 1
         here = slice(i * BLOCK, (i + 1) * BLOCK)
@@ -203,15 +208,10 @@
             tot_ref[here, kl] = tot
 
 
-def sibling_blocks(place, kinds, refs):
-    blocks = []
-    for kind, ref in zip(kinds, refs):
-        if kind == "near":
-            start = (1 - place[0]) * 2 * BLOCK + BLOCK
-            blocks.append(ref[pl.ds(pl.multiple_of(start, BLOCK), BLOCK), :])
-        else:
-            blocks.append(ref[...])
-    return jnp.concatenate(blocks, axis=0)
+def far_blocks(refs):
+    return jnp.concatenate(
+        [ref[BLOCK:, :] if ref.shape[0] == 2 * BLOCK else ref[...] for ref in refs], axis=0
+    )
 
 
 def far_sums(far, q, lanes, model):
@@ -220,10 +220,10 @@
     return attend_pair(q, keys, values, jnp.ones(values.shape, jnp.bfloat16))
 
 
-def far_kernel(kinds, place, q_ref, num_in, tot_in, *refs):
+def far_kernel(q_ref, num_in, tot_in, *refs):
     num_ref, tot_ref = refs[-2:]
     model = q_ref.shape[1]
-    far = sibling_blocks(place, kinds, refs[:-2])
+    far = far_blocks(refs[:-2])
     for lanes in range(0, model, 128):
         at = slice(lanes, lanes + 128)
         num, tot = far_sums(far, q_ref[:, at], lanes, model)
@@ -231,10 +231,10 @@
         tot_ref[:, at] = tot_in[:, at] + tot
 
 
-def final_kernel(kinds, place, q_ref, num_in, tot_in, w_ref, *refs):
+def final_kernel(q_ref, num_in, tot_in, w_ref, *refs):
     out_ref, att = refs[-2:]
     model = q_ref.shape[1]
-    far = sibling_blocks(place, kinds, refs[:-2])
+    far = far_blocks(refs[:-2])
     for lanes in range(0, model, 128):
         at = slice(lanes, lanes + 128)
         num, tot = far_sums(far, q_ref[:, at], lanes, model)
@@ -248,18 +248,16 @@
     rows, model = tokens.shape
     index = lax.axis_index(AXES)
     count = lax.axis_size(AXES)
-    place = jnp.stack(
-        [index & 1, (index == 0).astype(jnp.int32), (index == count - 1).astype(jnp.int32)]
-    ).astype(jnp.int32)
+    place = index.astype(jnp.int32).reshape(1)
     bf16 = lambda *shape: jax.ShapeDtypeStruct(shape, jnp.bfloat16)
     f32 = lambda *shape: jax.ShapeDtypeStruct(shape, jnp.float32)
     anywhere = pl.BlockSpec(memory_space=pl.ANY)
     steps = 2
     width = 2 * model // steps
     members = 32
-    packed = 2 * 2 * model // 128
+    packed = 4 * 2 * model // 128
     block = bf16(BLOCK, 2 * model)
-    kv, near, other, level_7 = call(
+    kv, near, other, level_6 = call(
         project_kernel,
         (bf16(rows, 2 * model), bf16(2 * BLOCK, 2 * model), block, bf16(members * packed, 128)),
         [SMEM, anywhere, anywhere],
@@ -273,12 +271,8 @@
         ),
         limit=56,
     )
-    pairs = [[i, i ^ 1] for i in range(0, count, 2)]
-    near_all = lax.all_gather(near, AXES, axis_index_groups=pairs, tiled=True)
     swap = [(i, i + 1) for i in range(1, count - 1, 2)]
     swap += [(j, i) for i, j in swap]
-    other_halo = lax.ppermute(other, AXES, swap)
-
     def exchange(own, bit):
         return lax.ppermute(own, AXES, list(enumerate(partners(bit, count))))
 
@@ -287,28 +281,37 @@
 
     def far(num, tot, *part, after=()):
         return call(
-            functools.partial(far_kernel, tuple(kind for kind, _ in part)),
+            far_kernel,
             (f32(rows, model), f32(rows, model)),
-            [SMEM, *vmem(3 + len(part))],
-            place, q, num, tot, *[got for _, got in part],
+            vmem(3 + len(part)),
+            q, num, tot, *part,
             flops=10**9,
             after=after,
         )
 
-    own_3 = call(pool_near_kernel, block, vmem(1), near_all)
+    teams = [list(range(i, i + members)) for i in range(0, count, members)]
+    spread = lax.all_to_all(level_6, AXES, 0, 0, axis_index_groups=teams, tiled=True)
+    near_sib = exchange(near, 0)
+    other_halo = lax.ppermute(other, AXES, swap)
+
+    own_3 = call(pool_near_kernel, block, vmem(2), near, near_sib)
     sib_3 = exchange(own_3, 1)
-    level_7, _ = lax.optimization_barrier((level_7, own_3))
-    teams = [list(range(i, i + members)) for i in range(0, count, members)]
-    spread = lax.all_to_all(level_7, AXES, 0, 0, axis_index_groups=teams, tiled=True)
-    own_7 = call(unpack_kernel, block, vmem(1), spread)
+    own_6, own_7 = call(
+        unpack_kernel, (block, block), [SMEM, *vmem(1)], place, spread, after=(own_3, other_halo)
+    )
     sib_7 = exchange(own_7, 5)
+    sib_6 = exchange(own_6, 4)
     own_4 = pool(own_3, sib_3, own_7)
     sib_4 = exchange(own_4, 2)
+    own_8 = pool(own_7, sib_7, own_4)
+    sib_8 = exchange(own_8, 6)
+    own_5 = pool(own_4, sib_4, own_8)
+    sib_5 = exchange(own_5, 3)
     q, num, tot = call(
-        local_kernel,
+        functools.partial(local_kernel, count),
         (bf16(rows, model), f32(rows, model), f32(rows, model)),
         [SMEM, *vmem(1), anywhere, *vmem(3)],
-        place, tokens, w_qkv, kv, near_all, other_halo,
+        place, tokens, w_qkv, kv, near_sib, other_halo,
         flops=10**9,
         scratch=(
             pltpu.VMEM((rows + 2 * BLOCK, 2 * model), jnp.bfloat16),
@@ -316,29 +319,19 @@
             pltpu.VMEM((model, model), jnp.bfloat16),
             pltpu.SemaphoreType.DMA(()),
         ),
-        after=(own_4,),
-    )
-    own_8 = pool(own_7, sib_7, q)
-    sib_8 = exchange(own_8, 6)
-    own_5 = pool(own_4, sib_4, own_8)
-    sib_5 = exchange(own_5, 3)
-    num, tot = far(
-        num, tot, ("near", near_all), ("pp", sib_3), ("pp", sib_4), ("pp", sib_7), after=(own_5,)
-    )
-    own_9 = pool(own_8, sib_8, num)
+        after=(own_5,),
+    )
+    own_9 = pool(own_8, sib_8, q, sib_6)
     sib_9 = exchange(own_9, 7)
-    own_6 = pool(own_5, sib_5, own_9)
-    sib_6 = exchange(own_6, 4)
-    own_10 = pool(own_9, sib_9, own_6)
+    own_10 = pool(own_9, sib_9)
+    num, tot = far(num, tot, near_sib, sib_3, sib_4, sib_6, after=(own_10,))
     sib_10 = exchange(own_10, 8)
-    num, tot = far(
-        num, tot, ("pp", sib_5), ("pp", sib_6), ("pp", sib_8), ("pp", sib_9), after=(own_10,)
-    )
+    num, tot = far(num, tot, sib_5, sib_7, sib_8, sib_9, after=(own_10,))
     return call(
-        functools.partial(final_kernel, ("pp",)),
+        final_kernel,
         bf16(rows, model),
-        [SMEM, *vmem(5)],
-        place, q, num, tot, w_out, sib_10,
+        vmem(5),
+        q, num, tot, w_out, sib_10,
         flops=10**9,
         scratch=(pltpu.VMEM((rows, model), jnp.bfloat16),),
     )

time: 69.4 us -> 68.5 us (0.987)
  blocking collectives: 2.52 us -> 0 us
  Pallas kernels: 12 us -> 10.2 us
  starting transfers between devices: 44.6 us -> 46.2 us
  waiting for transfers between devices: 8.05 us -> 9.62 us
  local copies, waits for them, and re-layouts: 0.02 us -> 0.96 us
    all_gather x1 -> x0, blocking collectives: 2.52 us -> none  [per_device(): near_all = lax.all_gather(near, AXES, axis_index_groups=pairs, tiled=True)]
    pallas_call x13 -> x12, Pallas kernels: 12 us -> 10.2 us  [call(): pl.pallas_call(body, out_shape=outs, in_specs=list(in_specs) + [pl.BlockS...]
    ppermute x8 -> x9, waiting for transfers between devices: 8.05 us -> 9.62 us  [exchange(): return lax.ppermute(own, AXES, list(enumerate(partners(bit, count))))]
    unnamed x10, local copies, waits for them, and re-layouts: 0.02 us -> 0.96 us
    ppermute x8 -> x9, starting transfers between devices: 25.7 us -> 26.4 us  [exchange(): return lax.ppermute(own, AXES, list(enumerate(partners(bit, count))))]
    ppermute x1, starting transfers between devices: 7.18 us -> 7.89 us  [per_device(): other_halo = lax.ppermute(other, AXES, swap)]
  transfers between devices with their start and end apart: 10 -> 11, of which waited for: 6 -> 5; matrix products, arithmetic and copies ran while one was open for 0% -> 0% of each run, Pallas kernels for 9% -> 8%
where the time goes in v4:
time: 68.5 us; the launch traced here: 67.3 us
  starting transfers between devices  46.2 us (67%)
  Pallas kernels  10.2 us (15%)
  waiting for transfers between devices  9.62 us (14%)
  local copies, waits for them, and re-layouts  0.96 us (1%)
    ppermute x9, starting transfers between devices, exchange(): return lax.ppermute(own, AXES, list(enumerate(partners(bit, count))))  26.4 us
    all_to_all x1, starting transfers between devices, per_device(): lax.all_to_all(level_6, AXES, 0, 0, axis_index_groups=teams, tiled=True)  11.9 us
    pallas_call x12, Pallas kernels, call(): pl.pallas_call(body, out_shape=outs, in_specs=list(in_specs) + [pl.BlockS...  10.2 us
    ppermute x9, waiting for transfers between devices, exchange(): return lax.ppermute(own, AXES, list(enumerate(partners(bit, count))))  9.62 us
    ppermute x1, starting transfers between devices, per_device(): other_halo = lax.ppermute(other, AXES, swap)  7.89 us
  transfers between devices with their start and end apart: 11, of which 5 were waited for; matrix products, arithmetic and copies ran while one was open for 0% of the time, Pallas kernels for 8%

profile of v4, /device:TPU:6, one launch (start us, length us, event | category | flops | bytes accessed | tf_op | source)
XLA Modules:
  0.0 67.3 jit_solution(15659141709725151571)
XLA Ops:
  0.0 3.0 %shard_map.37 = (bf16[256,1024]{1,0:T(8,128)(2,1)}, bf16[128,1024]{1,0:T(8,128)(2,1)}, bf16[64,1024]{1,0:T(8,128)(2,1)}, bf16[1024,128]{1,0:T(8,128)(2,1)}) custom-call(s32[1]{0:T(128)} %bitcast.refs_0_, bf16[256,512]{1,0:T(8,128)(2,1)} %refs_1_.3, bf16[512,1536]{1,0:T(8,128)(2,1)} %refs_2_.3), custom_call_target="tpu_custom_call" | custom-call | flops 268435456 | bytes 1048576 | tf_op jit(solution)/shard_map/pallas_call | solution.py:48
  3.0 11.9 %all-to-all-start = ((bf16[32,32,128]{2,1,0:T(8,128)(2,1)}), bf16[32,32,128]{2,1,0:T(8,128)(2,1)S(1)}, u32[]{:S(2)}, u32[]{:S(2)}) async-start(bf16[32,32,128]{2,1,0:T(8,128)(2,1)} %bitcast.4), calls=%async_computation | async-start | bytes 524288 | tf_op jit(solution)/shard_map/all_to_all | solution.py:293
  14.9 2.2 %collective-permute-start = (bf16[128,1024]{1,0:T(8,128)(2,1)}, bf16[128,1024]{1,0:T(8,128)(2,1)S(1)}, u32[]{:S(2)}, u32[]{:S(2)}) collective-permute-start(bf16[128,1024]{1,0:T(8,128)(2,1)} %get-tuple-element.19.refs_0_), channel_id=1, source_target_pairs={{0,1},{1,0},{2,3},{3,2},{4,5},{5,4},{6,7},{7,6},{8,9},{9,8},{10,11... | collective-permute-start | bytes 786440 | tf_op jit(solution)/shard_map/ppermute | solution.py:277
  17.1 7.9 %collective-permute-start.1 = (bf16[64,1024]{1,0:T(8,128)(2,1)}, bf16[64,1024]{1,0:T(8,128)(2,1)S(1)}, u32[]{:S(2)}, u32[]{:S(2)}) collective-permute-start(bf16[64,1024]{1,0:T(8,128)(2,1)} %get-tuple-element.20), channel_id=1, source_target_pairs={{1,2},{3,4},{5,6},{7,8},{9,10},{11,12},{13,14},{15,16},{17,18},{19... | collective-permute-start | bytes 393224 | tf_op jit(solution)/shard_map/ppermute | solution.py:295
  25.0 0.9 %copy-done.1 = bf16[128,1024]{1,0:T(8,128)(2,1)S(1)} copy-done((bf16[128,1024]{1,0:T(8,128)(2,1)S(1)}, bf16[128,1024]{1,0:T(8,128)(2,1)}, u32[]{:S(2)}) %copy-start.1) | copy-done | bytes 262168
  26.1 1.9 %collective-permute-start.2 = (bf16[64,1024]{1,0:T(8,128)(2,1)S(1)}, bf16[64,1024]{1,0:T(8,128)(2,1)S(1)}, u32[]{:S(2)}, u32[]{:S(2)}) collective-permute-start(bf16[64,1024]{1,0:T(8,128)(2,1)S(1)} %shard_map.38.refs_2_.refs_0_), channel_id=1, source_target_pairs={{0,2},{1,3},{2,0},{3,1},{4,6},{5,7},{6,4},{7,5},{8,10},{9,11},{10,... | collective-permute-start | bytes 393224 | tf_op jit(solution)/shard_map/ppermute | solution.py:277
  28.1 1.5 %shard_map.39 = (bf16[64,1024]{1,0:T(8,128)(2,1)S(1)}, bf16[64,1024]{1,0:T(8,128)(2,1)S(1)}) custom-call(s32[1]{0:T(128)} %bitcast.refs_0_, bf16[1024,128]{1,0:T(8,128)(2,1)S(1)} %bitcast.3, bf16[64,1024]{1,0:T(8,128)(2,1)S(1)} %shard_map.38.refs_2_.refs_0_, bf16[64,1024]{1,0:T(8,128)(2,1)S(1)} %collective-permute-done.1.refs_3_.refs_5_), custom_call_target="tpu_custom_call" | custom-call | bytes 1048576 | tf_op jit(solution)/shard_map/pallas_call | solution.py:48
  29.6 2.5 %collective-permute-start.4 = (bf16[64,1024]{1,0:T(8,128)(2,1)S(1)}, bf16[64,1024]{1,0:T(8,128)(2,1)S(1)}, u32[]{:S(2)}, u32[]{:S(2)}) collective-permute-start(bf16[64,1024]{1,0:T(8,128)(2,1)S(1)} %get-tuple-element.22.refs_2_.refs_0_), channel_id=1, source_target_pairs={{0,32},{1,33},{2,34},{3,35},{4,36},{5,37},{6,38},{7,39},{8,40},{9,... | collective-permute-start | bytes 393224 | tf_op jit(solution)/shard_map/ppermute | solution.py:277
  32.1 0.9 %collective-permute-done.2.refs_1_.refs_4_ = bf16[64,1024]{1,0:T(8,128)(2,1)S(1)} collective-permute-done((bf16[64,1024]{1,0:T(8,128)(2,1)S(1)}, bf16[64,1024]{1,0:T(8,128)(2,1)S(1)}, u32[]{:S(2)}, u32[]{:S(2)}) %collective-permute-start.2) | collective-permute-done | bytes 131104 | tf_op jit(solution)/shard_map/ppermute | solution.py:277
  33.2 2.8 %collective-permute-start.3 = (bf16[64,1024]{1,0:T(8,128)(2,1)S(1)}, bf16[64,1024]{1,0:T(8,128)(2,1)S(1)}, u32[]{:S(2)}, u32[]{:S(2)}) collective-permute-start(bf16[64,1024]{1,0:T(8,128)(2,1)S(1)} %shard_map.40.refs_2_.refs_0_), channel_id=1, source_target_pairs={{0,4},{1,5},{2,6},{3,7},{4,0},{5,1},{6,2},{7,3},{8,12},{9,13},{10,... | collective-permute-start | bytes 393224 | tf_op jit(solution)/shard_map/ppermute | solution.py:277
  36.0 3.4 %collective-permute-start.5 = (bf16[64,1024]{1,0:T(8,128)(2,1)S(1)}, bf16[64,1024]{1,0:T(8,128)(2,1)S(1)}, u32[]{:S(2)}, u32[]{:S(2)}) collective-permute-start(bf16[64,1024]{1,0:T(8,128)(2,1)S(1)} %get-tuple-element.26), channel_id=1, source_target_pairs={{0,16},{1,17},{2,18},{3,19},{4,20},{5,21},{6,22},{7,23},{8,24},{9,... | collective-permute-start | bytes 393224 | tf_op jit(solution)/shard_map/ppermute | solution.py:277
  39.4 0.2 shard_map.41.refs_2_.refs_0_
  39.5 4.8 %collective-permute-start.6 = (bf16[64,1024]{1,0:T(8,128)(2,1)S(1)}, bf16[64,1024]{1,0:T(8,128)(2,1)S(1)}, u32[]{:S(2)}, u32[]{:S(2)}) collective-permute-start(bf16[64,1024]{1,0:T(8,128)(2,1)S(1)} %shard_map.41.refs_2_.refs_0_), channel_id=1, source_target_pairs={{0,96},{1,97},{2,98},{3,99},{4,100},{5,101},{6,102},{7,103},{8,104... | collective-permute-start | bytes 393224 | tf_op jit(solution)/shard_map/ppermute | solution.py:277
  44.6 1.4 %shard_map.43 = (bf16[256,512]{1,0:T(8,128)(2,1)S(1)}, f32[256,512]{1,0:T(8,128)S(1)}, f32[256,512]{1,0:T(8,128)S(1)}) custom-call(s32[1]{0:T(128)} %bitcast.refs_0_, bf16[256,512]{1,0:T(8,128)(2,1)S(1)} %copy-done.2, bf16[512,1536]{1,0:T(8,128)(2,1)S(1)} %copy-done, bf16[256,1024]{1,0:T(8,128)(2,1)S(1)} %copy-done.4, ...), custom_call_target="tpu_custom_call" | custom-call | flops 1000000000 | bytes 1048576 | tf_op jit(solution)/shard_map/pallas_call | solution.py:48
  45.9 4.1 %collective-permute-done.6.refs_1_.refs_5_ = bf16[64,1024]{1,0:T(8,128)(2,1)S(1)} collective-permute-done((bf16[64,1024]{1,0:T(8,128)(2,1)S(1)}, bf16[64,1024]{1,0:T(8,128)(2,1)S(1)}, u32[]{:S(2)}, u32[]{:S(2)}) %collective-permute-start.6) | collective-permute-done | bytes 131104 | tf_op jit(solution)/shard_map/ppermute | solution.py:277
  50.2 2.7 %collective-permute-start.7 = (bf16[64,1024]{1,0:T(8,128)(2,1)S(1)}, bf16[64,1024]{1,0:T(8,128)(2,1)S(1)}, u32[]{:S(2)}, u32[]{:S(2)}) collective-permute-start(bf16[64,1024]{1,0:T(8,128)(2,1)S(1)} %shard_map.44.refs_0_), channel_id=1, source_target_pairs={{0,128},{1,129},{2,130},{3,131},{4,132},{5,133},{6,134},{7,135},{8... | collective-permute-start | bytes 393224 | tf_op jit(solution)/shard_map/ppermute | solution.py:277
  52.9 3.7 %collective-permute-start.8 = (bf16[64,1024]{1,0:T(8,128)(2,1)S(1)}, bf16[64,1024]{1,0:T(8,128)(2,1)S(1)}, u32[]{:S(2)}, u32[]{:S(2)}) collective-permute-start(bf16[64,1024]{1,0:T(8,128)(2,1)S(1)} %shard_map.42.refs_6_), channel_id=1, source_target_pairs={{0,12},{1,13},{2,14},{3,15},{4,8},{5,9},{6,10},{7,11},{8,4},{9,5},... | collective-permute-start | bytes 393224 | tf_op jit(solution)/shard_map/ppermute | solution.py:277
  56.6 0.7 %collective-permute-done.7.refs_1_.refs_6_ = bf16[64,1024]{1,0:T(8,128)(2,1)S(1)} collective-permute-done((bf16[64,1024]{1,0:T(8,128)(2,1)S(1)}, bf16[64,1024]{1,0:T(8,128)(2,1)S(1)}, u32[]{:S(2)}, u32[]{:S(2)}) %collective-permute-start.7) | collective-permute-done | bytes 131104 | tf_op jit(solution)/shard_map/ppermute | solution.py:277
  57.4 2.4 %collective-permute-start.9 = (bf16[64,1024]{1,0:T(8,128)(2,1)S(1)}, bf16[64,1024]{1,0:T(8,128)(2,1)S(1)}, u32[]{:S(2)}, u32[]{:S(2)}) collective-permute-start(bf16[64,1024]{1,0:T(8,128)(2,1)S(1)} %shard_map.45.refs_7_), channel_id=1, source_target_pairs={{0,384},{1,385},{2,386},{3,387},{4,388},{5,389},{6,390},{7,391},{8... | collective-permute-start | bytes 393224 | tf_op jit(solution)/shard_map/ppermute | solution.py:277
  59.8 0.8 %shard_map.46 = (f32[256,512]{1,0:T(8,128)S(1)}, f32[256,512]{1,0:T(8,128)S(1)}) custom-call(bf16[256,512]{1,0:T(8,128)(2,1)S(1)} %get-tuple-element.23.refs_2_.refs_0_, f32[256,512]{1,0:T(8,128)S(1)} %get-tuple-element.24.refs_1_, f32[256,512]{1,0:T(8,128)S(1)} %get-tuple-element.25.refs_2_, ...), custom_call_target="tpu_custom_call" | custom-call | flops 1000000000 | bytes 1048576 | tf_op jit(solution)/shard_map/pallas_call | solution.py:48
  60.7 1.3 %collective-permute-done.8.refs_3_ = bf16[64,1024]{1,0:T(8,128)(2,1)S(1)} collective-permute-done((bf16[64,1024]{1,0:T(8,128)(2,1)S(1)}, bf16[64,1024]{1,0:T(8,128)(2,1)S(1)}, u32[]{:S(2)}, u32[]{:S(2)}) %collective-permute-start.8) | collective-permute-done | bytes 131104 | tf_op jit(solution)/shard_map/ppermute | solution.py:277
  61.9 0.8 %shard_map.47 = (f32[256,512]{1,0:T(8,128)S(1)}, f32[256,512]{1,0:T(8,128)S(1)}) custom-call(bf16[256,512]{1,0:T(8,128)(2,1)S(1)} %get-tuple-element.23.refs_2_.refs_0_, f32[256,512]{1,0:T(8,128)S(1)} %get-tuple-element.27.refs_1_, f32[256,512]{1,0:T(8,128)S(1)} %get-tuple-element.28.refs_2_, bf16[64,1024]{1,0:T(8,128)(2,1)S(1)} %collective-permute-done.8.refs_3_, ...), custom_call_target="tpu_custom_call" | custom-call | flops 1000000000 | bytes 1048576 | tf_op jit(solution)/shard_map/pallas_call | solution.py:48
  62.8 2.7 %collective-permute-done.9.refs_4_ = bf16[64,1024]{1,0:T(8,128)(2,1)S(1)} collective-permute-done((bf16[64,1024]{1,0:T(8,128)(2,1)S(1)}, bf16[64,1024]{1,0:T(8,128)(2,1)S(1)}, u32[]{:S(2)}, u32[]{:S(2)}) %collective-permute-start.9) | collective-permute-done | bytes 131104 | tf_op jit(solution)/shard_map/ppermute | solution.py:277
  65.5 1.7 %shard_map.48 = bf16[256,512]{1,0:T(8,128)(2,1)} custom-call(bf16[256,512]{1,0:T(8,128)(2,1)S(1)} %get-tuple-element.23.refs_2_.refs_0_, f32[256,512]{1,0:T(8,128)S(1)} %get-tuple-element.29.refs_1_, f32[256,512]{1,0:T(8,128)S(1)} %get-tuple-element.30.refs_2_, bf16[512,512]{1,0:T(8,128)(2,1)S(1)} %copy-done.3, ...), custom_call_target="tpu_custom_call" | custom-call | flops 1000000000 | bytes 1048576 | tf_op jit(solution)/shard_map/pallas_call | solution.py:48
  (20 shorter events, 0.8 us)
Async XLA Ops:
  0.0 44.5 %copy-start.2 = (bf16[256,512]{1,0:T(8,128)(2,1)S(1)}, bf16[256,512]{1,0:T(8,128)(2,1)}, u32[]{:S(2)}) copy-start(bf16[256,512]{1,0:T(8,128)(2,1)} %refs_1_.3) | copy-start | bytes 786436
  3.0 41.5 %copy-start = (bf16[512,1536]{1,0:T(8,128)(2,1)S(1)}, bf16[512,1536]{1,0:T(8,128)(2,1)}, u32[]{:S(2)}) copy-start(bf16[512,1536]{1,0:T(8,128)(2,1)} %refs_2_.3) | copy-start | bytes 4718596
  3.0 25.0 %all-to-all-start = ((bf16[32,32,128]{2,1,0:T(8,128)(2,1)}), bf16[32,32,128]{2,1,0:T(8,128)(2,1)S(1)}, u32[]{:S(2)}, u32[]{:S(2)}) async-start(bf16[32,32,128]{2,1,0:T(8,128)(2,1)} %bitcast.4), calls=%async_computation | async-start | bytes 524288 | tf_op jit(solution)/shard_map/all_to_all | solution.py:293
  14.9 10.1 %collective-permute-start = (bf16[128,1024]{1,0:T(8,128)(2,1)}, bf16[128,1024]{1,0:T(8,128)(2,1)S(1)}, u32[]{:S(2)}, u32[]{:S(2)}) collective-permute-start(bf16[128,1024]{1,0:T(8,128)(2,1)} %get-tuple-element.19.refs_0_), channel_id=1, source_target_pairs={{0,1},{1,0},{2,3},{3,2},{4,5},{5,4},{6,7},{7,6},{8,9},{9,8},{10,11... | collective-permute-start | bytes 786440 | tf_op jit(solution)/shard_map/ppermute | solution.py:277
  17.1 11.0 %collective-permute-start.1 = (bf16[64,1024]{1,0:T(8,128)(2,1)}, bf16[64,1024]{1,0:T(8,128)(2,1)S(1)}, u32[]{:S(2)}, u32[]{:S(2)}) collective-permute-start(bf16[64,1024]{1,0:T(8,128)(2,1)} %get-tuple-element.20), channel_id=1, source_target_pairs={{1,2},{3,4},{5,6},{7,8},{9,10},{11,12},{13,14},{15,16},{17,18},{19... | collective-permute-start | bytes 393224 | tf_op jit(solution)/shard_map/ppermute | solution.py:295
  25.0 1.0 %copy-start.1 = (bf16[128,1024]{1,0:T(8,128)(2,1)S(1)}, bf16[128,1024]{1,0:T(8,128)(2,1)}, u32[]{:S(2)}) copy-start(bf16[128,1024]{1,0:T(8,128)(2,1)} %get-tuple-element.19.refs_0_) | copy-start | bytes 786436
  26.0 18.6 %copy-start.4 = (bf16[256,1024]{1,0:T(8,128)(2,1)S(1)}, bf16[256,1024]{1,0:T(8,128)(2,1)}, u32[]{:S(2)}) copy-start(bf16[256,1024]{1,0:T(8,128)(2,1)} %get-tuple-element.18.refs_3_) | copy-start | bytes 1572868
  26.1 6.9 %collective-permute-start.2 = (bf16[64,1024]{1,0:T(8,128)(2,1)S(1)}, bf16[64,1024]{1,0:T(8,128)(2,1)S(1)}, u32[]{:S(2)}, u32[]{:S(2)}) collective-permute-start(bf16[64,1024]{1,0:T(8,128)(2,1)S(1)} %shard_map.38.refs_2_.refs_0_), channel_id=1, source_target_pairs={{0,2},{1,3},{2,0},{3,1},{4,6},{5,7},{6,4},{7,5},{8,10},{9,11},{10,... | collective-permute-start | bytes 393224 | tf_op jit(solution)/shard_map/ppermute | solution.py:277
  29.6 9.8 %collective-permute-start.4 = (bf16[64,1024]{1,0:T(8,128)(2,1)S(1)}, bf16[64,1024]{1,0:T(8,128)(2,1)S(1)}, u32[]{:S(2)}, u32[]{:S(2)}) collective-permute-start(bf16[64,1024]{1,0:T(8,128)(2,1)S(1)} %get-tuple-element.22.refs_2_.refs_0_), channel_id=1, source_target_pairs={{0,32},{1,33},{2,34},{3,35},{4,36},{5,37},{6,38},{7,39},{8,40},{9,... | collective-permute-start | bytes 393224 | tf_op jit(solution)/shard_map/ppermute | solution.py:277
  33.2 11.2 %collective-permute-start.3 = (bf16[64,1024]{1,0:T(8,128)(2,1)S(1)}, bf16[64,1024]{1,0:T(8,128)(2,1)S(1)}, u32[]{:S(2)}, u32[]{:S(2)}) collective-permute-start(bf16[64,1024]{1,0:T(8,128)(2,1)S(1)} %shard_map.40.refs_2_.refs_0_), channel_id=1, source_target_pairs={{0,4},{1,5},{2,6},{3,7},{4,0},{5,1},{6,2},{7,3},{8,12},{9,13},{10,... | collective-permute-start | bytes 393224 | tf_op jit(solution)/shard_map/ppermute | solution.py:277
  36.0 10.0 %collective-permute-start.5 = (bf16[64,1024]{1,0:T(8,128)(2,1)S(1)}, bf16[64,1024]{1,0:T(8,128)(2,1)S(1)}, u32[]{:S(2)}, u32[]{:S(2)}) collective-permute-start(bf16[64,1024]{1,0:T(8,128)(2,1)S(1)} %get-tuple-element.26), channel_id=1, source_target_pairs={{0,16},{1,17},{2,18},{3,19},{4,20},{5,21},{6,22},{7,23},{8,24},{9,... | collective-permute-start | bytes 393224 | tf_op jit(solution)/shard_map/ppermute | solution.py:277
  39.5 10.5 %collective-permute-start.6 = (bf16[64,1024]{1,0:T(8,128)(2,1)S(1)}, bf16[64,1024]{1,0:T(8,128)(2,1)S(1)}, u32[]{:S(2)}, u32[]{:S(2)}) collective-permute-start(bf16[64,1024]{1,0:T(8,128)(2,1)S(1)} %shard_map.41.refs_2_.refs_0_), channel_id=1, source_target_pairs={{0,96},{1,97},{2,98},{3,99},{4,100},{5,101},{6,102},{7,103},{8,104... | collective-permute-start | bytes 393224 | tf_op jit(solution)/shard_map/ppermute | solution.py:277
  50.2 7.1 %collective-permute-start.7 = (bf16[64,1024]{1,0:T(8,128)(2,1)S(1)}, bf16[64,1024]{1,0:T(8,128)(2,1)S(1)}, u32[]{:S(2)}, u32[]{:S(2)}) collective-permute-start(bf16[64,1024]{1,0:T(8,128)(2,1)S(1)} %shard_map.44.refs_0_), channel_id=1, source_target_pairs={{0,128},{1,129},{2,130},{3,131},{4,132},{5,133},{6,134},{7,135},{8... | collective-permute-start | bytes 393224 | tf_op jit(solution)/shard_map/ppermute | solution.py:277
  52.9 9.0 %collective-permute-start.8 = (bf16[64,1024]{1,0:T(8,128)(2,1)S(1)}, bf16[64,1024]{1,0:T(8,128)(2,1)S(1)}, u32[]{:S(2)}, u32[]{:S(2)}) collective-permute-start(bf16[64,1024]{1,0:T(8,128)(2,1)S(1)} %shard_map.42.refs_6_), channel_id=1, source_target_pairs={{0,12},{1,13},{2,14},{3,15},{4,8},{5,9},{6,10},{7,11},{8,4},{9,5},... | collective-permute-start | bytes 393224 | tf_op jit(solution)/shard_map/ppermute | solution.py:277
  57.4 8.1 %collective-permute-start.9 = (bf16[64,1024]{1,0:T(8,128)(2,1)S(1)}, bf16[64,1024]{1,0:T(8,128)(2,1)S(1)}, u32[]{:S(2)}, u32[]{:S(2)}) collective-permute-start(bf16[64,1024]{1,0:T(8,128)(2,1)S(1)} %shard_map.45.refs_7_), channel_id=1, source_target_pairs={{0,384},{1,385},{2,386},{3,387},{4,388},{5,389},{6,390},{7,391},{8... | collective-permute-start | bytes 393224 | tf_op jit(solution)/shard_map/ppermute | solution.py:277
  61.9 3.6 %copy-start.3 = (bf16[512,512]{1,0:T(8,128)(2,1)S(1)}, bf16[512,512]{1,0:T(8,128)(2,1)}, u32[]{:S(2)}) copy-start(bf16[512,512]{1,0:T(8,128)(2,1)} %refs_3_.1) | copy-start | bytes 1572868

commit v5 on v4

--- a/solution.py
+++ b/solution.py
@@ -69,7 +69,7 @@
 
 
 def project_kernel(
-    place, x_hbm, w_hbm, kv_ref, near_ref, other_ref, packed_ref, x_buf, w_buf, part_buf, sems
+    place, x_hbm, w_hbm, kv_ref, near_ref, other_ref, l3_ref, packed_ref, x_buf, w_buf, part_buf, sems
 ):
     rows, model = x_buf.shape
     width = w_buf.shape[2]
@@ -102,6 +102,8 @@
                 level = ((even + odd) * 0.5).astype(jnp.bfloat16)
                 if size == BLOCK:
                     near_ref[BLOCK:, tile * 128 : (tile + 1) * 128] = level
+                if size == BLOCK // 2:
+                    l3_ref[:, tile * 128 : (tile + 1) * 128] = level
                 part_buf[tile, :size, :] = level.astype(jnp.float32)
             pieces.append(level.astype(jnp.float32))
     packed = pooled(jnp.concatenate(pieces, axis=0).astype(jnp.bfloat16))
@@ -116,27 +118,34 @@
     other_ref[...] = kv_ref[pl.ds(low, BLOCK), :]
 
 
-def unpack_kernel(place, in_ref, own_6_ref, own_7_ref):
-    half = in_ref.shape[0] // 2
-    tiles = own_6_ref.shape[1] // 128
-    row = lax.broadcasted_iota(jnp.int32, (BLOCK, half), 0)
-    column = lax.broadcasted_iota(jnp.int32, (BLOCK, half), 1)
-    source = (row >> 2) * (4 * tiles) + (row & 3)
+def unpack_kernel(place, in_ref, own_6_ref, own_7_ref, wide):
+    members, rows, _ = in_ref.shape
+    half = members // 2
+    wide[...] = in_ref[...].reshape(members * rows, 128).astype(jnp.float32)
     upper = (place[0] >> 4) & 1
-    for tile in range(tiles):
+    for tile in range(rows // 4):
         lanes = slice(tile * 128, (tile + 1) * 128)
-        pick = jnp.where(column == source + 4 * tile, 1.0, 0.0).astype(jnp.bfloat16)
         parts = [
-            jnp.dot(pick, in_ref[at : at + half, :], preferred_element_type=jnp.float32)
-            for at in (0, half)
+            wide[pl.ds(tile * 4 + row, members, stride=rows), :] for row in range(4)
         ]
-        own_6_ref[:, lanes] = jnp.where(upper == 1, parts[1], parts[0]).astype(jnp.bfloat16)
-        own_7_ref[:, lanes] = pooled(jnp.concatenate(parts, axis=0).astype(jnp.bfloat16))
-
-
-def pool_near_kernel(near_ref, sib_ref, out_ref):
-    out_ref[: BLOCK // 2, :] = pooled(near_ref[BLOCK:, :])
+        own = [jnp.where(upper == 1, part[half:], part[:half]) for part in parts]
+        own_6_ref[:, lanes] = jnp.concatenate(own, axis=0).astype(jnp.bfloat16)
+        pairs = [(parts[0] + parts[1]) * 0.5, (parts[2] + parts[3]) * 0.5]
+        own_7_ref[:, lanes] = jnp.concatenate(pairs, axis=0).astype(jnp.bfloat16)
+
+
+def pool_near_kernel(mine_ref, sib_ref, out_ref):
+    out_ref[: BLOCK // 2, :] = mine_ref[...]
     out_ref[BLOCK // 2 :, :] = pooled(sib_ref[BLOCK:, :])
+
+
+def pool_halves_kernel(own_ref, sib_ref, out_ref):
+    half = BLOCK // 2
+    for num, ref in enumerate((own_ref, sib_ref)):
+        block = ref[...].astype(jnp.float32)
+        out_ref[num * half : (num + 1) * half, :] = (
+            (block[:half] + block[half:]) * 0.5
+        ).astype(jnp.bfloat16)
 
 
 def pool_kernel(*refs):
@@ -257,9 +266,12 @@
     members = 32
     packed = 4 * 2 * model // 128
     block = bf16(BLOCK, 2 * model)
-    kv, near, other, level_6 = call(
+    kv, near, other, level_3, level_6 = call(
         project_kernel,
-        (bf16(rows, 2 * model), bf16(2 * BLOCK, 2 * model), block, bf16(members * packed, 128)),
+        (
+            bf16(rows, 2 * model), bf16(2 * BLOCK, 2 * model), block,
+            bf16(BLOCK // 2, 2 * model), bf16(members * packed, 128),
+        ),
         [SMEM, anywhere, anywhere],
         place, tokens, w_qkv,
         flops=4 * rows * model * model,
@@ -294,19 +306,26 @@
     near_sib = exchange(near, 0)
     other_halo = lax.ppermute(other, AXES, swap)
 
-    own_3 = call(pool_near_kernel, block, vmem(2), near, near_sib)
+    own_3 = call(pool_near_kernel, block, vmem(2), level_3, near_sib)
     sib_3 = exchange(own_3, 1)
     own_6, own_7 = call(
-        unpack_kernel, (block, block), [SMEM, *vmem(1)], place, spread, after=(own_3, other_halo)
+        unpack_kernel, (block, block), [SMEM, *vmem(1)],
+        place, spread.reshape(members, packed, 128),
+        scratch=(pltpu.VMEM((members * packed, 128), jnp.float32),),
+        after=(own_3, other_halo),
     )
     sib_7 = exchange(own_7, 5)
-    sib_6 = exchange(own_6, 4)
     own_4 = pool(own_3, sib_3, own_7)
     sib_4 = exchange(own_4, 2)
-    own_8 = pool(own_7, sib_7, own_4)
+    own_8 = call(pool_halves_kernel, block, vmem(2), own_7, sib_7, after=(own_4,))
     sib_8 = exchange(own_8, 6)
+    own_6, _ = lax.optimization_barrier((own_6, own_8))
+    sib_6 = exchange(own_6, 4)
     own_5 = pool(own_4, sib_4, own_8)
     sib_5 = exchange(own_5, 3)
+    own_9 = pool(own_8, sib_8, own_5)
+    sib_9 = exchange(own_9, 7)
+    own_10 = pool(own_9, sib_9, sib_6)
     q, num, tot = call(
         functools.partial(local_kernel, count),
         (bf16(rows, model), f32(rows, model), f32(rows, model)),
@@ -319,11 +338,8 @@
             pltpu.VMEM((model, model), jnp.bfloat16),
             pltpu.SemaphoreType.DMA(()),
         ),
-        after=(own_5,),
-    )
-    own_9 = pool(own_8, sib_8, q, sib_6)
-    sib_9 = exchange(own_9, 7)
-    own_10 = pool(own_9, sib_9)
+        after=(own_10,),
+    )
     num, tot = far(num, tot, near_sib, sib_3, sib_4, sib_6, after=(own_10,))
     sib_10 = exchange(own_10, 8)
     num, tot = far(num, tot, sib_5, sib_7, sib_8, sib_9, after=(own_10,))

time: 68.5 us -> 67.1 us (0.980)
  the two profiles are of different devices: /device:TPU:6 before, /device:TPU:72 now
where the time goes in v5:
time: 67.1 us; the launch traced here: 66.5 us
  starting transfers between devices  49.2 us (73%)
  Pallas kernels  8.92 us (13%)
  waiting for transfers between devices  7.27 us (11%)
  local copies, waits for them, and re-layouts  0.86 us (1%)
    ppermute x9, starting transfers between devices, exchange(): return lax.ppermute(own, AXES, list(enumerate(partners(bit, count))))  35.7 us
    all_to_all x1, starting transfers between devices, per_device(): lax.all_to_all(level_6, AXES, 0, 0, axis_index_groups=teams, tiled=True)  11 us
    pallas_call x12, Pallas kernels, call(): pl.pallas_call(body, out_shape=outs, in_specs=list(in_specs) + [pl.BlockS...  8.92 us
    ppermute x9, waiting for transfers between devices, exchange(): return lax.ppermute(own, AXES, list(enumerate(partners(bit, count))))  6.44 us
    ppermute x1, starting transfers between devices, per_device(): other_halo = lax.ppermute(other, AXES, swap)  2.44 us
  transfers between devices with their start and end apart: 11, of which 4 were waited for; matrix products, arithmetic and copies ran while one was open for 0% of the time, Pallas kernels for 6%

profile of v5, /device:TPU:72, one launch (start us, length us, event | category | flops | bytes accessed | tf_op | source)
XLA Modules:
  0.0 66.5 jit_solution(18279718168000587889)
XLA Ops:
  0.0 3.0 %shard_map.37 = (bf16[256,1024]{1,0:T(8,128)(2,1)}, bf16[128,1024]{1,0:T(8,128)(2,1)}, bf16[64,1024]{1,0:T(8,128)(2,1)}, bf16[32,1024]{1,0:T(8,128)(2,1)}, bf16[1024,128]{1,0:T(8,128)(2,1)}) custom-call(s32[1]{0:T(128)} %bitcast.refs_0_, bf16[256,512]{1,0:T(8,128)(2,1)} %refs_1_.3, bf16[512,1536]{1,0:T(8,128)(2,1)} %refs_2_.3), custom_call_target="tpu_custom_call" | custom-call | flops 268435456 | bytes 1048576 | tf_op jit(solution)/shard_map/pallas_call | solution.py:48
  3.0 11.0 %all-to-all-start = ((bf16[32,32,128]{2,1,0:T(8,128)(2,1)}), bf16[32,32,128]{2,1,0:T(8,128)(2,1)S(1)}, u32[]{:S(2)}, u32[]{:S(2)}) async-start(bf16[32,32,128]{2,1,0:T(8,128)(2,1)} %bitcast.2), calls=%async_computation | async-start | bytes 524288 | tf_op jit(solution)/shard_map/all_to_all | solution.py:305
  14.1 2.1 %collective-permute-start = (bf16[128,1024]{1,0:T(8,128)(2,1)}, bf16[128,1024]{1,0:T(8,128)(2,1)S(1)}, u32[]{:S(2)}, u32[]{:S(2)}) collective-permute-start(bf16[128,1024]{1,0:T(8,128)(2,1)} %get-tuple-element.21), channel_id=1, source_target_pairs={{0,1},{1,0},{2,3},{3,2},{4,5},{5,4},{6,7},{7,6},{8,9},{9,8},{10,11... | collective-permute-start | bytes 786440 | tf_op jit(solution)/shard_map/ppermute | solution.py:289
  16.1 2.4 %collective-permute-start.1 = (bf16[64,1024]{1,0:T(8,128)(2,1)}, bf16[64,1024]{1,0:T(8,128)(2,1)S(1)}, u32[]{:S(2)}, u32[]{:S(2)}) collective-permute-start(bf16[64,1024]{1,0:T(8,128)(2,1)} %get-tuple-element.22), channel_id=1, source_target_pairs={{1,2},{3,4},{5,6},{7,8},{9,10},{11,12},{13,14},{15,16},{17,18},{19... | collective-permute-start | bytes 393224 | tf_op jit(solution)/shard_map/ppermute | solution.py:307
  18.6 0.8 %copy-done.2 = bf16[32,1024]{1,0:T(8,128)(2,1)S(1)} copy-done((bf16[32,1024]{1,0:T(8,128)(2,1)S(1)}, bf16[32,1024]{1,0:T(8,128)(2,1)}, u32[]{:S(2)}) %copy-start.2) | copy-done | bytes 65560
  19.6 4.7 %collective-permute-start.3 = (bf16[64,1024]{1,0:T(8,128)(2,1)S(1)}, bf16[64,1024]{1,0:T(8,128)(2,1)S(1)}, u32[]{:S(2)}, u32[]{:S(2)}) collective-permute-start(bf16[64,1024]{1,0:T(8,128)(2,1)S(1)} %shard_map.38.refs_2_.refs_0_), channel_id=1, source_target_pairs={{0,2},{1,3},{2,0},{3,1},{4,6},{5,7},{6,4},{7,5},{8,10},{9,11},{10,... | collective-permute-start | bytes 393224 | tf_op jit(solution)/shard_map/ppermute | solution.py:289
  24.3 0.8 %all-to-all-done.refs_1_ = bf16[32,32,128]{2,1,0:T(8,128)(2,1)S(1)} async-done(((bf16[32,32,128]{2,1,0:T(8,128)(2,1)}), bf16[32,32,128]{2,1,0:T(8,128)(2,1)S(1)}, u32[]{:S(2)}, u32[]{:S(2)}) %all-to-all-start) | async-done | bytes 262176 | tf_op jit(solution)/shard_map/all_to_all | solution.py:305
  25.1 0.3 shard_map.39
  25.5 4.5 %collective-permute-start.2 = (bf16[64,1024]{1,0:T(8,128)(2,1)S(1)}, bf16[64,1024]{1,0:T(8,128)(2,1)S(1)}, u32[]{:S(2)}, u32[]{:S(2)}) collective-permute-start(bf16[64,1024]{1,0:T(8,128)(2,1)S(1)} %get-tuple-element.25.refs_2_.refs_0_), channel_id=1, source_target_pairs={{0,32},{1,33},{2,34},{3,35},{4,36},{5,37},{6,38},{7,39},{8,40},{9,... | collective-permute-start | bytes 393224 | tf_op jit(solution)/shard_map/ppermute | solution.py:289
  30.2 2.4 %collective-permute-start.5 = (bf16[64,1024]{1,0:T(8,128)(2,1)S(1)}, bf16[64,1024]{1,0:T(8,128)(2,1)S(1)}, u32[]{:S(2)}, u32[]{:S(2)}) collective-permute-start(bf16[64,1024]{1,0:T(8,128)(2,1)S(1)} %shard_map.40.refs_2_.refs_0_), channel_id=1, source_target_pairs={{0,4},{1,5},{2,6},{3,7},{4,0},{5,1},{6,2},{7,3},{8,12},{9,13},{10,... | collective-permute-start | bytes 393224 | tf_op jit(solution)/shard_map/ppermute | solution.py:289
  32.6 2.5 %collective-permute-done.2.refs_1_.refs_4_ = bf16[64,1024]{1,0:T(8,128)(2,1)S(1)} collective-permute-done((bf16[64,1024]{1,0:T(8,128)(2,1)S(1)}, bf16[64,1024]{1,0:T(8,128)(2,1)S(1)}, u32[]{:S(2)}, u32[]{:S(2)}) %collective-permute-start.2) | collective-permute-done | bytes 131104 | tf_op jit(solution)/shard_map/ppermute | solution.py:289
  35.1 6.1 %collective-permute-start.4 = (bf16[64,1024]{1,0:T(8,128)(2,1)S(1)}, bf16[64,1024]{1,0:T(8,128)(2,1)S(1)}, u32[]{:S(2)}, u32[]{:S(2)}) collective-permute-start(bf16[64,1024]{1,0:T(8,128)(2,1)S(1)} %shard_map.41.refs_2_.refs_0_), channel_id=1, source_target_pairs={{0,96},{1,97},{2,98},{3,99},{4,100},{5,101},{6,102},{7,103},{8,104... | collective-permute-start | bytes 393224 | tf_op jit(solution)/shard_map/ppermute | solution.py:289
  41.2 1.9 %collective-permute-start.7 = (bf16[64,1024]{1,0:T(8,128)(2,1)S(1)}, bf16[64,1024]{1,0:T(8,128)(2,1)S(1)}, u32[]{:S(2)}, u32[]{:S(2)}) collective-permute-start(bf16[64,1024]{1,0:T(8,128)(2,1)S(1)} %get-tuple-element.27), channel_id=1, source_target_pairs={{0,16},{1,17},{2,18},{3,19},{4,20},{5,21},{6,22},{7,23},{8,24},{9,... | collective-permute-start | bytes 393224 | tf_op jit(solution)/shard_map/ppermute | solution.py:289
  43.1 0.2 shard_map.42.refs_2_
  43.3 2.9 %collective-permute-done.4.refs_1_.refs_5_ = bf16[64,1024]{1,0:T(8,128)(2,1)S(1)} collective-permute-done((bf16[64,1024]{1,0:T(8,128)(2,1)S(1)}, bf16[64,1024]{1,0:T(8,128)(2,1)S(1)}, u32[]{:S(2)}, u32[]{:S(2)}) %collective-permute-start.4) | collective-permute-done | bytes 131104 | tf_op jit(solution)/shard_map/ppermute | solution.py:289
  46.4 3.4 %collective-permute-start.6 = (bf16[64,1024]{1,0:T(8,128)(2,1)S(1)}, bf16[64,1024]{1,0:T(8,128)(2,1)S(1)}, u32[]{:S(2)}, u32[]{:S(2)}) collective-permute-start(bf16[64,1024]{1,0:T(8,128)(2,1)S(1)} %shard_map.43.refs_0_), channel_id=1, source_target_pairs={{0,128},{1,129},{2,130},{3,131},{4,132},{5,133},{6,134},{7,135},{8... | collective-permute-start | bytes 393224 | tf_op jit(solution)/shard_map/ppermute | solution.py:289
  49.8 6.7 %collective-permute-start.8 = (bf16[64,1024]{1,0:T(8,128)(2,1)S(1)}, bf16[64,1024]{1,0:T(8,128)(2,1)S(1)}, u32[]{:S(2)}, u32[]{:S(2)}) collective-permute-start(bf16[64,1024]{1,0:T(8,128)(2,1)S(1)} %shard_map.42.refs_2_), channel_id=1, source_target_pairs={{0,12},{1,13},{2,14},{3,15},{4,8},{5,9},{6,10},{7,11},{8,4},{9,5},... | collective-permute-start | bytes 393224 | tf_op jit(solution)/shard_map/ppermute | solution.py:289
  56.5 0.2 shard_map.44.refs_6_.refs_7_
  56.7 4.0 %collective-permute-start.9 = (bf16[64,1024]{1,0:T(8,128)(2,1)S(1)}, bf16[64,1024]{1,0:T(8,128)(2,1)S(1)}, u32[]{:S(2)}, u32[]{:S(2)}) collective-permute-start(bf16[64,1024]{1,0:T(8,128)(2,1)S(1)} %shard_map.44.refs_6_.refs_7_), channel_id=1, source_target_pairs={{0,384},{1,385},{2,386},{3,387},{4,388},{5,389},{6,390},{7,391},{8... | collective-permute-start | bytes 393224 | tf_op jit(solution)/shard_map/ppermute | solution.py:289
  60.7 1.4 %shard_map.45 = (bf16[256,512]{1,0:T(8,128)(2,1)S(1)}, f32[256,512]{1,0:T(8,128)S(1)}, f32[256,512]{1,0:T(8,128)S(1)}) custom-call(s32[1]{0:T(128)} %bitcast.refs_0_, bf16[256,512]{1,0:T(8,128)(2,1)S(1)} %copy-done.1, bf16[512,1536]{1,0:T(8,128)(2,1)S(1)} %copy-done, bf16[256,1024]{1,0:T(8,128)(2,1)S(1)} %copy-done.4, ...), custom_call_target="tpu_custom_call" | custom-call | flops 1000000000 | bytes 1048576 | tf_op jit(solution)/shard_map/pallas_call | solution.py:48
  62.1 0.8 %shard_map.46 = (f32[256,512]{1,0:T(8,128)S(1)}, f32[256,512]{1,0:T(8,128)S(1)}) custom-call(bf16[256,512]{1,0:T(8,128)(2,1)S(1)} %get-tuple-element.28.refs_0_, f32[256,512]{1,0:T(8,128)S(1)} %get-tuple-element.29.refs_1_, f32[256,512]{1,0:T(8,128)S(1)} %get-tuple-element.30.refs_2_, bf16[128,1024]{1,0:T(8,128)(2,1)S(1)} %collective-permute-done.refs_1_.refs_4_.refs_3_, ...), custom_call_target="tpu_custom_call" | custom-call | flops 1000000000 | bytes 1048576 | tf_op jit(solution)/shard_map/pallas_call | solution.py:48
  63.0 0.8 %shard_map.47 = (f32[256,512]{1,0:T(8,128)S(1)}, f32[256,512]{1,0:T(8,128)S(1)}) custom-call(bf16[256,512]{1,0:T(8,128)(2,1)S(1)} %get-tuple-element.28.refs_0_, f32[256,512]{1,0:T(8,128)S(1)} %get-tuple-element.31.refs_1_, f32[256,512]{1,0:T(8,128)S(1)} %get-tuple-element.32.refs_2_, bf16[64,1024]{1,0:T(8,128)(2,1)S(1)} %collective-permute-done.8.refs_3_, ...), custom_call_target="tpu_custom_call" | custom-call | flops 1000000000 | bytes 1048576 | tf_op jit(solution)/shard_map/pallas_call | solution.py:48
  63.8 1.0 %collective-permute-done.9.refs_4_ = bf16[64,1024]{1,0:T(8,128)(2,1)S(1)} collective-permute-done((bf16[64,1024]{1,0:T(8,128)(2,1)S(1)}, bf16[64,1024]{1,0:T(8,128)(2,1)S(1)}, u32[]{:S(2)}, u32[]{:S(2)}) %collective-permute-start.9) | collective-permute-done | bytes 131104 | tf_op jit(solution)/shard_map/ppermute | solution.py:289
  64.8 1.7 %shard_map.48 = bf16[256,512]{1,0:T(8,128)(2,1)} custom-call(bf16[256,512]{1,0:T(8,128)(2,1)S(1)} %get-tuple-element.28.refs_0_, f32[256,512]{1,0:T(8,128)S(1)} %get-tuple-element.33.refs_1_, f32[256,512]{1,0:T(8,128)S(1)} %get-tuple-element.34.refs_2_, bf16[512,512]{1,0:T(8,128)(2,1)S(1)} %copy-done.3, bf16[64,1024]{1,0:T(8,128)(2,1)S(1)} %collective-permute-done.9.refs_4_), custom_call_target="tpu_custom_call" | custom-call | flops 1000000000 | bytes 1048576 | tf_op jit(solution)/shard_map/pallas_call | solution.py:48
  (20 shorter events, 0.5 us)
Async XLA Ops:
  3.0 22.1 %all-to-all-start = ((bf16[32,32,128]{2,1,0:T(8,128)(2,1)}), bf16[32,32,128]{2,1,0:T(8,128)(2,1)S(1)}, u32[]{:S(2)}, u32[]{:S(2)}) async-start(bf16[32,32,128]{2,1,0:T(8,128)(2,1)} %bitcast.2), calls=%async_computation | async-start | bytes 524288 | tf_op jit(solution)/shard_map/all_to_all | solution.py:305
  14.1 4.5 %collective-permute-start = (bf16[128,1024]{1,0:T(8,128)(2,1)}, bf16[128,1024]{1,0:T(8,128)(2,1)S(1)}, u32[]{:S(2)}, u32[]{:S(2)}) collective-permute-start(bf16[128,1024]{1,0:T(8,128)(2,1)} %get-tuple-element.21), channel_id=1, source_target_pairs={{0,1},{1,0},{2,3},{3,2},{4,5},{5,4},{6,7},{7,6},{8,9},{9,8},{10,11... | collective-permute-start | bytes 786440 | tf_op jit(solution)/shard_map/ppermute | solution.py:289
  16.1 8.2 %collective-permute-start.1 = (bf16[64,1024]{1,0:T(8,128)(2,1)}, bf16[64,1024]{1,0:T(8,128)(2,1)S(1)}, u32[]{:S(2)}, u32[]{:S(2)}) collective-permute-start(bf16[64,1024]{1,0:T(8,128)(2,1)} %get-tuple-element.22), channel_id=1, source_target_pairs={{1,2},{3,4},{5,6},{7,8},{9,10},{11,12},{13,14},{15,16},{17,18},{19... | collective-permute-start | bytes 393224 | tf_op jit(solution)/shard_map/ppermute | solution.py:307
  18.6 0.8 %copy-start.2 = (bf16[32,1024]{1,0:T(8,128)(2,1)S(1)}, bf16[32,1024]{1,0:T(8,128)(2,1)}, u32[]{:S(2)}) copy-start(bf16[32,1024]{1,0:T(8,128)(2,1)} %get-tuple-element.24.refs_0_) | copy-start | bytes 196612
  19.6 41.2 %copy-start = (bf16[512,1536]{1,0:T(8,128)(2,1)S(1)}, bf16[512,1536]{1,0:T(8,128)(2,1)}, u32[]{:S(2)}) copy-start(bf16[512,1536]{1,0:T(8,128)(2,1)} %refs_2_.3) | copy-start | bytes 4718596
  19.6 41.1 %copy-start.1 = (bf16[256,512]{1,0:T(8,128)(2,1)S(1)}, bf16[256,512]{1,0:T(8,128)(2,1)}, u32[]{:S(2)}) copy-start(bf16[256,512]{1,0:T(8,128)(2,1)} %refs_1_.3) | copy-start | bytes 786436
  19.6 41.1 %copy-start.4 = (bf16[256,1024]{1,0:T(8,128)(2,1)S(1)}, bf16[256,1024]{1,0:T(8,128)(2,1)}, u32[]{:S(2)}) copy-start(bf16[256,1024]{1,0:T(8,128)(2,1)} %get-tuple-element.20.refs_3_) | copy-start | bytes 1572868
  19.6 10.4 %collective-permute-start.3 = (bf16[64,1024]{1,0:T(8,128)(2,1)S(1)}, bf16[64,1024]{1,0:T(8,128)(2,1)S(1)}, u32[]{:S(2)}, u32[]{:S(2)}) collective-permute-start(bf16[64,1024]{1,0:T(8,128)(2,1)S(1)} %shard_map.38.refs_2_.refs_0_), channel_id=1, source_target_pairs={{0,2},{1,3},{2,0},{3,1},{4,6},{5,7},{6,4},{7,5},{8,10},{9,11},{10,... | collective-permute-start | bytes 393224 | tf_op jit(solution)/shard_map/ppermute | solution.py:289
  25.5 9.6 %collective-permute-start.2 = (bf16[64,1024]{1,0:T(8,128)(2,1)S(1)}, bf16[64,1024]{1,0:T(8,128)(2,1)S(1)}, u32[]{:S(2)}, u32[]{:S(2)}) collective-permute-start(bf16[64,1024]{1,0:T(8,128)(2,1)S(1)} %get-tuple-element.25.refs_2_.refs_0_), channel_id=1, source_target_pairs={{0,32},{1,33},{2,34},{3,35},{4,36},{5,37},{6,38},{7,39},{8,40},{9,... | collective-permute-start | bytes 393224 | tf_op jit(solution)/shard_map/ppermute | solution.py:289
  30.2 12.9 %collective-permute-start.5 = (bf16[64,1024]{1,0:T(8,128)(2,1)S(1)}, bf16[64,1024]{1,0:T(8,128)(2,1)S(1)}, u32[]{:S(2)}, u32[]{:S(2)}) collective-permute-start(bf16[64,1024]{1,0:T(8,128)(2,1)S(1)} %shard_map.40.refs_2_.refs_0_), channel_id=1, source_target_pairs={{0,4},{1,5},{2,6},{3,7},{4,0},{5,1},{6,2},{7,3},{8,12},{9,13},{10,... | collective-permute-start | bytes 393224 | tf_op jit(solution)/shard_map/ppermute | solution.py:289
  35.1 11.1 %collective-permute-start.4 = (bf16[64,1024]{1,0:T(8,128)(2,1)S(1)}, bf16[64,1024]{1,0:T(8,128)(2,1)S(1)}, u32[]{:S(2)}, u32[]{:S(2)}) collective-permute-start(bf16[64,1024]{1,0:T(8,128)(2,1)S(1)} %shard_map.41.refs_2_.refs_0_), channel_id=1, source_target_pairs={{0,96},{1,97},{2,98},{3,99},{4,100},{5,101},{6,102},{7,103},{8,104... | collective-permute-start | bytes 393224 | tf_op jit(solution)/shard_map/ppermute | solution.py:289
  41.2 15.3 %collective-permute-start.7 = (bf16[64,1024]{1,0:T(8,128)(2,1)S(1)}, bf16[64,1024]{1,0:T(8,128)(2,1)S(1)}, u32[]{:S(2)}, u32[]{:S(2)}) collective-permute-start(bf16[64,1024]{1,0:T(8,128)(2,1)S(1)} %get-tuple-element.27), channel_id=1, source_target_pairs={{0,16},{1,17},{2,18},{3,19},{4,20},{5,21},{6,22},{7,23},{8,24},{9,... | collective-permute-start | bytes 393224 | tf_op jit(solution)/shard_map/ppermute | solution.py:289
  46.4 10.1 %collective-permute-start.6 = (bf16[64,1024]{1,0:T(8,128)(2,1)S(1)}, bf16[64,1024]{1,0:T(8,128)(2,1)S(1)}, u32[]{:S(2)}, u32[]{:S(2)}) collective-permute-start(bf16[64,1024]{1,0:T(8,128)(2,1)S(1)} %shard_map.43.refs_0_), channel_id=1, source_target_pairs={{0,128},{1,129},{2,130},{3,131},{4,132},{5,133},{6,134},{7,135},{8... | collective-permute-start | bytes 393224 | tf_op jit(solution)/shard_map/ppermute | solution.py:289
  49.8 13.1 %collective-permute-start.8 = (bf16[64,1024]{1,0:T(8,128)(2,1)S(1)}, bf16[64,1024]{1,0:T(8,128)(2,1)S(1)}, u32[]{:S(2)}, u32[]{:S(2)}) collective-permute-start(bf16[64,1024]{1,0:T(8,128)(2,1)S(1)} %shard_map.42.refs_2_), channel_id=1, source_target_pairs={{0,12},{1,13},{2,14},{3,15},{4,8},{5,9},{6,10},{7,11},{8,4},{9,5},... | collective-permute-start | bytes 393224 | tf_op jit(solution)/shard_map/ppermute | solution.py:289
  56.7 8.1 %collective-permute-start.9 = (bf16[64,1024]{1,0:T(8,128)(2,1)S(1)}, bf16[64,1024]{1,0:T(8,128)(2,1)S(1)}, u32[]{:S(2)}, u32[]{:S(2)}) collective-permute-start(bf16[64,1024]{1,0:T(8,128)(2,1)S(1)} %shard_map.44.refs_6_.refs_7_), channel_id=1, source_target_pairs={{0,384},{1,385},{2,386},{3,387},{4,388},{5,389},{6,390},{7,391},{8... | collective-permute-start | bytes 393224 | tf_op jit(solution)/shard_map/ppermute | solution.py:289
  62.9 1.8 %copy-start.3 = (bf16[512,512]{1,0:T(8,128)(2,1)S(1)}, bf16[512,512]{1,0:T(8,128)(2,1)}, u32[]{:S(2)}) copy-start(bf16[512,512]{1,0:T(8,128)(2,1)} %refs_3_.1) | copy-start | bytes 1572868

commit v6 on v5

--- a/solution.py
+++ b/solution.py
@@ -12,21 +12,13 @@
 BLOCK = 64
 AXES = ("gx", "gy")
 FAR8 = (6, 7, 4, 5, 2, 3, 0, 1)
-FAR4 = (3, 2, 1, 0)
 
 
 def partners(bit, count):
     route = []
     for index in range(count):
         if bit == 3:
-            z = index >> 1 & 7
-            route.append(index & ~14 | FAR8[z] << 1)
-        elif bit == 6:
-            y = index >> 4 & 7
-            route.append(index & ~112 | FAR8[y] << 4)
-        elif bit == 8:
-            x = index >> 7 & 3
-            route.append(index & ~384 | FAR4[x] << 7)
+            route.append(index & ~14 | FAR8[index >> 1 & 7] << 1)
         else:
             route.append(index ^ 1 << bit)
     return route
@@ -118,34 +110,47 @@
     other_ref[...] = kv_ref[pl.ds(low, BLOCK), :]
 
 
-def unpack_kernel(place, in_ref, own_6_ref, own_7_ref, wide):
+def unpack_kernel(place, in_ref, out_ref, wide):
     members, rows, _ = in_ref.shape
-    half = members // 2
     wide[...] = in_ref[...].reshape(members * rows, 128).astype(jnp.float32)
-    upper = (place[0] >> 4) & 1
+    y = (place[0] >> 4) & 7
+
+    def mean(one, two):
+        return ((one + two) * 0.5).astype(jnp.bfloat16).astype(jnp.float32)
+
     for tile in range(rows // 4):
         lanes = slice(tile * 128, (tile + 1) * 128)
-        parts = [
-            wide[pl.ds(tile * 4 + row, members, stride=rows), :] for row in range(4)
-        ]
-        own = [jnp.where(upper == 1, part[half:], part[:half]) for part in parts]
-        own_6_ref[:, lanes] = jnp.concatenate(own, axis=0).astype(jnp.bfloat16)
-        pairs = [(parts[0] + parts[1]) * 0.5, (parts[2] + parts[3]) * 0.5]
-        own_7_ref[:, lanes] = jnp.concatenate(pairs, axis=0).astype(jnp.bfloat16)
+
+        def level_6(start, count):
+            return [
+                wide[pl.ds(start * rows + tile * 4 + row, count, stride=rows), :]
+                for row in range(4)
+            ]
+
+        def level_7(start, count):
+            r = level_6(start, count)
+            return [mean(r[0], r[1]), mean(r[2], r[3])]
+
+        parts = (
+            level_6((y ^ 1) * 8, 8)
+            + level_7(((y >> 1) ^ 1) * 16, 16)
+            + [mean(*level_7(((y >> 2) ^ 1) * 32, 32))]
+            + [mean(*level_7(0, members))]
+        )
+        out_ref[:, lanes] = jnp.concatenate(parts, axis=0).astype(jnp.bfloat16)
+
+
+def own_9_kernel(mine_ref, sib_ref, out_ref):
+    at = 3 * BLOCK // 2
+    both = mine_ref[at:, :].astype(jnp.float32) + sib_ref[at:, :].astype(jnp.float32)
+    block = (both * 0.5).astype(jnp.bfloat16)
+    for copy in range(out_ref.shape[0] // BLOCK):
+        out_ref[copy * BLOCK : (copy + 1) * BLOCK, :] = block
 
 
 def pool_near_kernel(mine_ref, sib_ref, out_ref):
     out_ref[: BLOCK // 2, :] = mine_ref[...]
     out_ref[BLOCK // 2 :, :] = pooled(sib_ref[BLOCK:, :])
-
-
-def pool_halves_kernel(own_ref, sib_ref, out_ref):
-    half = BLOCK // 2
-    for num, ref in enumerate((own_ref, sib_ref)):
-        block = ref[...].astype(jnp.float32)
-        out_ref[num * half : (num + 1) * half, :] = (
-            (block[:half] + block[half:]) * 0.5
-        ).astype(jnp.bfloat16)
 
 
 def pool_kernel(*refs):
@@ -218,9 +223,15 @@
 
 
 def far_blocks(refs):
-    return jnp.concatenate(
-        [ref[BLOCK:, :] if ref.shape[0] == 2 * BLOCK else ref[...] for ref in refs], axis=0
-    )
+    blocks = []
+    for ref in refs:
+        if ref.shape[0] == 2 * BLOCK:
+            blocks.append(ref[BLOCK:, :])
+        elif ref.shape[0] > 2 * BLOCK:
+            blocks.append(ref[: 3 * BLOCK // 2, :])
+        else:
+            blocks.append(ref[...])
+    return jnp.concatenate(blocks, axis=0)
 
 
 def far_sums(far, q, lanes, model):
@@ -240,10 +251,19 @@
         tot_ref[:, at] = tot_in[:, at] + tot
 
 
-def final_kernel(q_ref, num_in, tot_in, w_ref, *refs):
-    out_ref, att = refs[-2:]
+def final_kernel(place, q_ref, num_in, tot_in, w_ref, sib_5_ref, wide_ref, out_ref, att):
     model = q_ref.shape[1]
-    far = far_blocks(refs[:-2])
+    x = place[0] >> 7
+    near = pl.multiple_of((x ^ 1) * BLOCK, BLOCK)
+    other = pl.multiple_of(((x >> 1) ^ 1) * 2 * BLOCK, BLOCK)
+    far = jnp.concatenate(
+        [
+            sib_5_ref[...],
+            wide_ref[pl.ds(near, BLOCK), :],
+            pooled(wide_ref[pl.ds(other, 2 * BLOCK), :]),
+        ],
+        axis=0,
+    )
     for lanes in range(0, model, 128):
         at = slice(lanes, lanes + 128)
         num, tot = far_sums(far, q_ref[:, at], lanes, model)
@@ -263,7 +283,7 @@
     anywhere = pl.BlockSpec(memory_space=pl.ANY)
     steps = 2
     width = 2 * model // steps
-    members = 32
+    members = 64
     packed = 4 * 2 * model // 128
     block = bf16(BLOCK, 2 * model)
     kv, near, other, level_3, level_6 = call(
@@ -301,31 +321,30 @@
             after=after,
         )
 
-    teams = [list(range(i, i + members)) for i in range(0, count, members)]
+    teams = [
+        [i for i in range(count) if i >> 7 == x and i & 1 == core]
+        for x in range(count >> 7)
+        for core in range(2)
+    ]
     spread = lax.all_to_all(level_6, AXES, 0, 0, axis_index_groups=teams, tiled=True)
     near_sib = exchange(near, 0)
-    other_halo = lax.ppermute(other, AXES, swap)
-
     own_3 = call(pool_near_kernel, block, vmem(2), level_3, near_sib)
     sib_3 = exchange(own_3, 1)
-    own_6, own_7 = call(
-        unpack_kernel, (block, block), [SMEM, *vmem(1)],
+    other_halo = lax.ppermute(other, AXES, swap)
+    own_4 = pool(own_3, sib_3, other_halo)
+    sib_4 = exchange(own_4, 2)
+    mine = call(
+        unpack_kernel, bf16(5 * BLOCK // 2, 2 * model), [SMEM, *vmem(1)],
         place, spread.reshape(members, packed, 128),
         scratch=(pltpu.VMEM((members * packed, 128), jnp.float32),),
-        after=(own_3, other_halo),
-    )
-    sib_7 = exchange(own_7, 5)
-    own_4 = pool(own_3, sib_3, own_7)
-    sib_4 = exchange(own_4, 2)
-    own_8 = call(pool_halves_kernel, block, vmem(2), own_7, sib_7, after=(own_4,))
-    sib_8 = exchange(own_8, 6)
-    own_6, _ = lax.optimization_barrier((own_6, own_8))
-    sib_6 = exchange(own_6, 4)
-    own_5 = pool(own_4, sib_4, own_8)
+        after=(own_4,),
+    )
+    theirs = exchange(mine, 0)
+    own_9 = call(own_9_kernel, bf16(4 * BLOCK, 2 * model), vmem(2), mine, theirs)
+    own_5 = pool(own_4, sib_4, own_9)
+    columns = [list(range(i, count, count >> 2)) for i in range(count >> 2)]
+    wide = lax.all_to_all(own_9, AXES, 0, 0, axis_index_groups=columns, tiled=True)
     sib_5 = exchange(own_5, 3)
-    own_9 = pool(own_8, sib_8, own_5)
-    sib_9 = exchange(own_9, 7)
-    own_10 = pool(own_9, sib_9, sib_6)
     q, num, tot = call(
         functools.partial(local_kernel, count),
         (bf16(rows, model), f32(rows, model), f32(rows, model)),
@@ -338,16 +357,16 @@
             pltpu.VMEM((model, model), jnp.bfloat16),
             pltpu.SemaphoreType.DMA(()),
         ),
-        after=(own_10,),
-    )
-    num, tot = far(num, tot, near_sib, sib_3, sib_4, sib_6, after=(own_10,))
-    sib_10 = exchange(own_10, 8)
-    num, tot = far(num, tot, sib_5, sib_7, sib_8, sib_9, after=(own_10,))
+        limit=48,
+        after=(own_9,),
+    )
+    num, tot = far(num, tot, mine, theirs)
+    num, tot = far(num, tot, near_sib, sib_3, sib_4)
     return call(
         final_kernel,
         bf16(rows, model),
-        vmem(5),
-        q, num, tot, w_out, sib_10,
+        [SMEM, *vmem(6)],
+        place, q, num, tot, w_out, sib_5, wide,
         flops=10**9,
         scratch=(pltpu.VMEM((rows, model), jnp.bfloat16),),
     )

time: 67.1 us -> 69.8 us (1.040)
  the two profiles are of different devices: /device:TPU:72 before, /device:TPU:6 now
where the time goes in v6:
time: 69.8 us; the launch traced here: 69.1 us
  starting transfers between devices  42.9 us (61%)
  Pallas kernels  10.8 us (15%)
  waiting for transfers between devices  8.57 us (12%)
  local copies, waits for them, and re-layouts  6.6 us (9%)
    all_to_all x1, starting transfers between devices, per_device(): lax.all_to_all(level_6, AXES, 0, 0, axis_index_groups=teams, tiled=True)  16.6 us
    ppermute x5, starting transfers between devices, exchange(): return lax.ppermute(own, AXES, list(enumerate(partners(bit, count))))  14.1 us
    pallas_call x10, Pallas kernels, call(): pl.pallas_call(body, out_shape=outs, in_specs=list(in_specs) + [pl.BlockS...  10.8 us
    ppermute x1, starting transfers between devices, per_device(): other_halo = lax.ppermute(other, AXES, swap)  7.48 us
    unnamed x26, local copies, waits for them, and re-layouts  6.6 us
    ppermute x1, waiting for transfers between devices, per_device(): other_halo = lax.ppermute(other, AXES, swap)  5.37 us
    all_to_all x1, starting transfers between devices, per_device(): lax.all_to_all(own_9, AXES, 0, 0, axis_index_groups=columns, tiled=True)  4.77 us
    ppermute x5, waiting for transfers between devices, exchange(): return lax.ppermute(own, AXES, list(enumerate(partners(bit, count))))  3.2 us
  transfers between devices with their start and end apart: 8, of which 4 were waited for; matrix products, arithmetic and copies ran while one was open for 0% of the time, Pallas kernels for 7%

profile of v6, /device:TPU:6, one launch (start us, length us, event | category | flops | bytes accessed | tf_op | source)
XLA Modules:
  0.0 69.1 jit_solution(10013168430283124445)
XLA Ops:
  0.0 3.1 %shard_map.37 = (bf16[256,1024]{1,0:T(8,128)(2,1)}, bf16[128,1024]{1,0:T(8,128)(2,1)}, bf16[64,1024]{1,0:T(8,128)(2,1)}, bf16[32,1024]{1,0:T(8,128)(2,1)}, bf16[2048,128]{1,0:T(8,128)(2,1)}) custom-call(s32[1]{0:T(128)} %bitcast.refs_0_, bf16[256,512]{1,0:T(8,128)(2,1)} %refs_1_.3, bf16[512,1536]{1,0:T(8,128)(2,1)} %refs_2_.3), custom_call_target="tpu_custom_call" | custom-call | flops 268435456 | bytes 1048576 | tf_op jit(solution)/shard_map/pallas_call | solution.py:40
  3.1 16.6 %all-to-all-start = ((bf16[64,32,128]{2,1,0:T(8,128)(2,1)}), bf16[64,32,128]{2,1,0:T(8,128)(2,1)S(1)}, u32[]{:S(2)}, u32[]{:S(2)}) async-start(bf16[64,32,128]{2,1,0:T(8,128)(2,1)} %bitcast.5), calls=%async_computation | async-start | bytes 1048576 | tf_op jit(solution)/shard_map/all_to_all | solution.py:329
  19.7 1.9 %collective-permute-start = (bf16[128,1024]{1,0:T(8,128)(2,1)}, bf16[128,1024]{1,0:T(8,128)(2,1)S(1)}, u32[]{:S(2)}, u32[]{:S(2)}) collective-permute-start(bf16[128,1024]{1,0:T(8,128)(2,1)} %get-tuple-element.18), channel_id=1, source_target_pairs={{0,1},{1,0},{2,3},{3,2},{4,5},{5,4},{6,7},{7,6},{8,9},{9,8},{10,11... | collective-permute-start | bytes 786440 | tf_op jit(solution)/shard_map/ppermute | solution.py:309
  21.6 7.5 %collective-permute-start.1 = (bf16[64,1024]{1,0:T(8,128)(2,1)}, bf16[64,1024]{1,0:T(8,128)(2,1)S(1)}, u32[]{:S(2)}, u32[]{:S(2)}) collective-permute-start(bf16[64,1024]{1,0:T(8,128)(2,1)} %get-tuple-element.19), channel_id=1, source_target_pairs={{1,2},{3,4},{5,6},{7,8},{9,10},{11,12},{13,14},{15,16},{17,18},{19... | collective-permute-start | bytes 393224 | tf_op jit(solution)/shard_map/ppermute | solution.py:333
  29.1 0.8 %copy-done.6 = bf16[32,1024]{1,0:T(8,128)(2,1)S(1)} copy-done((bf16[32,1024]{1,0:T(8,128)(2,1)S(1)}, bf16[32,1024]{1,0:T(8,128)(2,1)}, u32[]{:S(2)}) %copy-start.6) | copy-done | bytes 65560
  30.1 1.9 %collective-permute-start.2 = (bf16[64,1024]{1,0:T(8,128)(2,1)S(1)}, bf16[64,1024]{1,0:T(8,128)(2,1)S(1)}, u32[]{:S(2)}, u32[]{:S(2)}) collective-permute-start(bf16[64,1024]{1,0:T(8,128)(2,1)S(1)} %shard_map.38.refs_0_), channel_id=1, source_target_pairs={{0,2},{1,3},{2,0},{3,1},{4,6},{5,7},{6,4},{7,5},{8,10},{9,11},{10,... | collective-permute-start | bytes 393224 | tf_op jit(solution)/shard_map/ppermute | solution.py:309
  32.0 5.4 %collective-permute-done.1.refs_2_.refs_5_ = bf16[64,1024]{1,0:T(8,128)(2,1)S(1)} collective-permute-done((bf16[64,1024]{1,0:T(8,128)(2,1)}, bf16[64,1024]{1,0:T(8,128)(2,1)S(1)}, u32[]{:S(2)}, u32[]{:S(2)}) %collective-permute-start.1) | collective-permute-done | bytes 131104 | tf_op jit(solution)/shard_map/ppermute | solution.py:333
  37.4 0.8 %collective-permute-done.2.refs_1_.refs_4_ = bf16[64,1024]{1,0:T(8,128)(2,1)S(1)} collective-permute-done((bf16[64,1024]{1,0:T(8,128)(2,1)S(1)}, bf16[64,1024]{1,0:T(8,128)(2,1)S(1)}, u32[]{:S(2)}, u32[]{:S(2)}) %collective-permute-start.2) | collective-permute-done | bytes 131104 | tf_op jit(solution)/shard_map/ppermute | solution.py:309
  39.7 1.2 %shard_map.40.refs_0_.refs_3_ = bf16[160,1024]{1,0:T(8,128)(2,1)S(1)} custom-call(s32[1]{0:T(128)} %bitcast.refs_0_, bf16[64,32,128]{2,1,0:T(8,128)(2,1)S(1)} %all-to-all-done.refs_1_, bf16[64,1024]{1,0:T(8,128)(2,1)S(1)} %shard_map.39.refs_2_.refs_0_), custom_call_target="tpu_custom_call" | custom-call | bytes 1048576 | tf_op jit(solution)/shard_map/pallas_call | solution.py:40
  40.9 2.1 %collective-permute-start.3 = (bf16[160,1024]{1,0:T(8,128)(2,1)S(1)}, bf16[160,1024]{1,0:T(8,128)(2,1)S(1)}, u32[]{:S(2)}, u32[]{:S(2)}) collective-permute-start(bf16[160,1024]{1,0:T(8,128)(2,1)S(1)} %shard_map.40.refs_0_.refs_3_), channel_id=1, source_target_pairs={{0,1},{1,0},{2,3},{3,2},{4,5},{5,4},{6,7},{7,6},{8,9},{9,8},{10,11... | collective-permute-start | bytes 983048 | tf_op jit(solution)/shard_map/ppermute | solution.py:309
  42.9 5.1 %collective-permute-start.4 = (bf16[64,1024]{1,0:T(8,128)(2,1)S(1)}, bf16[64,1024]{1,0:T(8,128)(2,1)S(1)}, u32[]{:S(2)}, u32[]{:S(2)}) collective-permute-start(bf16[64,1024]{1,0:T(8,128)(2,1)S(1)} %shard_map.39.refs_2_.refs_0_), channel_id=1, source_target_pairs={{0,4},{1,5},{2,6},{3,7},{4,0},{5,1},{6,2},{7,3},{8,12},{9,13},{10,... | collective-permute-start | bytes 393224 | tf_op jit(solution)/shard_map/ppermute | solution.py:309
  48.1 0.8 %shard_map.41.refs_6_.refs_2_ = bf16[256,1024]{1,0:T(8,128)(2,1)} custom-call(bf16[160,1024]{1,0:T(8,128)(2,1)S(1)} %shard_map.40.refs_0_.refs_3_, bf16[160,1024]{1,0:T(8,128)(2,1)S(1)} %collective-permute-done.3.refs_1_.refs_4_), custom_call_target="tpu_custom_call" | custom-call | bytes 1048576 | tf_op jit(solution)/shard_map/pallas_call | solution.py:40
  48.9 4.8 %all-to-all-start.1 = ((bf16[4,64,1024]{2,1,0:T(8,128)(2,1)}), bf16[4,64,1024]{2,1,0:T(8,128)(2,1)S(1)}, u32[]{:S(2)}, u32[]{:S(2)}) async-start(bf16[4,64,1024]{2,1,0:T(8,128)(2,1)} %bitcast.2), calls=%async_computation.1 | async-start | bytes 1048576 | tf_op jit(solution)/shard_map/all_to_all | solution.py:346
  53.7 1.2 %collective-permute-done.4.refs_5_.refs_1_ = bf16[64,1024]{1,0:T(8,128)(2,1)S(1)} collective-permute-done((bf16[64,1024]{1,0:T(8,128)(2,1)S(1)}, bf16[64,1024]{1,0:T(8,128)(2,1)S(1)}, u32[]{:S(2)}, u32[]{:S(2)}) %collective-permute-start.4) | collective-permute-done | bytes 131104 | tf_op jit(solution)/shard_map/ppermute | solution.py:309
  55.1 3.1 %collective-permute-start.5 = (bf16[64,1024]{1,0:T(8,128)(2,1)S(1)}, bf16[64,1024]{1,0:T(8,128)(2,1)S(1)}, u32[]{:S(2)}, u32[]{:S(2)}) collective-permute-start(bf16[64,1024]{1,0:T(8,128)(2,1)S(1)} %shard_map.45), channel_id=1, source_target_pairs={{0,12},{1,13},{2,14},{3,15},{4,8},{5,9},{6,10},{7,11},{8,4},{9,5},... | collective-permute-start | bytes 393224 | tf_op jit(solution)/shard_map/ppermute | solution.py:309
  58.1 0.9 %copy-done.5 = bf16[64,1024]{1,0:T(8,128)(2,1)S(1)} copy-done((bf16[64,1024]{1,0:T(8,128)(2,1)S(1)}, bf16[64,1024]{1,0:T(8,128)(2,1)}, u32[]{:S(2)}) %copy-start.5) | copy-done | bytes 131096
  59.0 1.0 %copy-done.8 = bf16[256,1024]{1,0:T(8,128)(2,1)S(1)} copy-done((bf16[256,1024]{1,0:T(8,128)(2,1)S(1)}, bf16[256,1024]{1,0:T(8,128)(2,1)}, u32[]{:S(2)}) %copy-start.8) | copy-done | bytes 524312
  60.1 1.4 %shard_map.42 = (bf16[256,512]{1,0:T(8,128)(2,1)S(1)}, f32[256,512]{1,0:T(8,128)S(1)}, f32[256,512]{1,0:T(8,128)S(1)}) custom-call(s32[1]{0:T(128)} %bitcast.refs_0_, bf16[256,512]{1,0:T(8,128)(2,1)S(1)} %copy-done.1, bf16[512,1536]{1,0:T(8,128)(2,1)S(1)} %copy-done, bf16[256,1024]{1,0:T(8,128)(2,1)S(1)} %copy-done.8, ...), custom_call_target="tpu_custom_call" | custom-call | flops 1000000000 | bytes 1048576 | tf_op jit(solution)/shard_map/pallas_call | solution.py:40
  61.5 1.0 %shard_map.43 = (f32[256,512]{1,0:T(8,128)S(1)}, f32[256,512]{1,0:T(8,128)S(1)}) custom-call(bf16[256,512]{1,0:T(8,128)(2,1)S(1)} %get-tuple-element.22.refs_0_.refs_1_, f32[256,512]{1,0:T(8,128)S(1)} %get-tuple-element.23.refs_1_, f32[256,512]{1,0:T(8,128)S(1)} %get-tuple-element.24.refs_2_, bf16[160,1024]{1,0:T(8,128)(2,1)S(1)} %shard_map.40.refs_0_.refs_3_, ...), custom_call_target="tpu_custom_call" | custom-call | flops 1000000000 | bytes 1048576 | tf_op jit(solution)/shard_map/pallas_call | solution.py:40
  62.5 1.0 %shard_map.44 = (f32[256,512]{1,0:T(8,128)S(1)}, f32[256,512]{1,0:T(8,128)S(1)}) custom-call(bf16[256,512]{1,0:T(8,128)(2,1)S(1)} %get-tuple-element.22.refs_0_.refs_1_, f32[256,512]{1,0:T(8,128)S(1)} %get-tuple-element.25.refs_1_, f32[256,512]{1,0:T(8,128)S(1)} %get-tuple-element.26.refs_2_, ...), custom_call_target="tpu_custom_call" | custom-call | flops 1000000000 | bytes 1048576 | tf_op jit(solution)/shard_map/pallas_call | solution.py:40
  63.4 1.2 %collective-permute-done.5.refs_5_ = bf16[64,1024]{1,0:T(8,128)(2,1)S(1)} collective-permute-done((bf16[64,1024]{1,0:T(8,128)(2,1)S(1)}, bf16[64,1024]{1,0:T(8,128)(2,1)S(1)}, u32[]{:S(2)}, u32[]{:S(2)}) %collective-permute-start.5) | collective-permute-done | bytes 131104 | tf_op jit(solution)/shard_map/ppermute | solution.py:309
  65.3 0.9 %copy-done.10 = bf16[64,1024]{1,0:T(8,128)(2,1)S(1)} copy-done((bf16[64,1024]{1,0:T(8,128)(2,1)S(1)}, bf16[64,1024]{1,0:T(8,128)(2,1)}, u32[]{:S(2)}) %copy-start.10) | copy-done | bytes 131096
  66.2 0.9 %copy-done.12 = bf16[256,512]{1,0:T(8,128)(2,1)S(1)} copy-done((bf16[256,512]{1,0:T(8,128)(2,1)S(1)}, bf16[256,512]{1,0:T(8,128)(2,1)}, u32[]{:S(2)}) %copy-start.12) | copy-done | bytes 262168
  67.2 1.9 %shard_map.46 = bf16[256,512]{1,0:T(8,128)(2,1)} custom-call(s32[1]{0:T(128)} %bitcast.refs_0_, bf16[256,512]{1,0:T(8,128)(2,1)S(1)} %copy-done.12, f32[256,512]{1,0:T(8,128)S(1)} %get-tuple-element.27.refs_2_, f32[256,512]{1,0:T(8,128)S(1)} %get-tuple-element.28.refs_3_, bf16[512,512]{1,0:T(8,128)(2,1)S(1)} %copy-done.7, bf16[64,1024]{1,0:T(8,128)(2,1)S(1)} %copy-done.10, ...), custom_call_target="tpu_custom_call" | custom-call | flops 1000000000 | bytes 1048576 | tf_op jit(solution)/shard_map/pallas_call | solution.py:40
  (28 shorter events, 2.4 us)
Async XLA Ops:
  3.1 36.5 %all-to-all-start = ((bf16[64,32,128]{2,1,0:T(8,128)(2,1)}), bf16[64,32,128]{2,1,0:T(8,128)(2,1)S(1)}, u32[]{:S(2)}, u32[]{:S(2)}) async-start(bf16[64,32,128]{2,1,0:T(8,128)(2,1)} %bitcast.5), calls=%async_computation | async-start | bytes 1048576 | tf_op jit(solution)/shard_map/all_to_all | solution.py:329
  19.7 9.4 %collective-permute-start = (bf16[128,1024]{1,0:T(8,128)(2,1)}, bf16[128,1024]{1,0:T(8,128)(2,1)S(1)}, u32[]{:S(2)}, u32[]{:S(2)}) collective-permute-start(bf16[128,1024]{1,0:T(8,128)(2,1)} %get-tuple-element.18), channel_id=1, source_target_pairs={{0,1},{1,0},{2,3},{3,2},{4,5},{5,4},{6,7},{7,6},{8,9},{9,8},{10,11... | collective-permute-start | bytes 786440 | tf_op jit(solution)/shard_map/ppermute | solution.py:309
  21.6 15.8 %collective-permute-start.1 = (bf16[64,1024]{1,0:T(8,128)(2,1)}, bf16[64,1024]{1,0:T(8,128)(2,1)S(1)}, u32[]{:S(2)}, u32[]{:S(2)}) collective-permute-start(bf16[64,1024]{1,0:T(8,128)(2,1)} %get-tuple-element.19), channel_id=1, source_target_pairs={{1,2},{3,4},{5,6},{7,8},{9,10},{11,12},{13,14},{15,16},{17,18},{19... | collective-permute-start | bytes 393224 | tf_op jit(solution)/shard_map/ppermute | solution.py:333
  29.1 0.8 %copy-start.6 = (bf16[32,1024]{1,0:T(8,128)(2,1)S(1)}, bf16[32,1024]{1,0:T(8,128)(2,1)}, u32[]{:S(2)}) copy-start(bf16[32,1024]{1,0:T(8,128)(2,1)} %get-tuple-element.21.refs_0_) | copy-start | bytes 196612
  30.1 8.1 %collective-permute-start.2 = (bf16[64,1024]{1,0:T(8,128)(2,1)S(1)}, bf16[64,1024]{1,0:T(8,128)(2,1)S(1)}, u32[]{:S(2)}, u32[]{:S(2)}) collective-permute-start(bf16[64,1024]{1,0:T(8,128)(2,1)S(1)} %shard_map.38.refs_0_), channel_id=1, source_target_pairs={{0,2},{1,3},{2,0},{3,1},{4,6},{5,7},{6,4},{7,5},{8,10},{9,11},{10,... | collective-permute-start | bytes 393224 | tf_op jit(solution)/shard_map/ppermute | solution.py:309
  38.4 0.6 copy-start.2
  39.0 0.7 copy-start.4
  40.8 17.3 %copy-start = (bf16[512,1536]{1,0:T(8,128)(2,1)S(1)}, bf16[512,1536]{1,0:T(8,128)(2,1)}, u32[]{:S(2)}) copy-start(bf16[512,1536]{1,0:T(8,128)(2,1)} %refs_2_.3) | copy-start | bytes 4718596
  40.9 17.3 %copy-start.1 = (bf16[256,512]{1,0:T(8,128)(2,1)S(1)}, bf16[256,512]{1,0:T(8,128)(2,1)}, u32[]{:S(2)}) copy-start(bf16[256,512]{1,0:T(8,128)(2,1)} %refs_1_.3) | copy-start | bytes 786436
  40.9 7.2 %collective-permute-start.3 = (bf16[160,1024]{1,0:T(8,128)(2,1)S(1)}, bf16[160,1024]{1,0:T(8,128)(2,1)S(1)}, u32[]{:S(2)}, u32[]{:S(2)}) collective-permute-start(bf16[160,1024]{1,0:T(8,128)(2,1)S(1)} %shard_map.40.refs_0_.refs_3_), channel_id=1, source_target_pairs={{0,1},{1,0},{2,3},{3,2},{4,5},{5,4},{6,7},{7,6},{8,9},{9,8},{10,11... | collective-permute-start | bytes 983048 | tf_op jit(solution)/shard_map/ppermute | solution.py:309
  42.9 12.0 %collective-permute-start.4 = (bf16[64,1024]{1,0:T(8,128)(2,1)S(1)}, bf16[64,1024]{1,0:T(8,128)(2,1)S(1)}, u32[]{:S(2)}, u32[]{:S(2)}) collective-permute-start(bf16[64,1024]{1,0:T(8,128)(2,1)S(1)} %shard_map.39.refs_2_.refs_0_), channel_id=1, source_target_pairs={{0,4},{1,5},{2,6},{3,7},{4,0},{5,1},{6,2},{7,3},{8,12},{9,13},{10,... | collective-permute-start | bytes 393224 | tf_op jit(solution)/shard_map/ppermute | solution.py:309
  48.9 16.4 %all-to-all-start.1 = ((bf16[4,64,1024]{2,1,0:T(8,128)(2,1)}), bf16[4,64,1024]{2,1,0:T(8,128)(2,1)S(1)}, u32[]{:S(2)}, u32[]{:S(2)}) async-start(bf16[4,64,1024]{2,1,0:T(8,128)(2,1)} %bitcast.2), calls=%async_computation.1 | async-start | bytes 1048576 | tf_op jit(solution)/shard_map/all_to_all | solution.py:346
  55.1 9.6 %collective-permute-start.5 = (bf16[64,1024]{1,0:T(8,128)(2,1)S(1)}, bf16[64,1024]{1,0:T(8,128)(2,1)S(1)}, u32[]{:S(2)}, u32[]{:S(2)}) collective-permute-start(bf16[64,1024]{1,0:T(8,128)(2,1)S(1)} %shard_map.45), channel_id=1, source_target_pairs={{0,12},{1,13},{2,14},{3,15},{4,8},{5,9},{6,10},{7,11},{8,4},{9,5},... | collective-permute-start | bytes 393224 | tf_op jit(solution)/shard_map/ppermute | solution.py:309
  58.1 0.9 %copy-start.5 = (bf16[64,1024]{1,0:T(8,128)(2,1)S(1)}, bf16[64,1024]{1,0:T(8,128)(2,1)}, u32[]{:S(2)}) copy-start(bf16[64,1024]{1,0:T(8,128)(2,1)} %copy-done.4) | copy-start | bytes 393220
  59.0 1.0 %copy-start.8 = (bf16[256,1024]{1,0:T(8,128)(2,1)S(1)}, bf16[256,1024]{1,0:T(8,128)(2,1)}, u32[]{:S(2)}) copy-start(bf16[256,1024]{1,0:T(8,128)(2,1)} %get-tuple-element.17.refs_3_) | copy-start | bytes 1572868
  61.4 1.0 %copy-start.11 = (bf16[256,512]{1,0:T(8,128)(2,1)}, bf16[256,512]{1,0:T(8,128)(2,1)S(1)}, u32[]{:S(2)}) copy-start(bf16[256,512]{1,0:T(8,128)(2,1)S(1)} %get-tuple-element.22.refs_0_.refs_1_) | copy-start | bytes 786436
  61.5 1.0 %copy-start.3 = (bf16[64,1024]{1,0:T(8,128)(2,1)S(1)}, bf16[64,1024]{1,0:T(8,128)(2,1)}, u32[]{:S(2)}) copy-start(bf16[64,1024]{1,0:T(8,128)(2,1)} %copy-done.2) | copy-start | bytes 393220
  62.5 2.9 %copy-start.7 = (bf16[512,512]{1,0:T(8,128)(2,1)S(1)}, bf16[512,512]{1,0:T(8,128)(2,1)}, u32[]{:S(2)}) copy-start(bf16[512,512]{1,0:T(8,128)(2,1)} %refs_4_.1) | copy-start | bytes 1572868
  64.7 0.7 copy-start.9
  65.3 0.9 %copy-start.10 = (bf16[64,1024]{1,0:T(8,128)(2,1)S(1)}, bf16[64,1024]{1,0:T(8,128)(2,1)}, u32[]{:S(2)}) copy-start(bf16[64,1024]{1,0:T(8,128)(2,1)} %copy-done.9) | copy-start | bytes 393220
  66.2 0.9 %copy-start.12 = (bf16[256,512]{1,0:T(8,128)(2,1)S(1)}, bf16[256,512]{1,0:T(8,128)(2,1)}, u32[]{:S(2)}) copy-start(bf16[256,512]{1,0:T(8,128)(2,1)} %copy-done.11) | copy-start | bytes 786436

commit v7 on v6

--- a/solution.py
+++ b/solution.py
@@ -12,6 +12,7 @@
 BLOCK = 64
 AXES = ("gx", "gy")
 FAR8 = (6, 7, 4, 5, 2, 3, 0, 1)
+FAR4 = (3, 2, 1, 0)
 
 
 def partners(bit, count):
@@ -19,6 +20,8 @@
     for index in range(count):
         if bit == 3:
             route.append(index & ~14 | FAR8[index >> 1 & 7] << 1)
+        elif bit == 8:
+            route.append(index & ~384 | FAR4[index >> 7 & 3] << 7)
         else:
             route.append(index ^ 1 << bit)
     return route
@@ -31,7 +34,7 @@
 SMEM = pl.BlockSpec(memory_space=pltpu.SMEM)
 
 
-def call(kernel, outs, in_specs, *args, flops=0, scratch=(), limit=24, after=()):
+def call(kernel, outs, in_specs, *args, flops=0, scratch=(), limit=10, after=()):
     count = len(args)
 
     def body(*refs):
@@ -143,9 +146,7 @@
 def own_9_kernel(mine_ref, sib_ref, out_ref):
     at = 3 * BLOCK // 2
     both = mine_ref[at:, :].astype(jnp.float32) + sib_ref[at:, :].astype(jnp.float32)
-    block = (both * 0.5).astype(jnp.bfloat16)
-    for copy in range(out_ref.shape[0] // BLOCK):
-        out_ref[copy * BLOCK : (copy + 1) * BLOCK, :] = block
+    out_ref[...] = (both * 0.5).astype(jnp.bfloat16)
 
 
 def pool_near_kernel(mine_ref, sib_ref, out_ref):
@@ -179,7 +180,8 @@
 
 
 def local_kernel(
-    count, place, x_ref, w_hbm, kv_ref, near_ref, other_ref, q_ref, num_ref, tot_ref, pad, l1, w_ref, sem
+    count, place, x_ref, w_hbm, kv_ref, near_ref, other_ref, mine_ref, theirs_ref, sib_3_ref,
+    sib_4_ref, q_ref, num_ref, tot_ref, pad, l1, w_ref, sem
 ):
     rows, model = x_ref.shape
     blocks = rows // BLOCK
@@ -220,6 +222,13 @@
             num, tot = attend_pair(q_ref[here, kl], keys, values, ones)
             num_ref[here, kl] = num
             tot_ref[here, kl] = tot
+    for refs in ((mine_ref, theirs_ref), (near_ref, sib_3_ref, sib_4_ref)):
+        far = far_blocks(refs)
+        for lanes in range(0, model, 128):
+            kl = slice(lanes, lanes + 128)
+            num, tot = far_sums(far, q_ref[:, kl], lanes, model)
+            num_ref[:, kl] += num
+            tot_ref[:, kl] += tot
 
 
 def far_blocks(refs):
@@ -240,34 +249,18 @@
     return attend_pair(q, keys, values, jnp.ones(values.shape, jnp.bfloat16))
 
 
-def far_kernel(q_ref, num_in, tot_in, *refs):
-    num_ref, tot_ref = refs[-2:]
+def final_kernel(
+    q_ref, num_in, tot_in, sib_5_ref, sib_9_ref, sib_10_ref, w_hbm, out_ref, att, w_ref, sem
+):
+    copy = pltpu.make_async_copy(w_hbm, w_ref, sem)
+    copy.start()
     model = q_ref.shape[1]
-    far = far_blocks(refs[:-2])
-    for lanes in range(0, model, 128):
-        at = slice(lanes, lanes + 128)
-        num, tot = far_sums(far, q_ref[:, at], lanes, model)
-        num_ref[:, at] = num_in[:, at] + num
-        tot_ref[:, at] = tot_in[:, at] + tot
-
-
-def final_kernel(place, q_ref, num_in, tot_in, w_ref, sib_5_ref, wide_ref, out_ref, att):
-    model = q_ref.shape[1]
-    x = place[0] >> 7
-    near = pl.multiple_of((x ^ 1) * BLOCK, BLOCK)
-    other = pl.multiple_of(((x >> 1) ^ 1) * 2 * BLOCK, BLOCK)
-    far = jnp.concatenate(
-        [
-            sib_5_ref[...],
-            wide_ref[pl.ds(near, BLOCK), :],
-            pooled(wide_ref[pl.ds(other, 2 * BLOCK), :]),
-        ],
-        axis=0,
-    )
+    far = far_blocks((sib_5_ref, sib_9_ref, sib_10_ref))
     for lanes in range(0, model, 128):
         at = slice(lanes, lanes + 128)
         num, tot = far_sums(far, q_ref[:, at], lanes, model)
         att[:, at] = ((num_in[:, at] + num) / (tot_in[:, at] + tot)).astype(jnp.bfloat16)
+    copy.wait()
     out_ref[...] = jnp.dot(att[...], w_ref[...], preferred_element_type=jnp.float32).astype(
         jnp.bfloat16
     )
@@ -280,7 +273,8 @@
     place = index.astype(jnp.int32).reshape(1)
     bf16 = lambda *shape: jax.ShapeDtypeStruct(shape, jnp.bfloat16)
     f32 = lambda *shape: jax.ShapeDtypeStruct(shape, jnp.float32)
-    anywhere = pl.BlockSpec(memory_space=pl.ANY)
+    in_hbm = pl.BlockSpec(memory_space=pl.ANY)
+    stay = lambda array: pltpu.with_memory_space_constraint(array, pltpu.HBM)
     steps = 2
     width = 2 * model // steps
     members = 64
@@ -292,8 +286,8 @@
             bf16(rows, 2 * model), bf16(2 * BLOCK, 2 * model), block,
             bf16(BLOCK // 2, 2 * model), bf16(members * packed, 128),
         ),
-        [SMEM, anywhere, anywhere],
-        place, tokens, w_qkv,
+        [SMEM, in_hbm, in_hbm],
+        place, stay(tokens), stay(w_qkv),
         flops=4 * rows * model * model,
         scratch=(
             pltpu.VMEM((rows, model), jnp.bfloat16),
@@ -301,7 +295,6 @@
             pltpu.VMEM((2 * model // 128, rows, 128), jnp.float32),
             pltpu.SemaphoreType.DMA((steps + 1,)),
         ),
-        limit=56,
     )
     swap = [(i, i + 1) for i in range(1, count - 1, 2)]
     swap += [(j, i) for i, j in swap]
@@ -310,16 +303,6 @@
 
     def pool(own, got, *after):
         return call(pool_kernel, block, vmem(2), own, got, after=after)
-
-    def far(num, tot, *part, after=()):
-        return call(
-            far_kernel,
-            (f32(rows, model), f32(rows, model)),
-            vmem(3 + len(part)),
-            q, num, tot, *part,
-            flops=10**9,
-            after=after,
-        )
 
     teams = [
         [i for i in range(count) if i >> 7 == x and i & 1 == core]
@@ -331,25 +314,26 @@
     own_3 = call(pool_near_kernel, block, vmem(2), level_3, near_sib)
     sib_3 = exchange(own_3, 1)
     other_halo = lax.ppermute(other, AXES, swap)
-    own_4 = pool(own_3, sib_3, other_halo)
+    own_4 = pool(own_3, sib_3)
     sib_4 = exchange(own_4, 2)
     mine = call(
         unpack_kernel, bf16(5 * BLOCK // 2, 2 * model), [SMEM, *vmem(1)],
         place, spread.reshape(members, packed, 128),
         scratch=(pltpu.VMEM((members * packed, 128), jnp.float32),),
-        after=(own_4,),
+        after=(own_4, other_halo),
     )
     theirs = exchange(mine, 0)
-    own_9 = call(own_9_kernel, bf16(4 * BLOCK, 2 * model), vmem(2), mine, theirs)
+    own_9 = call(own_9_kernel, block, vmem(2), mine, theirs)
+    sib_9 = exchange(own_9, 7)
     own_5 = pool(own_4, sib_4, own_9)
-    columns = [list(range(i, count, count >> 2)) for i in range(count >> 2)]
-    wide = lax.all_to_all(own_9, AXES, 0, 0, axis_index_groups=columns, tiled=True)
     sib_5 = exchange(own_5, 3)
+    own_10 = pool(own_9, sib_9, own_5)
+    sib_10 = exchange(own_10, 8)
     q, num, tot = call(
         functools.partial(local_kernel, count),
         (bf16(rows, model), f32(rows, model), f32(rows, model)),
-        [SMEM, *vmem(1), anywhere, *vmem(3)],
-        place, tokens, w_qkv, kv, near_sib, other_halo,
+        [SMEM, *vmem(1), in_hbm, *vmem(7)],
+        place, tokens, stay(w_qkv), kv, near_sib, other_halo, mine, theirs, sib_3, sib_4,
         flops=10**9,
         scratch=(
             pltpu.VMEM((rows + 2 * BLOCK, 2 * model), jnp.bfloat16),
@@ -357,18 +341,19 @@
             pltpu.VMEM((model, model), jnp.bfloat16),
             pltpu.SemaphoreType.DMA(()),
         ),
-        limit=48,
-        after=(own_9,),
-    )
-    num, tot = far(num, tot, mine, theirs)
-    num, tot = far(num, tot, near_sib, sib_3, sib_4)
+        after=(own_10,),
+    )
     return call(
         final_kernel,
         bf16(rows, model),
-        [SMEM, *vmem(6)],
-        place, q, num, tot, w_out, sib_5, wide,
+        [*vmem(6), in_hbm],
+        q, num, tot, sib_5, sib_9, sib_10, stay(w_out),
         flops=10**9,
-        scratch=(pltpu.VMEM((rows, model), jnp.bfloat16),),
+        scratch=(
+            pltpu.VMEM((rows, model), jnp.bfloat16),
+            pltpu.VMEM((model, model), jnp.bfloat16),
+            pltpu.SemaphoreType.DMA(()),
+        ),
     )
 
 

time: 69.8 us -> 67.2 us (0.963)
  local copies, waits for them, and re-layouts: 6.6 us -> 0.01 us
  waiting for transfers between devices: 8.57 us -> 13.6 us
  starting transfers between devices: 42.9 us -> 42 us
    ppermute x5 -> x7, waiting for transfers between devices: 3.2 us -> 11.3 us  [exchange(): return lax.ppermute(own, AXES, list(enumerate(partners(bit, count))))]
    unnamed x26 -> x2, local copies, waits for them, and re-layouts: 6.6 us -> 0.01 us
    all_to_all x1 -> x0, starting transfers between devices: 4.77 us -> none  [per_device(): lax.all_to_all(own_9, AXES, 0, 0, axis_index_groups=columns, tiled=True)]
    ppermute x5 -> x7, starting transfers between devices: 14.1 us -> 18.7 us  [exchange(): return lax.ppermute(own, AXES, list(enumerate(partners(bit, count))))]
    ppermute x1, waiting for transfers between devices: 5.37 us -> 1.48 us  [per_device(): other_halo = lax.ppermute(other, AXES, swap)]
    all_to_all x1, waiting for transfers between devices: 0.01 us -> 0.8 us  [per_device(): lax.all_to_all(level_6, AXES, 0, 0, axis_index_groups=teams, tiled=True)]
    ppermute x1, starting transfers between devices: 7.48 us -> 6.72 us  [per_device(): other_halo = lax.ppermute(other, AXES, swap)]
    pallas_call x10 -> x9, Pallas kernels: 10.8 us -> 10.3 us  [call(): pl.pallas_call(body, out_shape=outs, in_specs=list(in_specs) + [pl.BlockS...]
  transfers between devices with their start and end apart: 8 -> 9, of which waited for: 4 -> 7; matrix products, arithmetic and copies ran while one was open for 0% -> 0% of each run, Pallas kernels for 7% -> 6%
where the time goes in v7:
time: 67.2 us; the launch traced here: 66.1 us
  starting transfers between devices  42 us (62%)
  waiting for transfers between devices  13.6 us (20%)
  Pallas kernels  10.3 us (15%)
    ppermute x7, starting transfers between devices, exchange(): return lax.ppermute(own, AXES, list(enumerate(partners(bit, count))))  18.7 us
    all_to_all x1, starting transfers between devices, per_device(): lax.all_to_all(level_6, AXES, 0, 0, axis_index_groups=teams, tiled=True)  16.6 us
    ppermute x7, waiting for transfers between devices, exchange(): return lax.ppermute(own, AXES, list(enumerate(partners(bit, count))))  11.3 us
    pallas_call x9, Pallas kernels, call(): pl.pallas_call(body, out_shape=outs, in_specs=list(in_specs) + [pl.BlockS...  10.3 us
    ppermute x1, starting transfers between devices, per_device(): other_halo = lax.ppermute(other, AXES, swap)  6.72 us
    ppermute x1, waiting for transfers between devices, per_device(): other_halo = lax.ppermute(other, AXES, swap)  1.48 us
  transfers between devices with their start and end apart: 9, of which 7 were waited for; matrix products, arithmetic and copies ran while one was open for 0% of the time, Pallas kernels for 6%

profile of v7, /device:TPU:6, one launch (start us, length us, event | category | flops | bytes accessed | tf_op | source)
XLA Modules:
  0.0 66.1 jit_solution(7844244098466481501)
XLA Ops:
  0.0 3.0 %shard_map.37 = (bf16[256,1024]{1,0:T(8,128)(2,1)S(1)}, bf16[128,1024]{1,0:T(8,128)(2,1)S(1)}, bf16[64,1024]{1,0:T(8,128)(2,1)S(1)}, bf16[32,1024]{1,0:T(8,128)(2,1)S(1)}, bf16[2048,128]{1,0:T(8,128)(2,1)}) custom-call(s32[1]{0:T(128)} %bitcast.refs_0_, bf16[256,512]{1,0:T(8,128)(2,1)} %refs_1_.3, bf16[512,1536]{1,0:T(8,128)(2,1)} %refs_2_.3), custom_call_target="tpu_custom_call" | custom-call | flops 268435456 | bytes 1048576 | tf_op jit(solution)/shard_map/pallas_call | solution.py:43
  3.0 16.6 %all-to-all-start = ((bf16[64,32,128]{2,1,0:T(8,128)(2,1)}), bf16[64,32,128]{2,1,0:T(8,128)(2,1)S(1)}, u32[]{:S(2)}, u32[]{:S(2)}) async-start(bf16[64,32,128]{2,1,0:T(8,128)(2,1)} %bitcast.1), calls=%async_computation | async-start | bytes 1048576 | tf_op jit(solution)/shard_map/all_to_all | solution.py:312
  19.6 1.9 %collective-permute-start = (bf16[128,1024]{1,0:T(8,128)(2,1)S(1)}, bf16[128,1024]{1,0:T(8,128)(2,1)S(1)}, u32[]{:S(2)}, u32[]{:S(2)}) collective-permute-start(bf16[128,1024]{1,0:T(8,128)(2,1)S(1)} %get-tuple-element.14), channel_id=1, source_target_pairs={{0,1},{1,0},{2,3},{3,2},{4,5},{5,4},{6,7},{7,6},{8,9},{9,8},{10,11... | collective-permute-start | bytes 786440 | tf_op jit(solution)/shard_map/ppermute | solution.py:302
  21.5 1.5 %collective-permute-done.refs_1_.refs_4_ = bf16[128,1024]{1,0:T(8,128)(2,1)S(1)} collective-permute-done((bf16[128,1024]{1,0:T(8,128)(2,1)S(1)}, bf16[128,1024]{1,0:T(8,128)(2,1)S(1)}, u32[]{:S(2)}, u32[]{:S(2)}) %collective-permute-start) | collective-permute-done | bytes 262176 | tf_op jit(solution)/shard_map/ppermute | solution.py:302
  23.0 0.1 shard_map.38.refs_0_
  23.2 3.5 %collective-permute-start.2 = (bf16[64,1024]{1,0:T(8,128)(2,1)S(1)}, bf16[64,1024]{1,0:T(8,128)(2,1)S(1)}, u32[]{:S(2)}, u32[]{:S(2)}) collective-permute-start(bf16[64,1024]{1,0:T(8,128)(2,1)S(1)} %shard_map.38.refs_0_), channel_id=1, source_target_pairs={{0,2},{1,3},{2,0},{3,1},{4,6},{5,7},{6,4},{7,5},{8,10},{9,11},{10,... | collective-permute-start | bytes 393224 | tf_op jit(solution)/shard_map/ppermute | solution.py:302
  26.7 6.7 %collective-permute-start.1 = (bf16[64,1024]{1,0:T(8,128)(2,1)S(1)}, bf16[64,1024]{1,0:T(8,128)(2,1)S(1)}, u32[]{:S(2)}, u32[]{:S(2)}) collective-permute-start(bf16[64,1024]{1,0:T(8,128)(2,1)S(1)} %get-tuple-element.15), channel_id=1, source_target_pairs={{1,2},{3,4},{5,6},{7,8},{9,10},{11,12},{13,14},{15,16},{17,18},{19... | collective-permute-start | bytes 393224 | tf_op jit(solution)/shard_map/ppermute | solution.py:316
  33.4 3.0 %collective-permute-done.2.refs_1_.refs_8_ = bf16[64,1024]{1,0:T(8,128)(2,1)S(1)} collective-permute-done((bf16[64,1024]{1,0:T(8,128)(2,1)S(1)}, bf16[64,1024]{1,0:T(8,128)(2,1)S(1)}, u32[]{:S(2)}, u32[]{:S(2)}) %collective-permute-start.2) | collective-permute-done | bytes 131104 | tf_op jit(solution)/shard_map/ppermute | solution.py:302
  36.4 0.2 shard_map.39.refs_2_.refs_0_
  36.6 1.5 %collective-permute-done.1.refs_3_.refs_5_ = bf16[64,1024]{1,0:T(8,128)(2,1)S(1)} collective-permute-done((bf16[64,1024]{1,0:T(8,128)(2,1)S(1)}, bf16[64,1024]{1,0:T(8,128)(2,1)S(1)}, u32[]{:S(2)}, u32[]{:S(2)}) %collective-permute-start.1) | collective-permute-done | bytes 131104 | tf_op jit(solution)/shard_map/ppermute | solution.py:316
  38.1 0.8 %all-to-all-done.refs_1_ = bf16[64,32,128]{2,1,0:T(8,128)(2,1)S(1)} async-done(((bf16[64,32,128]{2,1,0:T(8,128)(2,1)}), bf16[64,32,128]{2,1,0:T(8,128)(2,1)S(1)}, u32[]{:S(2)}, u32[]{:S(2)}) %all-to-all-start) | async-done | bytes 524320 | tf_op jit(solution)/shard_map/all_to_all | solution.py:312
  38.9 1.2 %shard_map.40.refs_0_.refs_6_ = bf16[160,1024]{1,0:T(8,128)(2,1)S(1)} custom-call(s32[1]{0:T(128)} %bitcast.refs_0_, bf16[64,32,128]{2,1,0:T(8,128)(2,1)S(1)} %all-to-all-done.refs_1_, bf16[64,1024]{1,0:T(8,128)(2,1)S(1)} %shard_map.39.refs_2_.refs_0_, bf16[64,1024]{1,0:T(8,128)(2,1)S(1)} %collective-permute-done.1.refs_3_.refs_5_), custom_call_target="tpu_custom_call" | custom-call | bytes 1048576 | tf_op jit(solution)/shard_map/pallas_call | solution.py:43
  40.1 1.9 %collective-permute-start.3 = (bf16[160,1024]{1,0:T(8,128)(2,1)S(1)}, bf16[160,1024]{1,0:T(8,128)(2,1)S(1)}, u32[]{:S(2)}, u32[]{:S(2)}) collective-permute-start(bf16[160,1024]{1,0:T(8,128)(2,1)S(1)} %shard_map.40.refs_0_.refs_6_), channel_id=1, source_target_pairs={{0,1},{1,0},{2,3},{3,2},{4,5},{5,4},{6,7},{7,6},{8,9},{9,8},{10,11... | collective-permute-start | bytes 983048 | tf_op jit(solution)/shard_map/ppermute | solution.py:302
  42.0 4.2 %collective-permute-start.4 = (bf16[64,1024]{1,0:T(8,128)(2,1)S(1)}, bf16[64,1024]{1,0:T(8,128)(2,1)S(1)}, u32[]{:S(2)}, u32[]{:S(2)}) collective-permute-start(bf16[64,1024]{1,0:T(8,128)(2,1)S(1)} %shard_map.39.refs_2_.refs_0_), channel_id=1, source_target_pairs={{0,4},{1,5},{2,6},{3,7},{4,0},{5,1},{6,2},{7,3},{8,12},{9,13},{10,... | collective-permute-start | bytes 393224 | tf_op jit(solution)/shard_map/ppermute | solution.py:302
  46.2 2.7 %collective-permute-start.5 = (bf16[64,1024]{1,0:T(8,128)(2,1)S(1)}, bf16[64,1024]{1,0:T(8,128)(2,1)S(1)}, u32[]{:S(2)}, u32[]{:S(2)}) collective-permute-start(bf16[64,1024]{1,0:T(8,128)(2,1)S(1)} %shard_map.41.refs_2_.refs_0_), channel_id=1, source_target_pairs={{0,128},{1,129},{2,130},{3,131},{4,132},{5,133},{6,134},{7,135},{8... | collective-permute-start | bytes 393224 | tf_op jit(solution)/shard_map/ppermute | solution.py:302
  49.0 4.5 %collective-permute-done.4.refs_1_.refs_9_ = bf16[64,1024]{1,0:T(8,128)(2,1)S(1)} collective-permute-done((bf16[64,1024]{1,0:T(8,128)(2,1)S(1)}, bf16[64,1024]{1,0:T(8,128)(2,1)S(1)}, u32[]{:S(2)}, u32[]{:S(2)}) %collective-permute-start.4) | collective-permute-done | bytes 131104 | tf_op jit(solution)/shard_map/ppermute | solution.py:302
  53.5 0.2 shard_map.42.refs_2_
  53.7 2.1 %collective-permute-start.6 = (bf16[64,1024]{1,0:T(8,128)(2,1)S(1)}, bf16[64,1024]{1,0:T(8,128)(2,1)S(1)}, u32[]{:S(2)}, u32[]{:S(2)}) collective-permute-start(bf16[64,1024]{1,0:T(8,128)(2,1)S(1)} %shard_map.42.refs_2_), channel_id=1, source_target_pairs={{0,12},{1,13},{2,14},{3,15},{4,8},{5,9},{6,10},{7,11},{8,4},{9,5},... | collective-permute-start | bytes 393224 | tf_op jit(solution)/shard_map/ppermute | solution.py:302
  55.8 0.2 shard_map.43.refs_10_
  55.9 2.4 %collective-permute-start.7 = (bf16[64,1024]{1,0:T(8,128)(2,1)S(1)}, bf16[64,1024]{1,0:T(8,128)(2,1)S(1)}, u32[]{:S(2)}, u32[]{:S(2)}) collective-permute-start(bf16[64,1024]{1,0:T(8,128)(2,1)S(1)} %shard_map.43.refs_10_), channel_id=1, source_target_pairs={{0,384},{1,385},{2,386},{3,387},{4,388},{5,389},{6,390},{7,391},{8... | collective-permute-start | bytes 393224 | tf_op jit(solution)/shard_map/ppermute | solution.py:302
  58.3 3.4 %shard_map.44 = (bf16[256,512]{1,0:T(8,128)(2,1)S(1)}, f32[256,512]{1,0:T(8,128)S(1)}, f32[256,512]{1,0:T(8,128)S(1)}) custom-call(s32[1]{0:T(128)} %bitcast.refs_0_, bf16[256,512]{1,0:T(8,128)(2,1)S(1)} %copy-done, bf16[512,1536]{1,0:T(8,128)(2,1)} %refs_2_.3, bf16[256,1024]{1,0:T(8,128)(2,1)S(1)} %get-tuple-element.13.refs_3_, ...), custom_call_target="tpu_custom_call" | custom-call | flops 1000000000 | bytes 1048576 | tf_op jit(solution)/shard_map/pallas_call | solution.py:43
  61.7 1.2 %collective-permute-done.6.refs_3_ = bf16[64,1024]{1,0:T(8,128)(2,1)S(1)} collective-permute-done((bf16[64,1024]{1,0:T(8,128)(2,1)S(1)}, bf16[64,1024]{1,0:T(8,128)(2,1)S(1)}, u32[]{:S(2)}, u32[]{:S(2)}) %collective-permute-start.6) | collective-permute-done | bytes 131104 | tf_op jit(solution)/shard_map/ppermute | solution.py:302
  62.9 1.1 %collective-permute-done.7.refs_5_ = bf16[64,1024]{1,0:T(8,128)(2,1)S(1)} collective-permute-done((bf16[64,1024]{1,0:T(8,128)(2,1)S(1)}, bf16[64,1024]{1,0:T(8,128)(2,1)S(1)}, u32[]{:S(2)}, u32[]{:S(2)}) %collective-permute-start.7) | collective-permute-done | bytes 131104 | tf_op jit(solution)/shard_map/ppermute | solution.py:302
  64.0 2.1 %shard_map.45 = bf16[256,512]{1,0:T(8,128)(2,1)} custom-call(bf16[256,512]{1,0:T(8,128)(2,1)S(1)} %get-tuple-element.18.refs_0_, f32[256,512]{1,0:T(8,128)S(1)} %get-tuple-element.19.refs_1_, f32[256,512]{1,0:T(8,128)S(1)} %get-tuple-element.20.refs_2_, bf16[64,1024]{1,0:T(8,128)(2,1)S(1)} %collective-permute-done.6.refs_3_, ...), custom_call_target="tpu_custom_call" | custom-call | flops 1000000000 | bytes 1048576 | tf_op jit(solution)/shard_map/pallas_call | solution.py:43
  (5 shorter events, 0.1 us)
Async XLA Ops:
  3.0 35.9 %all-to-all-start = ((bf16[64,32,128]{2,1,0:T(8,128)(2,1)}), bf16[64,32,128]{2,1,0:T(8,128)(2,1)S(1)}, u32[]{:S(2)}, u32[]{:S(2)}) async-start(bf16[64,32,128]{2,1,0:T(8,128)(2,1)} %bitcast.1), calls=%async_computation | async-start | bytes 1048576 | tf_op jit(solution)/shard_map/all_to_all | solution.py:312
  19.6 3.4 %collective-permute-start = (bf16[128,1024]{1,0:T(8,128)(2,1)S(1)}, bf16[128,1024]{1,0:T(8,128)(2,1)S(1)}, u32[]{:S(2)}, u32[]{:S(2)}) collective-permute-start(bf16[128,1024]{1,0:T(8,128)(2,1)S(1)} %get-tuple-element.14), channel_id=1, source_target_pairs={{0,1},{1,0},{2,3},{3,2},{4,5},{5,4},{6,7},{7,6},{8,9},{9,8},{10,11... | collective-permute-start | bytes 786440 | tf_op jit(solution)/shard_map/ppermute | solution.py:302
  23.2 13.2 %collective-permute-start.2 = (bf16[64,1024]{1,0:T(8,128)(2,1)S(1)}, bf16[64,1024]{1,0:T(8,128)(2,1)S(1)}, u32[]{:S(2)}, u32[]{:S(2)}) collective-permute-start(bf16[64,1024]{1,0:T(8,128)(2,1)S(1)} %shard_map.38.refs_0_), channel_id=1, source_target_pairs={{0,2},{1,3},{2,0},{3,1},{4,6},{5,7},{6,4},{7,5},{8,10},{9,11},{10,... | collective-permute-start | bytes 393224 | tf_op jit(solution)/shard_map/ppermute | solution.py:302
  26.7 11.4 %collective-permute-start.1 = (bf16[64,1024]{1,0:T(8,128)(2,1)S(1)}, bf16[64,1024]{1,0:T(8,128)(2,1)S(1)}, u32[]{:S(2)}, u32[]{:S(2)}) collective-permute-start(bf16[64,1024]{1,0:T(8,128)(2,1)S(1)} %get-tuple-element.15), channel_id=1, source_target_pairs={{1,2},{3,4},{5,6},{7,8},{9,10},{11,12},{13,14},{15,16},{17,18},{19... | collective-permute-start | bytes 393224 | tf_op jit(solution)/shard_map/ppermute | solution.py:316
  36.6 21.7 %copy-start = (bf16[256,512]{1,0:T(8,128)(2,1)S(1)}, bf16[256,512]{1,0:T(8,128)(2,1)}, u32[]{:S(2)}) copy-start(bf16[256,512]{1,0:T(8,128)(2,1)} %refs_1_.3) | copy-start | bytes 786436
  40.1 6.1 %collective-permute-start.3 = (bf16[160,1024]{1,0:T(8,128)(2,1)S(1)}, bf16[160,1024]{1,0:T(8,128)(2,1)S(1)}, u32[]{:S(2)}, u32[]{:S(2)}) collective-permute-start(bf16[160,1024]{1,0:T(8,128)(2,1)S(1)} %shard_map.40.refs_0_.refs_6_), channel_id=1, source_target_pairs={{0,1},{1,0},{2,3},{3,2},{4,5},{5,4},{6,7},{7,6},{8,9},{9,8},{10,11... | collective-permute-start | bytes 983048 | tf_op jit(solution)/shard_map/ppermute | solution.py:302
  42.0 11.5 %collective-permute-start.4 = (bf16[64,1024]{1,0:T(8,128)(2,1)S(1)}, bf16[64,1024]{1,0:T(8,128)(2,1)S(1)}, u32[]{:S(2)}, u32[]{:S(2)}) collective-permute-start(bf16[64,1024]{1,0:T(8,128)(2,1)S(1)} %shard_map.39.refs_2_.refs_0_), channel_id=1, source_target_pairs={{0,4},{1,5},{2,6},{3,7},{4,0},{5,1},{6,2},{7,3},{8,12},{9,13},{10,... | collective-permute-start | bytes 393224 | tf_op jit(solution)/shard_map/ppermute | solution.py:302
  46.2 9.5 %collective-permute-start.5 = (bf16[64,1024]{1,0:T(8,128)(2,1)S(1)}, bf16[64,1024]{1,0:T(8,128)(2,1)S(1)}, u32[]{:S(2)}, u32[]{:S(2)}) collective-permute-start(bf16[64,1024]{1,0:T(8,128)(2,1)S(1)} %shard_map.41.refs_2_.refs_0_), channel_id=1, source_target_pairs={{0,128},{1,129},{2,130},{3,131},{4,132},{5,133},{6,134},{7,135},{8... | collective-permute-start | bytes 393224 | tf_op jit(solution)/shard_map/ppermute | solution.py:302
  53.7 9.2 %collective-permute-start.6 = (bf16[64,1024]{1,0:T(8,128)(2,1)S(1)}, bf16[64,1024]{1,0:T(8,128)(2,1)S(1)}, u32[]{:S(2)}, u32[]{:S(2)}) collective-permute-start(bf16[64,1024]{1,0:T(8,128)(2,1)S(1)} %shard_map.42.refs_2_), channel_id=1, source_target_pairs={{0,12},{1,13},{2,14},{3,15},{4,8},{5,9},{6,10},{7,11},{8,4},{9,5},... | collective-permute-start | bytes 393224 | tf_op jit(solution)/shard_map/ppermute | solution.py:302
  55.9 8.1 %collective-permute-start.7 = (bf16[64,1024]{1,0:T(8,128)(2,1)S(1)}, bf16[64,1024]{1,0:T(8,128)(2,1)S(1)}, u32[]{:S(2)}, u32[]{:S(2)}) collective-permute-start(bf16[64,1024]{1,0:T(8,128)(2,1)S(1)} %shard_map.43.refs_10_), channel_id=1, source_target_pairs={{0,384},{1,385},{2,386},{3,387},{4,388},{5,389},{6,390},{7,391},{8... | collective-permute-start | bytes 393224 | tf_op jit(solution)/shard_map/ppermute | solution.py:302

commit v8 on v5

--- a/solution.py
+++ b/solution.py
@@ -19,14 +19,11 @@
     route = []
     for index in range(count):
         if bit == 3:
-            z = index >> 1 & 7
-            route.append(index & ~14 | FAR8[z] << 1)
+            route.append(index & ~14 | FAR8[index >> 1 & 7] << 1)
         elif bit == 6:
-            y = index >> 4 & 7
-            route.append(index & ~112 | FAR8[y] << 4)
+            route.append(index & ~112 | FAR8[index >> 4 & 7] << 4)
         elif bit == 8:
-            x = index >> 7 & 3
-            route.append(index & ~384 | FAR4[x] << 7)
+            route.append(index & ~384 | FAR4[index >> 7 & 3] << 7)
         else:
             route.append(index ^ 1 << bit)
     return route
@@ -39,7 +36,7 @@
 SMEM = pl.BlockSpec(memory_space=pltpu.SMEM)
 
 
-def call(kernel, outs, in_specs, *args, flops=0, scratch=(), limit=24, after=()):
+def call(kernel, outs, in_specs, *args, flops=0, scratch=(), limit=10, after=()):
     count = len(args)
 
     def body(*refs):
@@ -118,7 +115,7 @@
     other_ref[...] = kv_ref[pl.ds(low, BLOCK), :]
 
 
-def unpack_kernel(place, in_ref, own_6_ref, own_7_ref, wide):
+def unpack_kernel(place, in_ref, sib_6_ref, own_7_ref, wide):
     members, rows, _ = in_ref.shape
     half = members // 2
     wide[...] = in_ref[...].reshape(members * rows, 128).astype(jnp.float32)
@@ -128,8 +125,8 @@
         parts = [
             wide[pl.ds(tile * 4 + row, members, stride=rows), :] for row in range(4)
         ]
-        own = [jnp.where(upper == 1, part[half:], part[:half]) for part in parts]
-        own_6_ref[:, lanes] = jnp.concatenate(own, axis=0).astype(jnp.bfloat16)
+        sib = [jnp.where(upper == 1, part[:half], part[half:]) for part in parts]
+        sib_6_ref[:, lanes] = jnp.concatenate(sib, axis=0).astype(jnp.bfloat16)
         pairs = [(parts[0] + parts[1]) * 0.5, (parts[2] + parts[3]) * 0.5]
         own_7_ref[:, lanes] = jnp.concatenate(pairs, axis=0).astype(jnp.bfloat16)
 
@@ -174,7 +171,8 @@
 
 
 def local_kernel(
-    count, place, x_ref, w_hbm, kv_ref, near_ref, other_ref, q_ref, num_ref, tot_ref, pad, l1, w_ref, sem
+    count, place, x_ref, w_hbm, kv_ref, near_ref, other_ref, sib_3_ref, sib_4_ref,
+    sib_5_ref, q_ref, num_ref, tot_ref, pad, l1, w_ref, sem
 ):
     rows, model = x_ref.shape
     blocks = rows // BLOCK
@@ -215,6 +213,12 @@
             num, tot = attend_pair(q_ref[here, kl], keys, values, ones)
             num_ref[here, kl] = num
             tot_ref[here, kl] = tot
+    far = far_blocks((near_ref, sib_3_ref, sib_4_ref, sib_5_ref))
+    for lanes in range(0, model, 128):
+        kl = slice(lanes, lanes + 128)
+        num, tot = far_sums(far, q_ref[:, kl], lanes, model)
+        num_ref[:, kl] += num
+        tot_ref[:, kl] += tot
 
 
 def far_blocks(refs):
@@ -240,14 +244,18 @@
         tot_ref[:, at] = tot_in[:, at] + tot
 
 
-def final_kernel(q_ref, num_in, tot_in, w_ref, *refs):
-    out_ref, att = refs[-2:]
+def final_kernel(
+    q_ref, num_in, tot_in, sib_ref, w_hbm, out_ref, att, w_ref, sem
+):
+    copy = pltpu.make_async_copy(w_hbm, w_ref, sem)
+    copy.start()
     model = q_ref.shape[1]
-    far = far_blocks(refs[:-2])
+    far = sib_ref[...]
     for lanes in range(0, model, 128):
         at = slice(lanes, lanes + 128)
         num, tot = far_sums(far, q_ref[:, at], lanes, model)
         att[:, at] = ((num_in[:, at] + num) / (tot_in[:, at] + tot)).astype(jnp.bfloat16)
+    copy.wait()
     out_ref[...] = jnp.dot(att[...], w_ref[...], preferred_element_type=jnp.float32).astype(
         jnp.bfloat16
     )
@@ -260,7 +268,8 @@
     place = index.astype(jnp.int32).reshape(1)
     bf16 = lambda *shape: jax.ShapeDtypeStruct(shape, jnp.bfloat16)
     f32 = lambda *shape: jax.ShapeDtypeStruct(shape, jnp.float32)
-    anywhere = pl.BlockSpec(memory_space=pl.ANY)
+    in_hbm = pl.BlockSpec(memory_space=pl.ANY)
+    stay = lambda array: pltpu.with_memory_space_constraint(array, pltpu.HBM)
     steps = 2
     width = 2 * model // steps
     members = 32
@@ -272,8 +281,8 @@
             bf16(rows, 2 * model), bf16(2 * BLOCK, 2 * model), block,
             bf16(BLOCK // 2, 2 * model), bf16(members * packed, 128),
         ),
-        [SMEM, anywhere, anywhere],
-        place, tokens, w_qkv,
+        [SMEM, in_hbm, in_hbm],
+        place, stay(tokens), stay(w_qkv),
         flops=4 * rows * model * model,
         scratch=(
             pltpu.VMEM((rows, model), jnp.bfloat16),
@@ -281,7 +290,6 @@
             pltpu.VMEM((2 * model // 128, rows, 128), jnp.float32),
             pltpu.SemaphoreType.DMA((steps + 1,)),
         ),
-        limit=56,
     )
     swap = [(i, i + 1) for i in range(1, count - 1, 2)]
     swap += [(j, i) for i, j in swap]
@@ -291,24 +299,13 @@
     def pool(own, got, *after):
         return call(pool_kernel, block, vmem(2), own, got, after=after)
 
-    def far(num, tot, *part, after=()):
-        return call(
-            far_kernel,
-            (f32(rows, model), f32(rows, model)),
-            vmem(3 + len(part)),
-            q, num, tot, *part,
-            flops=10**9,
-            after=after,
-        )
-
     teams = [list(range(i, i + members)) for i in range(0, count, members)]
     spread = lax.all_to_all(level_6, AXES, 0, 0, axis_index_groups=teams, tiled=True)
     near_sib = exchange(near, 0)
-    other_halo = lax.ppermute(other, AXES, swap)
-
     own_3 = call(pool_near_kernel, block, vmem(2), level_3, near_sib)
     sib_3 = exchange(own_3, 1)
-    own_6, own_7 = call(
+    other_halo = lax.ppermute(other, AXES, swap)
+    sib_6, own_7 = call(
         unpack_kernel, (block, block), [SMEM, *vmem(1)],
         place, spread.reshape(members, packed, 128),
         scratch=(pltpu.VMEM((members * packed, 128), jnp.float32),),
@@ -319,18 +316,15 @@
     sib_4 = exchange(own_4, 2)
     own_8 = call(pool_halves_kernel, block, vmem(2), own_7, sib_7, after=(own_4,))
     sib_8 = exchange(own_8, 6)
-    own_6, _ = lax.optimization_barrier((own_6, own_8))
-    sib_6 = exchange(own_6, 4)
     own_5 = pool(own_4, sib_4, own_8)
     sib_5 = exchange(own_5, 3)
     own_9 = pool(own_8, sib_8, own_5)
     sib_9 = exchange(own_9, 7)
-    own_10 = pool(own_9, sib_9, sib_6)
     q, num, tot = call(
         functools.partial(local_kernel, count),
         (bf16(rows, model), f32(rows, model), f32(rows, model)),
-        [SMEM, *vmem(1), anywhere, *vmem(3)],
-        place, tokens, w_qkv, kv, near_sib, other_halo,
+        [SMEM, *vmem(1), in_hbm, *vmem(6)],
+        place, tokens, stay(w_qkv), kv, near_sib, other_halo, sib_3, sib_4, sib_5,
         flops=10**9,
         scratch=(
             pltpu.VMEM((rows + 2 * BLOCK, 2 * model), jnp.bfloat16),
@@ -338,18 +332,29 @@
             pltpu.VMEM((model, model), jnp.bfloat16),
             pltpu.SemaphoreType.DMA(()),
         ),
+        after=(own_9,),
+    )
+    own_10 = pool(own_9, sib_9, q)
+    sib_10 = exchange(own_10, 8)
+    num, tot = call(
+        far_kernel,
+        (f32(rows, model), f32(rows, model)),
+        vmem(7),
+        q, num, tot, sib_6, sib_7, sib_8, sib_9,
+        flops=10**9,
         after=(own_10,),
     )
-    num, tot = far(num, tot, near_sib, sib_3, sib_4, sib_6, after=(own_10,))
-    sib_10 = exchange(own_10, 8)
-    num, tot = far(num, tot, sib_5, sib_7, sib_8, sib_9, after=(own_10,))
     return call(
         final_kernel,
         bf16(rows, model),
-        vmem(5),
-        q, num, tot, w_out, sib_10,
+        [*vmem(4), in_hbm],
+        q, num, tot, sib_10, stay(w_out),
         flops=10**9,
-        scratch=(pltpu.VMEM((rows, model), jnp.bfloat16),),
+        scratch=(
+            pltpu.VMEM((rows, model), jnp.bfloat16),
+            pltpu.VMEM((model, model), jnp.bfloat16),
+            pltpu.SemaphoreType.DMA(()),
+        ),
     )
 
 

time: 67.1 us -> 67 us (level)
  waiting for transfers between devices: 7.27 us -> 10.9 us
  starting transfers between devices: 49.2 us -> 45.8 us
  local copies, waits for them, and re-layouts: 0.86 us -> 0.01 us
  Pallas kernels: 8.92 us -> 9.61 us
    ppermute x9 -> x8, starting transfers between devices: 35.7 us -> 32.3 us  [exchange(): return lax.ppermute(own, AXES, list(enumerate(partners(bit, count))))]
    ppermute x9 -> x8, waiting for transfers between devices: 6.44 us -> 9.2 us  [exchange(): return lax.ppermute(own, AXES, list(enumerate(partners(bit, count))))]
    all_to_all x1, waiting for transfers between devices: 0.83 us -> 1.69 us  [per_device(): lax.all_to_all(level_6, AXES, 0, 0, axis_index_groups=teams, tiled=True)]
    unnamed x10 -> x2, local copies, waits for them, and re-layouts: 0.86 us -> 0.01 us
    pallas_call x12 -> x11, Pallas kernels: 8.92 us -> 9.61 us  [call(): pl.pallas_call(body, out_shape=outs, in_specs=list(in_specs) + [pl.BlockS...]
  transfers between devices with their start and end apart: 11 -> 10, of which waited for: 4 -> 5; matrix products, arithmetic and copies ran while one was open for 0% -> 0% of each run, Pallas kernels for 6% -> 7%
where the time goes in v8:
time: 67 us; the launch traced here: 66.5 us
  starting transfers between devices  45.8 us (68%)
  waiting for transfers between devices  10.9 us (16%)
  Pallas kernels  9.61 us (14%)
    ppermute x8, starting transfers between devices, exchange(): return lax.ppermute(own, AXES, list(enumerate(partners(bit, count))))  32.3 us
    all_to_all x1, starting transfers between devices, per_device(): lax.all_to_all(level_6, AXES, 0, 0, axis_index_groups=teams, tiled=True)  11 us
    pallas_call x11, Pallas kernels, call(): pl.pallas_call(body, out_shape=outs, in_specs=list(in_specs) + [pl.BlockS...  9.61 us
    ppermute x8, waiting for transfers between devices, exchange(): return lax.ppermute(own, AXES, list(enumerate(partners(bit, count))))  9.2 us
    ppermute x1, starting transfers between devices, per_device(): other_halo = lax.ppermute(other, AXES, swap)  2.44 us
    all_to_all x1, waiting for transfers between devices, per_device(): lax.all_to_all(level_6, AXES, 0, 0, axis_index_groups=teams, tiled=True)  1.69 us
  transfers between devices with their start and end apart: 10, of which 5 were waited for; matrix products, arithmetic and copies ran while one was open for 0% of the time, Pallas kernels for 7%

profile of v8, /device:TPU:72, one launch (start us, length us, event | category | flops | bytes accessed | tf_op | source)
XLA Modules:
  0.0 66.5 jit_solution(17774624492923916341)
XLA Ops:
  0.0 2.9 %shard_map.37 = (bf16[256,1024]{1,0:T(8,128)(2,1)S(1)}, bf16[128,1024]{1,0:T(8,128)(2,1)S(1)}, bf16[64,1024]{1,0:T(8,128)(2,1)S(1)}, bf16[32,1024]{1,0:T(8,128)(2,1)S(1)}, bf16[1024,128]{1,0:T(8,128)(2,1)}) custom-call(s32[1]{0:T(128)} %bitcast.refs_0_, bf16[256,512]{1,0:T(8,128)(2,1)} %refs_1_.3, bf16[512,1536]{1,0:T(8,128)(2,1)} %refs_2_.3), custom_call_target="tpu_custom_call" | custom-call | flops 268435456 | bytes 1048576 | tf_op jit(solution)/shard_map/pallas_call | solution.py:45
  2.9 11.0 %all-to-all-start = ((bf16[32,32,128]{2,1,0:T(8,128)(2,1)}), bf16[32,32,128]{2,1,0:T(8,128)(2,1)S(1)}, u32[]{:S(2)}, u32[]{:S(2)}) async-start(bf16[32,32,128]{2,1,0:T(8,128)(2,1)} %bitcast.1), calls=%async_computation | async-start | bytes 524288 | tf_op jit(solution)/shard_map/all_to_all | solution.py:303
  13.9 2.2 %collective-permute-start = (bf16[128,1024]{1,0:T(8,128)(2,1)S(1)}, bf16[128,1024]{1,0:T(8,128)(2,1)S(1)}, u32[]{:S(2)}, u32[]{:S(2)}) collective-permute-start(bf16[128,1024]{1,0:T(8,128)(2,1)S(1)} %get-tuple-element.18), channel_id=1, source_target_pairs={{0,1},{1,0},{2,3},{3,2},{4,5},{5,4},{6,7},{7,6},{8,9},{9,8},{10,11... | collective-permute-start | bytes 786440 | tf_op jit(solution)/shard_map/ppermute | solution.py:297
  16.1 2.4 %collective-permute-start.1 = (bf16[64,1024]{1,0:T(8,128)(2,1)S(1)}, bf16[64,1024]{1,0:T(8,128)(2,1)S(1)}, u32[]{:S(2)}, u32[]{:S(2)}) collective-permute-start(bf16[64,1024]{1,0:T(8,128)(2,1)S(1)} %get-tuple-element.19), channel_id=1, source_target_pairs={{1,2},{3,4},{5,6},{7,8},{9,10},{11,12},{13,14},{15,16},{17,18},{19... | collective-permute-start | bytes 393224 | tf_op jit(solution)/shard_map/ppermute | solution.py:307
  18.7 4.6 %collective-permute-start.2 = (bf16[64,1024]{1,0:T(8,128)(2,1)S(1)}, bf16[64,1024]{1,0:T(8,128)(2,1)S(1)}, u32[]{:S(2)}, u32[]{:S(2)}) collective-permute-start(bf16[64,1024]{1,0:T(8,128)(2,1)S(1)} %shard_map.38.refs_2_.refs_0_), channel_id=1, source_target_pairs={{0,2},{1,3},{2,0},{3,1},{4,6},{5,7},{6,4},{7,5},{8,10},{9,11},{10,... | collective-permute-start | bytes 393224 | tf_op jit(solution)/shard_map/ppermute | solution.py:297
  23.3 1.7 %all-to-all-done.refs_1_ = bf16[32,32,128]{2,1,0:T(8,128)(2,1)S(1)} async-done(((bf16[32,32,128]{2,1,0:T(8,128)(2,1)}), bf16[32,32,128]{2,1,0:T(8,128)(2,1)S(1)}, u32[]{:S(2)}, u32[]{:S(2)}) %all-to-all-start) | async-done | bytes 262176 | tf_op jit(solution)/shard_map/all_to_all | solution.py:303
  25.0 0.3 shard_map.39
  25.4 4.5 %collective-permute-start.4 = (bf16[64,1024]{1,0:T(8,128)(2,1)S(1)}, bf16[64,1024]{1,0:T(8,128)(2,1)S(1)}, u32[]{:S(2)}, u32[]{:S(2)}) collective-permute-start(bf16[64,1024]{1,0:T(8,128)(2,1)S(1)} %get-tuple-element.22.refs_2_.refs_0_), channel_id=1, source_target_pairs={{0,32},{1,33},{2,34},{3,35},{4,36},{5,37},{6,38},{7,39},{8,40},{9,... | collective-permute-start | bytes 393224 | tf_op jit(solution)/shard_map/ppermute | solution.py:297
  29.9 0.2 shard_map.40.refs_2_.refs_0_
  30.1 2.4 %collective-permute-start.3 = (bf16[64,1024]{1,0:T(8,128)(2,1)S(1)}, bf16[64,1024]{1,0:T(8,128)(2,1)S(1)}, u32[]{:S(2)}, u32[]{:S(2)}) collective-permute-start(bf16[64,1024]{1,0:T(8,128)(2,1)S(1)} %shard_map.40.refs_2_.refs_0_), channel_id=1, source_target_pairs={{0,4},{1,5},{2,6},{3,7},{4,0},{5,1},{6,2},{7,3},{8,12},{9,13},{10,... | collective-permute-start | bytes 393224 | tf_op jit(solution)/shard_map/ppermute | solution.py:297
  32.4 2.5 %collective-permute-done.4.refs_1_.refs_4_ = bf16[64,1024]{1,0:T(8,128)(2,1)S(1)} collective-permute-done((bf16[64,1024]{1,0:T(8,128)(2,1)S(1)}, bf16[64,1024]{1,0:T(8,128)(2,1)S(1)}, u32[]{:S(2)}, u32[]{:S(2)}) %collective-permute-start.4) | collective-permute-done | bytes 131104 | tf_op jit(solution)/shard_map/ppermute | solution.py:297
  35.0 6.1 %collective-permute-start.6 = (bf16[64,1024]{1,0:T(8,128)(2,1)S(1)}, bf16[64,1024]{1,0:T(8,128)(2,1)S(1)}, u32[]{:S(2)}, u32[]{:S(2)}) collective-permute-start(bf16[64,1024]{1,0:T(8,128)(2,1)S(1)} %shard_map.41.refs_2_.refs_0_), channel_id=1, source_target_pairs={{0,96},{1,97},{2,98},{3,99},{4,100},{5,101},{6,102},{7,103},{8,104... | collective-permute-start | bytes 393224 | tf_op jit(solution)/shard_map/ppermute | solution.py:297
  41.1 0.2 shard_map.42.refs_2_
  41.2 4.5 %collective-permute-start.5 = (bf16[64,1024]{1,0:T(8,128)(2,1)S(1)}, bf16[64,1024]{1,0:T(8,128)(2,1)S(1)}, u32[]{:S(2)}, u32[]{:S(2)}) collective-permute-start(bf16[64,1024]{1,0:T(8,128)(2,1)S(1)} %shard_map.42.refs_2_), channel_id=1, source_target_pairs={{0,12},{1,13},{2,14},{3,15},{4,8},{5,9},{6,10},{7,11},{8,4},{9,5},... | collective-permute-start | bytes 393224 | tf_op jit(solution)/shard_map/ppermute | solution.py:297
  45.8 0.3 collective-permute-done.6.refs_1_.refs_5_
  46.0 0.2 shard_map.43.refs_9_.refs_0_
  46.2 3.4 %collective-permute-start.7 = (bf16[64,1024]{1,0:T(8,128)(2,1)S(1)}, bf16[64,1024]{1,0:T(8,128)(2,1)S(1)}, u32[]{:S(2)}, u32[]{:S(2)}) collective-permute-start(bf16[64,1024]{1,0:T(8,128)(2,1)S(1)} %shard_map.43.refs_9_.refs_0_), channel_id=1, source_target_pairs={{0,128},{1,129},{2,130},{3,131},{4,132},{5,133},{6,134},{7,135},{8... | collective-permute-start | bytes 393224 | tf_op jit(solution)/shard_map/ppermute | solution.py:297
  49.6 3.5 %collective-permute-done.5.refs_8_ = bf16[64,1024]{1,0:T(8,128)(2,1)S(1)} collective-permute-done((bf16[64,1024]{1,0:T(8,128)(2,1)S(1)}, bf16[64,1024]{1,0:T(8,128)(2,1)S(1)}, u32[]{:S(2)}, u32[]{:S(2)}) %collective-permute-start.5) | collective-permute-done | bytes 131104 | tf_op jit(solution)/shard_map/ppermute | solution.py:297
  53.1 2.7 %shard_map.44 = (bf16[256,512]{1,0:T(8,128)(2,1)S(1)}, f32[256,512]{1,0:T(8,128)S(1)}, f32[256,512]{1,0:T(8,128)S(1)}) custom-call(s32[1]{0:T(128)} %bitcast.refs_0_, bf16[256,512]{1,0:T(8,128)(2,1)S(1)} %copy-done, bf16[512,1536]{1,0:T(8,128)(2,1)} %refs_2_.3, bf16[256,1024]{1,0:T(8,128)(2,1)S(1)} %get-tuple-element.17.refs_3_, ...), custom_call_target="tpu_custom_call" | custom-call | flops 1000000000 | bytes 1048576 | tf_op jit(solution)/shard_map/pallas_call | solution.py:45
  55.8 0.2 shard_map.45.refs_7_
  56.0 4.7 %collective-permute-start.8 = (bf16[64,1024]{1,0:T(8,128)(2,1)S(1)}, bf16[64,1024]{1,0:T(8,128)(2,1)S(1)}, u32[]{:S(2)}, u32[]{:S(2)}) collective-permute-start(bf16[64,1024]{1,0:T(8,128)(2,1)S(1)} %shard_map.45.refs_7_), channel_id=1, source_target_pairs={{0,384},{1,385},{2,386},{3,387},{4,388},{5,389},{6,390},{7,391},{8... | collective-permute-start | bytes 393224 | tf_op jit(solution)/shard_map/ppermute | solution.py:297
  60.6 0.8 %shard_map.46 = (f32[256,512]{1,0:T(8,128)S(1)}, f32[256,512]{1,0:T(8,128)S(1)}) custom-call(bf16[256,512]{1,0:T(8,128)(2,1)S(1)} %get-tuple-element.23.refs_2_.refs_0_, f32[256,512]{1,0:T(8,128)S(1)} %get-tuple-element.24.refs_1_, f32[256,512]{1,0:T(8,128)S(1)} %get-tuple-element.25.refs_2_, bf16[64,1024]{1,0:T(8,128)(2,1)S(1)} %get-tuple-element.26.refs_3_, ...), custom_call_target="tpu_custom_call" | custom-call | flops 1000000000 | bytes 1048576 | tf_op jit(solution)/shard_map/pallas_call | solution.py:45
  61.5 2.9 %collective-permute-done.8.refs_3_ = bf16[64,1024]{1,0:T(8,128)(2,1)S(1)} collective-permute-done((bf16[64,1024]{1,0:T(8,128)(2,1)S(1)}, bf16[64,1024]{1,0:T(8,128)(2,1)S(1)}, u32[]{:S(2)}, u32[]{:S(2)}) %collective-permute-start.8) | collective-permute-done | bytes 131104 | tf_op jit(solution)/shard_map/ppermute | solution.py:297
  64.4 2.1 %shard_map.47 = bf16[256,512]{1,0:T(8,128)(2,1)} custom-call(bf16[256,512]{1,0:T(8,128)(2,1)S(1)} %get-tuple-element.23.refs_2_.refs_0_, f32[256,512]{1,0:T(8,128)S(1)} %get-tuple-element.27.refs_1_, f32[256,512]{1,0:T(8,128)S(1)} %get-tuple-element.28.refs_2_, bf16[64,1024]{1,0:T(8,128)(2,1)S(1)} %collective-permute-done.8.refs_3_, bf16[512,512]{1,0:T(8,128)(2,1)} %refs_4_.1), custom_call_target="tpu_custom_call" | custom-call | flops 1000000000 | bytes 1048576 | tf_op jit(solution)/shard_map/pallas_call | solution.py:45
  (9 shorter events, 0.2 us)
Async XLA Ops:
  2.9 22.1 %all-to-all-start = ((bf16[32,32,128]{2,1,0:T(8,128)(2,1)}), bf16[32,32,128]{2,1,0:T(8,128)(2,1)S(1)}, u32[]{:S(2)}, u32[]{:S(2)}) async-start(bf16[32,32,128]{2,1,0:T(8,128)(2,1)} %bitcast.1), calls=%async_computation | async-start | bytes 524288 | tf_op jit(solution)/shard_map/all_to_all | solution.py:303
  13.9 39.2 %copy-start = (bf16[256,512]{1,0:T(8,128)(2,1)S(1)}, bf16[256,512]{1,0:T(8,128)(2,1)}, u32[]{:S(2)}) copy-start(bf16[256,512]{1,0:T(8,128)(2,1)} %refs_1_.3) | copy-start | bytes 786436
  13.9 4.6 %collective-permute-start = (bf16[128,1024]{1,0:T(8,128)(2,1)S(1)}, bf16[128,1024]{1,0:T(8,128)(2,1)S(1)}, u32[]{:S(2)}, u32[]{:S(2)}) collective-permute-start(bf16[128,1024]{1,0:T(8,128)(2,1)S(1)} %get-tuple-element.18), channel_id=1, source_target_pairs={{0,1},{1,0},{2,3},{3,2},{4,5},{5,4},{6,7},{7,6},{8,9},{9,8},{10,11... | collective-permute-start | bytes 786440 | tf_op jit(solution)/shard_map/ppermute | solution.py:297
  16.1 7.2 %collective-permute-start.1 = (bf16[64,1024]{1,0:T(8,128)(2,1)S(1)}, bf16[64,1024]{1,0:T(8,128)(2,1)S(1)}, u32[]{:S(2)}, u32[]{:S(2)}) collective-permute-start(bf16[64,1024]{1,0:T(8,128)(2,1)S(1)} %get-tuple-element.19), channel_id=1, source_target_pairs={{1,2},{3,4},{5,6},{7,8},{9,10},{11,12},{13,14},{15,16},{17,18},{19... | collective-permute-start | bytes 393224 | tf_op jit(solution)/shard_map/ppermute | solution.py:307
  18.7 11.1 %collective-permute-start.2 = (bf16[64,1024]{1,0:T(8,128)(2,1)S(1)}, bf16[64,1024]{1,0:T(8,128)(2,1)S(1)}, u32[]{:S(2)}, u32[]{:S(2)}) collective-permute-start(bf16[64,1024]{1,0:T(8,128)(2,1)S(1)} %shard_map.38.refs_2_.refs_0_), channel_id=1, source_target_pairs={{0,2},{1,3},{2,0},{3,1},{4,6},{5,7},{6,4},{7,5},{8,10},{9,11},{10,... | collective-permute-start | bytes 393224 | tf_op jit(solution)/shard_map/ppermute | solution.py:297
  25.4 9.6 %collective-permute-start.4 = (bf16[64,1024]{1,0:T(8,128)(2,1)S(1)}, bf16[64,1024]{1,0:T(8,128)(2,1)S(1)}, u32[]{:S(2)}, u32[]{:S(2)}) collective-permute-start(bf16[64,1024]{1,0:T(8,128)(2,1)S(1)} %get-tuple-element.22.refs_2_.refs_0_), channel_id=1, source_target_pairs={{0,32},{1,33},{2,34},{3,35},{4,36},{5,37},{6,38},{7,39},{8,40},{9,... | collective-permute-start | bytes 393224 | tf_op jit(solution)/shard_map/ppermute | solution.py:297
  30.1 11.0 %collective-permute-start.3 = (bf16[64,1024]{1,0:T(8,128)(2,1)S(1)}, bf16[64,1024]{1,0:T(8,128)(2,1)S(1)}, u32[]{:S(2)}, u32[]{:S(2)}) collective-permute-start(bf16[64,1024]{1,0:T(8,128)(2,1)S(1)} %shard_map.40.refs_2_.refs_0_), channel_id=1, source_target_pairs={{0,4},{1,5},{2,6},{3,7},{4,0},{5,1},{6,2},{7,3},{8,12},{9,13},{10,... | collective-permute-start | bytes 393224 | tf_op jit(solution)/shard_map/ppermute | solution.py:297
  35.0 11.0 %collective-permute-start.6 = (bf16[64,1024]{1,0:T(8,128)(2,1)S(1)}, bf16[64,1024]{1,0:T(8,128)(2,1)S(1)}, u32[]{:S(2)}, u32[]{:S(2)}) collective-permute-start(bf16[64,1024]{1,0:T(8,128)(2,1)S(1)} %shard_map.41.refs_2_.refs_0_), channel_id=1, source_target_pairs={{0,96},{1,97},{2,98},{3,99},{4,100},{5,101},{6,102},{7,103},{8,104... | collective-permute-start | bytes 393224 | tf_op jit(solution)/shard_map/ppermute | solution.py:297
  41.2 11.9 %collective-permute-start.5 = (bf16[64,1024]{1,0:T(8,128)(2,1)S(1)}, bf16[64,1024]{1,0:T(8,128)(2,1)S(1)}, u32[]{:S(2)}, u32[]{:S(2)}) collective-permute-start(bf16[64,1024]{1,0:T(8,128)(2,1)S(1)} %shard_map.42.refs_2_), channel_id=1, source_target_pairs={{0,12},{1,13},{2,14},{3,15},{4,8},{5,9},{6,10},{7,11},{8,4},{9,5},... | collective-permute-start | bytes 393224 | tf_op jit(solution)/shard_map/ppermute | solution.py:297
  46.2 9.6 %collective-permute-start.7 = (bf16[64,1024]{1,0:T(8,128)(2,1)S(1)}, bf16[64,1024]{1,0:T(8,128)(2,1)S(1)}, u32[]{:S(2)}, u32[]{:S(2)}) collective-permute-start(bf16[64,1024]{1,0:T(8,128)(2,1)S(1)} %shard_map.43.refs_9_.refs_0_), channel_id=1, source_target_pairs={{0,128},{1,129},{2,130},{3,131},{4,132},{5,133},{6,134},{7,135},{8... | collective-permute-start | bytes 393224 | tf_op jit(solution)/shard_map/ppermute | solution.py:297
  56.0 8.5 %collective-permute-start.8 = (bf16[64,1024]{1,0:T(8,128)(2,1)S(1)}, bf16[64,1024]{1,0:T(8,128)(2,1)S(1)}, u32[]{:S(2)}, u32[]{:S(2)}) collective-permute-start(bf16[64,1024]{1,0:T(8,128)(2,1)S(1)} %shard_map.45.refs_7_), channel_id=1, source_target_pairs={{0,384},{1,385},{2,386},{3,387},{4,388},{5,389},{6,390},{7,391},{8... | collective-permute-start | bytes 393224 | tf_op jit(solution)/shard_map/ppermute | solution.py:297

commit v9 on v7

--- a/solution.py
+++ b/solution.py
@@ -20,6 +20,8 @@
     for index in range(count):
         if bit == 3:
             route.append(index & ~14 | FAR8[index >> 1 & 7] << 1)
+        elif bit == 6:
+            route.append(index & ~112 | FAR8[index >> 4 & 7] << 4)
         elif bit == 8:
             route.append(index & ~384 | FAR4[index >> 7 & 3] << 7)
         else:
@@ -116,7 +118,7 @@
 def unpack_kernel(place, in_ref, out_ref, wide):
     members, rows, _ = in_ref.shape
     wide[...] = in_ref[...].reshape(members * rows, 128).astype(jnp.float32)
-    y = (place[0] >> 4) & 7
+    y = (place[0] >> 4) & 3
 
     def mean(one, two):
         return ((one + two) * 0.5).astype(jnp.bfloat16).astype(jnp.float32)
@@ -137,21 +139,29 @@
         parts = (
             level_6((y ^ 1) * 8, 8)
             + level_7(((y >> 1) ^ 1) * 16, 16)
-            + [mean(*level_7(((y >> 2) ^ 1) * 32, 32))]
             + [mean(*level_7(0, members))]
         )
         out_ref[:, lanes] = jnp.concatenate(parts, axis=0).astype(jnp.bfloat16)
 
 
-def own_9_kernel(mine_ref, sib_ref, out_ref):
-    at = 3 * BLOCK // 2
-    both = mine_ref[at:, :].astype(jnp.float32) + sib_ref[at:, :].astype(jnp.float32)
-    out_ref[...] = (both * 0.5).astype(jnp.bfloat16)
+def own_8_kernel(mine_ref, sib_ref, out_ref):
+    half = BLOCK // 2
+    out_ref[:half, :] = mine_ref[BLOCK:, :]
+    out_ref[half:, :] = sib_ref[BLOCK:, :]
 
 
 def pool_near_kernel(mine_ref, sib_ref, out_ref):
     out_ref[: BLOCK // 2, :] = mine_ref[...]
     out_ref[BLOCK // 2 :, :] = pooled(sib_ref[BLOCK:, :])
+
+
+def pool_halves_kernel(own_ref, sib_ref, out_ref):
+    half = BLOCK // 2
+    for num, ref in enumerate((own_ref, sib_ref)):
+        block = ref[...].astype(jnp.float32)
+        out_ref[num * half : (num + 1) * half, :] = (
+            (block[:half] + block[half:]) * 0.5
+        ).astype(jnp.bfloat16)
 
 
 def pool_kernel(*refs):
@@ -180,8 +190,8 @@
 
 
 def local_kernel(
-    count, place, x_ref, w_hbm, kv_ref, near_ref, other_ref, mine_ref, theirs_ref, sib_3_ref,
-    sib_4_ref, q_ref, num_ref, tot_ref, pad, l1, w_ref, sem
+    count, place, x_ref, w_hbm, kv_ref, near_ref, other_ref, sib_3_ref, sib_4_ref,
+    mine_ref, theirs_ref, sib_8_ref, q_ref, num_ref, tot_ref, pad, l1, w_ref, sem
 ):
     rows, model = x_ref.shape
     blocks = rows // BLOCK
@@ -222,13 +232,12 @@
             num, tot = attend_pair(q_ref[here, kl], keys, values, ones)
             num_ref[here, kl] = num
             tot_ref[here, kl] = tot
-    for refs in ((mine_ref, theirs_ref), (near_ref, sib_3_ref, sib_4_ref)):
-        far = far_blocks(refs)
-        for lanes in range(0, model, 128):
-            kl = slice(lanes, lanes + 128)
-            num, tot = far_sums(far, q_ref[:, kl], lanes, model)
-            num_ref[:, kl] += num
-            tot_ref[:, kl] += tot
+    far = far_blocks((near_ref, sib_3_ref, sib_4_ref, mine_ref, theirs_ref, sib_8_ref))
+    for lanes in range(0, model, 128):
+        kl = slice(lanes, lanes + 128)
+        num, tot = far_sums(far, q_ref[:, kl], lanes, model)
+        num_ref[:, kl] += num
+        tot_ref[:, kl] += tot
 
 
 def far_blocks(refs):
@@ -236,10 +245,8 @@
     for ref in refs:
         if ref.shape[0] == 2 * BLOCK:
             blocks.append(ref[BLOCK:, :])
-        elif ref.shape[0] > 2 * BLOCK:
-            blocks.append(ref[: 3 * BLOCK // 2, :])
         else:
-            blocks.append(ref[...])
+            blocks.append(ref[:BLOCK, :])
     return jnp.concatenate(blocks, axis=0)
 
 
@@ -250,12 +257,15 @@
 
 
 def final_kernel(
-    q_ref, num_in, tot_in, sib_5_ref, sib_9_ref, sib_10_ref, w_hbm, out_ref, att, w_ref, sem
+    place, q_ref, num_in, tot_in, sib_5_ref, sib_9_ref, pair_ref, w_hbm, out_ref, att, w_ref, sem
 ):
     copy = pltpu.make_async_copy(w_hbm, w_ref, sem)
     copy.start()
     model = q_ref.shape[1]
-    far = far_blocks((sib_5_ref, sib_9_ref, sib_10_ref))
+    start = pl.multiple_of((1 - (place[0] >> 8)) * BLOCK, BLOCK)
+    far = jnp.concatenate(
+        [sib_5_ref[...], sib_9_ref[...], pair_ref[pl.ds(start, BLOCK), :]], axis=0
+    )
     for lanes in range(0, model, 128):
         at = slice(lanes, lanes + 128)
         num, tot = far_sums(far, q_ref[:, at], lanes, model)
@@ -277,7 +287,7 @@
     stay = lambda array: pltpu.with_memory_space_constraint(array, pltpu.HBM)
     steps = 2
     width = 2 * model // steps
-    members = 64
+    members = 32
     packed = 4 * 2 * model // 128
     block = bf16(BLOCK, 2 * model)
     kv, near, other, level_3, level_6 = call(
@@ -305,8 +315,8 @@
         return call(pool_kernel, block, vmem(2), own, got, after=after)
 
     teams = [
-        [i for i in range(count) if i >> 7 == x and i & 1 == core]
-        for x in range(count >> 7)
+        [i for i in range(count) if i >> 6 == part and i & 1 == core]
+        for part in range(count >> 6)
         for core in range(2)
     ]
     spread = lax.all_to_all(level_6, AXES, 0, 0, axis_index_groups=teams, tiled=True)
@@ -315,25 +325,25 @@
     sib_3 = exchange(own_3, 1)
     other_halo = lax.ppermute(other, AXES, swap)
     own_4 = pool(own_3, sib_3)
-    sib_4 = exchange(own_4, 2)
     mine = call(
-        unpack_kernel, bf16(5 * BLOCK // 2, 2 * model), [SMEM, *vmem(1)],
+        unpack_kernel, bf16(3 * BLOCK // 2, 2 * model), [SMEM, *vmem(1)],
         place, spread.reshape(members, packed, 128),
         scratch=(pltpu.VMEM((members * packed, 128), jnp.float32),),
         after=(own_4, other_halo),
     )
     theirs = exchange(mine, 0)
-    own_9 = call(own_9_kernel, block, vmem(2), mine, theirs)
+    sib_4 = exchange(own_4, 2)
+    own_8 = call(own_8_kernel, block, vmem(2), mine, theirs)
+    sib_8 = exchange(own_8, 6)
+    own_5 = pool(own_4, sib_4, own_8)
+    sib_5 = exchange(own_5, 3)
+    own_9 = call(pool_halves_kernel, block, vmem(2), own_8, sib_8, after=(own_5,))
     sib_9 = exchange(own_9, 7)
-    own_5 = pool(own_4, sib_4, own_9)
-    sib_5 = exchange(own_5, 3)
-    own_10 = pool(own_9, sib_9, own_5)
-    sib_10 = exchange(own_10, 8)
     q, num, tot = call(
         functools.partial(local_kernel, count),
         (bf16(rows, model), f32(rows, model), f32(rows, model)),
-        [SMEM, *vmem(1), in_hbm, *vmem(7)],
-        place, tokens, stay(w_qkv), kv, near_sib, other_halo, mine, theirs, sib_3, sib_4,
+        [SMEM, *vmem(1), in_hbm, *vmem(8)],
+        place, tokens, stay(w_qkv), kv, near_sib, other_halo, sib_3, sib_4, mine, theirs, sib_8,
         flops=10**9,
         scratch=(
             pltpu.VMEM((rows + 2 * BLOCK, 2 * model), jnp.bfloat16),
@@ -341,13 +351,17 @@
             pltpu.VMEM((model, model), jnp.bfloat16),
             pltpu.SemaphoreType.DMA(()),
         ),
-        after=(own_10,),
-    )
+        after=(own_9,),
+    )
+    own_10 = pool(own_9, sib_9, q, sib_5)
+    to = partners(8, count)
+    pairs = [[i, to[i]] for i in range(count >> 1)]
+    pair = lax.all_gather(own_10, AXES, axis_index_groups=pairs, tiled=True)
     return call(
         final_kernel,
         bf16(rows, model),
-        [*vmem(6), in_hbm],
-        q, num, tot, sib_5, sib_9, sib_10, stay(w_out),
+        [SMEM, *vmem(6), in_hbm],
+        place, q, num, tot, sib_5, sib_9, pair, stay(w_out),
         flops=10**9,
         scratch=(
             pltpu.VMEM((rows, model), jnp.bfloat16),

time: 67.2 us -> 66.3 us (0.987)
  blocking collectives: 0 us -> 6.86 us
  waiting for transfers between devices: 13.6 us -> 9.48 us
  starting transfers between devices: 42 us -> 39.3 us
  Pallas kernels: 10.3 us -> 9.3 us
    all_gather x0 -> x1, blocking collectives: none -> 6.86 us  [per_device(): pair = lax.all_gather(own_10, AXES, axis_index_groups=pairs, tiled=True)]
    ppermute x7, waiting for transfers between devices: 11.3 us -> 6.12 us  [exchange(): return lax.ppermute(own, AXES, list(enumerate(partners(bit, count))))]
    all_to_all x1, starting transfers between devices: 16.6 us -> 13.8 us  [per_device(): lax.all_to_all(level_6, AXES, 0, 0, axis_index_groups=teams, tiled=True)]
    ppermute x1, waiting for transfers between devices: 1.48 us -> 3.36 us  [per_device(): other_halo = lax.ppermute(other, AXES, swap)]
    pallas_call x9 -> x10, Pallas kernels: 10.3 us -> 9.3 us  [call(): pl.pallas_call(body, out_shape=outs, in_specs=list(in_specs) + [pl.BlockS...]
    all_to_all x1, waiting for transfers between devices: 0.8 us -> 0.01 us  [per_device(): lax.all_to_all(level_6, AXES, 0, 0, axis_index_groups=teams, tiled=True)]
  transfers between devices with their start and end apart: 9 -> 9, of which waited for: 7 -> 5; matrix products, arithmetic and copies ran while one was open for 0% -> 0% of each run, Pallas kernels for 6% -> 6%
where the time goes in v9:
time: 66.3 us; the launch traced here: 65.1 us
  starting transfers between devices  39.3 us (59%)
  waiting for transfers between devices  9.48 us (14%)
  Pallas kernels  9.3 us (14%)
  blocking collectives  6.86 us (10%)
    ppermute x7, starting transfers between devices, exchange(): return lax.ppermute(own, AXES, list(enumerate(partners(bit, count))))  18.6 us
    all_to_all x1, starting transfers between devices, per_device(): lax.all_to_all(level_6, AXES, 0, 0, axis_index_groups=teams, tiled=True)  13.8 us
    pallas_call x10, Pallas kernels, call(): pl.pallas_call(body, out_shape=outs, in_specs=list(in_specs) + [pl.BlockS...  9.3 us
    ppermute x1, starting transfers between devices, per_device(): other_halo = lax.ppermute(other, AXES, swap)  6.96 us
    all_gather x1, blocking collectives, per_device(): pair = lax.all_gather(own_10, AXES, axis_index_groups=pairs, tiled=True)  6.86 us
    ppermute x7, waiting for transfers between devices, exchange(): return lax.ppermute(own, AXES, list(enumerate(partners(bit, count))))  6.12 us
    ppermute x1, waiting for transfers between devices, per_device(): other_halo = lax.ppermute(other, AXES, swap)  3.36 us
  transfers between devices with their start and end apart: 9, of which 5 were waited for; matrix products, arithmetic and copies ran while one was open for 0% of the time, Pallas kernels for 6%

profile of v9, /device:TPU:6, one launch (start us, length us, event | category | flops | bytes accessed | tf_op | source)
XLA Modules:
  0.0 65.1 jit_solution(8895927362961308401)
XLA Ops:
  0.0 2.9 %shard_map.37 = (bf16[256,1024]{1,0:T(8,128)(2,1)S(1)}, bf16[128,1024]{1,0:T(8,128)(2,1)S(1)}, bf16[64,1024]{1,0:T(8,128)(2,1)S(1)}, bf16[32,1024]{1,0:T(8,128)(2,1)S(1)}, bf16[1024,128]{1,0:T(8,128)(2,1)}) custom-call(s32[1]{0:T(128)} %bitcast.refs_0_, bf16[256,512]{1,0:T(8,128)(2,1)} %refs_1_.3, bf16[512,1536]{1,0:T(8,128)(2,1)} %refs_2_.3), custom_call_target="tpu_custom_call" | custom-call | flops 268435456 | bytes 1048576 | tf_op jit(solution)/shard_map/pallas_call | solution.py:45
  2.9 13.8 %all-to-all-start = ((bf16[32,32,128]{2,1,0:T(8,128)(2,1)}), bf16[32,32,128]{2,1,0:T(8,128)(2,1)S(1)}, u32[]{:S(2)}, u32[]{:S(2)}) async-start(bf16[32,32,128]{2,1,0:T(8,128)(2,1)} %bitcast.1), calls=%async_computation | async-start | bytes 524288 | tf_op jit(solution)/shard_map/all_to_all | solution.py:322
  16.6 1.9 %collective-permute-start = (bf16[128,1024]{1,0:T(8,128)(2,1)S(1)}, bf16[128,1024]{1,0:T(8,128)(2,1)S(1)}, u32[]{:S(2)}, u32[]{:S(2)}) collective-permute-start(bf16[128,1024]{1,0:T(8,128)(2,1)S(1)} %get-tuple-element.14), channel_id=1, source_target_pairs={{0,1},{1,0},{2,3},{3,2},{4,5},{5,4},{6,7},{7,6},{8,9},{9,8},{10,11... | collective-permute-start | bytes 786440 | tf_op jit(solution)/shard_map/ppermute | solution.py:312
  18.6 1.5 %collective-permute-done.refs_1_.refs_4_ = bf16[128,1024]{1,0:T(8,128)(2,1)S(1)} collective-permute-done((bf16[128,1024]{1,0:T(8,128)(2,1)S(1)}, bf16[128,1024]{1,0:T(8,128)(2,1)S(1)}, u32[]{:S(2)}, u32[]{:S(2)}) %collective-permute-start) | collective-permute-done | bytes 262176 | tf_op jit(solution)/shard_map/ppermute | solution.py:312
  20.1 0.1 shard_map.38.refs_0_
  20.2 3.7 %collective-permute-start.2 = (bf16[64,1024]{1,0:T(8,128)(2,1)S(1)}, bf16[64,1024]{1,0:T(8,128)(2,1)S(1)}, u32[]{:S(2)}, u32[]{:S(2)}) collective-permute-start(bf16[64,1024]{1,0:T(8,128)(2,1)S(1)} %shard_map.38.refs_0_), channel_id=1, source_target_pairs={{0,2},{1,3},{2,0},{3,1},{4,6},{5,7},{6,4},{7,5},{8,10},{9,11},{10,... | collective-permute-start | bytes 393224 | tf_op jit(solution)/shard_map/ppermute | solution.py:312
  23.9 7.0 %collective-permute-start.1 = (bf16[64,1024]{1,0:T(8,128)(2,1)S(1)}, bf16[64,1024]{1,0:T(8,128)(2,1)S(1)}, u32[]{:S(2)}, u32[]{:S(2)}) collective-permute-start(bf16[64,1024]{1,0:T(8,128)(2,1)S(1)} %get-tuple-element.15), channel_id=1, source_target_pairs={{1,2},{3,4},{5,6},{7,8},{9,10},{11,12},{13,14},{15,16},{17,18},{19... | collective-permute-start | bytes 393224 | tf_op jit(solution)/shard_map/ppermute | solution.py:326
  30.9 0.2 shard_map.39.refs_2_.refs_0_
  31.1 3.4 %collective-permute-done.1.refs_3_.refs_5_ = bf16[64,1024]{1,0:T(8,128)(2,1)S(1)} collective-permute-done((bf16[64,1024]{1,0:T(8,128)(2,1)S(1)}, bf16[64,1024]{1,0:T(8,128)(2,1)S(1)}, u32[]{:S(2)}, u32[]{:S(2)}) %collective-permute-start.1) | collective-permute-done | bytes 131104 | tf_op jit(solution)/shard_map/ppermute | solution.py:326
  34.4 0.6 shard_map.40.refs_0_.refs_8_
  35.0 1.9 %collective-permute-start.4 = (bf16[96,1024]{1,0:T(8,128)(2,1)S(1)}, bf16[96,1024]{1,0:T(8,128)(2,1)S(1)}, u32[]{:S(2)}, u32[]{:S(2)}) collective-permute-start(bf16[96,1024]{1,0:T(8,128)(2,1)S(1)} %shard_map.40.refs_0_.refs_8_), channel_id=1, source_target_pairs={{0,1},{1,0},{2,3},{3,2},{4,5},{5,4},{6,7},{7,6},{8,9},{9,8},{10,11... | collective-permute-start | bytes 589832 | tf_op jit(solution)/shard_map/ppermute | solution.py:312
  36.9 1.9 %collective-permute-start.3 = (bf16[64,1024]{1,0:T(8,128)(2,1)S(1)}, bf16[64,1024]{1,0:T(8,128)(2,1)S(1)}, u32[]{:S(2)}, u32[]{:S(2)}) collective-permute-start(bf16[64,1024]{1,0:T(8,128)(2,1)S(1)} %shard_map.39.refs_2_.refs_0_), channel_id=1, source_target_pairs={{0,4},{1,5},{2,6},{3,7},{4,0},{5,1},{6,2},{7,3},{8,12},{9,13},{10,... | collective-permute-start | bytes 393224 | tf_op jit(solution)/shard_map/ppermute | solution.py:312
  38.9 3.3 %collective-permute-start.5 = (bf16[64,1024]{1,0:T(8,128)(2,1)S(1)}, bf16[64,1024]{1,0:T(8,128)(2,1)S(1)}, u32[]{:S(2)}, u32[]{:S(2)}) collective-permute-start(bf16[64,1024]{1,0:T(8,128)(2,1)S(1)} %shard_map.41.refs_2_.refs_0_), channel_id=1, source_target_pairs={{0,96},{1,97},{2,98},{3,99},{4,100},{5,101},{6,102},{7,103},{8,104... | collective-permute-start | bytes 393224 | tf_op jit(solution)/shard_map/ppermute | solution.py:312
  42.2 3.4 %collective-permute-done.3.refs_1_.refs_7_ = bf16[64,1024]{1,0:T(8,128)(2,1)S(1)} collective-permute-done((bf16[64,1024]{1,0:T(8,128)(2,1)S(1)}, bf16[64,1024]{1,0:T(8,128)(2,1)S(1)}, u32[]{:S(2)}, u32[]{:S(2)}) %collective-permute-start.3) | collective-permute-done | bytes 131104 | tf_op jit(solution)/shard_map/ppermute | solution.py:312
  45.6 0.2 shard_map.42.refs_2_
  45.8 3.1 %collective-permute-start.6 = (bf16[64,1024]{1,0:T(8,128)(2,1)S(1)}, bf16[64,1024]{1,0:T(8,128)(2,1)S(1)}, u32[]{:S(2)}, u32[]{:S(2)}) collective-permute-start(bf16[64,1024]{1,0:T(8,128)(2,1)S(1)} %shard_map.42.refs_2_), channel_id=1, source_target_pairs={{0,12},{1,13},{2,14},{3,15},{4,8},{5,9},{6,10},{7,11},{8,4},{9,5},... | collective-permute-start | bytes 393224 | tf_op jit(solution)/shard_map/ppermute | solution.py:312
  48.9 0.0 collective-permute-done.5.refs_1_.refs_10_
  48.9 2.7 %collective-permute-start.7 = (bf16[64,1024]{1,0:T(8,128)(2,1)S(1)}, bf16[64,1024]{1,0:T(8,128)(2,1)S(1)}, u32[]{:S(2)}, u32[]{:S(2)}) collective-permute-start(bf16[64,1024]{1,0:T(8,128)(2,1)S(1)} %shard_map.43.refs_11_.refs_0_), channel_id=1, source_target_pairs={{0,128},{1,129},{2,130},{3,131},{4,132},{5,133},{6,134},{7,135},{8... | collective-permute-start | bytes 393224 | tf_op jit(solution)/shard_map/ppermute | solution.py:312
  51.7 3.1 %shard_map.44 = (bf16[256,512]{1,0:T(8,128)(2,1)S(1)}, f32[256,512]{1,0:T(8,128)S(1)}, f32[256,512]{1,0:T(8,128)S(1)}) custom-call(s32[1]{0:T(128)} %bitcast.refs_0_, bf16[256,512]{1,0:T(8,128)(2,1)S(1)} %copy-done, bf16[512,1536]{1,0:T(8,128)(2,1)} %refs_2_.3, bf16[256,1024]{1,0:T(8,128)(2,1)S(1)} %get-tuple-element.13.refs_3_, ...), custom_call_target="tpu_custom_call" | custom-call | flops 1000000000 | bytes 1048576 | tf_op jit(solution)/shard_map/pallas_call | solution.py:45
  54.8 0.2 collective-permute-done.6.refs_3_.refs_4_
  55.0 1.0 %collective-permute-done.7.refs_1_.refs_5_ = bf16[64,1024]{1,0:T(8,128)(2,1)S(1)} collective-permute-done((bf16[64,1024]{1,0:T(8,128)(2,1)S(1)}, bf16[64,1024]{1,0:T(8,128)(2,1)S(1)}, u32[]{:S(2)}, u32[]{:S(2)}) %collective-permute-start.7) | collective-permute-done | bytes 131104 | tf_op jit(solution)/shard_map/ppermute | solution.py:312
  56.0 0.2 shard_map.45
  56.2 6.9 %all_gather.3.refs_6_ = bf16[128,1024]{1,0:T(8,128)(2,1)S(1)} all-gather(bf16[64,1024]{1,0:T(8,128)(2,1)S(1)} %shard_map.45), channel_id=1, replica_groups={{0,384},{1,385},{2,386},{3,387},{4,388},{5,389},{6,390},{7,391},{8,392}..., dimensions={0}, use_global_device_ids=true | all-gather | bytes 393216 | tf_op jit(solution)/shard_map/all_gather | solution.py:359
  63.0 2.1 %shard_map.46 = bf16[256,512]{1,0:T(8,128)(2,1)} custom-call(s32[1]{0:T(128)} %bitcast.refs_0_, bf16[256,512]{1,0:T(8,128)(2,1)S(1)} %get-tuple-element.18.refs_2_.refs_1_, f32[256,512]{1,0:T(8,128)S(1)} %get-tuple-element.19.refs_2_, f32[256,512]{1,0:T(8,128)S(1)} %get-tuple-element.20.refs_3_, bf16[64,1024]{1,0:T(8,128)(2,1)S(1)} %collective-permute-done.6.refs_3_.refs_4_, ...), custom_call_target="tpu_custom_call" | custom-call | flops 1000000000 | bytes 1048576 | tf_op jit(solution)/shard_map/pallas_call | solution.py:45
  (7 shorter events, 0.1 us)
Async XLA Ops:
  2.9 31.6 %all-to-all-start = ((bf16[32,32,128]{2,1,0:T(8,128)(2,1)}), bf16[32,32,128]{2,1,0:T(8,128)(2,1)S(1)}, u32[]{:S(2)}, u32[]{:S(2)}) async-start(bf16[32,32,128]{2,1,0:T(8,128)(2,1)} %bitcast.1), calls=%async_computation | async-start | bytes 524288 | tf_op jit(solution)/shard_map/all_to_all | solution.py:322
  16.6 3.4 %collective-permute-start = (bf16[128,1024]{1,0:T(8,128)(2,1)S(1)}, bf16[128,1024]{1,0:T(8,128)(2,1)S(1)}, u32[]{:S(2)}, u32[]{:S(2)}) collective-permute-start(bf16[128,1024]{1,0:T(8,128)(2,1)S(1)} %get-tuple-element.14), channel_id=1, source_target_pairs={{0,1},{1,0},{2,3},{3,2},{4,5},{5,4},{6,7},{7,6},{8,9},{9,8},{10,11... | collective-permute-start | bytes 786440 | tf_op jit(solution)/shard_map/ppermute | solution.py:312
  20.1 31.6 %copy-start = (bf16[256,512]{1,0:T(8,128)(2,1)S(1)}, bf16[256,512]{1,0:T(8,128)(2,1)}, u32[]{:S(2)}) copy-start(bf16[256,512]{1,0:T(8,128)(2,1)} %refs_1_.3) | copy-start | bytes 786436
  20.2 10.7 %collective-permute-start.2 = (bf16[64,1024]{1,0:T(8,128)(2,1)S(1)}, bf16[64,1024]{1,0:T(8,128)(2,1)S(1)}, u32[]{:S(2)}, u32[]{:S(2)}) collective-permute-start(bf16[64,1024]{1,0:T(8,128)(2,1)S(1)} %shard_map.38.refs_0_), channel_id=1, source_target_pairs={{0,2},{1,3},{2,0},{3,1},{4,6},{5,7},{6,4},{7,5},{8,10},{9,11},{10,... | collective-permute-start | bytes 393224 | tf_op jit(solution)/shard_map/ppermute | solution.py:312
  23.9 10.5 %collective-permute-start.1 = (bf16[64,1024]{1,0:T(8,128)(2,1)S(1)}, bf16[64,1024]{1,0:T(8,128)(2,1)S(1)}, u32[]{:S(2)}, u32[]{:S(2)}) collective-permute-start(bf16[64,1024]{1,0:T(8,128)(2,1)S(1)} %get-tuple-element.15), channel_id=1, source_target_pairs={{1,2},{3,4},{5,6},{7,8},{9,10},{11,12},{13,14},{15,16},{17,18},{19... | collective-permute-start | bytes 393224 | tf_op jit(solution)/shard_map/ppermute | solution.py:326
  35.0 3.9 %collective-permute-start.4 = (bf16[96,1024]{1,0:T(8,128)(2,1)S(1)}, bf16[96,1024]{1,0:T(8,128)(2,1)S(1)}, u32[]{:S(2)}, u32[]{:S(2)}) collective-permute-start(bf16[96,1024]{1,0:T(8,128)(2,1)S(1)} %shard_map.40.refs_0_.refs_8_), channel_id=1, source_target_pairs={{0,1},{1,0},{2,3},{3,2},{4,5},{5,4},{6,7},{7,6},{8,9},{9,8},{10,11... | collective-permute-start | bytes 589832 | tf_op jit(solution)/shard_map/ppermute | solution.py:312
  36.9 8.7 %collective-permute-start.3 = (bf16[64,1024]{1,0:T(8,128)(2,1)S(1)}, bf16[64,1024]{1,0:T(8,128)(2,1)S(1)}, u32[]{:S(2)}, u32[]{:S(2)}) collective-permute-start(bf16[64,1024]{1,0:T(8,128)(2,1)S(1)} %shard_map.39.refs_2_.refs_0_), channel_id=1, source_target_pairs={{0,4},{1,5},{2,6},{3,7},{4,0},{5,1},{6,2},{7,3},{8,12},{9,13},{10,... | collective-permute-start | bytes 393224 | tf_op jit(solution)/shard_map/ppermute | solution.py:312
  38.9 10.0 %collective-permute-start.5 = (bf16[64,1024]{1,0:T(8,128)(2,1)S(1)}, bf16[64,1024]{1,0:T(8,128)(2,1)S(1)}, u32[]{:S(2)}, u32[]{:S(2)}) collective-permute-start(bf16[64,1024]{1,0:T(8,128)(2,1)S(1)} %shard_map.41.refs_2_.refs_0_), channel_id=1, source_target_pairs={{0,96},{1,97},{2,98},{3,99},{4,100},{5,101},{6,102},{7,103},{8,104... | collective-permute-start | bytes 393224 | tf_op jit(solution)/shard_map/ppermute | solution.py:312
  45.8 9.2 %collective-permute-start.6 = (bf16[64,1024]{1,0:T(8,128)(2,1)S(1)}, bf16[64,1024]{1,0:T(8,128)(2,1)S(1)}, u32[]{:S(2)}, u32[]{:S(2)}) collective-permute-start(bf16[64,1024]{1,0:T(8,128)(2,1)S(1)} %shard_map.42.refs_2_), channel_id=1, source_target_pairs={{0,12},{1,13},{2,14},{3,15},{4,8},{5,9},{6,10},{7,11},{8,4},{9,5},... | collective-permute-start | bytes 393224 | tf_op jit(solution)/shard_map/ppermute | solution.py:312
  48.9 7.1 %collective-permute-start.7 = (bf16[64,1024]{1,0:T(8,128)(2,1)S(1)}, bf16[64,1024]{1,0:T(8,128)(2,1)S(1)}, u32[]{:S(2)}, u32[]{:S(2)}) collective-permute-start(bf16[64,1024]{1,0:T(8,128)(2,1)S(1)} %shard_map.43.refs_11_.refs_0_), channel_id=1, source_target_pairs={{0,128},{1,129},{2,130},{3,131},{4,132},{5,133},{6,134},{7,135},{8... | collective-permute-start | bytes 393224 | tf_op jit(solution)/shard_map/ppermute | solution.py:312

commit v10 on v9

--- a/solution.py
+++ b/solution.py
@@ -190,7 +190,7 @@
 
 
 def local_kernel(
-    count, place, x_ref, w_hbm, kv_ref, near_ref, other_ref, sib_3_ref, sib_4_ref,
+    count, place, x_ref, w_hbm, kv_ref, near_ref, other_ref, both_3_ref, sib_4_ref,
     mine_ref, theirs_ref, sib_8_ref, q_ref, num_ref, tot_ref, pad, l1, w_ref, sem
 ):
     rows, model = x_ref.shape
@@ -232,7 +232,9 @@
             num, tot = attend_pair(q_ref[here, kl], keys, values, ones)
             num_ref[here, kl] = num
             tot_ref[here, kl] = tot
-    far = far_blocks((near_ref, sib_3_ref, sib_4_ref, mine_ref, theirs_ref, sib_8_ref))
+    start = pl.multiple_of((1 - ((place[0] >> 1) & 1)) * BLOCK, BLOCK)
+    sib_3 = both_3_ref[pl.ds(start, BLOCK), :]
+    far = far_blocks((near_ref, sib_3, sib_4_ref, mine_ref, theirs_ref, sib_8_ref))
     for lanes in range(0, model, 128):
         kl = slice(lanes, lanes + 128)
         num, tot = far_sums(far, q_ref[:, kl], lanes, model)
@@ -322,16 +324,17 @@
     spread = lax.all_to_all(level_6, AXES, 0, 0, axis_index_groups=teams, tiled=True)
     near_sib = exchange(near, 0)
     own_3 = call(pool_near_kernel, block, vmem(2), level_3, near_sib)
-    sib_3 = exchange(own_3, 1)
+    z_pairs = [[i, i ^ 2] for i in range(count) if not i & 2]
+    both_3 = lax.all_gather(own_3, AXES, axis_index_groups=z_pairs, tiled=True)
     other_halo = lax.ppermute(other, AXES, swap)
-    own_4 = pool(own_3, sib_3)
     mine = call(
         unpack_kernel, bf16(3 * BLOCK // 2, 2 * model), [SMEM, *vmem(1)],
         place, spread.reshape(members, packed, 128),
         scratch=(pltpu.VMEM((members * packed, 128), jnp.float32),),
-        after=(own_4, other_halo),
+        after=(both_3, other_halo),
     )
     theirs = exchange(mine, 0)
+    own_4 = call(pool_kernel, block, vmem(1), both_3, after=(mine,))
     sib_4 = exchange(own_4, 2)
     own_8 = call(own_8_kernel, block, vmem(2), mine, theirs)
     sib_8 = exchange(own_8, 6)
@@ -343,7 +346,7 @@
         functools.partial(local_kernel, count),
         (bf16(rows, model), f32(rows, model), f32(rows, model)),
         [SMEM, *vmem(1), in_hbm, *vmem(8)],
-        place, tokens, stay(w_qkv), kv, near_sib, other_halo, sib_3, sib_4, mine, theirs, sib_8,
+        place, tokens, stay(w_qkv), kv, near_sib, other_halo, both_3, sib_4, mine, theirs, sib_8,
         flops=10**9,
         scratch=(
             pltpu.VMEM((rows + 2 * BLOCK, 2 * model), jnp.bfloat16),

time: 66.3 us -> 66.1 us (level)
  the two profiles are of different devices: /device:TPU:6 before, /device:TPU:8 now
where the time goes in v10:
time: 66.1 us; the launch traced here: 65.6 us
  starting transfers between devices  39 us (59%)
  blocking collectives  12.5 us (19%)
  Pallas kernels  9.31 us (14%)
  waiting for transfers between devices  4.63 us (7%)
    ppermute x6, starting transfers between devices, exchange(): return lax.ppermute(own, AXES, list(enumerate(partners(bit, count))))  20.3 us
    all_to_all x1, starting transfers between devices, per_device(): lax.all_to_all(level_6, AXES, 0, 0, axis_index_groups=teams, tiled=True)  14 us
    pallas_call x10, Pallas kernels, call(): pl.pallas_call(body, out_shape=outs, in_specs=list(in_specs) + [pl.BlockS...  9.31 us
    all_gather x1, blocking collectives, per_device(): pair = lax.all_gather(own_10, AXES, axis_index_groups=pairs, tiled=True)  6.86 us
    all_gather x1, blocking collectives, per_device(): both_3 = lax.all_gather(own_3, AXES, axis_index_groups=z_pairs, tiled=True)  5.64 us
    ppermute x1, starting transfers between devices, per_device(): other_halo = lax.ppermute(other, AXES, swap)  4.68 us
    ppermute x6, waiting for transfers between devices, exchange(): return lax.ppermute(own, AXES, list(enumerate(partners(bit, count))))  4.63 us
  transfers between devices with their start and end apart: 8, of which 3 were waited for; matrix products, arithmetic and copies ran while one was open for 0% of the time, Pallas kernels for 6%

profile of v10, /device:TPU:8, one launch (start us, length us, event | category | flops | bytes accessed | tf_op | source)
XLA Modules:
  0.0 65.6 jit_solution(5993540429619379502)
XLA Ops:
  0.0 2.9 %shard_map.37 = (bf16[256,1024]{1,0:T(8,128)(2,1)S(1)}, bf16[128,1024]{1,0:T(8,128)(2,1)S(1)}, bf16[64,1024]{1,0:T(8,128)(2,1)S(1)}, bf16[32,1024]{1,0:T(8,128)(2,1)S(1)}, bf16[1024,128]{1,0:T(8,128)(2,1)}) custom-call(s32[1]{0:T(128)} %bitcast.refs_0_, bf16[256,512]{1,0:T(8,128)(2,1)} %refs_1_.3, bf16[512,1536]{1,0:T(8,128)(2,1)} %refs_2_.3), custom_call_target="tpu_custom_call" | custom-call | flops 268435456 | bytes 1048576 | tf_op jit(solution)/shard_map/pallas_call | solution.py:45
  2.9 14.0 %all-to-all-start = ((bf16[32,32,128]{2,1,0:T(8,128)(2,1)}), bf16[32,32,128]{2,1,0:T(8,128)(2,1)S(1)}, u32[]{:S(2)}, u32[]{:S(2)}) async-start(bf16[32,32,128]{2,1,0:T(8,128)(2,1)} %bitcast.1), calls=%async_computation | async-start | bytes 524288 | tf_op jit(solution)/shard_map/all_to_all | solution.py:324
  16.8 1.9 %collective-permute-start = (bf16[128,1024]{1,0:T(8,128)(2,1)S(1)}, bf16[128,1024]{1,0:T(8,128)(2,1)S(1)}, u32[]{:S(2)}, u32[]{:S(2)}) collective-permute-start(bf16[128,1024]{1,0:T(8,128)(2,1)S(1)} %get-tuple-element.14), channel_id=1, source_target_pairs={{0,1},{1,0},{2,3},{3,2},{4,5},{5,4},{6,7},{7,6},{8,9},{9,8},{10,11... | collective-permute-start | bytes 786440 | tf_op jit(solution)/shard_map/ppermute | solution.py:314
  18.8 4.7 %collective-permute-start.1 = (bf16[64,1024]{1,0:T(8,128)(2,1)S(1)}, bf16[64,1024]{1,0:T(8,128)(2,1)S(1)}, u32[]{:S(2)}, u32[]{:S(2)}) collective-permute-start(bf16[64,1024]{1,0:T(8,128)(2,1)S(1)} %get-tuple-element.15), channel_id=1, source_target_pairs={{1,2},{3,4},{5,6},{7,8},{9,10},{11,12},{13,14},{15,16},{17,18},{19... | collective-permute-start | bytes 393224 | tf_op jit(solution)/shard_map/ppermute | solution.py:329
  23.5 0.0 collective-permute-done.refs_1_.refs_4_
  23.5 0.1 shard_map.38
  23.6 5.6 %all_gather.6.refs_2_.refs_0_.refs_6_ = bf16[128,1024]{1,0:T(8,128)(2,1)S(1)} all-gather(bf16[64,1024]{1,0:T(8,128)(2,1)S(1)} %shard_map.38), channel_id=1, replica_groups={{0,2},{1,3},{4,6},{5,7},{8,10},{9,11},{12,14},{13,15},{16,18},{17,19},{..., dimensions={0}, use_global_device_ids=true | all-gather | bytes 393216 | tf_op jit(solution)/shard_map/all_gather | solution.py:328
  29.3 0.0 collective-permute-done.1.refs_3_.refs_5_
  29.3 0.6 shard_map.39.refs_1_.refs_0_.refs_8_
  29.9 1.9 %collective-permute-start.3 = (bf16[96,1024]{1,0:T(8,128)(2,1)S(1)}, bf16[96,1024]{1,0:T(8,128)(2,1)S(1)}, u32[]{:S(2)}, u32[]{:S(2)}) collective-permute-start(bf16[96,1024]{1,0:T(8,128)(2,1)S(1)} %shard_map.39.refs_1_.refs_0_.refs_8_), channel_id=1, source_target_pairs={{0,1},{1,0},{2,3},{3,2},{4,5},{5,4},{6,7},{7,6},{8,9},{9,8},{10,11... | collective-permute-start | bytes 589832 | tf_op jit(solution)/shard_map/ppermute | solution.py:314
  31.8 0.2 shard_map.40.refs_0_
  32.0 4.9 %collective-permute-start.2 = (bf16[64,1024]{1,0:T(8,128)(2,1)S(1)}, bf16[64,1024]{1,0:T(8,128)(2,1)S(1)}, u32[]{:S(2)}, u32[]{:S(2)}) collective-permute-start(bf16[64,1024]{1,0:T(8,128)(2,1)S(1)} %shard_map.40.refs_0_), channel_id=1, source_target_pairs={{0,4},{1,5},{2,6},{3,7},{4,0},{5,1},{6,2},{7,3},{8,12},{9,13},{10,... | collective-permute-start | bytes 393224 | tf_op jit(solution)/shard_map/ppermute | solution.py:314
  36.9 4.8 %collective-permute-start.4 = (bf16[64,1024]{1,0:T(8,128)(2,1)S(1)}, bf16[64,1024]{1,0:T(8,128)(2,1)S(1)}, u32[]{:S(2)}, u32[]{:S(2)}) collective-permute-start(bf16[64,1024]{1,0:T(8,128)(2,1)S(1)} %shard_map.41.refs_2_.refs_0_), channel_id=1, source_target_pairs={{0,96},{1,97},{2,98},{3,99},{4,100},{5,101},{6,102},{7,103},{8,104... | collective-permute-start | bytes 393224 | tf_op jit(solution)/shard_map/ppermute | solution.py:314
  41.7 2.1 %collective-permute-done.2.refs_1_.refs_7_ = bf16[64,1024]{1,0:T(8,128)(2,1)S(1)} collective-permute-done((bf16[64,1024]{1,0:T(8,128)(2,1)S(1)}, bf16[64,1024]{1,0:T(8,128)(2,1)S(1)}, u32[]{:S(2)}, u32[]{:S(2)}) %collective-permute-start.2) | collective-permute-done | bytes 131104 | tf_op jit(solution)/shard_map/ppermute | solution.py:314
  43.8 0.2 shard_map.42.refs_2_
  44.0 3.4 %collective-permute-start.5 = (bf16[64,1024]{1,0:T(8,128)(2,1)S(1)}, bf16[64,1024]{1,0:T(8,128)(2,1)S(1)}, u32[]{:S(2)}, u32[]{:S(2)}) collective-permute-start(bf16[64,1024]{1,0:T(8,128)(2,1)S(1)} %shard_map.42.refs_2_), channel_id=1, source_target_pairs={{0,12},{1,13},{2,14},{3,15},{4,8},{5,9},{6,10},{7,11},{8,4},{9,5},... | collective-permute-start | bytes 393224 | tf_op jit(solution)/shard_map/ppermute | solution.py:314
  47.4 1.9 %collective-permute-done.4.refs_1_.refs_10_ = bf16[64,1024]{1,0:T(8,128)(2,1)S(1)} collective-permute-done((bf16[64,1024]{1,0:T(8,128)(2,1)S(1)}, bf16[64,1024]{1,0:T(8,128)(2,1)S(1)}, u32[]{:S(2)}, u32[]{:S(2)}) %collective-permute-start.4) | collective-permute-done | bytes 131104 | tf_op jit(solution)/shard_map/ppermute | solution.py:314
  49.4 3.4 %collective-permute-start.6 = (bf16[64,1024]{1,0:T(8,128)(2,1)S(1)}, bf16[64,1024]{1,0:T(8,128)(2,1)S(1)}, u32[]{:S(2)}, u32[]{:S(2)}) collective-permute-start(bf16[64,1024]{1,0:T(8,128)(2,1)S(1)} %shard_map.43.refs_11_.refs_0_), channel_id=1, source_target_pairs={{0,128},{1,129},{2,130},{3,131},{4,132},{5,133},{6,134},{7,135},{8... | collective-permute-start | bytes 393224 | tf_op jit(solution)/shard_map/ppermute | solution.py:314
  52.8 3.1 %shard_map.44 = (bf16[256,512]{1,0:T(8,128)(2,1)S(1)}, f32[256,512]{1,0:T(8,128)S(1)}, f32[256,512]{1,0:T(8,128)S(1)}) custom-call(s32[1]{0:T(128)} %bitcast.refs_0_, bf16[256,512]{1,0:T(8,128)(2,1)S(1)} %copy-done, bf16[512,1536]{1,0:T(8,128)(2,1)} %refs_2_.3, bf16[256,1024]{1,0:T(8,128)(2,1)S(1)} %get-tuple-element.13.refs_3_, ...), custom_call_target="tpu_custom_call" | custom-call | flops 1000000000 | bytes 1048576 | tf_op jit(solution)/shard_map/pallas_call | solution.py:45
  55.9 0.0 collective-permute-done.5.refs_3_.refs_4_
  55.9 0.6 collective-permute-done.6.refs_1_.refs_5_
  56.5 0.2 shard_map.45
  56.7 6.9 %all_gather.7.refs_6_ = bf16[128,1024]{1,0:T(8,128)(2,1)S(1)} all-gather(bf16[64,1024]{1,0:T(8,128)(2,1)S(1)} %shard_map.45), channel_id=1, replica_groups={{0,384},{1,385},{2,386},{3,387},{4,388},{5,389},{6,390},{7,391},{8,392}..., dimensions={0}, use_global_device_ids=true | all-gather | bytes 393216 | tf_op jit(solution)/shard_map/all_gather | solution.py:362
  63.5 2.1 %shard_map.46 = bf16[256,512]{1,0:T(8,128)(2,1)} custom-call(s32[1]{0:T(128)} %bitcast.refs_0_, bf16[256,512]{1,0:T(8,128)(2,1)S(1)} %get-tuple-element.18.refs_2_.refs_1_, f32[256,512]{1,0:T(8,128)S(1)} %get-tuple-element.19.refs_2_, f32[256,512]{1,0:T(8,128)S(1)} %get-tuple-element.20.refs_3_, bf16[64,1024]{1,0:T(8,128)(2,1)S(1)} %collective-permute-done.5.refs_3_.refs_4_, ...), custom_call_target="tpu_custom_call" | custom-call | flops 1000000000 | bytes 1048576 | tf_op jit(solution)/shard_map/pallas_call | solution.py:45
  (6 shorter events, 0.1 us)
Async XLA Ops:
  2.9 26.4 %all-to-all-start = ((bf16[32,32,128]{2,1,0:T(8,128)(2,1)}), bf16[32,32,128]{2,1,0:T(8,128)(2,1)S(1)}, u32[]{:S(2)}, u32[]{:S(2)}) async-start(bf16[32,32,128]{2,1,0:T(8,128)(2,1)} %bitcast.1), calls=%async_computation | async-start | bytes 524288 | tf_op jit(solution)/shard_map/all_to_all | solution.py:324
  16.8 6.6 %collective-permute-start = (bf16[128,1024]{1,0:T(8,128)(2,1)S(1)}, bf16[128,1024]{1,0:T(8,128)(2,1)S(1)}, u32[]{:S(2)}, u32[]{:S(2)}) collective-permute-start(bf16[128,1024]{1,0:T(8,128)(2,1)S(1)} %get-tuple-element.14), channel_id=1, source_target_pairs={{0,1},{1,0},{2,3},{3,2},{4,5},{5,4},{6,7},{7,6},{8,9},{9,8},{10,11... | collective-permute-start | bytes 786440 | tf_op jit(solution)/shard_map/ppermute | solution.py:314
  18.8 10.5 %collective-permute-start.1 = (bf16[64,1024]{1,0:T(8,128)(2,1)S(1)}, bf16[64,1024]{1,0:T(8,128)(2,1)S(1)}, u32[]{:S(2)}, u32[]{:S(2)}) collective-permute-start(bf16[64,1024]{1,0:T(8,128)(2,1)S(1)} %get-tuple-element.15), channel_id=1, source_target_pairs={{1,2},{3,4},{5,6},{7,8},{9,10},{11,12},{13,14},{15,16},{17,18},{19... | collective-permute-start | bytes 393224 | tf_op jit(solution)/shard_map/ppermute | solution.py:329
  29.3 23.5 %copy-start = (bf16[256,512]{1,0:T(8,128)(2,1)S(1)}, bf16[256,512]{1,0:T(8,128)(2,1)}, u32[]{:S(2)}) copy-start(bf16[256,512]{1,0:T(8,128)(2,1)} %refs_1_.3) | copy-start | bytes 786436
  29.9 7.0 %collective-permute-start.3 = (bf16[96,1024]{1,0:T(8,128)(2,1)S(1)}, bf16[96,1024]{1,0:T(8,128)(2,1)S(1)}, u32[]{:S(2)}, u32[]{:S(2)}) collective-permute-start(bf16[96,1024]{1,0:T(8,128)(2,1)S(1)} %shard_map.39.refs_1_.refs_0_.refs_8_), channel_id=1, source_target_pairs={{0,1},{1,0},{2,3},{3,2},{4,5},{5,4},{6,7},{7,6},{8,9},{9,8},{10,11... | collective-permute-start | bytes 589832 | tf_op jit(solution)/shard_map/ppermute | solution.py:314
  32.0 11.9 %collective-permute-start.2 = (bf16[64,1024]{1,0:T(8,128)(2,1)S(1)}, bf16[64,1024]{1,0:T(8,128)(2,1)S(1)}, u32[]{:S(2)}, u32[]{:S(2)}) collective-permute-start(bf16[64,1024]{1,0:T(8,128)(2,1)S(1)} %shard_map.40.refs_0_), channel_id=1, source_target_pairs={{0,4},{1,5},{2,6},{3,7},{4,0},{5,1},{6,2},{7,3},{8,12},{9,13},{10,... | collective-permute-start | bytes 393224 | tf_op jit(solution)/shard_map/ppermute | solution.py:314
  36.9 12.4 %collective-permute-start.4 = (bf16[64,1024]{1,0:T(8,128)(2,1)S(1)}, bf16[64,1024]{1,0:T(8,128)(2,1)S(1)}, u32[]{:S(2)}, u32[]{:S(2)}) collective-permute-start(bf16[64,1024]{1,0:T(8,128)(2,1)S(1)} %shard_map.41.refs_2_.refs_0_), channel_id=1, source_target_pairs={{0,96},{1,97},{2,98},{3,99},{4,100},{5,101},{6,102},{7,103},{8,104... | collective-permute-start | bytes 393224 | tf_op jit(solution)/shard_map/ppermute | solution.py:314
  44.0 11.9 %collective-permute-start.5 = (bf16[64,1024]{1,0:T(8,128)(2,1)S(1)}, bf16[64,1024]{1,0:T(8,128)(2,1)S(1)}, u32[]{:S(2)}, u32[]{:S(2)}) collective-permute-start(bf16[64,1024]{1,0:T(8,128)(2,1)S(1)} %shard_map.42.refs_2_), channel_id=1, source_target_pairs={{0,12},{1,13},{2,14},{3,15},{4,8},{5,9},{6,10},{7,11},{8,4},{9,5},... | collective-permute-start | bytes 393224 | tf_op jit(solution)/shard_map/ppermute | solution.py:314
  49.4 7.1 %collective-permute-start.6 = (bf16[64,1024]{1,0:T(8,128)(2,1)S(1)}, bf16[64,1024]{1,0:T(8,128)(2,1)S(1)}, u32[]{:S(2)}, u32[]{:S(2)}) collective-permute-start(bf16[64,1024]{1,0:T(8,128)(2,1)S(1)} %shard_map.43.refs_11_.refs_0_), channel_id=1, source_target_pairs={{0,128},{1,129},{2,130},{3,131},{4,132},{5,133},{6,134},{7,135},{8... | collective-permute-start | bytes 393224 | tf_op jit(solution)/shard_map/ppermute | solution.py:314

commit v11 on v10

--- a/solution.py
+++ b/solution.py
@@ -259,15 +259,12 @@
 
 
 def final_kernel(
-    place, q_ref, num_in, tot_in, sib_5_ref, sib_9_ref, pair_ref, w_hbm, out_ref, att, w_ref, sem
+    q_ref, num_in, tot_in, sib_5_ref, sib_9_ref, sib_10_ref, w_hbm, out_ref, att, w_ref, sem
 ):
     copy = pltpu.make_async_copy(w_hbm, w_ref, sem)
     copy.start()
     model = q_ref.shape[1]
-    start = pl.multiple_of((1 - (place[0] >> 8)) * BLOCK, BLOCK)
-    far = jnp.concatenate(
-        [sib_5_ref[...], sib_9_ref[...], pair_ref[pl.ds(start, BLOCK), :]], axis=0
-    )
+    far = far_blocks((sib_5_ref, sib_9_ref, sib_10_ref))
     for lanes in range(0, model, 128):
         at = slice(lanes, lanes + 128)
         num, tot = far_sums(far, q_ref[:, at], lanes, model)
@@ -326,12 +323,11 @@
     own_3 = call(pool_near_kernel, block, vmem(2), level_3, near_sib)
     z_pairs = [[i, i ^ 2] for i in range(count) if not i & 2]
     both_3 = lax.all_gather(own_3, AXES, axis_index_groups=z_pairs, tiled=True)
-    other_halo = lax.ppermute(other, AXES, swap)
     mine = call(
         unpack_kernel, bf16(3 * BLOCK // 2, 2 * model), [SMEM, *vmem(1)],
         place, spread.reshape(members, packed, 128),
         scratch=(pltpu.VMEM((members * packed, 128), jnp.float32),),
-        after=(both_3, other_halo),
+        after=(both_3,),
     )
     theirs = exchange(mine, 0)
     own_4 = call(pool_kernel, block, vmem(1), both_3, after=(mine,))
@@ -339,9 +335,13 @@
     own_8 = call(own_8_kernel, block, vmem(2), mine, theirs)
     sib_8 = exchange(own_8, 6)
     own_5 = pool(own_4, sib_4, own_8)
+    other, _ = lax.optimization_barrier((other, own_5))
+    other_halo = lax.ppermute(other, AXES, swap)
     sib_5 = exchange(own_5, 3)
     own_9 = call(pool_halves_kernel, block, vmem(2), own_8, sib_8, after=(own_5,))
     sib_9 = exchange(own_9, 7)
+    own_10 = pool(own_9, sib_9, other_halo)
+    sib_10 = exchange(own_10, 8)
     q, num, tot = call(
         functools.partial(local_kernel, count),
         (bf16(rows, model), f32(rows, model), f32(rows, model)),
@@ -354,17 +354,13 @@
             pltpu.VMEM((model, model), jnp.bfloat16),
             pltpu.SemaphoreType.DMA(()),
         ),
-        after=(own_9,),
-    )
-    own_10 = pool(own_9, sib_9, q, sib_5)
-    to = partners(8, count)
-    pairs = [[i, to[i]] for i in range(count >> 1)]
-    pair = lax.all_gather(own_10, AXES, axis_index_groups=pairs, tiled=True)
+        after=(own_10,),
+    )
     return call(
         final_kernel,
         bf16(rows, model),
-        [SMEM, *vmem(6), in_hbm],
-        place, q, num, tot, sib_5, sib_9, pair, stay(w_out),
+        [*vmem(6), in_hbm],
+        q, num, tot, sib_5, sib_9, sib_10, stay(w_out),
         flops=10**9,
         scratch=(
             pltpu.VMEM((rows, model), jnp.bfloat16),

time: 66.1 us -> 66.2 us (level)
  the two profiles are of different devices: /device:TPU:8 before, /device:TPU:6 now
where the time goes in v11:
time: 66.2 us; the launch traced here: 65.8 us
  starting transfers between devices  38.2 us (58%)
  waiting for transfers between devices  10 us (15%)
  Pallas kernels  9.3 us (14%)
  blocking collectives  8.08 us (12%)
    ppermute x7, starting transfers between devices, exchange(): return lax.ppermute(own, AXES, list(enumerate(partners(bit, count))))  18.9 us
    all_to_all x1, starting transfers between devices, per_device(): lax.all_to_all(level_6, AXES, 0, 0, axis_index_groups=teams, tiled=True)  13.8 us
    pallas_call x10, Pallas kernels, call(): pl.pallas_call(body, out_shape=outs, in_specs=list(in_specs) + [pl.BlockS...  9.3 us
    ppermute x7, waiting for transfers between devices, exchange(): return lax.ppermute(own, AXES, list(enumerate(partners(bit, count))))  9.18 us
    all_gather x1, blocking collectives, per_device(): both_3 = lax.all_gather(own_3, AXES, axis_index_groups=z_pairs, tiled=True)  8.08 us
    ppermute x1, starting transfers between devices, per_device(): other_halo = lax.ppermute(other, AXES, swap)  5.51 us
  transfers between devices with their start and end apart: 9, of which 6 were waited for; matrix products, arithmetic and copies ran while one was open for 0% of the time, Pallas kernels for 6%

profile of v11, /device:TPU:6, one launch (start us, length us, event | category | flops | bytes accessed | tf_op | source)
XLA Modules:
  0.0 65.8 jit_solution(8049051529805583601)
XLA Ops:
  0.0 2.9 %shard_map.37 = (bf16[256,1024]{1,0:T(8,128)(2,1)S(1)}, bf16[128,1024]{1,0:T(8,128)(2,1)S(1)}, bf16[64,1024]{1,0:T(8,128)(2,1)S(1)}, bf16[32,1024]{1,0:T(8,128)(2,1)S(1)}, bf16[1024,128]{1,0:T(8,128)(2,1)}) custom-call(s32[1]{0:T(128)} %bitcast.refs_0_, bf16[256,512]{1,0:T(8,128)(2,1)} %refs_1_.3, bf16[512,1536]{1,0:T(8,128)(2,1)} %refs_2_.3), custom_call_target="tpu_custom_call" | custom-call | flops 268435456 | bytes 1048576 | tf_op jit(solution)/shard_map/pallas_call | solution.py:45
  2.9 13.8 %all-to-all-start = ((bf16[32,32,128]{2,1,0:T(8,128)(2,1)}), bf16[32,32,128]{2,1,0:T(8,128)(2,1)S(1)}, u32[]{:S(2)}, u32[]{:S(2)}) async-start(bf16[32,32,128]{2,1,0:T(8,128)(2,1)} %bitcast.1), calls=%async_computation | async-start | bytes 524288 | tf_op jit(solution)/shard_map/all_to_all | solution.py:321
  16.6 1.9 %collective-permute-start = (bf16[128,1024]{1,0:T(8,128)(2,1)S(1)}, bf16[128,1024]{1,0:T(8,128)(2,1)S(1)}, u32[]{:S(2)}, u32[]{:S(2)}) collective-permute-start(bf16[128,1024]{1,0:T(8,128)(2,1)S(1)} %get-tuple-element.15), channel_id=1, source_target_pairs={{0,1},{1,0},{2,3},{3,2},{4,5},{5,4},{6,7},{7,6},{8,9},{9,8},{10,11... | collective-permute-start | bytes 786440 | tf_op jit(solution)/shard_map/ppermute | solution.py:311
  18.6 1.5 %collective-permute-done.refs_1_.refs_4_ = bf16[128,1024]{1,0:T(8,128)(2,1)S(1)} collective-permute-done((bf16[128,1024]{1,0:T(8,128)(2,1)S(1)}, bf16[128,1024]{1,0:T(8,128)(2,1)S(1)}, u32[]{:S(2)}, u32[]{:S(2)}) %collective-permute-start) | collective-permute-done | bytes 262176 | tf_op jit(solution)/shard_map/ppermute | solution.py:311
  20.1 0.1 shard_map.38
  20.2 8.1 %all_gather.3.refs_2_.refs_0_.refs_6_ = bf16[128,1024]{1,0:T(8,128)(2,1)S(1)} all-gather(bf16[64,1024]{1,0:T(8,128)(2,1)S(1)} %shard_map.38), channel_id=1, replica_groups={{0,2},{1,3},{4,6},{5,7},{8,10},{9,11},{12,14},{13,15},{16,18},{17,19},{..., dimensions={0}, use_global_device_ids=true | all-gather | bytes 393216 | tf_op jit(solution)/shard_map/all_gather | solution.py:325
  28.3 0.4 all-to-all-done.refs_1_
  28.6 0.6 shard_map.39.refs_1_.refs_0_.refs_8_
  29.2 1.9 %collective-permute-start.2 = (bf16[96,1024]{1,0:T(8,128)(2,1)S(1)}, bf16[96,1024]{1,0:T(8,128)(2,1)S(1)}, u32[]{:S(2)}, u32[]{:S(2)}) collective-permute-start(bf16[96,1024]{1,0:T(8,128)(2,1)S(1)} %shard_map.39.refs_1_.refs_0_.refs_8_), channel_id=1, source_target_pairs={{0,1},{1,0},{2,3},{3,2},{4,5},{5,4},{6,7},{7,6},{8,9},{9,8},{10,11... | collective-permute-start | bytes 589832 | tf_op jit(solution)/shard_map/ppermute | solution.py:311
  31.1 0.2 shard_map.40.refs_0_
  31.3 4.3 %collective-permute-start.1 = (bf16[64,1024]{1,0:T(8,128)(2,1)S(1)}, bf16[64,1024]{1,0:T(8,128)(2,1)S(1)}, u32[]{:S(2)}, u32[]{:S(2)}) collective-permute-start(bf16[64,1024]{1,0:T(8,128)(2,1)S(1)} %shard_map.40.refs_0_), channel_id=1, source_target_pairs={{0,4},{1,5},{2,6},{3,7},{4,0},{5,1},{6,2},{7,3},{8,12},{9,13},{10,... | collective-permute-start | bytes 393224 | tf_op jit(solution)/shard_map/ppermute | solution.py:311
  35.7 4.4 %collective-permute-start.4 = (bf16[64,1024]{1,0:T(8,128)(2,1)S(1)}, bf16[64,1024]{1,0:T(8,128)(2,1)S(1)}, u32[]{:S(2)}, u32[]{:S(2)}) collective-permute-start(bf16[64,1024]{1,0:T(8,128)(2,1)S(1)} %shard_map.41.refs_2_.refs_0_), channel_id=1, source_target_pairs={{0,96},{1,97},{2,98},{3,99},{4,100},{5,101},{6,102},{7,103},{8,104... | collective-permute-start | bytes 393224 | tf_op jit(solution)/shard_map/ppermute | solution.py:311
  40.1 2.7 %collective-permute-done.1.refs_1_.refs_7_ = bf16[64,1024]{1,0:T(8,128)(2,1)S(1)} collective-permute-done((bf16[64,1024]{1,0:T(8,128)(2,1)S(1)}, bf16[64,1024]{1,0:T(8,128)(2,1)S(1)}, u32[]{:S(2)}, u32[]{:S(2)}) %collective-permute-start.1) | collective-permute-done | bytes 131104 | tf_op jit(solution)/shard_map/ppermute | solution.py:311
  42.8 0.2 shard_map.42.refs_2_
  43.0 5.5 %collective-permute-start.3 = (bf16[64,1024]{1,0:T(8,128)(2,1)S(1)}, bf16[64,1024]{1,0:T(8,128)(2,1)S(1)}, u32[]{:S(2)}, u32[]{:S(2)}) collective-permute-start(bf16[64,1024]{1,0:T(8,128)(2,1)S(1)} %get-tuple-element.19), channel_id=1, source_target_pairs={{1,2},{3,4},{5,6},{7,8},{9,10},{11,12},{13,14},{15,16},{17,18},{19... | collective-permute-start | bytes 393224 | tf_op jit(solution)/shard_map/ppermute | solution.py:339
  48.6 2.4 %collective-permute-start.5 = (bf16[64,1024]{1,0:T(8,128)(2,1)S(1)}, bf16[64,1024]{1,0:T(8,128)(2,1)S(1)}, u32[]{:S(2)}, u32[]{:S(2)}) collective-permute-start(bf16[64,1024]{1,0:T(8,128)(2,1)S(1)} %shard_map.43.refs_0_), channel_id=1, source_target_pairs={{0,128},{1,129},{2,130},{3,131},{4,132},{5,133},{6,134},{7,135},{8... | collective-permute-start | bytes 393224 | tf_op jit(solution)/shard_map/ppermute | solution.py:311
  51.0 2.0 %collective-permute-start.6 = (bf16[64,1024]{1,0:T(8,128)(2,1)S(1)}, bf16[64,1024]{1,0:T(8,128)(2,1)S(1)}, u32[]{:S(2)}, u32[]{:S(2)}) collective-permute-start(bf16[64,1024]{1,0:T(8,128)(2,1)S(1)} %shard_map.42.refs_2_), channel_id=1, source_target_pairs={{0,12},{1,13},{2,14},{3,15},{4,8},{5,9},{6,10},{7,11},{8,4},{9,5},... | collective-permute-start | bytes 393224 | tf_op jit(solution)/shard_map/ppermute | solution.py:311
  53.0 0.5 collective-permute-done.3.refs_2_.refs_5_
  53.5 1.9 %collective-permute-done.5.refs_1_.refs_4_ = bf16[64,1024]{1,0:T(8,128)(2,1)S(1)} collective-permute-done((bf16[64,1024]{1,0:T(8,128)(2,1)S(1)}, bf16[64,1024]{1,0:T(8,128)(2,1)S(1)}, u32[]{:S(2)}, u32[]{:S(2)}) %collective-permute-start.5) | collective-permute-done | bytes 131104 | tf_op jit(solution)/shard_map/ppermute | solution.py:311
  55.4 0.2 shard_map.44.refs_11_
  55.6 1.9 %collective-permute-start.7 = (bf16[64,1024]{1,0:T(8,128)(2,1)S(1)}, bf16[64,1024]{1,0:T(8,128)(2,1)S(1)}, u32[]{:S(2)}, u32[]{:S(2)}) collective-permute-start(bf16[64,1024]{1,0:T(8,128)(2,1)S(1)} %shard_map.44.refs_11_), channel_id=1, source_target_pairs={{0,384},{1,385},{2,386},{3,387},{4,388},{5,389},{6,390},{7,391},{8... | collective-permute-start | bytes 393224 | tf_op jit(solution)/shard_map/ppermute | solution.py:311
  57.5 3.1 %shard_map.45 = (bf16[256,512]{1,0:T(8,128)(2,1)S(1)}, f32[256,512]{1,0:T(8,128)S(1)}, f32[256,512]{1,0:T(8,128)S(1)}) custom-call(s32[1]{0:T(128)} %bitcast.refs_0_, bf16[256,512]{1,0:T(8,128)(2,1)S(1)} %copy-done, bf16[512,1536]{1,0:T(8,128)(2,1)} %refs_2_.3, bf16[256,1024]{1,0:T(8,128)(2,1)S(1)} %get-tuple-element.14.refs_3_, ...), custom_call_target="tpu_custom_call" | custom-call | flops 1000000000 | bytes 1048576 | tf_op jit(solution)/shard_map/pallas_call | solution.py:45
  60.7 3.0 %collective-permute-done.7.refs_5_ = bf16[64,1024]{1,0:T(8,128)(2,1)S(1)} collective-permute-done((bf16[64,1024]{1,0:T(8,128)(2,1)S(1)}, bf16[64,1024]{1,0:T(8,128)(2,1)S(1)}, u32[]{:S(2)}, u32[]{:S(2)}) %collective-permute-start.7) | collective-permute-done | bytes 131104 | tf_op jit(solution)/shard_map/ppermute | solution.py:311
  63.7 2.1 %shard_map.46 = bf16[256,512]{1,0:T(8,128)(2,1)} custom-call(bf16[256,512]{1,0:T(8,128)(2,1)S(1)} %get-tuple-element.20.refs_0_, f32[256,512]{1,0:T(8,128)S(1)} %get-tuple-element.21.refs_1_, f32[256,512]{1,0:T(8,128)S(1)} %get-tuple-element.22.refs_2_, bf16[64,1024]{1,0:T(8,128)(2,1)S(1)} %collective-permute-done.6.refs_3_, ...), custom_call_target="tpu_custom_call" | custom-call | flops 1000000000 | bytes 1048576 | tf_op jit(solution)/shard_map/pallas_call | solution.py:45
  (7 shorter events, 0.1 us)
Async XLA Ops:
  2.9 25.8 %all-to-all-start = ((bf16[32,32,128]{2,1,0:T(8,128)(2,1)}), bf16[32,32,128]{2,1,0:T(8,128)(2,1)S(1)}, u32[]{:S(2)}, u32[]{:S(2)}) async-start(bf16[32,32,128]{2,1,0:T(8,128)(2,1)} %bitcast.1), calls=%async_computation | async-start | bytes 524288 | tf_op jit(solution)/shard_map/all_to_all | solution.py:321
  16.6 3.4 %collective-permute-start = (bf16[128,1024]{1,0:T(8,128)(2,1)S(1)}, bf16[128,1024]{1,0:T(8,128)(2,1)S(1)}, u32[]{:S(2)}, u32[]{:S(2)}) collective-permute-start(bf16[128,1024]{1,0:T(8,128)(2,1)S(1)} %get-tuple-element.15), channel_id=1, source_target_pairs={{0,1},{1,0},{2,3},{3,2},{4,5},{5,4},{6,7},{7,6},{8,9},{9,8},{10,11... | collective-permute-start | bytes 786440 | tf_op jit(solution)/shard_map/ppermute | solution.py:311
  28.3 29.2 %copy-start = (bf16[256,512]{1,0:T(8,128)(2,1)S(1)}, bf16[256,512]{1,0:T(8,128)(2,1)}, u32[]{:S(2)}) copy-start(bf16[256,512]{1,0:T(8,128)(2,1)} %refs_1_.3) | copy-start | bytes 786436
  29.2 6.4 %collective-permute-start.2 = (bf16[96,1024]{1,0:T(8,128)(2,1)S(1)}, bf16[96,1024]{1,0:T(8,128)(2,1)S(1)}, u32[]{:S(2)}, u32[]{:S(2)}) collective-permute-start(bf16[96,1024]{1,0:T(8,128)(2,1)S(1)} %shard_map.39.refs_1_.refs_0_.refs_8_), channel_id=1, source_target_pairs={{0,1},{1,0},{2,3},{3,2},{4,5},{5,4},{6,7},{7,6},{8,9},{9,8},{10,11... | collective-permute-start | bytes 589832 | tf_op jit(solution)/shard_map/ppermute | solution.py:311
  31.3 11.5 %collective-permute-start.1 = (bf16[64,1024]{1,0:T(8,128)(2,1)S(1)}, bf16[64,1024]{1,0:T(8,128)(2,1)S(1)}, u32[]{:S(2)}, u32[]{:S(2)}) collective-permute-start(bf16[64,1024]{1,0:T(8,128)(2,1)S(1)} %shard_map.40.refs_0_), channel_id=1, source_target_pairs={{0,4},{1,5},{2,6},{3,7},{4,0},{5,1},{6,2},{7,3},{8,12},{9,13},{10,... | collective-permute-start | bytes 393224 | tf_op jit(solution)/shard_map/ppermute | solution.py:311
  35.7 12.8 %collective-permute-start.4 = (bf16[64,1024]{1,0:T(8,128)(2,1)S(1)}, bf16[64,1024]{1,0:T(8,128)(2,1)S(1)}, u32[]{:S(2)}, u32[]{:S(2)}) collective-permute-start(bf16[64,1024]{1,0:T(8,128)(2,1)S(1)} %shard_map.41.refs_2_.refs_0_), channel_id=1, source_target_pairs={{0,96},{1,97},{2,98},{3,99},{4,100},{5,101},{6,102},{7,103},{8,104... | collective-permute-start | bytes 393224 | tf_op jit(solution)/shard_map/ppermute | solution.py:311
  43.0 10.5 %collective-permute-start.3 = (bf16[64,1024]{1,0:T(8,128)(2,1)S(1)}, bf16[64,1024]{1,0:T(8,128)(2,1)S(1)}, u32[]{:S(2)}, u32[]{:S(2)}) collective-permute-start(bf16[64,1024]{1,0:T(8,128)(2,1)S(1)} %get-tuple-element.19), channel_id=1, source_target_pairs={{1,2},{3,4},{5,6},{7,8},{9,10},{11,12},{13,14},{15,16},{17,18},{19... | collective-permute-start | bytes 393224 | tf_op jit(solution)/shard_map/ppermute | solution.py:339
  48.6 6.9 %collective-permute-start.5 = (bf16[64,1024]{1,0:T(8,128)(2,1)S(1)}, bf16[64,1024]{1,0:T(8,128)(2,1)S(1)}, u32[]{:S(2)}, u32[]{:S(2)}) collective-permute-start(bf16[64,1024]{1,0:T(8,128)(2,1)S(1)} %shard_map.43.refs_0_), channel_id=1, source_target_pairs={{0,128},{1,129},{2,130},{3,131},{4,132},{5,133},{6,134},{7,135},{8... | collective-permute-start | bytes 393224 | tf_op jit(solution)/shard_map/ppermute | solution.py:311
  51.0 9.6 %collective-permute-start.6 = (bf16[64,1024]{1,0:T(8,128)(2,1)S(1)}, bf16[64,1024]{1,0:T(8,128)(2,1)S(1)}, u32[]{:S(2)}, u32[]{:S(2)}) collective-permute-start(bf16[64,1024]{1,0:T(8,128)(2,1)S(1)} %shard_map.42.refs_2_), channel_id=1, source_target_pairs={{0,12},{1,13},{2,14},{3,15},{4,8},{5,9},{6,10},{7,11},{8,4},{9,5},... | collective-permute-start | bytes 393224 | tf_op jit(solution)/shard_map/ppermute | solution.py:311
  55.6 8.1 %collective-permute-start.7 = (bf16[64,1024]{1,0:T(8,128)(2,1)S(1)}, bf16[64,1024]{1,0:T(8,128)(2,1)S(1)}, u32[]{:S(2)}, u32[]{:S(2)}) collective-permute-start(bf16[64,1024]{1,0:T(8,128)(2,1)S(1)} %shard_map.44.refs_11_), channel_id=1, source_target_pairs={{0,384},{1,385},{2,386},{3,387},{4,388},{5,389},{6,390},{7,391},{8... | collective-permute-start | bytes 393224 | tf_op jit(solution)/shard_map/ppermute | solution.py:311

commit v12 on v11

--- a/solution.py
+++ b/solution.py
@@ -323,11 +323,12 @@
     own_3 = call(pool_near_kernel, block, vmem(2), level_3, near_sib)
     z_pairs = [[i, i ^ 2] for i in range(count) if not i & 2]
     both_3 = lax.all_gather(own_3, AXES, axis_index_groups=z_pairs, tiled=True)
+    other_halo = lax.ppermute(other, AXES, swap)
     mine = call(
         unpack_kernel, bf16(3 * BLOCK // 2, 2 * model), [SMEM, *vmem(1)],
         place, spread.reshape(members, packed, 128),
         scratch=(pltpu.VMEM((members * packed, 128), jnp.float32),),
-        after=(both_3,),
+        after=(both_3, other_halo),
     )
     theirs = exchange(mine, 0)
     own_4 = call(pool_kernel, block, vmem(1), both_3, after=(mine,))
@@ -335,12 +336,10 @@
     own_8 = call(own_8_kernel, block, vmem(2), mine, theirs)
     sib_8 = exchange(own_8, 6)
     own_5 = pool(own_4, sib_4, own_8)
-    other, _ = lax.optimization_barrier((other, own_5))
-    other_halo = lax.ppermute(other, AXES, swap)
     sib_5 = exchange(own_5, 3)
     own_9 = call(pool_halves_kernel, block, vmem(2), own_8, sib_8, after=(own_5,))
     sib_9 = exchange(own_9, 7)
-    own_10 = pool(own_9, sib_9, other_halo)
+    own_10 = pool(own_9, sib_9)
     sib_10 = exchange(own_10, 8)
     q, num, tot = call(
         functools.partial(local_kernel, count),

time: 66.2 us -> 67.8 us (1.024)
  the two profiles are of different devices: /device:TPU:6 before, /device:TPU:8 now
where the time goes in v12:
time: 67.8 us; the launch traced here: 67.3 us
  starting transfers between devices  43.9 us (65%)
  Pallas kernels  9.31 us (14%)
  waiting for transfers between devices  8.21 us (12%)
  blocking collectives  5.64 us (8%)
    ppermute x7, starting transfers between devices, exchange(): return lax.ppermute(own, AXES, list(enumerate(partners(bit, count))))  25.3 us
    all_to_all x1, starting transfers between devices, per_device(): lax.all_to_all(level_6, AXES, 0, 0, axis_index_groups=teams, tiled=True)  14 us
    pallas_call x10, Pallas kernels, call(): pl.pallas_call(body, out_shape=outs, in_specs=list(in_specs) + [pl.BlockS...  9.31 us
    ppermute x7, waiting for transfers between devices, exchange(): return lax.ppermute(own, AXES, list(enumerate(partners(bit, count))))  8.2 us
    all_gather x1, blocking collectives, per_device(): both_3 = lax.all_gather(own_3, AXES, axis_index_groups=z_pairs, tiled=True)  5.64 us
    ppermute x1, starting transfers between devices, per_device(): other_halo = lax.ppermute(other, AXES, swap)  4.68 us
  transfers between devices with their start and end apart: 9, of which 3 were waited for; matrix products, arithmetic and copies ran while one was open for 0% of the time, Pallas kernels for 6%

profile of v12, /device:TPU:8, one launch (start us, length us, event | category | flops | bytes accessed | tf_op | source)
XLA Modules:
  0.0 67.3 jit_solution(8522139464931895834)
XLA Ops:
  0.0 2.9 %shard_map.37 = (bf16[256,1024]{1,0:T(8,128)(2,1)S(1)}, bf16[128,1024]{1,0:T(8,128)(2,1)S(1)}, bf16[64,1024]{1,0:T(8,128)(2,1)S(1)}, bf16[32,1024]{1,0:T(8,128)(2,1)S(1)}, bf16[1024,128]{1,0:T(8,128)(2,1)}) custom-call(s32[1]{0:T(128)} %bitcast.refs_0_, bf16[256,512]{1,0:T(8,128)(2,1)} %refs_1_.3, bf16[512,1536]{1,0:T(8,128)(2,1)} %refs_2_.3), custom_call_target="tpu_custom_call" | custom-call | flops 268435456 | bytes 1048576 | tf_op jit(solution)/shard_map/pallas_call | solution.py:45
  2.9 14.0 %all-to-all-start = ((bf16[32,32,128]{2,1,0:T(8,128)(2,1)}), bf16[32,32,128]{2,1,0:T(8,128)(2,1)S(1)}, u32[]{:S(2)}, u32[]{:S(2)}) async-start(bf16[32,32,128]{2,1,0:T(8,128)(2,1)} %bitcast.1), calls=%async_computation | async-start | bytes 524288 | tf_op jit(solution)/shard_map/all_to_all | solution.py:321
  16.8 1.9 %collective-permute-start = (bf16[128,1024]{1,0:T(8,128)(2,1)S(1)}, bf16[128,1024]{1,0:T(8,128)(2,1)S(1)}, u32[]{:S(2)}, u32[]{:S(2)}) collective-permute-start(bf16[128,1024]{1,0:T(8,128)(2,1)S(1)} %get-tuple-element.14), channel_id=1, source_target_pairs={{0,1},{1,0},{2,3},{3,2},{4,5},{5,4},{6,7},{7,6},{8,9},{9,8},{10,11... | collective-permute-start | bytes 786440 | tf_op jit(solution)/shard_map/ppermute | solution.py:311
  18.8 4.7 %collective-permute-start.1 = (bf16[64,1024]{1,0:T(8,128)(2,1)S(1)}, bf16[64,1024]{1,0:T(8,128)(2,1)S(1)}, u32[]{:S(2)}, u32[]{:S(2)}) collective-permute-start(bf16[64,1024]{1,0:T(8,128)(2,1)S(1)} %get-tuple-element.15), channel_id=1, source_target_pairs={{1,2},{3,4},{5,6},{7,8},{9,10},{11,12},{13,14},{15,16},{17,18},{19... | collective-permute-start | bytes 393224 | tf_op jit(solution)/shard_map/ppermute | solution.py:326
  23.5 0.0 collective-permute-done.refs_1_.refs_4_
  23.5 0.1 shard_map.38
  23.6 5.6 %all_gather.3.refs_2_.refs_0_.refs_6_ = bf16[128,1024]{1,0:T(8,128)(2,1)S(1)} all-gather(bf16[64,1024]{1,0:T(8,128)(2,1)S(1)} %shard_map.38), channel_id=1, replica_groups={{0,2},{1,3},{4,6},{5,7},{8,10},{9,11},{12,14},{13,15},{16,18},{17,19},{..., dimensions={0}, use_global_device_ids=true | all-gather | bytes 393216 | tf_op jit(solution)/shard_map/all_gather | solution.py:325
  29.3 0.0 collective-permute-done.1.refs_3_.refs_5_
  29.3 0.6 shard_map.39.refs_1_.refs_0_.refs_8_
  29.9 1.9 %collective-permute-start.3 = (bf16[96,1024]{1,0:T(8,128)(2,1)S(1)}, bf16[96,1024]{1,0:T(8,128)(2,1)S(1)}, u32[]{:S(2)}, u32[]{:S(2)}) collective-permute-start(bf16[96,1024]{1,0:T(8,128)(2,1)S(1)} %shard_map.39.refs_1_.refs_0_.refs_8_), channel_id=1, source_target_pairs={{0,1},{1,0},{2,3},{3,2},{4,5},{5,4},{6,7},{7,6},{8,9},{9,8},{10,11... | collective-permute-start | bytes 589832 | tf_op jit(solution)/shard_map/ppermute | solution.py:311
  31.8 0.2 shard_map.40.refs_0_
  32.0 4.9 %collective-permute-start.2 = (bf16[64,1024]{1,0:T(8,128)(2,1)S(1)}, bf16[64,1024]{1,0:T(8,128)(2,1)S(1)}, u32[]{:S(2)}, u32[]{:S(2)}) collective-permute-start(bf16[64,1024]{1,0:T(8,128)(2,1)S(1)} %shard_map.40.refs_0_), channel_id=1, source_target_pairs={{0,4},{1,5},{2,6},{3,7},{4,0},{5,1},{6,2},{7,3},{8,12},{9,13},{10,... | collective-permute-start | bytes 393224 | tf_op jit(solution)/shard_map/ppermute | solution.py:311
  36.9 4.8 %collective-permute-start.4 = (bf16[64,1024]{1,0:T(8,128)(2,1)S(1)}, bf16[64,1024]{1,0:T(8,128)(2,1)S(1)}, u32[]{:S(2)}, u32[]{:S(2)}) collective-permute-start(bf16[64,1024]{1,0:T(8,128)(2,1)S(1)} %shard_map.41.refs_2_.refs_0_), channel_id=1, source_target_pairs={{0,96},{1,97},{2,98},{3,99},{4,100},{5,101},{6,102},{7,103},{8,104... | collective-permute-start | bytes 393224 | tf_op jit(solution)/shard_map/ppermute | solution.py:311
  41.7 2.1 %collective-permute-done.2.refs_1_.refs_7_ = bf16[64,1024]{1,0:T(8,128)(2,1)S(1)} collective-permute-done((bf16[64,1024]{1,0:T(8,128)(2,1)S(1)}, bf16[64,1024]{1,0:T(8,128)(2,1)S(1)}, u32[]{:S(2)}, u32[]{:S(2)}) %collective-permute-start.2) | collective-permute-done | bytes 131104 | tf_op jit(solution)/shard_map/ppermute | solution.py:311
  43.8 0.2 shard_map.42.refs_2_
  44.0 5.3 %collective-permute-done.4.refs_1_.refs_10_ = bf16[64,1024]{1,0:T(8,128)(2,1)S(1)} collective-permute-done((bf16[64,1024]{1,0:T(8,128)(2,1)S(1)}, bf16[64,1024]{1,0:T(8,128)(2,1)S(1)}, u32[]{:S(2)}, u32[]{:S(2)}) %collective-permute-start.4) | collective-permute-done | bytes 131104 | tf_op jit(solution)/shard_map/ppermute | solution.py:311
  49.4 3.4 %collective-permute-start.5 = (bf16[64,1024]{1,0:T(8,128)(2,1)S(1)}, bf16[64,1024]{1,0:T(8,128)(2,1)S(1)}, u32[]{:S(2)}, u32[]{:S(2)}) collective-permute-start(bf16[64,1024]{1,0:T(8,128)(2,1)S(1)} %shard_map.43.refs_0_), channel_id=1, source_target_pairs={{0,128},{1,129},{2,130},{3,131},{4,132},{5,133},{6,134},{7,135},{8... | collective-permute-start | bytes 393224 | tf_op jit(solution)/shard_map/ppermute | solution.py:311
  52.8 4.1 %collective-permute-start.6 = (bf16[64,1024]{1,0:T(8,128)(2,1)S(1)}, bf16[64,1024]{1,0:T(8,128)(2,1)S(1)}, u32[]{:S(2)}, u32[]{:S(2)}) collective-permute-start(bf16[64,1024]{1,0:T(8,128)(2,1)S(1)} %shard_map.42.refs_2_), channel_id=1, source_target_pairs={{0,12},{1,13},{2,14},{3,15},{4,8},{5,9},{6,10},{7,11},{8,4},{9,5},... | collective-permute-start | bytes 393224 | tf_op jit(solution)/shard_map/ppermute | solution.py:311
  56.9 0.2 shard_map.44.refs_11_
  57.1 4.2 %collective-permute-start.7 = (bf16[64,1024]{1,0:T(8,128)(2,1)S(1)}, bf16[64,1024]{1,0:T(8,128)(2,1)S(1)}, u32[]{:S(2)}, u32[]{:S(2)}) collective-permute-start(bf16[64,1024]{1,0:T(8,128)(2,1)S(1)} %shard_map.44.refs_11_), channel_id=1, source_target_pairs={{0,384},{1,385},{2,386},{3,387},{4,388},{5,389},{6,390},{7,391},{8... | collective-permute-start | bytes 393224 | tf_op jit(solution)/shard_map/ppermute | solution.py:311
  61.3 3.1 %shard_map.45 = (bf16[256,512]{1,0:T(8,128)(2,1)S(1)}, f32[256,512]{1,0:T(8,128)S(1)}, f32[256,512]{1,0:T(8,128)S(1)}) custom-call(s32[1]{0:T(128)} %bitcast.refs_0_, bf16[256,512]{1,0:T(8,128)(2,1)S(1)} %copy-done, bf16[512,1536]{1,0:T(8,128)(2,1)} %refs_2_.3, bf16[256,1024]{1,0:T(8,128)(2,1)S(1)} %get-tuple-element.13.refs_3_, ...), custom_call_target="tpu_custom_call" | custom-call | flops 1000000000 | bytes 1048576 | tf_op jit(solution)/shard_map/pallas_call | solution.py:45
  64.4 0.0 collective-permute-done.6.refs_3_
  64.4 0.7 %collective-permute-done.7.refs_5_ = bf16[64,1024]{1,0:T(8,128)(2,1)S(1)} collective-permute-done((bf16[64,1024]{1,0:T(8,128)(2,1)S(1)}, bf16[64,1024]{1,0:T(8,128)(2,1)S(1)}, u32[]{:S(2)}, u32[]{:S(2)}) %collective-permute-start.7) | collective-permute-done | bytes 131104 | tf_op jit(solution)/shard_map/ppermute | solution.py:311
  65.2 2.1 %shard_map.46 = bf16[256,512]{1,0:T(8,128)(2,1)} custom-call(bf16[256,512]{1,0:T(8,128)(2,1)S(1)} %get-tuple-element.18.refs_0_, f32[256,512]{1,0:T(8,128)S(1)} %get-tuple-element.19.refs_1_, f32[256,512]{1,0:T(8,128)S(1)} %get-tuple-element.20.refs_2_, bf16[64,1024]{1,0:T(8,128)(2,1)S(1)} %collective-permute-done.6.refs_3_, ...), custom_call_target="tpu_custom_call" | custom-call | flops 1000000000 | bytes 1048576 | tf_op jit(solution)/shard_map/pallas_call | solution.py:45
  (7 shorter events, 0.1 us)
Async XLA Ops:
  2.9 26.4 %all-to-all-start = ((bf16[32,32,128]{2,1,0:T(8,128)(2,1)}), bf16[32,32,128]{2,1,0:T(8,128)(2,1)S(1)}, u32[]{:S(2)}, u32[]{:S(2)}) async-start(bf16[32,32,128]{2,1,0:T(8,128)(2,1)} %bitcast.1), calls=%async_computation | async-start | bytes 524288 | tf_op jit(solution)/shard_map/all_to_all | solution.py:321
  16.8 6.6 %collective-permute-start = (bf16[128,1024]{1,0:T(8,128)(2,1)S(1)}, bf16[128,1024]{1,0:T(8,128)(2,1)S(1)}, u32[]{:S(2)}, u32[]{:S(2)}) collective-permute-start(bf16[128,1024]{1,0:T(8,128)(2,1)S(1)} %get-tuple-element.14), channel_id=1, source_target_pairs={{0,1},{1,0},{2,3},{3,2},{4,5},{5,4},{6,7},{7,6},{8,9},{9,8},{10,11... | collective-permute-start | bytes 786440 | tf_op jit(solution)/shard_map/ppermute | solution.py:311
  18.8 10.5 %collective-permute-start.1 = (bf16[64,1024]{1,0:T(8,128)(2,1)S(1)}, bf16[64,1024]{1,0:T(8,128)(2,1)S(1)}, u32[]{:S(2)}, u32[]{:S(2)}) collective-permute-start(bf16[64,1024]{1,0:T(8,128)(2,1)S(1)} %get-tuple-element.15), channel_id=1, source_target_pairs={{1,2},{3,4},{5,6},{7,8},{9,10},{11,12},{13,14},{15,16},{17,18},{19... | collective-permute-start | bytes 393224 | tf_op jit(solution)/shard_map/ppermute | solution.py:326
  29.3 32.0 %copy-start = (bf16[256,512]{1,0:T(8,128)(2,1)S(1)}, bf16[256,512]{1,0:T(8,128)(2,1)}, u32[]{:S(2)}) copy-start(bf16[256,512]{1,0:T(8,128)(2,1)} %refs_1_.3) | copy-start | bytes 786436
  29.9 7.0 %collective-permute-start.3 = (bf16[96,1024]{1,0:T(8,128)(2,1)S(1)}, bf16[96,1024]{1,0:T(8,128)(2,1)S(1)}, u32[]{:S(2)}, u32[]{:S(2)}) collective-permute-start(bf16[96,1024]{1,0:T(8,128)(2,1)S(1)} %shard_map.39.refs_1_.refs_0_.refs_8_), channel_id=1, source_target_pairs={{0,1},{1,0},{2,3},{3,2},{4,5},{5,4},{6,7},{7,6},{8,9},{9,8},{10,11... | collective-permute-start | bytes 589832 | tf_op jit(solution)/shard_map/ppermute | solution.py:311
  32.0 11.9 %collective-permute-start.2 = (bf16[64,1024]{1,0:T(8,128)(2,1)S(1)}, bf16[64,1024]{1,0:T(8,128)(2,1)S(1)}, u32[]{:S(2)}, u32[]{:S(2)}) collective-permute-start(bf16[64,1024]{1,0:T(8,128)(2,1)S(1)} %shard_map.40.refs_0_), channel_id=1, source_target_pairs={{0,4},{1,5},{2,6},{3,7},{4,0},{5,1},{6,2},{7,3},{8,12},{9,13},{10,... | collective-permute-start | bytes 393224 | tf_op jit(solution)/shard_map/ppermute | solution.py:311
  36.9 12.4 %collective-permute-start.4 = (bf16[64,1024]{1,0:T(8,128)(2,1)S(1)}, bf16[64,1024]{1,0:T(8,128)(2,1)S(1)}, u32[]{:S(2)}, u32[]{:S(2)}) collective-permute-start(bf16[64,1024]{1,0:T(8,128)(2,1)S(1)} %shard_map.41.refs_2_.refs_0_), channel_id=1, source_target_pairs={{0,96},{1,97},{2,98},{3,99},{4,100},{5,101},{6,102},{7,103},{8,104... | collective-permute-start | bytes 393224 | tf_op jit(solution)/shard_map/ppermute | solution.py:311
  49.4 7.6 %collective-permute-start.5 = (bf16[64,1024]{1,0:T(8,128)(2,1)S(1)}, bf16[64,1024]{1,0:T(8,128)(2,1)S(1)}, u32[]{:S(2)}, u32[]{:S(2)}) collective-permute-start(bf16[64,1024]{1,0:T(8,128)(2,1)S(1)} %shard_map.43.refs_0_), channel_id=1, source_target_pairs={{0,128},{1,129},{2,130},{3,131},{4,132},{5,133},{6,134},{7,135},{8... | collective-permute-start | bytes 393224 | tf_op jit(solution)/shard_map/ppermute | solution.py:311
  52.8 11.7 %collective-permute-start.6 = (bf16[64,1024]{1,0:T(8,128)(2,1)S(1)}, bf16[64,1024]{1,0:T(8,128)(2,1)S(1)}, u32[]{:S(2)}, u32[]{:S(2)}) collective-permute-start(bf16[64,1024]{1,0:T(8,128)(2,1)S(1)} %shard_map.42.refs_2_), channel_id=1, source_target_pairs={{0,12},{1,13},{2,14},{3,15},{4,8},{5,9},{6,10},{7,11},{8,4},{9,5},... | collective-permute-start | bytes 393224 | tf_op jit(solution)/shard_map/ppermute | solution.py:311
  57.1 8.1 %collective-permute-start.7 = (bf16[64,1024]{1,0:T(8,128)(2,1)S(1)}, bf16[64,1024]{1,0:T(8,128)(2,1)S(1)}, u32[]{:S(2)}, u32[]{:S(2)}) collective-permute-start(bf16[64,1024]{1,0:T(8,128)(2,1)S(1)} %shard_map.44.refs_11_), channel_id=1, source_target_pairs={{0,384},{1,385},{2,386},{3,387},{4,388},{5,389},{6,390},{7,391},{8... | collective-permute-start | bytes 393224 | tf_op jit(solution)/shard_map/ppermute | solution.py:311

commit v13 on v12

--- a/solution.py
+++ b/solution.py
@@ -190,8 +190,8 @@
 
 
 def local_kernel(
-    count, place, x_ref, w_hbm, kv_ref, near_ref, other_ref, both_3_ref, sib_4_ref,
-    mine_ref, theirs_ref, sib_8_ref, q_ref, num_ref, tot_ref, pad, l1, w_ref, sem
+    count, place, x_ref, w_hbm, kv_ref, near_ref, other_ref, both_3_ref,
+    mine_ref, theirs_ref, q_ref, num_ref, tot_ref, pad, l1, w_ref, sem
 ):
     rows, model = x_ref.shape
     blocks = rows // BLOCK
@@ -234,7 +234,7 @@
             tot_ref[here, kl] = tot
     start = pl.multiple_of((1 - ((place[0] >> 1) & 1)) * BLOCK, BLOCK)
     sib_3 = both_3_ref[pl.ds(start, BLOCK), :]
-    far = far_blocks((near_ref, sib_3, sib_4_ref, mine_ref, theirs_ref, sib_8_ref))
+    far = far_blocks((near_ref, sib_3, mine_ref, theirs_ref))
     for lanes in range(0, model, 128):
         kl = slice(lanes, lanes + 128)
         num, tot = far_sums(far, q_ref[:, kl], lanes, model)
@@ -258,13 +258,24 @@
     return attend_pair(q, keys, values, jnp.ones(values.shape, jnp.bfloat16))
 
 
+def far_kernel(q_ref, num_in, tot_in, *refs):
+    num_ref, tot_ref = refs[-2:]
+    model = q_ref.shape[1]
+    far = far_blocks(refs[:-2])
+    for lanes in range(0, model, 128):
+        at = slice(lanes, lanes + 128)
+        num, tot = far_sums(far, q_ref[:, at], lanes, model)
+        num_ref[:, at] = num_in[:, at] + num
+        tot_ref[:, at] = tot_in[:, at] + tot
+
+
 def final_kernel(
-    q_ref, num_in, tot_in, sib_5_ref, sib_9_ref, sib_10_ref, w_hbm, out_ref, att, w_ref, sem
+    q_ref, num_in, tot_in, sib_5_ref, sib_10_ref, w_hbm, out_ref, att, w_ref, sem
 ):
     copy = pltpu.make_async_copy(w_hbm, w_ref, sem)
     copy.start()
     model = q_ref.shape[1]
-    far = far_blocks((sib_5_ref, sib_9_ref, sib_10_ref))
+    far = far_blocks((sib_5_ref, sib_10_ref))
     for lanes in range(0, model, 128):
         at = slice(lanes, lanes + 128)
         num, tot = far_sums(far, q_ref[:, at], lanes, model)
@@ -331,21 +342,15 @@
         after=(both_3, other_halo),
     )
     theirs = exchange(mine, 0)
-    own_4 = call(pool_kernel, block, vmem(1), both_3, after=(mine,))
-    sib_4 = exchange(own_4, 2)
     own_8 = call(own_8_kernel, block, vmem(2), mine, theirs)
     sib_8 = exchange(own_8, 6)
-    own_5 = pool(own_4, sib_4, own_8)
-    sib_5 = exchange(own_5, 3)
-    own_9 = call(pool_halves_kernel, block, vmem(2), own_8, sib_8, after=(own_5,))
-    sib_9 = exchange(own_9, 7)
-    own_10 = pool(own_9, sib_9)
-    sib_10 = exchange(own_10, 8)
+    own_4 = call(pool_kernel, block, vmem(1), both_3, after=(own_8,))
+    sib_4 = exchange(own_4, 2)
     q, num, tot = call(
         functools.partial(local_kernel, count),
         (bf16(rows, model), f32(rows, model), f32(rows, model)),
-        [SMEM, *vmem(1), in_hbm, *vmem(8)],
-        place, tokens, stay(w_qkv), kv, near_sib, other_halo, both_3, sib_4, mine, theirs, sib_8,
+        [SMEM, *vmem(1), in_hbm, *vmem(6)],
+        place, tokens, stay(w_qkv), kv, near_sib, other_halo, both_3, mine, theirs,
         flops=10**9,
         scratch=(
             pltpu.VMEM((rows + 2 * BLOCK, 2 * model), jnp.bfloat16),
@@ -353,13 +358,27 @@
             pltpu.VMEM((model, model), jnp.bfloat16),
             pltpu.SemaphoreType.DMA(()),
         ),
+        after=(own_4,),
+    )
+    own_9 = call(pool_halves_kernel, block, vmem(2), own_8, sib_8, after=(q,))
+    sib_9 = exchange(own_9, 7)
+    own_5 = pool(own_4, sib_4, own_9)
+    sib_5 = exchange(own_5, 3)
+    own_10 = pool(own_9, sib_9, own_5)
+    sib_10 = exchange(own_10, 8)
+    num, tot = call(
+        far_kernel,
+        (f32(rows, model), f32(rows, model)),
+        vmem(6),
+        q, num, tot, sib_4, sib_8, sib_9,
+        flops=10**9,
         after=(own_10,),
     )
     return call(
         final_kernel,
         bf16(rows, model),
-        [*vmem(6), in_hbm],
-        q, num, tot, sib_5, sib_9, sib_10, stay(w_out),
+        [*vmem(5), in_hbm],
+        q, num, tot, sib_5, sib_10, stay(w_out),
         flops=10**9,
         scratch=(
             pltpu.VMEM((rows, model), jnp.bfloat16),

time: 67.8 us -> 65.1 us (0.960)
  waiting for transfers between devices: 8.21 us -> 4.64 us
    ppermute x7, waiting for transfers between devices: 8.2 us -> 4.64 us  [exchange(): return lax.ppermute(own, AXES, list(enumerate(partners(bit, count))))]
    pallas_call x10 -> x11, Pallas kernels: 9.31 us -> 9.83 us  [call(): pl.pallas_call(body, out_shape=outs, in_specs=list(in_specs) + [pl.BlockS...]
  transfers between devices with their start and end apart: 9 -> 9, of which waited for: 3 -> 4; matrix products, arithmetic and copies ran while one was open for 0% -> 0% of each run, Pallas kernels for 6% -> 7%
where the time goes in v13:
time: 65.1 us; the launch traced here: 64.6 us
  starting transfers between devices  44.3 us (68%)
  Pallas kernels  9.83 us (15%)
  blocking collectives  5.64 us (9%)
  waiting for transfers between devices  4.64 us (7%)
    ppermute x7, starting transfers between devices, exchange(): return lax.ppermute(own, AXES, list(enumerate(partners(bit, count))))  25.5 us
    all_to_all x1, starting transfers between devices, per_device(): lax.all_to_all(level_6, AXES, 0, 0, axis_index_groups=teams, tiled=True)  14.1 us
    pallas_call x11, Pallas kernels, call(): pl.pallas_call(body, out_shape=outs, in_specs=list(in_specs) + [pl.BlockS...  9.83 us
    all_gather x1, blocking collectives, per_device(): both_3 = lax.all_gather(own_3, AXES, axis_index_groups=z_pairs, tiled=True)  5.64 us
    ppermute x1, starting transfers between devices, per_device(): other_halo = lax.ppermute(other, AXES, swap)  4.68 us
    ppermute x7, waiting for transfers between devices, exchange(): return lax.ppermute(own, AXES, list(enumerate(partners(bit, count))))  4.64 us
  transfers between devices with their start and end apart: 9, of which 4 were waited for; matrix products, arithmetic and copies ran while one was open for 0% of the time, Pallas kernels for 7%

profile of v13, /device:TPU:8, one launch (start us, length us, event | category | flops | bytes accessed | tf_op | source)
XLA Modules:
  0.0 64.6 jit_solution(5095999753484857322)
XLA Ops:
  0.0 2.9 %shard_map.37 = (bf16[256,1024]{1,0:T(8,128)(2,1)S(1)}, bf16[128,1024]{1,0:T(8,128)(2,1)S(1)}, bf16[64,1024]{1,0:T(8,128)(2,1)S(1)}, bf16[32,1024]{1,0:T(8,128)(2,1)S(1)}, bf16[1024,128]{1,0:T(8,128)(2,1)}) custom-call(s32[1]{0:T(128)} %bitcast.refs_0_, bf16[256,512]{1,0:T(8,128)(2,1)} %refs_1_.3, bf16[512,1536]{1,0:T(8,128)(2,1)} %refs_2_.3), custom_call_target="tpu_custom_call" | custom-call | flops 268435456 | bytes 1048576 | tf_op jit(solution)/shard_map/pallas_call | solution.py:45
  2.9 0.0 copy-start
  2.9 14.1 %all-to-all-start = ((bf16[32,32,128]{2,1,0:T(8,128)(2,1)}), bf16[32,32,128]{2,1,0:T(8,128)(2,1)S(1)}, u32[]{:S(2)}, u32[]{:S(2)}) async-start(bf16[32,32,128]{2,1,0:T(8,128)(2,1)} %bitcast.1), calls=%async_computation | async-start | bytes 524288 | tf_op jit(solution)/shard_map/all_to_all | solution.py:332
  17.0 1.9 %collective-permute-start = (bf16[128,1024]{1,0:T(8,128)(2,1)S(1)}, bf16[128,1024]{1,0:T(8,128)(2,1)S(1)}, u32[]{:S(2)}, u32[]{:S(2)}) collective-permute-start(bf16[128,1024]{1,0:T(8,128)(2,1)S(1)} %get-tuple-element.16), channel_id=1, source_target_pairs={{0,1},{1,0},{2,3},{3,2},{4,5},{5,4},{6,7},{7,6},{8,9},{9,8},{10,11... | collective-permute-start | bytes 786440 | tf_op jit(solution)/shard_map/ppermute | solution.py:322
  18.9 4.7 %collective-permute-start.1 = (bf16[64,1024]{1,0:T(8,128)(2,1)S(1)}, bf16[64,1024]{1,0:T(8,128)(2,1)S(1)}, u32[]{:S(2)}, u32[]{:S(2)}) collective-permute-start(bf16[64,1024]{1,0:T(8,128)(2,1)S(1)} %get-tuple-element.17), channel_id=1, source_target_pairs={{1,2},{3,4},{5,6},{7,8},{9,10},{11,12},{13,14},{15,16},{17,18},{19... | collective-permute-start | bytes 393224 | tf_op jit(solution)/shard_map/ppermute | solution.py:337
  23.6 0.1 shard_map.38
  23.8 5.6 %all_gather.3.refs_2_.refs_0_.refs_6_ = bf16[128,1024]{1,0:T(8,128)(2,1)S(1)} all-gather(bf16[64,1024]{1,0:T(8,128)(2,1)S(1)} %shard_map.38), channel_id=1, replica_groups={{0,2},{1,3},{4,6},{5,7},{8,10},{9,11},{12,14},{13,15},{16,18},{17,19},{..., dimensions={0}, use_global_device_ids=true | all-gather | bytes 393216 | tf_op jit(solution)/shard_map/all_gather | solution.py:336
  29.4 0.6 shard_map.39.refs_0_.refs_7_
  30.0 1.9 %collective-permute-start.2 = (bf16[96,1024]{1,0:T(8,128)(2,1)S(1)}, bf16[96,1024]{1,0:T(8,128)(2,1)S(1)}, u32[]{:S(2)}, u32[]{:S(2)}) collective-permute-start(bf16[96,1024]{1,0:T(8,128)(2,1)S(1)} %shard_map.39.refs_0_.refs_7_), channel_id=1, source_target_pairs={{0,1},{1,0},{2,3},{3,2},{4,5},{5,4},{6,7},{7,6},{8,9},{9,8},{10,11... | collective-permute-start | bytes 589832 | tf_op jit(solution)/shard_map/ppermute | solution.py:322
  31.9 1.4 %collective-permute-done.2.refs_1_.refs_8_ = bf16[96,1024]{1,0:T(8,128)(2,1)S(1)} collective-permute-done((bf16[96,1024]{1,0:T(8,128)(2,1)S(1)}, bf16[96,1024]{1,0:T(8,128)(2,1)S(1)}, u32[]{:S(2)}, u32[]{:S(2)}) %collective-permute-start.2) | collective-permute-done | bytes 196640 | tf_op jit(solution)/shard_map/ppermute | solution.py:322
  33.3 5.1 %collective-permute-start.4 = (bf16[64,1024]{1,0:T(8,128)(2,1)S(1)}, bf16[64,1024]{1,0:T(8,128)(2,1)S(1)}, u32[]{:S(2)}, u32[]{:S(2)}) collective-permute-start(bf16[64,1024]{1,0:T(8,128)(2,1)S(1)} %shard_map.40.refs_1_.refs_0_), channel_id=1, source_target_pairs={{0,96},{1,97},{2,98},{3,99},{4,100},{5,101},{6,102},{7,103},{8,104... | collective-permute-start | bytes 393224 | tf_op jit(solution)/shard_map/ppermute | solution.py:322
  38.4 0.2 shard_map.41.refs_9_.refs_0_
  38.6 4.6 %collective-permute-start.3 = (bf16[64,1024]{1,0:T(8,128)(2,1)S(1)}, bf16[64,1024]{1,0:T(8,128)(2,1)S(1)}, u32[]{:S(2)}, u32[]{:S(2)}) collective-permute-start(bf16[64,1024]{1,0:T(8,128)(2,1)S(1)} %shard_map.41.refs_9_.refs_0_), channel_id=1, source_target_pairs={{0,4},{1,5},{2,6},{3,7},{4,0},{5,1},{6,2},{7,3},{8,12},{9,13},{10,... | collective-permute-start | bytes 393224 | tf_op jit(solution)/shard_map/ppermute | solution.py:322
  43.2 2.7 %shard_map.42 = (bf16[256,512]{1,0:T(8,128)(2,1)S(1)}, f32[256,512]{1,0:T(8,128)S(1)}, f32[256,512]{1,0:T(8,128)S(1)}) custom-call(s32[1]{0:T(128)} %bitcast.refs_0_, bf16[256,512]{1,0:T(8,128)(2,1)S(1)} %copy-done, bf16[512,1536]{1,0:T(8,128)(2,1)} %refs_2_.3, bf16[256,1024]{1,0:T(8,128)(2,1)S(1)} %get-tuple-element.15.refs_3_, ...), custom_call_target="tpu_custom_call" | custom-call | flops 1000000000 | bytes 1048576 | tf_op jit(solution)/shard_map/pallas_call | solution.py:45
  45.9 3.4 %collective-permute-start.5 = (bf16[64,1024]{1,0:T(8,128)(2,1)S(1)}, bf16[64,1024]{1,0:T(8,128)(2,1)S(1)}, u32[]{:S(2)}, u32[]{:S(2)}) collective-permute-start(bf16[64,1024]{1,0:T(8,128)(2,1)S(1)} %shard_map.43.refs_2_.refs_0_), channel_id=1, source_target_pairs={{0,128},{1,129},{2,130},{3,131},{4,132},{5,133},{6,134},{7,135},{8... | collective-permute-start | bytes 393224 | tf_op jit(solution)/shard_map/ppermute | solution.py:322
  49.3 0.1 collective-permute-done.3.refs_1_.refs_3_
  49.5 0.2 shard_map.44.refs_2_
  49.6 4.6 %collective-permute-start.6 = (bf16[64,1024]{1,0:T(8,128)(2,1)S(1)}, bf16[64,1024]{1,0:T(8,128)(2,1)S(1)}, u32[]{:S(2)}, u32[]{:S(2)}) collective-permute-start(bf16[64,1024]{1,0:T(8,128)(2,1)S(1)} %shard_map.44.refs_2_), channel_id=1, source_target_pairs={{0,12},{1,13},{2,14},{3,15},{4,8},{5,9},{6,10},{7,11},{8,4},{9,5},... | collective-permute-start | bytes 393224 | tf_op jit(solution)/shard_map/ppermute | solution.py:322
  54.3 0.2 shard_map.45.refs_6_
  54.4 4.0 %collective-permute-start.7 = (bf16[64,1024]{1,0:T(8,128)(2,1)S(1)}, bf16[64,1024]{1,0:T(8,128)(2,1)S(1)}, u32[]{:S(2)}, u32[]{:S(2)}) collective-permute-start(bf16[64,1024]{1,0:T(8,128)(2,1)S(1)} %shard_map.45.refs_6_), channel_id=1, source_target_pairs={{0,384},{1,385},{2,386},{3,387},{4,388},{5,389},{6,390},{7,391},{8... | collective-permute-start | bytes 393224 | tf_op jit(solution)/shard_map/ppermute | solution.py:322
  58.4 1.0 %shard_map.46 = (f32[256,512]{1,0:T(8,128)S(1)}, f32[256,512]{1,0:T(8,128)S(1)}) custom-call(bf16[256,512]{1,0:T(8,128)(2,1)S(1)} %get-tuple-element.20.refs_2_.refs_0_, f32[256,512]{1,0:T(8,128)S(1)} %get-tuple-element.21.refs_1_, f32[256,512]{1,0:T(8,128)S(1)} %get-tuple-element.22.refs_2_, bf16[64,1024]{1,0:T(8,128)(2,1)S(1)} %collective-permute-done.3.refs_1_.refs_3_, ...), custom_call_target="tpu_custom_call" | custom-call | flops 1000000000 | bytes 1048576 | tf_op jit(solution)/shard_map/pallas_call | solution.py:45
  59.4 0.1 collective-permute-done.6.refs_3_
  59.6 2.9 %collective-permute-done.7.refs_4_ = bf16[64,1024]{1,0:T(8,128)(2,1)S(1)} collective-permute-done((bf16[64,1024]{1,0:T(8,128)(2,1)S(1)}, bf16[64,1024]{1,0:T(8,128)(2,1)S(1)}, u32[]{:S(2)}, u32[]{:S(2)}) %collective-permute-start.7) | collective-permute-done | bytes 131104 | tf_op jit(solution)/shard_map/ppermute | solution.py:322
  62.5 2.1 %shard_map.47 = bf16[256,512]{1,0:T(8,128)(2,1)} custom-call(bf16[256,512]{1,0:T(8,128)(2,1)S(1)} %get-tuple-element.20.refs_2_.refs_0_, f32[256,512]{1,0:T(8,128)S(1)} %get-tuple-element.23.refs_1_, f32[256,512]{1,0:T(8,128)S(1)} %get-tuple-element.24.refs_2_, bf16[64,1024]{1,0:T(8,128)(2,1)S(1)} %collective-permute-done.6.refs_3_, ...), custom_call_target="tpu_custom_call" | custom-call | flops 1000000000 | bytes 1048576 | tf_op jit(solution)/shard_map/pallas_call | solution.py:45
  (8 shorter events, 0.1 us)
Async XLA Ops:
  2.9 40.3 %copy-start = (bf16[256,512]{1,0:T(8,128)(2,1)S(1)}, bf16[256,512]{1,0:T(8,128)(2,1)}, u32[]{:S(2)}) copy-start(bf16[256,512]{1,0:T(8,128)(2,1)} %refs_1_.3) | copy-start | bytes 786436
  2.9 26.5 %all-to-all-start = ((bf16[32,32,128]{2,1,0:T(8,128)(2,1)}), bf16[32,32,128]{2,1,0:T(8,128)(2,1)S(1)}, u32[]{:S(2)}, u32[]{:S(2)}) async-start(bf16[32,32,128]{2,1,0:T(8,128)(2,1)} %bitcast.1), calls=%async_computation | async-start | bytes 524288 | tf_op jit(solution)/shard_map/all_to_all | solution.py:332
  17.0 6.6 %collective-permute-start = (bf16[128,1024]{1,0:T(8,128)(2,1)S(1)}, bf16[128,1024]{1,0:T(8,128)(2,1)S(1)}, u32[]{:S(2)}, u32[]{:S(2)}) collective-permute-start(bf16[128,1024]{1,0:T(8,128)(2,1)S(1)} %get-tuple-element.16), channel_id=1, source_target_pairs={{0,1},{1,0},{2,3},{3,2},{4,5},{5,4},{6,7},{7,6},{8,9},{9,8},{10,11... | collective-permute-start | bytes 786440 | tf_op jit(solution)/shard_map/ppermute | solution.py:322
  18.9 10.5 %collective-permute-start.1 = (bf16[64,1024]{1,0:T(8,128)(2,1)S(1)}, bf16[64,1024]{1,0:T(8,128)(2,1)S(1)}, u32[]{:S(2)}, u32[]{:S(2)}) collective-permute-start(bf16[64,1024]{1,0:T(8,128)(2,1)S(1)} %get-tuple-element.17), channel_id=1, source_target_pairs={{1,2},{3,4},{5,6},{7,8},{9,10},{11,12},{13,14},{15,16},{17,18},{19... | collective-permute-start | bytes 393224 | tf_op jit(solution)/shard_map/ppermute | solution.py:337
  30.0 3.3 %collective-permute-start.2 = (bf16[96,1024]{1,0:T(8,128)(2,1)S(1)}, bf16[96,1024]{1,0:T(8,128)(2,1)S(1)}, u32[]{:S(2)}, u32[]{:S(2)}) collective-permute-start(bf16[96,1024]{1,0:T(8,128)(2,1)S(1)} %shard_map.39.refs_0_.refs_7_), channel_id=1, source_target_pairs={{0,1},{1,0},{2,3},{3,2},{4,5},{5,4},{6,7},{7,6},{8,9},{9,8},{10,11... | collective-permute-start | bytes 589832 | tf_op jit(solution)/shard_map/ppermute | solution.py:322
  33.3 12.5 %collective-permute-start.4 = (bf16[64,1024]{1,0:T(8,128)(2,1)S(1)}, bf16[64,1024]{1,0:T(8,128)(2,1)S(1)}, u32[]{:S(2)}, u32[]{:S(2)}) collective-permute-start(bf16[64,1024]{1,0:T(8,128)(2,1)S(1)} %shard_map.40.refs_1_.refs_0_), channel_id=1, source_target_pairs={{0,96},{1,97},{2,98},{3,99},{4,100},{5,101},{6,102},{7,103},{8,104... | collective-permute-start | bytes 393224 | tf_op jit(solution)/shard_map/ppermute | solution.py:322
  38.6 10.9 %collective-permute-start.3 = (bf16[64,1024]{1,0:T(8,128)(2,1)S(1)}, bf16[64,1024]{1,0:T(8,128)(2,1)S(1)}, u32[]{:S(2)}, u32[]{:S(2)}) collective-permute-start(bf16[64,1024]{1,0:T(8,128)(2,1)S(1)} %shard_map.41.refs_9_.refs_0_), channel_id=1, source_target_pairs={{0,4},{1,5},{2,6},{3,7},{4,0},{5,1},{6,2},{7,3},{8,12},{9,13},{10,... | collective-permute-start | bytes 393224 | tf_op jit(solution)/shard_map/ppermute | solution.py:322
  45.9 8.3 %collective-permute-start.5 = (bf16[64,1024]{1,0:T(8,128)(2,1)S(1)}, bf16[64,1024]{1,0:T(8,128)(2,1)S(1)}, u32[]{:S(2)}, u32[]{:S(2)}) collective-permute-start(bf16[64,1024]{1,0:T(8,128)(2,1)S(1)} %shard_map.43.refs_2_.refs_0_), channel_id=1, source_target_pairs={{0,128},{1,129},{2,130},{3,131},{4,132},{5,133},{6,134},{7,135},{8... | collective-permute-start | bytes 393224 | tf_op jit(solution)/shard_map/ppermute | solution.py:322
  49.6 9.9 %collective-permute-start.6 = (bf16[64,1024]{1,0:T(8,128)(2,1)S(1)}, bf16[64,1024]{1,0:T(8,128)(2,1)S(1)}, u32[]{:S(2)}, u32[]{:S(2)}) collective-permute-start(bf16[64,1024]{1,0:T(8,128)(2,1)S(1)} %shard_map.44.refs_2_), channel_id=1, source_target_pairs={{0,12},{1,13},{2,14},{3,15},{4,8},{5,9},{6,10},{7,11},{8,4},{9,5},... | collective-permute-start | bytes 393224 | tf_op jit(solution)/shard_map/ppermute | solution.py:322
  54.4 8.1 %collective-permute-start.7 = (bf16[64,1024]{1,0:T(8,128)(2,1)S(1)}, bf16[64,1024]{1,0:T(8,128)(2,1)S(1)}, u32[]{:S(2)}, u32[]{:S(2)}) collective-permute-start(bf16[64,1024]{1,0:T(8,128)(2,1)S(1)} %shard_map.45.refs_6_), channel_id=1, source_target_pairs={{0,384},{1,385},{2,386},{3,387},{4,388},{5,389},{6,390},{7,391},{8... | collective-permute-start | bytes 393224 | tf_op jit(solution)/shard_map/ppermute | solution.py:322

commit v14 on v12

--- a/solution.py
+++ b/solution.py
@@ -331,15 +331,15 @@
         after=(both_3, other_halo),
     )
     theirs = exchange(mine, 0)
-    own_4 = call(pool_kernel, block, vmem(1), both_3, after=(mine,))
-    sib_4 = exchange(own_4, 2)
     own_8 = call(own_8_kernel, block, vmem(2), mine, theirs)
     sib_8 = exchange(own_8, 6)
-    own_5 = pool(own_4, sib_4, own_8)
+    own_4 = call(pool_kernel, block, vmem(1), both_3, after=(own_8,))
+    sib_4 = exchange(own_4, 2)
+    own_9 = call(pool_halves_kernel, block, vmem(2), own_8, sib_8, after=(own_4,))
+    sib_9 = exchange(own_9, 7)
+    own_5 = pool(own_4, sib_4, own_9)
     sib_5 = exchange(own_5, 3)
-    own_9 = call(pool_halves_kernel, block, vmem(2), own_8, sib_8, after=(own_5,))
-    sib_9 = exchange(own_9, 7)
-    own_10 = pool(own_9, sib_9)
+    own_10 = pool(own_9, sib_9, own_5)
     sib_10 = exchange(own_10, 8)
     q, num, tot = call(
         functools.partial(local_kernel, count),

time: 67.8 us -> 64.9 us (0.957)
  waiting for transfers between devices: 8.21 us -> 5.21 us
    ppermute x7, waiting for transfers between devices: 8.2 us -> 5.2 us  [exchange(): return lax.ppermute(own, AXES, list(enumerate(partners(bit, count))))]
  transfers between devices with their start and end apart: 9 -> 9, of which waited for: 3 -> 4; matrix products, arithmetic and copies ran while one was open for 0% -> 0% of each run, Pallas kernels for 6% -> 6%
where the time goes in v14:
time: 64.9 us; the launch traced here: 64.5 us
  starting transfers between devices  44.1 us (68%)
  Pallas kernels  9.3 us (14%)
  blocking collectives  5.64 us (9%)
  waiting for transfers between devices  5.21 us (8%)
    ppermute x7, starting transfers between devices, exchange(): return lax.ppermute(own, AXES, list(enumerate(partners(bit, count))))  25.5 us
    all_to_all x1, starting transfers between devices, per_device(): lax.all_to_all(level_6, AXES, 0, 0, axis_index_groups=teams, tiled=True)  14 us
    pallas_call x10, Pallas kernels, call(): pl.pallas_call(body, out_shape=outs, in_specs=list(in_specs) + [pl.BlockS...  9.3 us
    all_gather x1, blocking collectives, per_device(): both_3 = lax.all_gather(own_3, AXES, axis_index_groups=z_pairs, tiled=True)  5.64 us
    ppermute x7, waiting for transfers between devices, exchange(): return lax.ppermute(own, AXES, list(enumerate(partners(bit, count))))  5.2 us
    ppermute x1, starting transfers between devices, per_device(): other_halo = lax.ppermute(other, AXES, swap)  4.68 us
  transfers between devices with their start and end apart: 9, of which 4 were waited for; matrix products, arithmetic and copies ran while one was open for 0% of the time, Pallas kernels for 6%

profile of v14, /device:TPU:8, one launch (start us, length us, event | category | flops | bytes accessed | tf_op | source)
XLA Modules:
  0.0 64.5 jit_solution(10015388353373013652)
XLA Ops:
  0.0 2.9 %shard_map.37 = (bf16[256,1024]{1,0:T(8,128)(2,1)S(1)}, bf16[128,1024]{1,0:T(8,128)(2,1)S(1)}, bf16[64,1024]{1,0:T(8,128)(2,1)S(1)}, bf16[32,1024]{1,0:T(8,128)(2,1)S(1)}, bf16[1024,128]{1,0:T(8,128)(2,1)}) custom-call(s32[1]{0:T(128)} %bitcast.refs_0_, bf16[256,512]{1,0:T(8,128)(2,1)} %refs_1_.3, bf16[512,1536]{1,0:T(8,128)(2,1)} %refs_2_.3), custom_call_target="tpu_custom_call" | custom-call | flops 268435456 | bytes 1048576 | tf_op jit(solution)/shard_map/pallas_call | solution.py:45
  2.9 14.0 %all-to-all-start = ((bf16[32,32,128]{2,1,0:T(8,128)(2,1)}), bf16[32,32,128]{2,1,0:T(8,128)(2,1)S(1)}, u32[]{:S(2)}, u32[]{:S(2)}) async-start(bf16[32,32,128]{2,1,0:T(8,128)(2,1)} %bitcast.1), calls=%async_computation | async-start | bytes 524288 | tf_op jit(solution)/shard_map/all_to_all | solution.py:321
  16.8 1.9 %collective-permute-start = (bf16[128,1024]{1,0:T(8,128)(2,1)S(1)}, bf16[128,1024]{1,0:T(8,128)(2,1)S(1)}, u32[]{:S(2)}, u32[]{:S(2)}) collective-permute-start(bf16[128,1024]{1,0:T(8,128)(2,1)S(1)} %get-tuple-element.14), channel_id=1, source_target_pairs={{0,1},{1,0},{2,3},{3,2},{4,5},{5,4},{6,7},{7,6},{8,9},{9,8},{10,11... | collective-permute-start | bytes 786440 | tf_op jit(solution)/shard_map/ppermute | solution.py:311
  18.8 4.7 %collective-permute-start.1 = (bf16[64,1024]{1,0:T(8,128)(2,1)S(1)}, bf16[64,1024]{1,0:T(8,128)(2,1)S(1)}, u32[]{:S(2)}, u32[]{:S(2)}) collective-permute-start(bf16[64,1024]{1,0:T(8,128)(2,1)S(1)} %get-tuple-element.15), channel_id=1, source_target_pairs={{1,2},{3,4},{5,6},{7,8},{9,10},{11,12},{13,14},{15,16},{17,18},{19... | collective-permute-start | bytes 393224 | tf_op jit(solution)/shard_map/ppermute | solution.py:326
  23.5 0.0 collective-permute-done.refs_1_.refs_4_
  23.5 0.1 shard_map.38
  23.6 5.6 %all_gather.3.refs_2_.refs_0_.refs_6_ = bf16[128,1024]{1,0:T(8,128)(2,1)S(1)} all-gather(bf16[64,1024]{1,0:T(8,128)(2,1)S(1)} %shard_map.38), channel_id=1, replica_groups={{0,2},{1,3},{4,6},{5,7},{8,10},{9,11},{12,14},{13,15},{16,18},{17,19},{..., dimensions={0}, use_global_device_ids=true | all-gather | bytes 393216 | tf_op jit(solution)/shard_map/all_gather | solution.py:325
  29.3 0.6 shard_map.39.refs_0_.refs_8_
  29.9 1.9 %collective-permute-start.2 = (bf16[96,1024]{1,0:T(8,128)(2,1)S(1)}, bf16[96,1024]{1,0:T(8,128)(2,1)S(1)}, u32[]{:S(2)}, u32[]{:S(2)}) collective-permute-start(bf16[96,1024]{1,0:T(8,128)(2,1)S(1)} %shard_map.39.refs_0_.refs_8_), channel_id=1, source_target_pairs={{0,1},{1,0},{2,3},{3,2},{4,5},{5,4},{6,7},{7,6},{8,9},{9,8},{10,11... | collective-permute-start | bytes 589832 | tf_op jit(solution)/shard_map/ppermute | solution.py:311
  31.8 1.4 %collective-permute-done.2.refs_1_.refs_9_ = bf16[96,1024]{1,0:T(8,128)(2,1)S(1)} collective-permute-done((bf16[96,1024]{1,0:T(8,128)(2,1)S(1)}, bf16[96,1024]{1,0:T(8,128)(2,1)S(1)}, u32[]{:S(2)}, u32[]{:S(2)}) %collective-permute-start.2) | collective-permute-done | bytes 196640 | tf_op jit(solution)/shard_map/ppermute | solution.py:311
  33.2 5.1 %collective-permute-start.4 = (bf16[64,1024]{1,0:T(8,128)(2,1)S(1)}, bf16[64,1024]{1,0:T(8,128)(2,1)S(1)}, u32[]{:S(2)}, u32[]{:S(2)}) collective-permute-start(bf16[64,1024]{1,0:T(8,128)(2,1)S(1)} %shard_map.40.refs_1_.refs_0_), channel_id=1, source_target_pairs={{0,96},{1,97},{2,98},{3,99},{4,100},{5,101},{6,102},{7,103},{8,104... | collective-permute-start | bytes 393224 | tf_op jit(solution)/shard_map/ppermute | solution.py:311
  38.3 0.2 shard_map.41.refs_2_.refs_0_
  38.5 4.6 %collective-permute-start.3 = (bf16[64,1024]{1,0:T(8,128)(2,1)S(1)}, bf16[64,1024]{1,0:T(8,128)(2,1)S(1)}, u32[]{:S(2)}, u32[]{:S(2)}) collective-permute-start(bf16[64,1024]{1,0:T(8,128)(2,1)S(1)} %shard_map.41.refs_2_.refs_0_), channel_id=1, source_target_pairs={{0,4},{1,5},{2,6},{3,7},{4,0},{5,1},{6,2},{7,3},{8,12},{9,13},{10,... | collective-permute-start | bytes 393224 | tf_op jit(solution)/shard_map/ppermute | solution.py:311
  43.0 2.5 %collective-permute-done.4.refs_1_.refs_10_ = bf16[64,1024]{1,0:T(8,128)(2,1)S(1)} collective-permute-done((bf16[64,1024]{1,0:T(8,128)(2,1)S(1)}, bf16[64,1024]{1,0:T(8,128)(2,1)S(1)}, u32[]{:S(2)}, u32[]{:S(2)}) %collective-permute-start.4) | collective-permute-done | bytes 131104 | tf_op jit(solution)/shard_map/ppermute | solution.py:311
  45.6 3.4 %collective-permute-start.5 = (bf16[64,1024]{1,0:T(8,128)(2,1)S(1)}, bf16[64,1024]{1,0:T(8,128)(2,1)S(1)}, u32[]{:S(2)}, u32[]{:S(2)}) collective-permute-start(bf16[64,1024]{1,0:T(8,128)(2,1)S(1)} %shard_map.42.refs_2_.refs_0_), channel_id=1, source_target_pairs={{0,128},{1,129},{2,130},{3,131},{4,132},{5,133},{6,134},{7,135},{8... | collective-permute-start | bytes 393224 | tf_op jit(solution)/shard_map/ppermute | solution.py:311
  49.0 0.3 collective-permute-done.3.refs_1_.refs_7_
  49.3 0.2 shard_map.43.refs_2_
  49.5 4.6 %collective-permute-start.6 = (bf16[64,1024]{1,0:T(8,128)(2,1)S(1)}, bf16[64,1024]{1,0:T(8,128)(2,1)S(1)}, u32[]{:S(2)}, u32[]{:S(2)}) collective-permute-start(bf16[64,1024]{1,0:T(8,128)(2,1)S(1)} %shard_map.43.refs_2_), channel_id=1, source_target_pairs={{0,12},{1,13},{2,14},{3,15},{4,8},{5,9},{6,10},{7,11},{8,4},{9,5},... | collective-permute-start | bytes 393224 | tf_op jit(solution)/shard_map/ppermute | solution.py:311
  54.1 0.0 collective-permute-done.5.refs_1_.refs_4_
  54.1 0.2 shard_map.44.refs_11_
  54.3 4.0 %collective-permute-start.7 = (bf16[64,1024]{1,0:T(8,128)(2,1)S(1)}, bf16[64,1024]{1,0:T(8,128)(2,1)S(1)}, u32[]{:S(2)}, u32[]{:S(2)}) collective-permute-start(bf16[64,1024]{1,0:T(8,128)(2,1)S(1)} %shard_map.44.refs_11_), channel_id=1, source_target_pairs={{0,384},{1,385},{2,386},{3,387},{4,388},{5,389},{6,390},{7,391},{8... | collective-permute-start | bytes 393224 | tf_op jit(solution)/shard_map/ppermute | solution.py:311
  58.3 3.1 %shard_map.45 = (bf16[256,512]{1,0:T(8,128)(2,1)S(1)}, f32[256,512]{1,0:T(8,128)S(1)}, f32[256,512]{1,0:T(8,128)S(1)}) custom-call(s32[1]{0:T(128)} %bitcast.refs_0_, bf16[256,512]{1,0:T(8,128)(2,1)S(1)} %copy-done, bf16[512,1536]{1,0:T(8,128)(2,1)} %refs_2_.3, bf16[256,1024]{1,0:T(8,128)(2,1)S(1)} %get-tuple-element.13.refs_3_, ...), custom_call_target="tpu_custom_call" | custom-call | flops 1000000000 | bytes 1048576 | tf_op jit(solution)/shard_map/pallas_call | solution.py:45
  61.4 0.9 %collective-permute-done.7.refs_5_ = bf16[64,1024]{1,0:T(8,128)(2,1)S(1)} collective-permute-done((bf16[64,1024]{1,0:T(8,128)(2,1)S(1)}, bf16[64,1024]{1,0:T(8,128)(2,1)S(1)}, u32[]{:S(2)}, u32[]{:S(2)}) %collective-permute-start.7) | collective-permute-done | bytes 131104 | tf_op jit(solution)/shard_map/ppermute | solution.py:311
  62.4 2.1 %shard_map.46 = bf16[256,512]{1,0:T(8,128)(2,1)} custom-call(bf16[256,512]{1,0:T(8,128)(2,1)S(1)} %get-tuple-element.18.refs_0_, f32[256,512]{1,0:T(8,128)S(1)} %get-tuple-element.19.refs_1_, f32[256,512]{1,0:T(8,128)S(1)} %get-tuple-element.20.refs_2_, bf16[64,1024]{1,0:T(8,128)(2,1)S(1)} %collective-permute-done.6.refs_3_, ...), custom_call_target="tpu_custom_call" | custom-call | flops 1000000000 | bytes 1048576 | tf_op jit(solution)/shard_map/pallas_call | solution.py:45
  (7 shorter events, 0.1 us)
Async XLA Ops:
  2.9 26.4 %all-to-all-start = ((bf16[32,32,128]{2,1,0:T(8,128)(2,1)}), bf16[32,32,128]{2,1,0:T(8,128)(2,1)S(1)}, u32[]{:S(2)}, u32[]{:S(2)}) async-start(bf16[32,32,128]{2,1,0:T(8,128)(2,1)} %bitcast.1), calls=%async_computation | async-start | bytes 524288 | tf_op jit(solution)/shard_map/all_to_all | solution.py:321
  16.8 6.6 %collective-permute-start = (bf16[128,1024]{1,0:T(8,128)(2,1)S(1)}, bf16[128,1024]{1,0:T(8,128)(2,1)S(1)}, u32[]{:S(2)}, u32[]{:S(2)}) collective-permute-start(bf16[128,1024]{1,0:T(8,128)(2,1)S(1)} %get-tuple-element.14), channel_id=1, source_target_pairs={{0,1},{1,0},{2,3},{3,2},{4,5},{5,4},{6,7},{7,6},{8,9},{9,8},{10,11... | collective-permute-start | bytes 786440 | tf_op jit(solution)/shard_map/ppermute | solution.py:311
  18.8 10.5 %collective-permute-start.1 = (bf16[64,1024]{1,0:T(8,128)(2,1)S(1)}, bf16[64,1024]{1,0:T(8,128)(2,1)S(1)}, u32[]{:S(2)}, u32[]{:S(2)}) collective-permute-start(bf16[64,1024]{1,0:T(8,128)(2,1)S(1)} %get-tuple-element.15), channel_id=1, source_target_pairs={{1,2},{3,4},{5,6},{7,8},{9,10},{11,12},{13,14},{15,16},{17,18},{19... | collective-permute-start | bytes 393224 | tf_op jit(solution)/shard_map/ppermute | solution.py:326
  29.3 29.0 %copy-start = (bf16[256,512]{1,0:T(8,128)(2,1)S(1)}, bf16[256,512]{1,0:T(8,128)(2,1)}, u32[]{:S(2)}) copy-start(bf16[256,512]{1,0:T(8,128)(2,1)} %refs_1_.3) | copy-start | bytes 786436
  29.9 3.3 %collective-permute-start.2 = (bf16[96,1024]{1,0:T(8,128)(2,1)S(1)}, bf16[96,1024]{1,0:T(8,128)(2,1)S(1)}, u32[]{:S(2)}, u32[]{:S(2)}) collective-permute-start(bf16[96,1024]{1,0:T(8,128)(2,1)S(1)} %shard_map.39.refs_0_.refs_8_), channel_id=1, source_target_pairs={{0,1},{1,0},{2,3},{3,2},{4,5},{5,4},{6,7},{7,6},{8,9},{9,8},{10,11... | collective-permute-start | bytes 589832 | tf_op jit(solution)/shard_map/ppermute | solution.py:311
  33.2 12.4 %collective-permute-start.4 = (bf16[64,1024]{1,0:T(8,128)(2,1)S(1)}, bf16[64,1024]{1,0:T(8,128)(2,1)S(1)}, u32[]{:S(2)}, u32[]{:S(2)}) collective-permute-start(bf16[64,1024]{1,0:T(8,128)(2,1)S(1)} %shard_map.40.refs_1_.refs_0_), channel_id=1, source_target_pairs={{0,96},{1,97},{2,98},{3,99},{4,100},{5,101},{6,102},{7,103},{8,104... | collective-permute-start | bytes 393224 | tf_op jit(solution)/shard_map/ppermute | solution.py:311
  38.5 10.9 %collective-permute-start.3 = (bf16[64,1024]{1,0:T(8,128)(2,1)S(1)}, bf16[64,1024]{1,0:T(8,128)(2,1)S(1)}, u32[]{:S(2)}, u32[]{:S(2)}) collective-permute-start(bf16[64,1024]{1,0:T(8,128)(2,1)S(1)} %shard_map.41.refs_2_.refs_0_), channel_id=1, source_target_pairs={{0,4},{1,5},{2,6},{3,7},{4,0},{5,1},{6,2},{7,3},{8,12},{9,13},{10,... | collective-permute-start | bytes 393224 | tf_op jit(solution)/shard_map/ppermute | solution.py:311
  45.6 8.5 %collective-permute-start.5 = (bf16[64,1024]{1,0:T(8,128)(2,1)S(1)}, bf16[64,1024]{1,0:T(8,128)(2,1)S(1)}, u32[]{:S(2)}, u32[]{:S(2)}) collective-permute-start(bf16[64,1024]{1,0:T(8,128)(2,1)S(1)} %shard_map.42.refs_2_.refs_0_), channel_id=1, source_target_pairs={{0,128},{1,129},{2,130},{3,131},{4,132},{5,133},{6,134},{7,135},{8... | collective-permute-start | bytes 393224 | tf_op jit(solution)/shard_map/ppermute | solution.py:311
  49.5 11.9 %collective-permute-start.6 = (bf16[64,1024]{1,0:T(8,128)(2,1)S(1)}, bf16[64,1024]{1,0:T(8,128)(2,1)S(1)}, u32[]{:S(2)}, u32[]{:S(2)}) collective-permute-start(bf16[64,1024]{1,0:T(8,128)(2,1)S(1)} %shard_map.43.refs_2_), channel_id=1, source_target_pairs={{0,12},{1,13},{2,14},{3,15},{4,8},{5,9},{6,10},{7,11},{8,4},{9,5},... | collective-permute-start | bytes 393224 | tf_op jit(solution)/shard_map/ppermute | solution.py:311
  54.3 8.1 %collective-permute-start.7 = (bf16[64,1024]{1,0:T(8,128)(2,1)S(1)}, bf16[64,1024]{1,0:T(8,128)(2,1)S(1)}, u32[]{:S(2)}, u32[]{:S(2)}) collective-permute-start(bf16[64,1024]{1,0:T(8,128)(2,1)S(1)} %shard_map.44.refs_11_), channel_id=1, source_target_pairs={{0,384},{1,385},{2,386},{3,387},{4,388},{5,389},{6,390},{7,391},{8... | collective-permute-start | bytes 393224 | tf_op jit(solution)/shard_map/ppermute | solution.py:311

commit v15 on v7

--- a/solution.py
+++ b/solution.py
@@ -180,8 +180,8 @@
 
 
 def local_kernel(
-    count, place, x_ref, w_hbm, kv_ref, near_ref, other_ref, mine_ref, theirs_ref, sib_3_ref,
-    sib_4_ref, q_ref, num_ref, tot_ref, pad, l1, w_ref, sem
+    count, place, x_ref, w_hbm, kv_ref, near_ref, other_ref, mine_ref, theirs_ref, both_3_ref,
+    both_4_ref, q_ref, num_ref, tot_ref, pad, l1, w_ref, sem
 ):
     rows, model = x_ref.shape
     blocks = rows // BLOCK
@@ -222,7 +222,11 @@
             num, tot = attend_pair(q_ref[here, kl], keys, values, ones)
             num_ref[here, kl] = num
             tot_ref[here, kl] = tot
-    for refs in ((mine_ref, theirs_ref), (near_ref, sib_3_ref, sib_4_ref)):
+    picked = []
+    for bit, ref in ((1, both_3_ref), (2, both_4_ref)):
+        start = pl.multiple_of((1 - ((place[0] >> bit) & 1)) * BLOCK, BLOCK)
+        picked.append(ref[pl.ds(start, BLOCK), :])
+    for refs in ((mine_ref, theirs_ref), (near_ref, *picked)):
         far = far_blocks(refs)
         for lanes in range(0, model, 128):
             kl = slice(lanes, lanes + 128)
@@ -312,20 +316,25 @@
     spread = lax.all_to_all(level_6, AXES, 0, 0, axis_index_groups=teams, tiled=True)
     near_sib = exchange(near, 0)
     own_3 = call(pool_near_kernel, block, vmem(2), level_3, near_sib)
-    sib_3 = exchange(own_3, 1)
     other_halo = lax.ppermute(other, AXES, swap)
-    own_4 = pool(own_3, sib_3)
-    sib_4 = exchange(own_4, 2)
+
+    def pair_gather(own, bit):
+        pairs = [[i, i ^ 1 << bit] for i in range(count) if not i >> bit & 1]
+        return lax.all_gather(own, AXES, axis_index_groups=pairs, tiled=True)
+
+    both_3 = pair_gather(own_3, 1)
+    own_4 = call(pool_kernel, block, vmem(1), both_3)
+    both_4 = pair_gather(own_4, 2)
     mine = call(
         unpack_kernel, bf16(5 * BLOCK // 2, 2 * model), [SMEM, *vmem(1)],
         place, spread.reshape(members, packed, 128),
         scratch=(pltpu.VMEM((members * packed, 128), jnp.float32),),
-        after=(own_4, other_halo),
+        after=(both_4, other_halo),
     )
     theirs = exchange(mine, 0)
     own_9 = call(own_9_kernel, block, vmem(2), mine, theirs)
     sib_9 = exchange(own_9, 7)
-    own_5 = pool(own_4, sib_4, own_9)
+    own_5 = call(pool_kernel, block, vmem(1), both_4, after=(own_9,))
     sib_5 = exchange(own_5, 3)
     own_10 = pool(own_9, sib_9, own_5)
     sib_10 = exchange(own_10, 8)
@@ -333,7 +342,7 @@
         functools.partial(local_kernel, count),
         (bf16(rows, model), f32(rows, model), f32(rows, model)),
         [SMEM, *vmem(1), in_hbm, *vmem(7)],
-        place, tokens, stay(w_qkv), kv, near_sib, other_halo, mine, theirs, sib_3, sib_4,
+        place, tokens, stay(w_qkv), kv, near_sib, other_halo, mine, theirs, both_3, both_4,
         flops=10**9,
         scratch=(
             pltpu.VMEM((rows + 2 * BLOCK, 2 * model), jnp.bfloat16),

time: 67.2 us -> 70.4 us (1.048)
  blocking collectives: 0 us -> 18.1 us
  waiting for transfers between devices: 13.6 us -> 5.34 us
  starting transfers between devices: 42 us -> 36.1 us
    all_gather x0 -> x2, blocking collectives: none -> 18.1 us  [pair_gather(): return lax.all_gather(own, AXES, axis_index_groups=pairs, tiled=True)]
    ppermute x7 -> x5, starting transfers between devices: 18.7 us -> 12 us  [exchange(): return lax.ppermute(own, AXES, list(enumerate(partners(bit, count))))]
    ppermute x7 -> x5, waiting for transfers between devices: 11.3 us -> 5.33 us  [exchange(): return lax.ppermute(own, AXES, list(enumerate(partners(bit, count))))]
    ppermute x1, waiting for transfers between devices: 1.48 us -> 0.01 us  [per_device(): other_halo = lax.ppermute(other, AXES, swap)]
    all_to_all x1, waiting for transfers between devices: 0.8 us -> 0.01 us  [per_device(): lax.all_to_all(level_6, AXES, 0, 0, axis_index_groups=teams, tiled=True)]
    ppermute x1, starting transfers between devices: 6.72 us -> 7.48 us  [per_device(): other_halo = lax.ppermute(other, AXES, swap)]
  transfers between devices with their start and end apart: 9 -> 7, of which waited for: 7 -> 3; matrix products, arithmetic and copies ran while one was open for 0% -> 0% of each run, Pallas kernels for 6% -> 6%
where the time goes in v15:
time: 70.4 us; the launch traced here: 69.9 us
  starting transfers between devices  36.1 us (51%)
  blocking collectives  18.1 us (26%)
  Pallas kernels  10.3 us (15%)
  waiting for transfers between devices  5.34 us (8%)
    all_gather x2, blocking collectives, pair_gather(): return lax.all_gather(own, AXES, axis_index_groups=pairs, tiled=True)  18.1 us
    all_to_all x1, starting transfers between devices, per_device(): lax.all_to_all(level_6, AXES, 0, 0, axis_index_groups=teams, tiled=True)  16.6 us
    ppermute x5, starting transfers between devices, exchange(): return lax.ppermute(own, AXES, list(enumerate(partners(bit, count))))  12 us
    pallas_call x9, Pallas kernels, call(): pl.pallas_call(body, out_shape=outs, in_specs=list(in_specs) + [pl.BlockS...  10.3 us
    ppermute x1, starting transfers between devices, per_device(): other_halo = lax.ppermute(other, AXES, swap)  7.48 us
    ppermute x5, waiting for transfers between devices, exchange(): return lax.ppermute(own, AXES, list(enumerate(partners(bit, count))))  5.33 us
  transfers between devices with their start and end apart: 7, of which 3 were waited for; matrix products, arithmetic and copies ran while one was open for 0% of the time, Pallas kernels for 6%

profile of v15, /device:TPU:6, one launch (start us, length us, event | category | flops | bytes accessed | tf_op | source)
XLA Modules:
  0.0 69.9 jit_solution(449322829461821009)
XLA Ops:
  0.0 3.0 %shard_map.37 = (bf16[256,1024]{1,0:T(8,128)(2,1)S(1)}, bf16[128,1024]{1,0:T(8,128)(2,1)S(1)}, bf16[64,1024]{1,0:T(8,128)(2,1)S(1)}, bf16[32,1024]{1,0:T(8,128)(2,1)S(1)}, bf16[2048,128]{1,0:T(8,128)(2,1)}) custom-call(s32[1]{0:T(128)} %bitcast.refs_0_, bf16[256,512]{1,0:T(8,128)(2,1)} %refs_1_.3, bf16[512,1536]{1,0:T(8,128)(2,1)} %refs_2_.3), custom_call_target="tpu_custom_call" | custom-call | flops 268435456 | bytes 1048576 | tf_op jit(solution)/shard_map/pallas_call | solution.py:43
  3.0 16.6 %all-to-all-start = ((bf16[64,32,128]{2,1,0:T(8,128)(2,1)}), bf16[64,32,128]{2,1,0:T(8,128)(2,1)S(1)}, u32[]{:S(2)}, u32[]{:S(2)}) async-start(bf16[64,32,128]{2,1,0:T(8,128)(2,1)} %bitcast.1), calls=%async_computation | async-start | bytes 1048576 | tf_op jit(solution)/shard_map/all_to_all | solution.py:316
  19.6 1.9 %collective-permute-start = (bf16[128,1024]{1,0:T(8,128)(2,1)S(1)}, bf16[128,1024]{1,0:T(8,128)(2,1)S(1)}, u32[]{:S(2)}, u32[]{:S(2)}) collective-permute-start(bf16[128,1024]{1,0:T(8,128)(2,1)S(1)} %get-tuple-element.14), channel_id=1, source_target_pairs={{0,1},{1,0},{2,3},{3,2},{4,5},{5,4},{6,7},{7,6},{8,9},{9,8},{10,11... | collective-permute-start | bytes 786440 | tf_op jit(solution)/shard_map/ppermute | solution.py:306
  21.5 7.5 %collective-permute-start.1 = (bf16[64,1024]{1,0:T(8,128)(2,1)S(1)}, bf16[64,1024]{1,0:T(8,128)(2,1)S(1)}, u32[]{:S(2)}, u32[]{:S(2)}) collective-permute-start(bf16[64,1024]{1,0:T(8,128)(2,1)S(1)} %get-tuple-element.15), channel_id=1, source_target_pairs={{1,2},{3,4},{5,6},{7,8},{9,10},{11,12},{13,14},{15,16},{17,18},{19... | collective-permute-start | bytes 393224 | tf_op jit(solution)/shard_map/ppermute | solution.py:319
  29.0 0.0 collective-permute-done.refs_1_.refs_4_
  29.0 0.1 shard_map.38
  29.2 8.9 %all_gather.6.refs_0_.refs_8_ = bf16[128,1024]{1,0:T(8,128)(2,1)S(1)} all-gather(bf16[64,1024]{1,0:T(8,128)(2,1)S(1)} %shard_map.38), channel_id=1, replica_groups={{0,2},{1,3},{4,6},{5,7},{8,10},{9,11},{12,14},{13,15},{16,18},{17,19},{..., dimensions={0}, use_global_device_ids=true | all-gather | bytes 393216 | tf_op jit(solution)/shard_map/all_gather | solution.py:323
  38.1 0.2 shard_map.39
  38.2 9.1 %all_gather.7.refs_2_.refs_0_.refs_9_ = bf16[128,1024]{1,0:T(8,128)(2,1)S(1)} all-gather(bf16[64,1024]{1,0:T(8,128)(2,1)S(1)} %shard_map.39), channel_id=1, replica_groups={{0,4},{1,5},{2,6},{3,7},{8,12},{9,13},{10,14},{11,15},{16,20},{17,21},{..., dimensions={0}, use_global_device_ids=true | all-gather | bytes 393216 | tf_op jit(solution)/shard_map/all_gather | solution.py:323
  47.4 0.0 collective-permute-done.1.refs_3_.refs_5_
  47.4 0.0 all-to-all-done.refs_1_
  47.4 1.2 %shard_map.40.refs_0_.refs_6_ = bf16[160,1024]{1,0:T(8,128)(2,1)S(1)} custom-call(s32[1]{0:T(128)} %bitcast.refs_0_, bf16[64,32,128]{2,1,0:T(8,128)(2,1)S(1)} %all-to-all-done.refs_1_, bf16[128,1024]{1,0:T(8,128)(2,1)S(1)} %all_gather.7.refs_2_.refs_0_.refs_9_, bf16[64,1024]{1,0:T(8,128)(2,1)S(1)} %collective-permute-done.1.refs_3_.refs_5_), custom_call_target="tpu_custom_call" | custom-call | bytes 1048576 | tf_op jit(solution)/shard_map/pallas_call | solution.py:43
  48.6 1.9 %collective-permute-start.2 = (bf16[160,1024]{1,0:T(8,128)(2,1)S(1)}, bf16[160,1024]{1,0:T(8,128)(2,1)S(1)}, u32[]{:S(2)}, u32[]{:S(2)}) collective-permute-start(bf16[160,1024]{1,0:T(8,128)(2,1)S(1)} %shard_map.40.refs_0_.refs_6_), channel_id=1, source_target_pairs={{0,1},{1,0},{2,3},{3,2},{4,5},{5,4},{6,7},{7,6},{8,9},{9,8},{10,11... | collective-permute-start | bytes 983048 | tf_op jit(solution)/shard_map/ppermute | solution.py:306
  50.5 1.6 %collective-permute-done.2.refs_1_.refs_7_ = bf16[160,1024]{1,0:T(8,128)(2,1)S(1)} collective-permute-done((bf16[160,1024]{1,0:T(8,128)(2,1)S(1)}, bf16[160,1024]{1,0:T(8,128)(2,1)S(1)}, u32[]{:S(2)}, u32[]{:S(2)}) %collective-permute-start.2) | collective-permute-done | bytes 327712 | tf_op jit(solution)/shard_map/ppermute | solution.py:306
  52.2 2.7 %collective-permute-start.3 = (bf16[64,1024]{1,0:T(8,128)(2,1)S(1)}, bf16[64,1024]{1,0:T(8,128)(2,1)S(1)}, u32[]{:S(2)}, u32[]{:S(2)}) collective-permute-start(bf16[64,1024]{1,0:T(8,128)(2,1)S(1)} %shard_map.41.refs_1_.refs_0_), channel_id=1, source_target_pairs={{0,128},{1,129},{2,130},{3,131},{4,132},{5,133},{6,134},{7,135},{8... | collective-permute-start | bytes 393224 | tf_op jit(solution)/shard_map/ppermute | solution.py:306
  54.8 0.2 shard_map.42.refs_2_
  55.0 3.2 %collective-permute-start.4 = (bf16[64,1024]{1,0:T(8,128)(2,1)S(1)}, bf16[64,1024]{1,0:T(8,128)(2,1)S(1)}, u32[]{:S(2)}, u32[]{:S(2)}) collective-permute-start(bf16[64,1024]{1,0:T(8,128)(2,1)S(1)} %shard_map.42.refs_2_), channel_id=1, source_target_pairs={{0,12},{1,13},{2,14},{3,15},{4,8},{5,9},{6,10},{7,11},{8,4},{9,5},... | collective-permute-start | bytes 393224 | tf_op jit(solution)/shard_map/ppermute | solution.py:306
  58.2 1.4 %collective-permute-done.3.refs_1_.refs_4_ = bf16[64,1024]{1,0:T(8,128)(2,1)S(1)} collective-permute-done((bf16[64,1024]{1,0:T(8,128)(2,1)S(1)}, bf16[64,1024]{1,0:T(8,128)(2,1)S(1)}, u32[]{:S(2)}, u32[]{:S(2)}) %collective-permute-start.3) | collective-permute-done | bytes 131104 | tf_op jit(solution)/shard_map/ppermute | solution.py:306
  59.6 0.2 shard_map.43.refs_10_
  59.8 2.3 %collective-permute-start.5 = (bf16[64,1024]{1,0:T(8,128)(2,1)S(1)}, bf16[64,1024]{1,0:T(8,128)(2,1)S(1)}, u32[]{:S(2)}, u32[]{:S(2)}) collective-permute-start(bf16[64,1024]{1,0:T(8,128)(2,1)S(1)} %shard_map.43.refs_10_), channel_id=1, source_target_pairs={{0,384},{1,385},{2,386},{3,387},{4,388},{5,389},{6,390},{7,391},{8... | collective-permute-start | bytes 393224 | tf_op jit(solution)/shard_map/ppermute | solution.py:306
  62.1 3.4 %shard_map.44 = (bf16[256,512]{1,0:T(8,128)(2,1)S(1)}, f32[256,512]{1,0:T(8,128)S(1)}, f32[256,512]{1,0:T(8,128)S(1)}) custom-call(s32[1]{0:T(128)} %bitcast.refs_0_, bf16[256,512]{1,0:T(8,128)(2,1)S(1)} %copy-done, bf16[512,1536]{1,0:T(8,128)(2,1)} %refs_2_.3, bf16[256,1024]{1,0:T(8,128)(2,1)S(1)} %get-tuple-element.13.refs_3_, ...), custom_call_target="tpu_custom_call" | custom-call | flops 1000000000 | bytes 1048576 | tf_op jit(solution)/shard_map/pallas_call | solution.py:43
  65.5 0.0 collective-permute-done.4.refs_3_
  65.5 2.3 %collective-permute-done.5.refs_5_ = bf16[64,1024]{1,0:T(8,128)(2,1)S(1)} collective-permute-done((bf16[64,1024]{1,0:T(8,128)(2,1)S(1)}, bf16[64,1024]{1,0:T(8,128)(2,1)S(1)}, u32[]{:S(2)}, u32[]{:S(2)}) %collective-permute-start.5) | collective-permute-done | bytes 131104 | tf_op jit(solution)/shard_map/ppermute | solution.py:306
  67.8 2.1 %shard_map.45 = bf16[256,512]{1,0:T(8,128)(2,1)} custom-call(bf16[256,512]{1,0:T(8,128)(2,1)S(1)} %get-tuple-element.18.refs_0_, f32[256,512]{1,0:T(8,128)S(1)} %get-tuple-element.19.refs_1_, f32[256,512]{1,0:T(8,128)S(1)} %get-tuple-element.20.refs_2_, bf16[64,1024]{1,0:T(8,128)(2,1)S(1)} %collective-permute-done.4.refs_3_, ...), custom_call_target="tpu_custom_call" | custom-call | flops 1000000000 | bytes 1048576 | tf_op jit(solution)/shard_map/pallas_call | solution.py:43
  (3 shorter events, 0.0 us)
Async XLA Ops:
  3.0 44.4 %all-to-all-start = ((bf16[64,32,128]{2,1,0:T(8,128)(2,1)}), bf16[64,32,128]{2,1,0:T(8,128)(2,1)S(1)}, u32[]{:S(2)}, u32[]{:S(2)}) async-start(bf16[64,32,128]{2,1,0:T(8,128)(2,1)} %bitcast.1), calls=%async_computation | async-start | bytes 1048576 | tf_op jit(solution)/shard_map/all_to_all | solution.py:316
  19.6 9.4 %collective-permute-start = (bf16[128,1024]{1,0:T(8,128)(2,1)S(1)}, bf16[128,1024]{1,0:T(8,128)(2,1)S(1)}, u32[]{:S(2)}, u32[]{:S(2)}) collective-permute-start(bf16[128,1024]{1,0:T(8,128)(2,1)S(1)} %get-tuple-element.14), channel_id=1, source_target_pairs={{0,1},{1,0},{2,3},{3,2},{4,5},{5,4},{6,7},{7,6},{8,9},{9,8},{10,11... | collective-permute-start | bytes 786440 | tf_op jit(solution)/shard_map/ppermute | solution.py:306
  21.5 25.9 %collective-permute-start.1 = (bf16[64,1024]{1,0:T(8,128)(2,1)S(1)}, bf16[64,1024]{1,0:T(8,128)(2,1)S(1)}, u32[]{:S(2)}, u32[]{:S(2)}) collective-permute-start(bf16[64,1024]{1,0:T(8,128)(2,1)S(1)} %get-tuple-element.15), channel_id=1, source_target_pairs={{1,2},{3,4},{5,6},{7,8},{9,10},{11,12},{13,14},{15,16},{17,18},{19... | collective-permute-start | bytes 393224 | tf_op jit(solution)/shard_map/ppermute | solution.py:319
  47.4 14.7 %copy-start = (bf16[256,512]{1,0:T(8,128)(2,1)S(1)}, bf16[256,512]{1,0:T(8,128)(2,1)}, u32[]{:S(2)}) copy-start(bf16[256,512]{1,0:T(8,128)(2,1)} %refs_1_.3) | copy-start | bytes 786436
  48.6 3.5 %collective-permute-start.2 = (bf16[160,1024]{1,0:T(8,128)(2,1)S(1)}, bf16[160,1024]{1,0:T(8,128)(2,1)S(1)}, u32[]{:S(2)}, u32[]{:S(2)}) collective-permute-start(bf16[160,1024]{1,0:T(8,128)(2,1)S(1)} %shard_map.40.refs_0_.refs_6_), channel_id=1, source_target_pairs={{0,1},{1,0},{2,3},{3,2},{4,5},{5,4},{6,7},{7,6},{8,9},{9,8},{10,11... | collective-permute-start | bytes 983048 | tf_op jit(solution)/shard_map/ppermute | solution.py:306
  52.2 7.4 %collective-permute-start.3 = (bf16[64,1024]{1,0:T(8,128)(2,1)S(1)}, bf16[64,1024]{1,0:T(8,128)(2,1)S(1)}, u32[]{:S(2)}, u32[]{:S(2)}) collective-permute-start(bf16[64,1024]{1,0:T(8,128)(2,1)S(1)} %shard_map.41.refs_1_.refs_0_), channel_id=1, source_target_pairs={{0,128},{1,129},{2,130},{3,131},{4,132},{5,133},{6,134},{7,135},{8... | collective-permute-start | bytes 393224 | tf_op jit(solution)/shard_map/ppermute | solution.py:306
  55.0 10.5 %collective-permute-start.4 = (bf16[64,1024]{1,0:T(8,128)(2,1)S(1)}, bf16[64,1024]{1,0:T(8,128)(2,1)S(1)}, u32[]{:S(2)}, u32[]{:S(2)}) collective-permute-start(bf16[64,1024]{1,0:T(8,128)(2,1)S(1)} %shard_map.42.refs_2_), channel_id=1, source_target_pairs={{0,12},{1,13},{2,14},{3,15},{4,8},{5,9},{6,10},{7,11},{8,4},{9,5},... | collective-permute-start | bytes 393224 | tf_op jit(solution)/shard_map/ppermute | solution.py:306
  59.8 8.1 %collective-permute-start.5 = (bf16[64,1024]{1,0:T(8,128)(2,1)S(1)}, bf16[64,1024]{1,0:T(8,128)(2,1)S(1)}, u32[]{:S(2)}, u32[]{:S(2)}) collective-permute-start(bf16[64,1024]{1,0:T(8,128)(2,1)S(1)} %shard_map.43.refs_10_), channel_id=1, source_target_pairs={{0,384},{1,385},{2,386},{3,387},{4,388},{5,389},{6,390},{7,391},{8... | collective-permute-start | bytes 393224 | tf_op jit(solution)/shard_map/ppermute | solution.py:306

commit v16 on v14

--- a/solution.py
+++ b/solution.py
@@ -144,10 +144,10 @@
         out_ref[:, lanes] = jnp.concatenate(parts, axis=0).astype(jnp.bfloat16)
 
 
-def own_8_kernel(mine_ref, sib_ref, out_ref):
+def own_8_kernel(both_ref, out_ref):
     half = BLOCK // 2
-    out_ref[:half, :] = mine_ref[BLOCK:, :]
-    out_ref[half:, :] = sib_ref[BLOCK:, :]
+    out_ref[:half, :] = both_ref[BLOCK : BLOCK + half, :]
+    out_ref[half:, :] = both_ref[2 * BLOCK + half :, :]
 
 
 def pool_near_kernel(mine_ref, sib_ref, out_ref):
@@ -190,8 +190,8 @@
 
 
 def local_kernel(
-    count, place, x_ref, w_hbm, kv_ref, near_ref, other_ref, both_3_ref, sib_4_ref,
-    mine_ref, theirs_ref, sib_8_ref, q_ref, num_ref, tot_ref, pad, l1, w_ref, sem
+    count, place, x_ref, w_hbm, kv_ref, near_ref, other_ref, both_3_ref, both_ref,
+    q_ref, num_ref, tot_ref, pad, l1, w_ref, sem
 ):
     rows, model = x_ref.shape
     blocks = rows // BLOCK
@@ -234,7 +234,7 @@
             tot_ref[here, kl] = tot
     start = pl.multiple_of((1 - ((place[0] >> 1) & 1)) * BLOCK, BLOCK)
     sib_3 = both_3_ref[pl.ds(start, BLOCK), :]
-    far = far_blocks((near_ref, sib_3, sib_4_ref, mine_ref, theirs_ref, sib_8_ref))
+    far = far_blocks((near_ref, sib_3, both_ref[:BLOCK, :], both_ref[3 * BLOCK // 2 : 5 * BLOCK // 2, :]))
     for lanes in range(0, model, 128):
         kl = slice(lanes, lanes + 128)
         num, tot = far_sums(far, q_ref[:, kl], lanes, model)
@@ -259,12 +259,15 @@
 
 
 def final_kernel(
-    q_ref, num_in, tot_in, sib_5_ref, sib_9_ref, sib_10_ref, w_hbm, out_ref, att, w_ref, sem
+    place, q_ref, num_in, tot_in, sib_4_ref, sib_5_ref, sib_8_ref, sib_9_ref, pair_ref, w_hbm,
+    out_ref, att, w_ref, sem
 ):
     copy = pltpu.make_async_copy(w_hbm, w_ref, sem)
     copy.start()
     model = q_ref.shape[1]
-    far = far_blocks((sib_5_ref, sib_9_ref, sib_10_ref))
+    start = pl.multiple_of((1 - ((place[0] >> 8) & 1)) * BLOCK, BLOCK)
+    sib_10 = pair_ref[pl.ds(start, BLOCK), :]
+    far = far_blocks((sib_4_ref, sib_5_ref, sib_8_ref, sib_9_ref, sib_10))
     for lanes in range(0, model, 128):
         at = slice(lanes, lanes + 128)
         num, tot = far_sums(far, q_ref[:, at], lanes, model)
@@ -330,22 +333,22 @@
         scratch=(pltpu.VMEM((members * packed, 128), jnp.float32),),
         after=(both_3, other_halo),
     )
-    theirs = exchange(mine, 0)
-    own_8 = call(own_8_kernel, block, vmem(2), mine, theirs)
+
+    def pair_gather(own, bit):
+        to = partners(bit, count)
+        pairs = [[i, to[i]] for i in range(count) if not i >> bit & 1]
+        return lax.all_gather(own, AXES, axis_index_groups=pairs, tiled=True)
+
+    both = pair_gather(mine, 0)
+    own_8 = call(own_8_kernel, block, vmem(1), both)
     sib_8 = exchange(own_8, 6)
     own_4 = call(pool_kernel, block, vmem(1), both_3, after=(own_8,))
     sib_4 = exchange(own_4, 2)
-    own_9 = call(pool_halves_kernel, block, vmem(2), own_8, sib_8, after=(own_4,))
-    sib_9 = exchange(own_9, 7)
-    own_5 = pool(own_4, sib_4, own_9)
-    sib_5 = exchange(own_5, 3)
-    own_10 = pool(own_9, sib_9, own_5)
-    sib_10 = exchange(own_10, 8)
     q, num, tot = call(
         functools.partial(local_kernel, count),
         (bf16(rows, model), f32(rows, model), f32(rows, model)),
-        [SMEM, *vmem(1), in_hbm, *vmem(8)],
-        place, tokens, stay(w_qkv), kv, near_sib, other_halo, both_3, sib_4, mine, theirs, sib_8,
+        [SMEM, *vmem(1), in_hbm, *vmem(5)],
+        place, tokens, stay(w_qkv), kv, near_sib, other_halo, both_3, both,
         flops=10**9,
         scratch=(
             pltpu.VMEM((rows + 2 * BLOCK, 2 * model), jnp.bfloat16),
@@ -353,13 +356,19 @@
             pltpu.VMEM((model, model), jnp.bfloat16),
             pltpu.SemaphoreType.DMA(()),
         ),
-        after=(own_10,),
-    )
+        after=(own_4,),
+    )
+    own_9 = call(pool_halves_kernel, block, vmem(2), own_8, sib_8, after=(q,))
+    sib_9 = exchange(own_9, 7)
+    own_5 = pool(own_4, sib_4, own_9)
+    sib_5 = exchange(own_5, 3)
+    own_10 = pool(own_9, sib_9, own_5)
+    pair = pair_gather(own_10, 8)
     return call(
         final_kernel,
         bf16(rows, model),
-        [*vmem(6), in_hbm],
-        q, num, tot, sib_5, sib_9, sib_10, stay(w_out),
+        [SMEM, *vmem(8), in_hbm],
+        place, q, num, tot, sib_4, sib_5, sib_8, sib_9, pair, stay(w_out),
         flops=10**9,
         scratch=(
             pltpu.VMEM((rows, model), jnp.bfloat16),

time: 64.9 us -> 62.8 us (0.968)
  the two profiles are of different devices: /device:TPU:8 before, /device:TPU:6 now
where the time goes in v16:
time: 62.8 us; the launch traced here: 61.6 us
  starting transfers between devices  36.6 us (58%)
  blocking collectives  14.6 us (23%)
  Pallas kernels  9.28 us (15%)
  waiting for transfers between devices  0.88 us (1%)
    ppermute x5, starting transfers between devices, exchange(): return lax.ppermute(own, AXES, list(enumerate(partners(bit, count))))  15 us
    all_to_all x1, starting transfers between devices, per_device(): lax.all_to_all(level_6, AXES, 0, 0, axis_index_groups=teams, tiled=True)  13.8 us
    pallas_call x10, Pallas kernels, call(): pl.pallas_call(body, out_shape=outs, in_specs=list(in_specs) + [pl.BlockS...  9.28 us
    all_gather x2, blocking collectives, pair_gather(): return lax.all_gather(own, AXES, axis_index_groups=pairs, tiled=True)  8.96 us
    ppermute x1, starting transfers between devices, per_device(): other_halo = lax.ppermute(other, AXES, swap)  7.93 us
    all_gather x1, blocking collectives, per_device(): both_3 = lax.all_gather(own_3, AXES, axis_index_groups=z_pairs, tiled=True)  5.64 us
  transfers between devices with their start and end apart: 7, of which 1 were waited for; matrix products, arithmetic and copies ran while one was open for 0% of the time, Pallas kernels for 5%

profile of v16, /device:TPU:6, one launch (start us, length us, event | category | flops | bytes accessed | tf_op | source)
XLA Modules:
  0.0 61.6 jit_solution(5083607825270196389)
XLA Ops:
  0.0 2.9 %shard_map.37 = (bf16[256,1024]{1,0:T(8,128)(2,1)S(1)}, bf16[128,1024]{1,0:T(8,128)(2,1)S(1)}, bf16[64,1024]{1,0:T(8,128)(2,1)S(1)}, bf16[32,1024]{1,0:T(8,128)(2,1)S(1)}, bf16[1024,128]{1,0:T(8,128)(2,1)}) custom-call(s32[1]{0:T(128)} %bitcast.refs_0_, bf16[256,512]{1,0:T(8,128)(2,1)} %refs_1_.3, bf16[512,1536]{1,0:T(8,128)(2,1)} %refs_2_.3), custom_call_target="tpu_custom_call" | custom-call | flops 268435456 | bytes 1048576 | tf_op jit(solution)/shard_map/pallas_call | solution.py:45
  2.9 13.8 %all-to-all-start = ((bf16[32,32,128]{2,1,0:T(8,128)(2,1)}), bf16[32,32,128]{2,1,0:T(8,128)(2,1)S(1)}, u32[]{:S(2)}, u32[]{:S(2)}) async-start(bf16[32,32,128]{2,1,0:T(8,128)(2,1)} %bitcast.1), calls=%async_computation | async-start | bytes 524288 | tf_op jit(solution)/shard_map/all_to_all | solution.py:324
  16.6 1.9 %collective-permute-start = (bf16[128,1024]{1,0:T(8,128)(2,1)S(1)}, bf16[128,1024]{1,0:T(8,128)(2,1)S(1)}, u32[]{:S(2)}, u32[]{:S(2)}) collective-permute-start(bf16[128,1024]{1,0:T(8,128)(2,1)S(1)} %get-tuple-element.14), channel_id=1, source_target_pairs={{0,1},{1,0},{2,3},{3,2},{4,5},{5,4},{6,7},{7,6},{8,9},{9,8},{10,11... | collective-permute-start | bytes 786440 | tf_op jit(solution)/shard_map/ppermute | solution.py:314
  18.6 7.9 %collective-permute-start.1 = (bf16[64,1024]{1,0:T(8,128)(2,1)S(1)}, bf16[64,1024]{1,0:T(8,128)(2,1)S(1)}, u32[]{:S(2)}, u32[]{:S(2)}) collective-permute-start(bf16[64,1024]{1,0:T(8,128)(2,1)S(1)} %get-tuple-element.15), channel_id=1, source_target_pairs={{1,2},{3,4},{5,6},{7,8},{9,10},{11,12},{13,14},{15,16},{17,18},{19... | collective-permute-start | bytes 393224 | tf_op jit(solution)/shard_map/ppermute | solution.py:329
  26.5 0.0 collective-permute-done.refs_1_.refs_4_
  26.5 0.0 copy-start
  26.5 0.1 shard_map.38
  26.7 5.6 %all_gather.9.refs_2_.refs_0_.refs_6_ = bf16[128,1024]{1,0:T(8,128)(2,1)S(1)} all-gather(bf16[64,1024]{1,0:T(8,128)(2,1)S(1)} %shard_map.38), channel_id=1, replica_groups={{0,2},{1,3},{4,6},{5,7},{8,10},{9,11},{12,14},{13,15},{16,18},{17,19},{..., dimensions={0}, use_global_device_ids=true | all-gather | bytes 393216 | tf_op jit(solution)/shard_map/all_gather | solution.py:328
  32.3 0.0 collective-permute-done.1.refs_3_.refs_5_
  32.3 0.0 all-to-all-done.refs_1_
  32.3 0.6 shard_map.39
  32.9 2.1 %all_gather.10.refs_0_.refs_7_ = bf16[192,1024]{1,0:T(8,128)(2,1)S(1)} all-gather(bf16[96,1024]{1,0:T(8,128)(2,1)S(1)} %shard_map.39), channel_id=1, replica_groups={{0,1},{2,3},{4,5},{6,7},{8,9},{10,11},{12,13},{14,15},{16,17},{18,19},{..., dimensions={0}, use_global_device_ids=true | all-gather | bytes 589824 | tf_op jit(solution)/shard_map/all_gather | solution.py:340
  35.0 2.1 %collective-permute-start.3 = (bf16[64,1024]{1,0:T(8,128)(2,1)S(1)}, bf16[64,1024]{1,0:T(8,128)(2,1)S(1)}, u32[]{:S(2)}, u32[]{:S(2)}) collective-permute-start(bf16[64,1024]{1,0:T(8,128)(2,1)S(1)} %shard_map.40.refs_1_.refs_0_), channel_id=1, source_target_pairs={{0,96},{1,97},{2,98},{3,99},{4,100},{5,101},{6,102},{7,103},{8,104... | collective-permute-start | bytes 393224 | tf_op jit(solution)/shard_map/ppermute | solution.py:314
  37.1 0.2 shard_map.41.refs_8_.refs_0_
  37.3 4.6 %collective-permute-start.2 = (bf16[64,1024]{1,0:T(8,128)(2,1)S(1)}, bf16[64,1024]{1,0:T(8,128)(2,1)S(1)}, u32[]{:S(2)}, u32[]{:S(2)}) collective-permute-start(bf16[64,1024]{1,0:T(8,128)(2,1)S(1)} %shard_map.41.refs_8_.refs_0_), channel_id=1, source_target_pairs={{0,4},{1,5},{2,6},{3,7},{4,0},{5,1},{6,2},{7,3},{8,12},{9,13},{10,... | collective-permute-start | bytes 393224 | tf_op jit(solution)/shard_map/ppermute | solution.py:314
  41.9 2.7 %shard_map.42 = (bf16[256,512]{1,0:T(8,128)(2,1)S(1)}, f32[256,512]{1,0:T(8,128)S(1)}, f32[256,512]{1,0:T(8,128)S(1)}) custom-call(s32[1]{0:T(128)} %bitcast.refs_0_, bf16[256,512]{1,0:T(8,128)(2,1)S(1)} %copy-done, bf16[512,1536]{1,0:T(8,128)(2,1)} %refs_2_.3, bf16[256,1024]{1,0:T(8,128)(2,1)S(1)} %get-tuple-element.13.refs_3_, ...), custom_call_target="tpu_custom_call" | custom-call | flops 1000000000 | bytes 1048576 | tf_op jit(solution)/shard_map/pallas_call | solution.py:45
  44.6 0.0 collective-permute-done.3.refs_1_.refs_6_
  44.6 2.7 %collective-permute-start.5 = (bf16[64,1024]{1,0:T(8,128)(2,1)S(1)}, bf16[64,1024]{1,0:T(8,128)(2,1)S(1)}, u32[]{:S(2)}, u32[]{:S(2)}) collective-permute-start(bf16[64,1024]{1,0:T(8,128)(2,1)S(1)} %shard_map.43.refs_2_.refs_0_), channel_id=1, source_target_pairs={{0,128},{1,129},{2,130},{3,131},{4,132},{5,133},{6,134},{7,135},{8... | collective-permute-start | bytes 393224 | tf_op jit(solution)/shard_map/ppermute | solution.py:314
  47.4 0.9 %collective-permute-done.2.refs_1_.refs_4_ = bf16[64,1024]{1,0:T(8,128)(2,1)S(1)} collective-permute-done((bf16[64,1024]{1,0:T(8,128)(2,1)S(1)}, bf16[64,1024]{1,0:T(8,128)(2,1)S(1)}, u32[]{:S(2)}, u32[]{:S(2)}) %collective-permute-start.2) | collective-permute-done | bytes 131104 | tf_op jit(solution)/shard_map/ppermute | solution.py:314
  48.2 0.2 shard_map.44.refs_2_
  48.4 3.6 %collective-permute-start.4 = (bf16[64,1024]{1,0:T(8,128)(2,1)S(1)}, bf16[64,1024]{1,0:T(8,128)(2,1)S(1)}, u32[]{:S(2)}, u32[]{:S(2)}) collective-permute-start(bf16[64,1024]{1,0:T(8,128)(2,1)S(1)} %shard_map.44.refs_2_), channel_id=1, source_target_pairs={{0,12},{1,13},{2,14},{3,15},{4,8},{5,9},{6,10},{7,11},{8,4},{9,5},... | collective-permute-start | bytes 393224 | tf_op jit(solution)/shard_map/ppermute | solution.py:314
  52.0 0.2 shard_map.45
  52.2 6.9 %all_gather.11.refs_8_ = bf16[128,1024]{1,0:T(8,128)(2,1)S(1)} all-gather(bf16[64,1024]{1,0:T(8,128)(2,1)S(1)} %shard_map.45), channel_id=1, replica_groups={{0,384},{1,385},{2,386},{3,387},{4,388},{5,389},{6,390},{7,391},{8,392}..., dimensions={0}, use_global_device_ids=true | all-gather | bytes 393216 | tf_op jit(solution)/shard_map/all_gather | solution.py:340
  59.1 2.5 %shard_map.46 = bf16[256,512]{1,0:T(8,128)(2,1)} custom-call(s32[1]{0:T(128)} %bitcast.refs_0_, bf16[256,512]{1,0:T(8,128)(2,1)S(1)} %get-tuple-element.18.refs_2_.refs_1_, f32[256,512]{1,0:T(8,128)S(1)} %get-tuple-element.19.refs_2_, f32[256,512]{1,0:T(8,128)S(1)} %get-tuple-element.20.refs_3_, bf16[64,1024]{1,0:T(8,128)(2,1)S(1)} %collective-permute-done.2.refs_1_.refs_4_, ...), custom_call_target="tpu_custom_call" | custom-call | flops 1000000000 | bytes 1048576 | tf_op jit(solution)/shard_map/pallas_call | solution.py:45
  (5 shorter events, 0.1 us)
Async XLA Ops:
  2.9 29.4 %all-to-all-start = ((bf16[32,32,128]{2,1,0:T(8,128)(2,1)}), bf16[32,32,128]{2,1,0:T(8,128)(2,1)S(1)}, u32[]{:S(2)}, u32[]{:S(2)}) async-start(bf16[32,32,128]{2,1,0:T(8,128)(2,1)} %bitcast.1), calls=%async_computation | async-start | bytes 524288 | tf_op jit(solution)/shard_map/all_to_all | solution.py:324
  16.6 9.9 %collective-permute-start = (bf16[128,1024]{1,0:T(8,128)(2,1)S(1)}, bf16[128,1024]{1,0:T(8,128)(2,1)S(1)}, u32[]{:S(2)}, u32[]{:S(2)}) collective-permute-start(bf16[128,1024]{1,0:T(8,128)(2,1)S(1)} %get-tuple-element.14), channel_id=1, source_target_pairs={{0,1},{1,0},{2,3},{3,2},{4,5},{5,4},{6,7},{7,6},{8,9},{9,8},{10,11... | collective-permute-start | bytes 786440 | tf_op jit(solution)/shard_map/ppermute | solution.py:314
  18.6 13.8 %collective-permute-start.1 = (bf16[64,1024]{1,0:T(8,128)(2,1)S(1)}, bf16[64,1024]{1,0:T(8,128)(2,1)S(1)}, u32[]{:S(2)}, u32[]{:S(2)}) collective-permute-start(bf16[64,1024]{1,0:T(8,128)(2,1)S(1)} %get-tuple-element.15), channel_id=1, source_target_pairs={{1,2},{3,4},{5,6},{7,8},{9,10},{11,12},{13,14},{15,16},{17,18},{19... | collective-permute-start | bytes 393224 | tf_op jit(solution)/shard_map/ppermute | solution.py:329
  26.5 15.4 %copy-start = (bf16[256,512]{1,0:T(8,128)(2,1)S(1)}, bf16[256,512]{1,0:T(8,128)(2,1)}, u32[]{:S(2)}) copy-start(bf16[256,512]{1,0:T(8,128)(2,1)} %refs_1_.3) | copy-start | bytes 786436
  35.0 9.6 %collective-permute-start.3 = (bf16[64,1024]{1,0:T(8,128)(2,1)S(1)}, bf16[64,1024]{1,0:T(8,128)(2,1)S(1)}, u32[]{:S(2)}, u32[]{:S(2)}) collective-permute-start(bf16[64,1024]{1,0:T(8,128)(2,1)S(1)} %shard_map.40.refs_1_.refs_0_), channel_id=1, source_target_pairs={{0,96},{1,97},{2,98},{3,99},{4,100},{5,101},{6,102},{7,103},{8,104... | collective-permute-start | bytes 393224 | tf_op jit(solution)/shard_map/ppermute | solution.py:314
  37.3 10.9 %collective-permute-start.2 = (bf16[64,1024]{1,0:T(8,128)(2,1)S(1)}, bf16[64,1024]{1,0:T(8,128)(2,1)S(1)}, u32[]{:S(2)}, u32[]{:S(2)}) collective-permute-start(bf16[64,1024]{1,0:T(8,128)(2,1)S(1)} %shard_map.41.refs_8_.refs_0_), channel_id=1, source_target_pairs={{0,4},{1,5},{2,6},{3,7},{4,0},{5,1},{6,2},{7,3},{8,12},{9,13},{10,... | collective-permute-start | bytes 393224 | tf_op jit(solution)/shard_map/ppermute | solution.py:314
  44.6 7.4 %collective-permute-start.5 = (bf16[64,1024]{1,0:T(8,128)(2,1)S(1)}, bf16[64,1024]{1,0:T(8,128)(2,1)S(1)}, u32[]{:S(2)}, u32[]{:S(2)}) collective-permute-start(bf16[64,1024]{1,0:T(8,128)(2,1)S(1)} %shard_map.43.refs_2_.refs_0_), channel_id=1, source_target_pairs={{0,128},{1,129},{2,130},{3,131},{4,132},{5,133},{6,134},{7,135},{8... | collective-permute-start | bytes 393224 | tf_op jit(solution)/shard_map/ppermute | solution.py:314
  48.4 10.7 %collective-permute-start.4 = (bf16[64,1024]{1,0:T(8,128)(2,1)S(1)}, bf16[64,1024]{1,0:T(8,128)(2,1)S(1)}, u32[]{:S(2)}, u32[]{:S(2)}) collective-permute-start(bf16[64,1024]{1,0:T(8,128)(2,1)S(1)} %shard_map.44.refs_2_), channel_id=1, source_target_pairs={{0,12},{1,13},{2,14},{3,15},{4,8},{5,9},{6,10},{7,11},{8,4},{9,5},... | collective-permute-start | bytes 393224 | tf_op jit(solution)/shard_map/ppermute | solution.py:314

commit v17 on v14

--- a/solution.py
+++ b/solution.py
@@ -115,7 +115,7 @@
     other_ref[...] = kv_ref[pl.ds(low, BLOCK), :]
 
 
-def unpack_kernel(place, in_ref, out_ref, wide):
+def unpack_kernel(place, in_ref, out_ref, l8_ref, wide):
     members, rows, _ = in_ref.shape
     wide[...] = in_ref[...].reshape(members * rows, 128).astype(jnp.float32)
     y = (place[0] >> 4) & 3
@@ -139,29 +139,27 @@
         parts = (
             level_6((y ^ 1) * 8, 8)
             + level_7(((y >> 1) ^ 1) * 16, 16)
-            + [mean(*level_7(0, members))]
         )
+        l8_ref[:, lanes] = mean(*level_7(0, members)).astype(jnp.bfloat16)
         out_ref[:, lanes] = jnp.concatenate(parts, axis=0).astype(jnp.bfloat16)
 
 
-def own_8_kernel(mine_ref, sib_ref, out_ref):
+def stack_kernel(mine_ref, l8_ref, got_ref, out_ref):
     half = BLOCK // 2
-    out_ref[:half, :] = mine_ref[BLOCK:, :]
-    out_ref[half:, :] = sib_ref[BLOCK:, :]
+    out_ref[:BLOCK, :] = mine_ref[...]
+    out_ref[BLOCK : BLOCK + half, :] = l8_ref[...]
+    out_ref[BLOCK + half :, :] = got_ref[...]
+
+
+def own_9_kernel(both_ref, out_ref):
+    one = both_ref[BLOCK : 2 * BLOCK, :].astype(jnp.float32)
+    two = both_ref[3 * BLOCK :, :].astype(jnp.float32)
+    out_ref[...] = ((one + two) * 0.5).astype(jnp.bfloat16)
 
 
 def pool_near_kernel(mine_ref, sib_ref, out_ref):
     out_ref[: BLOCK // 2, :] = mine_ref[...]
     out_ref[BLOCK // 2 :, :] = pooled(sib_ref[BLOCK:, :])
-
-
-def pool_halves_kernel(own_ref, sib_ref, out_ref):
-    half = BLOCK // 2
-    for num, ref in enumerate((own_ref, sib_ref)):
-        block = ref[...].astype(jnp.float32)
-        out_ref[num * half : (num + 1) * half, :] = (
-            (block[:half] + block[half:]) * 0.5
-        ).astype(jnp.bfloat16)
 
 
 def pool_kernel(*refs):
@@ -190,8 +188,8 @@
 
 
 def local_kernel(
-    count, place, x_ref, w_hbm, kv_ref, near_ref, other_ref, both_3_ref, sib_4_ref,
-    mine_ref, theirs_ref, sib_8_ref, q_ref, num_ref, tot_ref, pad, l1, w_ref, sem
+    count, place, x_ref, w_hbm, kv_ref, near_ref, other_ref, both_3_ref, sib_4_ref, both_ref,
+    q_ref, num_ref, tot_ref, pad, l1, w_ref, sem
 ):
     rows, model = x_ref.shape
     blocks = rows // BLOCK
@@ -234,7 +232,12 @@
             tot_ref[here, kl] = tot
     start = pl.multiple_of((1 - ((place[0] >> 1) & 1)) * BLOCK, BLOCK)
     sib_3 = both_3_ref[pl.ds(start, BLOCK), :]
-    far = far_blocks((near_ref, sib_3, sib_4_ref, mine_ref, theirs_ref, sib_8_ref))
+    half = BLOCK // 2
+    far = jnp.concatenate(
+        [near_ref[BLOCK:, :], sib_3, sib_4_ref[...], both_ref[:BLOCK, :]]
+        + [both_ref[BLOCK + half : 3 * BLOCK, :], both_ref[3 * BLOCK + half :, :]],
+        axis=0,
+    )
     for lanes in range(0, model, 128):
         kl = slice(lanes, lanes + 128)
         num, tot = far_sums(far, q_ref[:, kl], lanes, model)
@@ -324,18 +327,25 @@
     z_pairs = [[i, i ^ 2] for i in range(count) if not i & 2]
     both_3 = lax.all_gather(own_3, AXES, axis_index_groups=z_pairs, tiled=True)
     other_halo = lax.ppermute(other, AXES, swap)
-    mine = call(
-        unpack_kernel, bf16(3 * BLOCK // 2, 2 * model), [SMEM, *vmem(1)],
+    def pair_gather(own, bit):
+        to = partners(bit, count)
+        pairs = [[i, to[i]] for i in range(count) if not i >> bit & 1]
+        return lax.all_gather(own, AXES, axis_index_groups=pairs, tiled=True)
+
+    mine, l8 = call(
+        unpack_kernel, (block, bf16(BLOCK // 2, 2 * model)), [SMEM, *vmem(1)],
         place, spread.reshape(members, packed, 128),
         scratch=(pltpu.VMEM((members * packed, 128), jnp.float32),),
         after=(both_3, other_halo),
     )
-    theirs = exchange(mine, 0)
-    own_8 = call(own_8_kernel, block, vmem(2), mine, theirs)
-    sib_8 = exchange(own_8, 6)
-    own_4 = call(pool_kernel, block, vmem(1), both_3, after=(own_8,))
+    got_8 = exchange(l8, 6)
+    own_4 = call(pool_kernel, block, vmem(1), both_3, after=(mine,))
     sib_4 = exchange(own_4, 2)
-    own_9 = call(pool_halves_kernel, block, vmem(2), own_8, sib_8, after=(own_4,))
+    stack = call(
+        stack_kernel, bf16(2 * BLOCK, 2 * model), vmem(3), mine, l8, got_8, after=(own_4,)
+    )
+    both = pair_gather(stack, 0)
+    own_9 = call(own_9_kernel, block, vmem(1), both)
     sib_9 = exchange(own_9, 7)
     own_5 = pool(own_4, sib_4, own_9)
     sib_5 = exchange(own_5, 3)
@@ -344,8 +354,8 @@
     q, num, tot = call(
         functools.partial(local_kernel, count),
         (bf16(rows, model), f32(rows, model), f32(rows, model)),
-        [SMEM, *vmem(1), in_hbm, *vmem(8)],
-        place, tokens, stay(w_qkv), kv, near_sib, other_halo, both_3, sib_4, mine, theirs, sib_8,
+        [SMEM, *vmem(1), in_hbm, *vmem(6)],
+        place, tokens, stay(w_qkv), kv, near_sib, other_halo, both_3, sib_4, both,
         flops=10**9,
         scratch=(
             pltpu.VMEM((rows + 2 * BLOCK, 2 * model), jnp.bfloat16),

time: 64.9 us -> 61.6 us (0.949)
  the two profiles are of different devices: /device:TPU:8 before, /device:TPU:6 now
where the time goes in v17:
time: 61.6 us; the launch traced here: 61.1 us
  starting transfers between devices  38.3 us (62%)
  Pallas kernels  9.3 us (15%)
  blocking collectives  7.83 us (13%)
  waiting for transfers between devices  5.6 us (9%)
    ppermute x6, starting transfers between devices, exchange(): return lax.ppermute(own, AXES, list(enumerate(partners(bit, count))))  16.6 us
    all_to_all x1, starting transfers between devices, per_device(): lax.all_to_all(level_6, AXES, 0, 0, axis_index_groups=teams, tiled=True)  13.8 us
    pallas_call x10, Pallas kernels, call(): pl.pallas_call(body, out_shape=outs, in_specs=list(in_specs) + [pl.BlockS...  9.3 us
    ppermute x1, starting transfers between devices, per_device(): other_halo = lax.ppermute(other, AXES, swap)  7.93 us
    all_gather x1, blocking collectives, per_device(): both_3 = lax.all_gather(own_3, AXES, axis_index_groups=z_pairs, tiled=True)  5.64 us
    ppermute x6, waiting for transfers between devices, exchange(): return lax.ppermute(own, AXES, list(enumerate(partners(bit, count))))  5.6 us
    all_gather x1, blocking collectives, pair_gather(): return lax.all_gather(own, AXES, axis_index_groups=pairs, tiled=True)  2.18 us
  transfers between devices with their start and end apart: 8, of which 4 were waited for; matrix products, arithmetic and copies ran while one was open for 0% of the time, Pallas kernels for 6%

profile of v17, /device:TPU:6, one launch (start us, length us, event | category | flops | bytes accessed | tf_op | source)
XLA Modules:
  0.0 61.1 jit_solution(150263434738487969)
XLA Ops:
  0.0 2.9 %shard_map.37 = (bf16[256,1024]{1,0:T(8,128)(2,1)S(1)}, bf16[128,1024]{1,0:T(8,128)(2,1)S(1)}, bf16[64,1024]{1,0:T(8,128)(2,1)S(1)}, bf16[32,1024]{1,0:T(8,128)(2,1)S(1)}, bf16[1024,128]{1,0:T(8,128)(2,1)}) custom-call(s32[1]{0:T(128)} %bitcast.refs_0_, bf16[256,512]{1,0:T(8,128)(2,1)} %refs_1_.3, bf16[512,1536]{1,0:T(8,128)(2,1)} %refs_2_.3), custom_call_target="tpu_custom_call" | custom-call | flops 268435456 | bytes 1048576 | tf_op jit(solution)/shard_map/pallas_call | solution.py:45
  2.9 13.8 %all-to-all-start = ((bf16[32,32,128]{2,1,0:T(8,128)(2,1)}), bf16[32,32,128]{2,1,0:T(8,128)(2,1)S(1)}, u32[]{:S(2)}, u32[]{:S(2)}) async-start(bf16[32,32,128]{2,1,0:T(8,128)(2,1)} %bitcast.1), calls=%async_computation | async-start | bytes 524288 | tf_op jit(solution)/shard_map/all_to_all | solution.py:324
  16.6 1.9 %collective-permute-start = (bf16[128,1024]{1,0:T(8,128)(2,1)S(1)}, bf16[128,1024]{1,0:T(8,128)(2,1)S(1)}, u32[]{:S(2)}, u32[]{:S(2)}) collective-permute-start(bf16[128,1024]{1,0:T(8,128)(2,1)S(1)} %get-tuple-element.16), channel_id=1, source_target_pairs={{0,1},{1,0},{2,3},{3,2},{4,5},{5,4},{6,7},{7,6},{8,9},{9,8},{10,11... | collective-permute-start | bytes 786440 | tf_op jit(solution)/shard_map/ppermute | solution.py:314
  18.6 7.9 %collective-permute-start.1 = (bf16[64,1024]{1,0:T(8,128)(2,1)S(1)}, bf16[64,1024]{1,0:T(8,128)(2,1)S(1)}, u32[]{:S(2)}, u32[]{:S(2)}) collective-permute-start(bf16[64,1024]{1,0:T(8,128)(2,1)S(1)} %get-tuple-element.17), channel_id=1, source_target_pairs={{1,2},{3,4},{5,6},{7,8},{9,10},{11,12},{13,14},{15,16},{17,18},{19... | collective-permute-start | bytes 393224 | tf_op jit(solution)/shard_map/ppermute | solution.py:329
  26.5 0.0 collective-permute-done.refs_1_.refs_4_
  26.5 0.1 shard_map.38
  26.7 5.6 %all_gather.6.refs_2_.refs_0_.refs_6_ = bf16[128,1024]{1,0:T(8,128)(2,1)S(1)} all-gather(bf16[64,1024]{1,0:T(8,128)(2,1)S(1)} %shard_map.38), channel_id=1, replica_groups={{0,2},{1,3},{4,6},{5,7},{8,10},{9,11},{12,14},{13,15},{16,18},{17,19},{..., dimensions={0}, use_global_device_ids=true | all-gather | bytes 393216 | tf_op jit(solution)/shard_map/all_gather | solution.py:328
  32.3 0.6 shard_map.39
  32.9 2.1 %collective-permute-start.3 = (bf16[32,1024]{1,0:T(8,128)(2,1)S(1)}, bf16[32,1024]{1,0:T(8,128)(2,1)S(1)}, u32[]{:S(2)}, u32[]{:S(2)}) collective-permute-start(bf16[32,1024]{1,0:T(8,128)(2,1)S(1)} %get-tuple-element.21.refs_1_), channel_id=1, source_target_pairs={{0,96},{1,97},{2,98},{3,99},{4,100},{5,101},{6,102},{7,103},{8,104... | collective-permute-start | bytes 196616 | tf_op jit(solution)/shard_map/ppermute | solution.py:314
  35.0 0.2 shard_map.40.refs_3_.refs_0_
  35.2 0.0 copy-start
  35.2 4.7 %collective-permute-start.2 = (bf16[64,1024]{1,0:T(8,128)(2,1)S(1)}, bf16[64,1024]{1,0:T(8,128)(2,1)S(1)}, u32[]{:S(2)}, u32[]{:S(2)}) collective-permute-start(bf16[64,1024]{1,0:T(8,128)(2,1)S(1)} %shard_map.40.refs_3_.refs_0_), channel_id=1, source_target_pairs={{0,4},{1,5},{2,6},{3,7},{4,0},{5,1},{6,2},{7,3},{8,12},{9,13},{10,... | collective-permute-start | bytes 393224 | tf_op jit(solution)/shard_map/ppermute | solution.py:314
  39.9 1.2 %collective-permute-done.3.refs_2_ = bf16[32,1024]{1,0:T(8,128)(2,1)S(1)} collective-permute-done((bf16[32,1024]{1,0:T(8,128)(2,1)S(1)}, bf16[32,1024]{1,0:T(8,128)(2,1)S(1)}, u32[]{:S(2)}, u32[]{:S(2)}) %collective-permute-start.3) | collective-permute-done | bytes 65568 | tf_op jit(solution)/shard_map/ppermute | solution.py:314
  41.2 2.2 %all_gather.7.refs_0_.refs_8_ = bf16[256,1024]{1,0:T(8,128)(2,1)S(1)} all-gather(bf16[128,1024]{1,0:T(8,128)(2,1)S(1)} %shard_map.41), channel_id=1, replica_groups={{0,1},{2,3},{4,5},{6,7},{8,9},{10,11},{12,13},{14,15},{16,17},{18,19},{..., dimensions={0}, use_global_device_ids=true | all-gather | bytes 786432 | tf_op jit(solution)/shard_map/all_gather | solution.py:333
  43.4 2.4 %collective-permute-start.4 = (bf16[64,1024]{1,0:T(8,128)(2,1)S(1)}, bf16[64,1024]{1,0:T(8,128)(2,1)S(1)}, u32[]{:S(2)}, u32[]{:S(2)}) collective-permute-start(bf16[64,1024]{1,0:T(8,128)(2,1)S(1)} %shard_map.42.refs_2_.refs_0_), channel_id=1, source_target_pairs={{0,128},{1,129},{2,130},{3,131},{4,132},{5,133},{6,134},{7,135},{8... | collective-permute-start | bytes 393224 | tf_op jit(solution)/shard_map/ppermute | solution.py:314
  45.8 0.1 collective-permute-done.2.refs_1_.refs_7_
  45.9 0.2 shard_map.43.refs_2_
  46.1 3.5 %collective-permute-start.5 = (bf16[64,1024]{1,0:T(8,128)(2,1)S(1)}, bf16[64,1024]{1,0:T(8,128)(2,1)S(1)}, u32[]{:S(2)}, u32[]{:S(2)}) collective-permute-start(bf16[64,1024]{1,0:T(8,128)(2,1)S(1)} %shard_map.43.refs_2_), channel_id=1, source_target_pairs={{0,12},{1,13},{2,14},{3,15},{4,8},{5,9},{6,10},{7,11},{8,4},{9,5},... | collective-permute-start | bytes 393224 | tf_op jit(solution)/shard_map/ppermute | solution.py:314
  49.6 1.2 %collective-permute-done.4.refs_1_.refs_4_ = bf16[64,1024]{1,0:T(8,128)(2,1)S(1)} collective-permute-done((bf16[64,1024]{1,0:T(8,128)(2,1)S(1)}, bf16[64,1024]{1,0:T(8,128)(2,1)S(1)}, u32[]{:S(2)}, u32[]{:S(2)}) %collective-permute-start.4) | collective-permute-done | bytes 131104 | tf_op jit(solution)/shard_map/ppermute | solution.py:314
  50.8 0.2 shard_map.44.refs_9_
  51.0 1.9 %collective-permute-start.6 = (bf16[64,1024]{1,0:T(8,128)(2,1)S(1)}, bf16[64,1024]{1,0:T(8,128)(2,1)S(1)}, u32[]{:S(2)}, u32[]{:S(2)}) collective-permute-start(bf16[64,1024]{1,0:T(8,128)(2,1)S(1)} %shard_map.44.refs_9_), channel_id=1, source_target_pairs={{0,384},{1,385},{2,386},{3,387},{4,388},{5,389},{6,390},{7,391},{8... | collective-permute-start | bytes 393224 | tf_op jit(solution)/shard_map/ppermute | solution.py:314
  52.9 3.1 %shard_map.45 = (bf16[256,512]{1,0:T(8,128)(2,1)S(1)}, f32[256,512]{1,0:T(8,128)S(1)}, f32[256,512]{1,0:T(8,128)S(1)}) custom-call(s32[1]{0:T(128)} %bitcast.refs_0_, bf16[256,512]{1,0:T(8,128)(2,1)S(1)} %copy-done, bf16[512,1536]{1,0:T(8,128)(2,1)} %refs_2_.3, bf16[256,1024]{1,0:T(8,128)(2,1)S(1)} %get-tuple-element.15.refs_3_, ...), custom_call_target="tpu_custom_call" | custom-call | flops 1000000000 | bytes 1048576 | tf_op jit(solution)/shard_map/pallas_call | solution.py:45
  56.1 3.0 %collective-permute-done.6.refs_5_ = bf16[64,1024]{1,0:T(8,128)(2,1)S(1)} collective-permute-done((bf16[64,1024]{1,0:T(8,128)(2,1)S(1)}, bf16[64,1024]{1,0:T(8,128)(2,1)S(1)}, u32[]{:S(2)}, u32[]{:S(2)}) %collective-permute-start.6) | collective-permute-done | bytes 131104 | tf_op jit(solution)/shard_map/ppermute | solution.py:314
  59.1 2.1 %shard_map.46 = bf16[256,512]{1,0:T(8,128)(2,1)} custom-call(bf16[256,512]{1,0:T(8,128)(2,1)S(1)} %get-tuple-element.22.refs_0_, f32[256,512]{1,0:T(8,128)S(1)} %get-tuple-element.23.refs_1_, f32[256,512]{1,0:T(8,128)S(1)} %get-tuple-element.24.refs_2_, bf16[64,1024]{1,0:T(8,128)(2,1)S(1)} %collective-permute-done.5.refs_3_, ...), custom_call_target="tpu_custom_call" | custom-call | flops 1000000000 | bytes 1048576 | tf_op jit(solution)/shard_map/pallas_call | solution.py:45
  (6 shorter events, 0.1 us)
Async XLA Ops:
  2.9 29.4 %all-to-all-start = ((bf16[32,32,128]{2,1,0:T(8,128)(2,1)}), bf16[32,32,128]{2,1,0:T(8,128)(2,1)S(1)}, u32[]{:S(2)}, u32[]{:S(2)}) async-start(bf16[32,32,128]{2,1,0:T(8,128)(2,1)} %bitcast.1), calls=%async_computation | async-start | bytes 524288 | tf_op jit(solution)/shard_map/all_to_all | solution.py:324
  16.6 9.9 %collective-permute-start = (bf16[128,1024]{1,0:T(8,128)(2,1)S(1)}, bf16[128,1024]{1,0:T(8,128)(2,1)S(1)}, u32[]{:S(2)}, u32[]{:S(2)}) collective-permute-start(bf16[128,1024]{1,0:T(8,128)(2,1)S(1)} %get-tuple-element.16), channel_id=1, source_target_pairs={{0,1},{1,0},{2,3},{3,2},{4,5},{5,4},{6,7},{7,6},{8,9},{9,8},{10,11... | collective-permute-start | bytes 786440 | tf_op jit(solution)/shard_map/ppermute | solution.py:314
  18.6 13.7 %collective-permute-start.1 = (bf16[64,1024]{1,0:T(8,128)(2,1)S(1)}, bf16[64,1024]{1,0:T(8,128)(2,1)S(1)}, u32[]{:S(2)}, u32[]{:S(2)}) collective-permute-start(bf16[64,1024]{1,0:T(8,128)(2,1)S(1)} %get-tuple-element.17), channel_id=1, source_target_pairs={{1,2},{3,4},{5,6},{7,8},{9,10},{11,12},{13,14},{15,16},{17,18},{19... | collective-permute-start | bytes 393224 | tf_op jit(solution)/shard_map/ppermute | solution.py:329
  32.9 8.3 %collective-permute-start.3 = (bf16[32,1024]{1,0:T(8,128)(2,1)S(1)}, bf16[32,1024]{1,0:T(8,128)(2,1)S(1)}, u32[]{:S(2)}, u32[]{:S(2)}) collective-permute-start(bf16[32,1024]{1,0:T(8,128)(2,1)S(1)} %get-tuple-element.21.refs_1_), channel_id=1, source_target_pairs={{0,96},{1,97},{2,98},{3,99},{4,100},{5,101},{6,102},{7,103},{8,104... | collective-permute-start | bytes 196616 | tf_op jit(solution)/shard_map/ppermute | solution.py:314
  35.2 17.7 %copy-start = (bf16[256,512]{1,0:T(8,128)(2,1)S(1)}, bf16[256,512]{1,0:T(8,128)(2,1)}, u32[]{:S(2)}) copy-start(bf16[256,512]{1,0:T(8,128)(2,1)} %refs_1_.3) | copy-start | bytes 786436
  35.2 10.7 %collective-permute-start.2 = (bf16[64,1024]{1,0:T(8,128)(2,1)S(1)}, bf16[64,1024]{1,0:T(8,128)(2,1)S(1)}, u32[]{:S(2)}, u32[]{:S(2)}) collective-permute-start(bf16[64,1024]{1,0:T(8,128)(2,1)S(1)} %shard_map.40.refs_3_.refs_0_), channel_id=1, source_target_pairs={{0,4},{1,5},{2,6},{3,7},{4,0},{5,1},{6,2},{7,3},{8,12},{9,13},{10,... | collective-permute-start | bytes 393224 | tf_op jit(solution)/shard_map/ppermute | solution.py:314
  43.4 7.4 %collective-permute-start.4 = (bf16[64,1024]{1,0:T(8,128)(2,1)S(1)}, bf16[64,1024]{1,0:T(8,128)(2,1)S(1)}, u32[]{:S(2)}, u32[]{:S(2)}) collective-permute-start(bf16[64,1024]{1,0:T(8,128)(2,1)S(1)} %shard_map.42.refs_2_.refs_0_), channel_id=1, source_target_pairs={{0,128},{1,129},{2,130},{3,131},{4,132},{5,133},{6,134},{7,135},{8... | collective-permute-start | bytes 393224 | tf_op jit(solution)/shard_map/ppermute | solution.py:314
  46.1 9.9 %collective-permute-start.5 = (bf16[64,1024]{1,0:T(8,128)(2,1)S(1)}, bf16[64,1024]{1,0:T(8,128)(2,1)S(1)}, u32[]{:S(2)}, u32[]{:S(2)}) collective-permute-start(bf16[64,1024]{1,0:T(8,128)(2,1)S(1)} %shard_map.43.refs_2_), channel_id=1, source_target_pairs={{0,12},{1,13},{2,14},{3,15},{4,8},{5,9},{6,10},{7,11},{8,4},{9,5},... | collective-permute-start | bytes 393224 | tf_op jit(solution)/shard_map/ppermute | solution.py:314
  51.0 8.1 %collective-permute-start.6 = (bf16[64,1024]{1,0:T(8,128)(2,1)S(1)}, bf16[64,1024]{1,0:T(8,128)(2,1)S(1)}, u32[]{:S(2)}, u32[]{:S(2)}) collective-permute-start(bf16[64,1024]{1,0:T(8,128)(2,1)S(1)} %shard_map.44.refs_9_), channel_id=1, source_target_pairs={{0,384},{1,385},{2,386},{3,387},{4,388},{5,389},{6,390},{7,391},{8... | collective-permute-start | bytes 393224 | tf_op jit(solution)/shard_map/ppermute | solution.py:314

commit v18 on v17

--- a/solution.py
+++ b/solution.py
@@ -326,7 +326,6 @@
     own_3 = call(pool_near_kernel, block, vmem(2), level_3, near_sib)
     z_pairs = [[i, i ^ 2] for i in range(count) if not i & 2]
     both_3 = lax.all_gather(own_3, AXES, axis_index_groups=z_pairs, tiled=True)
-    other_halo = lax.ppermute(other, AXES, swap)
     def pair_gather(own, bit):
         to = partners(bit, count)
         pairs = [[i, to[i]] for i in range(count) if not i >> bit & 1]
@@ -336,11 +335,13 @@
         unpack_kernel, (block, bf16(BLOCK // 2, 2 * model)), [SMEM, *vmem(1)],
         place, spread.reshape(members, packed, 128),
         scratch=(pltpu.VMEM((members * packed, 128), jnp.float32),),
-        after=(both_3, other_halo),
+        after=(both_3,),
     )
     got_8 = exchange(l8, 6)
     own_4 = call(pool_kernel, block, vmem(1), both_3, after=(mine,))
     sib_4 = exchange(own_4, 2)
+    other, _ = lax.optimization_barrier((other, own_4))
+    other_halo = lax.ppermute(other, AXES, swap)
     stack = call(
         stack_kernel, bf16(2 * BLOCK, 2 * model), vmem(3), mine, l8, got_8, after=(own_4,)
     )
@@ -349,7 +350,7 @@
     sib_9 = exchange(own_9, 7)
     own_5 = pool(own_4, sib_4, own_9)
     sib_5 = exchange(own_5, 3)
-    own_10 = pool(own_9, sib_9, own_5)
+    own_10 = pool(own_9, sib_9, own_5, other_halo)
     sib_10 = exchange(own_10, 8)
     q, num, tot = call(
         functools.partial(local_kernel, count),

time: 61.6 us -> 62.5 us (1.015)
  blocking collectives: 7.83 us -> 10.3 us
  starting transfers between devices: 38.3 us -> 35.9 us
  waiting for transfers between devices: 5.6 us -> 6.35 us
    ppermute x1, starting transfers between devices: 7.93 us -> 3.37 us  [per_device(): other_halo = lax.ppermute(other, AXES, swap)]
    all_gather x1, blocking collectives: 5.64 us -> 8.08 us  [per_device(): both_3 = lax.all_gather(own_3, AXES, axis_index_groups=z_pairs, tiled=True)]
    ppermute x6, starting transfers between devices: 16.6 us -> 18.8 us  [exchange(): return lax.ppermute(own, AXES, list(enumerate(partners(bit, count))))]
where the time goes in v18:
time: 62.5 us; the launch traced here: 62 us
  starting transfers between devices  35.9 us (57%)
  blocking collectives  10.3 us (16%)
  Pallas kernels  9.31 us (15%)
  waiting for transfers between devices  6.35 us (10%)
    ppermute x6, starting transfers between devices, exchange(): return lax.ppermute(own, AXES, list(enumerate(partners(bit, count))))  18.8 us
    all_to_all x1, starting transfers between devices, per_device(): lax.all_to_all(level_6, AXES, 0, 0, axis_index_groups=teams, tiled=True)  13.8 us
    pallas_call x10, Pallas kernels, call(): pl.pallas_call(body, out_shape=outs, in_specs=list(in_specs) + [pl.BlockS...  9.31 us
    all_gather x1, blocking collectives, per_device(): both_3 = lax.all_gather(own_3, AXES, axis_index_groups=z_pairs, tiled=True)  8.08 us
    ppermute x6, waiting for transfers between devices, exchange(): return lax.ppermute(own, AXES, list(enumerate(partners(bit, count))))  6 us
    ppermute x1, starting transfers between devices, per_device(): other_halo = lax.ppermute(other, AXES, swap)  3.37 us
    all_gather x1, blocking collectives, pair_gather(): return lax.all_gather(own, AXES, axis_index_groups=pairs, tiled=True)  2.18 us
  transfers between devices with their start and end apart: 8, of which 4 were waited for; matrix products, arithmetic and copies ran while one was open for 0% of the time, Pallas kernels for 6%

profile of v18, /device:TPU:6, one launch (start us, length us, event | category | flops | bytes accessed | tf_op | source)
XLA Modules:
  0.0 62.0 jit_solution(2278266652791684708)
XLA Ops:
  0.0 2.9 %shard_map.37 = (bf16[256,1024]{1,0:T(8,128)(2,1)S(1)}, bf16[128,1024]{1,0:T(8,128)(2,1)S(1)}, bf16[64,1024]{1,0:T(8,128)(2,1)S(1)}, bf16[32,1024]{1,0:T(8,128)(2,1)S(1)}, bf16[1024,128]{1,0:T(8,128)(2,1)}) custom-call(s32[1]{0:T(128)} %bitcast.refs_0_, bf16[256,512]{1,0:T(8,128)(2,1)} %refs_1_.3, bf16[512,1536]{1,0:T(8,128)(2,1)} %refs_2_.3), custom_call_target="tpu_custom_call" | custom-call | flops 268435456 | bytes 1048576 | tf_op jit(solution)/shard_map/pallas_call | solution.py:45
  2.9 13.8 %all-to-all-start = ((bf16[32,32,128]{2,1,0:T(8,128)(2,1)}), bf16[32,32,128]{2,1,0:T(8,128)(2,1)S(1)}, u32[]{:S(2)}, u32[]{:S(2)}) async-start(bf16[32,32,128]{2,1,0:T(8,128)(2,1)} %bitcast.1), calls=%async_computation | async-start | bytes 524288 | tf_op jit(solution)/shard_map/all_to_all | solution.py:324
  16.6 1.9 %collective-permute-start = (bf16[128,1024]{1,0:T(8,128)(2,1)S(1)}, bf16[128,1024]{1,0:T(8,128)(2,1)S(1)}, u32[]{:S(2)}, u32[]{:S(2)}) collective-permute-start(bf16[128,1024]{1,0:T(8,128)(2,1)S(1)} %get-tuple-element.17), channel_id=1, source_target_pairs={{0,1},{1,0},{2,3},{3,2},{4,5},{5,4},{6,7},{7,6},{8,9},{9,8},{10,11... | collective-permute-start | bytes 786440 | tf_op jit(solution)/shard_map/ppermute | solution.py:314
  18.6 1.5 %collective-permute-done.refs_1_.refs_4_ = bf16[128,1024]{1,0:T(8,128)(2,1)S(1)} collective-permute-done((bf16[128,1024]{1,0:T(8,128)(2,1)S(1)}, bf16[128,1024]{1,0:T(8,128)(2,1)S(1)}, u32[]{:S(2)}, u32[]{:S(2)}) %collective-permute-start) | collective-permute-done | bytes 262176 | tf_op jit(solution)/shard_map/ppermute | solution.py:314
  20.1 0.1 shard_map.38
  20.2 8.1 %all_gather.6.refs_2_.refs_0_.refs_6_ = bf16[128,1024]{1,0:T(8,128)(2,1)S(1)} all-gather(bf16[64,1024]{1,0:T(8,128)(2,1)S(1)} %shard_map.38), channel_id=1, replica_groups={{0,2},{1,3},{4,6},{5,7},{8,10},{9,11},{12,14},{13,15},{16,18},{17,19},{..., dimensions={0}, use_global_device_ids=true | all-gather | bytes 393216 | tf_op jit(solution)/shard_map/all_gather | solution.py:328
  28.3 0.4 all-to-all-done.refs_1_
  28.6 0.6 shard_map.39
  29.2 4.0 %collective-permute-start.3 = (bf16[32,1024]{1,0:T(8,128)(2,1)S(1)}, bf16[32,1024]{1,0:T(8,128)(2,1)S(1)}, u32[]{:S(2)}, u32[]{:S(2)}) collective-permute-start(bf16[32,1024]{1,0:T(8,128)(2,1)S(1)} %get-tuple-element.23.refs_1_), channel_id=1, source_target_pairs={{0,96},{1,97},{2,98},{3,99},{4,100},{5,101},{6,102},{7,103},{8,104... | collective-permute-start | bytes 196616 | tf_op jit(solution)/shard_map/ppermute | solution.py:314
  33.2 0.2 shard_map.40.refs_3_.refs_0_
  33.4 4.7 %collective-permute-start.2 = (bf16[64,1024]{1,0:T(8,128)(2,1)S(1)}, bf16[64,1024]{1,0:T(8,128)(2,1)S(1)}, u32[]{:S(2)}, u32[]{:S(2)}) collective-permute-start(bf16[64,1024]{1,0:T(8,128)(2,1)S(1)} %shard_map.40.refs_3_.refs_0_), channel_id=1, source_target_pairs={{0,4},{1,5},{2,6},{3,7},{4,0},{5,1},{6,2},{7,3},{8,12},{9,13},{10,... | collective-permute-start | bytes 393224 | tf_op jit(solution)/shard_map/ppermute | solution.py:314
  38.1 0.0 copy-start
  38.1 3.4 %collective-permute-start.1 = (bf16[64,1024]{1,0:T(8,128)(2,1)S(1)}, bf16[64,1024]{1,0:T(8,128)(2,1)S(1)}, u32[]{:S(2)}, u32[]{:S(2)}) collective-permute-start(bf16[64,1024]{1,0:T(8,128)(2,1)S(1)} %get-tuple-element.22), channel_id=1, source_target_pairs={{1,2},{3,4},{5,6},{7,8},{9,10},{11,12},{13,14},{15,16},{17,18},{19... | collective-permute-start | bytes 393224 | tf_op jit(solution)/shard_map/ppermute | solution.py:344
  41.5 0.0 collective-permute-done.3.refs_2_
  41.6 2.2 %all_gather.7.refs_0_.refs_8_ = bf16[256,1024]{1,0:T(8,128)(2,1)S(1)} all-gather(bf16[128,1024]{1,0:T(8,128)(2,1)S(1)} %shard_map.41), channel_id=1, replica_groups={{0,1},{2,3},{4,5},{6,7},{8,9},{10,11},{12,13},{14,15},{16,17},{18,19},{..., dimensions={0}, use_global_device_ids=true | all-gather | bytes 786432 | tf_op jit(solution)/shard_map/all_gather | solution.py:332
  43.8 2.4 %collective-permute-start.4 = (bf16[64,1024]{1,0:T(8,128)(2,1)S(1)}, bf16[64,1024]{1,0:T(8,128)(2,1)S(1)}, u32[]{:S(2)}, u32[]{:S(2)}) collective-permute-start(bf16[64,1024]{1,0:T(8,128)(2,1)S(1)} %shard_map.42.refs_2_.refs_0_), channel_id=1, source_target_pairs={{0,128},{1,129},{2,130},{3,131},{4,132},{5,133},{6,134},{7,135},{8... | collective-permute-start | bytes 393224 | tf_op jit(solution)/shard_map/ppermute | solution.py:314
  46.2 0.2 shard_map.43.refs_2_
  46.4 3.8 %collective-permute-start.5 = (bf16[64,1024]{1,0:T(8,128)(2,1)S(1)}, bf16[64,1024]{1,0:T(8,128)(2,1)S(1)}, u32[]{:S(2)}, u32[]{:S(2)}) collective-permute-start(bf16[64,1024]{1,0:T(8,128)(2,1)S(1)} %shard_map.43.refs_2_), channel_id=1, source_target_pairs={{0,12},{1,13},{2,14},{3,15},{4,8},{5,9},{6,10},{7,11},{8,4},{9,5},... | collective-permute-start | bytes 393224 | tf_op jit(solution)/shard_map/ppermute | solution.py:314
  50.2 1.4 %collective-permute-done.4.refs_1_.refs_4_ = bf16[64,1024]{1,0:T(8,128)(2,1)S(1)} collective-permute-done((bf16[64,1024]{1,0:T(8,128)(2,1)S(1)}, bf16[64,1024]{1,0:T(8,128)(2,1)S(1)}, u32[]{:S(2)}, u32[]{:S(2)}) %collective-permute-start.4) | collective-permute-done | bytes 131104 | tf_op jit(solution)/shard_map/ppermute | solution.py:314
  51.6 0.2 shard_map.44.refs_9_
  51.8 1.9 %collective-permute-start.6 = (bf16[64,1024]{1,0:T(8,128)(2,1)S(1)}, bf16[64,1024]{1,0:T(8,128)(2,1)S(1)}, u32[]{:S(2)}, u32[]{:S(2)}) collective-permute-start(bf16[64,1024]{1,0:T(8,128)(2,1)S(1)} %shard_map.44.refs_9_), channel_id=1, source_target_pairs={{0,384},{1,385},{2,386},{3,387},{4,388},{5,389},{6,390},{7,391},{8... | collective-permute-start | bytes 393224 | tf_op jit(solution)/shard_map/ppermute | solution.py:314
  53.7 3.1 %shard_map.45 = (bf16[256,512]{1,0:T(8,128)(2,1)S(1)}, f32[256,512]{1,0:T(8,128)S(1)}, f32[256,512]{1,0:T(8,128)S(1)}) custom-call(s32[1]{0:T(128)} %bitcast.refs_0_, bf16[256,512]{1,0:T(8,128)(2,1)S(1)} %copy-done, bf16[512,1536]{1,0:T(8,128)(2,1)} %refs_2_.3, bf16[256,1024]{1,0:T(8,128)(2,1)S(1)} %get-tuple-element.16.refs_3_, ...), custom_call_target="tpu_custom_call" | custom-call | flops 1000000000 | bytes 1048576 | tf_op jit(solution)/shard_map/pallas_call | solution.py:45
  56.8 3.1 %collective-permute-done.6.refs_5_ = bf16[64,1024]{1,0:T(8,128)(2,1)S(1)} collective-permute-done((bf16[64,1024]{1,0:T(8,128)(2,1)S(1)}, bf16[64,1024]{1,0:T(8,128)(2,1)S(1)}, u32[]{:S(2)}, u32[]{:S(2)}) %collective-permute-start.6) | collective-permute-done | bytes 131104 | tf_op jit(solution)/shard_map/ppermute | solution.py:314
  59.9 2.1 %shard_map.46 = bf16[256,512]{1,0:T(8,128)(2,1)} custom-call(bf16[256,512]{1,0:T(8,128)(2,1)S(1)} %get-tuple-element.24.refs_0_, f32[256,512]{1,0:T(8,128)S(1)} %get-tuple-element.25.refs_1_, f32[256,512]{1,0:T(8,128)S(1)} %get-tuple-element.26.refs_2_, bf16[64,1024]{1,0:T(8,128)(2,1)S(1)} %collective-permute-done.5.refs_3_, ...), custom_call_target="tpu_custom_call" | custom-call | flops 1000000000 | bytes 1048576 | tf_op jit(solution)/shard_map/pallas_call | solution.py:45
  (6 shorter events, 0.1 us)
Async XLA Ops:
  2.9 25.8 %all-to-all-start = ((bf16[32,32,128]{2,1,0:T(8,128)(2,1)}), bf16[32,32,128]{2,1,0:T(8,128)(2,1)S(1)}, u32[]{:S(2)}, u32[]{:S(2)}) async-start(bf16[32,32,128]{2,1,0:T(8,128)(2,1)} %bitcast.1), calls=%async_computation | async-start | bytes 524288 | tf_op jit(solution)/shard_map/all_to_all | solution.py:324
  16.6 3.4 %collective-permute-start = (bf16[128,1024]{1,0:T(8,128)(2,1)S(1)}, bf16[128,1024]{1,0:T(8,128)(2,1)S(1)}, u32[]{:S(2)}, u32[]{:S(2)}) collective-permute-start(bf16[128,1024]{1,0:T(8,128)(2,1)S(1)} %get-tuple-element.17), channel_id=1, source_target_pairs={{0,1},{1,0},{2,3},{3,2},{4,5},{5,4},{6,7},{7,6},{8,9},{9,8},{10,11... | collective-permute-start | bytes 786440 | tf_op jit(solution)/shard_map/ppermute | solution.py:314
  29.2 12.3 %collective-permute-start.3 = (bf16[32,1024]{1,0:T(8,128)(2,1)S(1)}, bf16[32,1024]{1,0:T(8,128)(2,1)S(1)}, u32[]{:S(2)}, u32[]{:S(2)}) collective-permute-start(bf16[32,1024]{1,0:T(8,128)(2,1)S(1)} %get-tuple-element.23.refs_1_), channel_id=1, source_target_pairs={{0,96},{1,97},{2,98},{3,99},{4,100},{5,101},{6,102},{7,103},{8,104... | collective-permute-start | bytes 196616 | tf_op jit(solution)/shard_map/ppermute | solution.py:314
  33.4 12.8 %collective-permute-start.2 = (bf16[64,1024]{1,0:T(8,128)(2,1)S(1)}, bf16[64,1024]{1,0:T(8,128)(2,1)S(1)}, u32[]{:S(2)}, u32[]{:S(2)}) collective-permute-start(bf16[64,1024]{1,0:T(8,128)(2,1)S(1)} %shard_map.40.refs_3_.refs_0_), channel_id=1, source_target_pairs={{0,4},{1,5},{2,6},{3,7},{4,0},{5,1},{6,2},{7,3},{8,12},{9,13},{10,... | collective-permute-start | bytes 393224 | tf_op jit(solution)/shard_map/ppermute | solution.py:314
  38.1 15.6 %copy-start = (bf16[256,512]{1,0:T(8,128)(2,1)S(1)}, bf16[256,512]{1,0:T(8,128)(2,1)}, u32[]{:S(2)}) copy-start(bf16[256,512]{1,0:T(8,128)(2,1)} %refs_1_.3) | copy-start | bytes 786436
  38.1 12.1 %collective-permute-start.1 = (bf16[64,1024]{1,0:T(8,128)(2,1)S(1)}, bf16[64,1024]{1,0:T(8,128)(2,1)S(1)}, u32[]{:S(2)}, u32[]{:S(2)}) collective-permute-start(bf16[64,1024]{1,0:T(8,128)(2,1)S(1)} %get-tuple-element.22), channel_id=1, source_target_pairs={{1,2},{3,4},{5,6},{7,8},{9,10},{11,12},{13,14},{15,16},{17,18},{19... | collective-permute-start | bytes 393224 | tf_op jit(solution)/shard_map/ppermute | solution.py:344
  43.8 7.8 %collective-permute-start.4 = (bf16[64,1024]{1,0:T(8,128)(2,1)S(1)}, bf16[64,1024]{1,0:T(8,128)(2,1)S(1)}, u32[]{:S(2)}, u32[]{:S(2)}) collective-permute-start(bf16[64,1024]{1,0:T(8,128)(2,1)S(1)} %shard_map.42.refs_2_.refs_0_), channel_id=1, source_target_pairs={{0,128},{1,129},{2,130},{3,131},{4,132},{5,133},{6,134},{7,135},{8... | collective-permute-start | bytes 393224 | tf_op jit(solution)/shard_map/ppermute | solution.py:314
  46.4 10.4 %collective-permute-start.5 = (bf16[64,1024]{1,0:T(8,128)(2,1)S(1)}, bf16[64,1024]{1,0:T(8,128)(2,1)S(1)}, u32[]{:S(2)}, u32[]{:S(2)}) collective-permute-start(bf16[64,1024]{1,0:T(8,128)(2,1)S(1)} %shard_map.43.refs_2_), channel_id=1, source_target_pairs={{0,12},{1,13},{2,14},{3,15},{4,8},{5,9},{6,10},{7,11},{8,4},{9,5},... | collective-permute-start | bytes 393224 | tf_op jit(solution)/shard_map/ppermute | solution.py:314
  51.8 8.2 %collective-permute-start.6 = (bf16[64,1024]{1,0:T(8,128)(2,1)S(1)}, bf16[64,1024]{1,0:T(8,128)(2,1)S(1)}, u32[]{:S(2)}, u32[]{:S(2)}) collective-permute-start(bf16[64,1024]{1,0:T(8,128)(2,1)S(1)} %shard_map.44.refs_9_), channel_id=1, source_target_pairs={{0,384},{1,385},{2,386},{3,387},{4,388},{5,389},{6,390},{7,391},{8... | collective-permute-start | bytes 393224 | tf_op jit(solution)/shard_map/ppermute | solution.py:314

commit v19 on v17

--- a/solution.py
+++ b/solution.py
@@ -189,7 +189,7 @@
 
 def local_kernel(
     count, place, x_ref, w_hbm, kv_ref, near_ref, other_ref, both_3_ref, sib_4_ref, both_ref,
-    q_ref, num_ref, tot_ref, pad, l1, w_ref, sem
+    sib_9_ref, q_ref, num_ref, tot_ref, pad, l1, w_ref, sem
 ):
     rows, model = x_ref.shape
     blocks = rows // BLOCK
@@ -235,7 +235,7 @@
     half = BLOCK // 2
     far = jnp.concatenate(
         [near_ref[BLOCK:, :], sib_3, sib_4_ref[...], both_ref[:BLOCK, :]]
-        + [both_ref[BLOCK + half : 3 * BLOCK, :], both_ref[3 * BLOCK + half :, :]],
+        + [both_ref[BLOCK + half : 3 * BLOCK, :], both_ref[3 * BLOCK + half :, :], sib_9_ref[...]],
         axis=0,
     )
     for lanes in range(0, model, 128):
@@ -262,12 +262,12 @@
 
 
 def final_kernel(
-    q_ref, num_in, tot_in, sib_5_ref, sib_9_ref, sib_10_ref, w_hbm, out_ref, att, w_ref, sem
+    q_ref, num_in, tot_in, sib_5_ref, sib_10_ref, w_hbm, out_ref, att, w_ref, sem
 ):
     copy = pltpu.make_async_copy(w_hbm, w_ref, sem)
     copy.start()
     model = q_ref.shape[1]
-    far = far_blocks((sib_5_ref, sib_9_ref, sib_10_ref))
+    far = far_blocks((sib_5_ref, sib_10_ref))
     for lanes in range(0, model, 128):
         at = slice(lanes, lanes + 128)
         num, tot = far_sums(far, q_ref[:, at], lanes, model)
@@ -354,8 +354,8 @@
     q, num, tot = call(
         functools.partial(local_kernel, count),
         (bf16(rows, model), f32(rows, model), f32(rows, model)),
-        [SMEM, *vmem(1), in_hbm, *vmem(6)],
-        place, tokens, stay(w_qkv), kv, near_sib, other_halo, both_3, sib_4, both,
+        [SMEM, *vmem(1), in_hbm, *vmem(7)],
+        place, tokens, stay(w_qkv), kv, near_sib, other_halo, both_3, sib_4, both, sib_9,
         flops=10**9,
         scratch=(
             pltpu.VMEM((rows + 2 * BLOCK, 2 * model), jnp.bfloat16),
@@ -368,8 +368,8 @@
     return call(
         final_kernel,
         bf16(rows, model),
-        [*vmem(6), in_hbm],
-        q, num, tot, sib_5, sib_9, sib_10, stay(w_out),
+        [*vmem(5), in_hbm],
+        q, num, tot, sib_5, sib_10, stay(w_out),
         flops=10**9,
         scratch=(
             pltpu.VMEM((rows, model), jnp.bfloat16),

time: 61.6 us -> 61.6 us (level)
  transfers between devices with their start and end apart: 8 -> 8, of which waited for: 4 -> 4; matrix products, arithmetic and copies ran while one was open for 0% -> 0% of each run, Pallas kernels for 6% -> 7%
where the time goes in v19:
time: 61.6 us; the launch traced here: 61.1 us
  starting transfers between devices  38.3 us (62%)
  Pallas kernels  9.54 us (15%)
  blocking collectives  7.83 us (13%)
  waiting for transfers between devices  5.35 us (9%)
    ppermute x6, starting transfers between devices, exchange(): return lax.ppermute(own, AXES, list(enumerate(partners(bit, count))))  16.6 us
    all_to_all x1, starting transfers between devices, per_device(): lax.all_to_all(level_6, AXES, 0, 0, axis_index_groups=teams, tiled=True)  13.8 us
    pallas_call x10, Pallas kernels, call(): pl.pallas_call(body, out_shape=outs, in_specs=list(in_specs) + [pl.BlockS...  9.54 us
    ppermute x1, starting transfers between devices, per_device(): other_halo = lax.ppermute(other, AXES, swap)  7.93 us
    all_gather x1, blocking collectives, per_device(): both_3 = lax.all_gather(own_3, AXES, axis_index_groups=z_pairs, tiled=True)  5.64 us
    ppermute x6, waiting for transfers between devices, exchange(): return lax.ppermute(own, AXES, list(enumerate(partners(bit, count))))  5.35 us
    all_gather x1, blocking collectives, pair_gather(): return lax.all_gather(own, AXES, axis_index_groups=pairs, tiled=True)  2.18 us
  transfers between devices with their start and end apart: 8, of which 4 were waited for; matrix products, arithmetic and copies ran while one was open for 0% of the time, Pallas kernels for 7%

profile of v19, /device:TPU:6, one launch (start us, length us, event | category | flops | bytes accessed | tf_op | source)
XLA Modules:
  0.0 61.1 jit_solution(14488588110776102824)
XLA Ops:
  0.0 2.9 %shard_map.37 = (bf16[256,1024]{1,0:T(8,128)(2,1)S(1)}, bf16[128,1024]{1,0:T(8,128)(2,1)S(1)}, bf16[64,1024]{1,0:T(8,128)(2,1)S(1)}, bf16[32,1024]{1,0:T(8,128)(2,1)S(1)}, bf16[1024,128]{1,0:T(8,128)(2,1)}) custom-call(s32[1]{0:T(128)} %bitcast.refs_0_, bf16[256,512]{1,0:T(8,128)(2,1)} %refs_1_.3, bf16[512,1536]{1,0:T(8,128)(2,1)} %refs_2_.3), custom_call_target="tpu_custom_call" | custom-call | flops 268435456 | bytes 1048576 | tf_op jit(solution)/shard_map/pallas_call | solution.py:45
  2.9 13.8 %all-to-all-start = ((bf16[32,32,128]{2,1,0:T(8,128)(2,1)}), bf16[32,32,128]{2,1,0:T(8,128)(2,1)S(1)}, u32[]{:S(2)}, u32[]{:S(2)}) async-start(bf16[32,32,128]{2,1,0:T(8,128)(2,1)} %bitcast.1), calls=%async_computation | async-start | bytes 524288 | tf_op jit(solution)/shard_map/all_to_all | solution.py:324
  16.6 1.9 %collective-permute-start = (bf16[128,1024]{1,0:T(8,128)(2,1)S(1)}, bf16[128,1024]{1,0:T(8,128)(2,1)S(1)}, u32[]{:S(2)}, u32[]{:S(2)}) collective-permute-start(bf16[128,1024]{1,0:T(8,128)(2,1)S(1)} %get-tuple-element.16), channel_id=1, source_target_pairs={{0,1},{1,0},{2,3},{3,2},{4,5},{5,4},{6,7},{7,6},{8,9},{9,8},{10,11... | collective-permute-start | bytes 786440 | tf_op jit(solution)/shard_map/ppermute | solution.py:314
  18.6 7.9 %collective-permute-start.1 = (bf16[64,1024]{1,0:T(8,128)(2,1)S(1)}, bf16[64,1024]{1,0:T(8,128)(2,1)S(1)}, u32[]{:S(2)}, u32[]{:S(2)}) collective-permute-start(bf16[64,1024]{1,0:T(8,128)(2,1)S(1)} %get-tuple-element.17), channel_id=1, source_target_pairs={{1,2},{3,4},{5,6},{7,8},{9,10},{11,12},{13,14},{15,16},{17,18},{19... | collective-permute-start | bytes 393224 | tf_op jit(solution)/shard_map/ppermute | solution.py:329
  26.5 0.0 collective-permute-done.refs_1_.refs_4_
  26.5 0.1 shard_map.38
  26.7 5.6 %all_gather.6.refs_2_.refs_0_.refs_6_ = bf16[128,1024]{1,0:T(8,128)(2,1)S(1)} all-gather(bf16[64,1024]{1,0:T(8,128)(2,1)S(1)} %shard_map.38), channel_id=1, replica_groups={{0,2},{1,3},{4,6},{5,7},{8,10},{9,11},{12,14},{13,15},{16,18},{17,19},{..., dimensions={0}, use_global_device_ids=true | all-gather | bytes 393216 | tf_op jit(solution)/shard_map/all_gather | solution.py:328
  32.3 0.6 shard_map.39
  32.9 2.1 %collective-permute-start.3 = (bf16[32,1024]{1,0:T(8,128)(2,1)S(1)}, bf16[32,1024]{1,0:T(8,128)(2,1)S(1)}, u32[]{:S(2)}, u32[]{:S(2)}) collective-permute-start(bf16[32,1024]{1,0:T(8,128)(2,1)S(1)} %get-tuple-element.21.refs_1_), channel_id=1, source_target_pairs={{0,96},{1,97},{2,98},{3,99},{4,100},{5,101},{6,102},{7,103},{8,104... | collective-permute-start | bytes 196616 | tf_op jit(solution)/shard_map/ppermute | solution.py:314
  35.0 0.2 shard_map.40.refs_3_.refs_0_
  35.2 0.0 copy-start
  35.2 4.7 %collective-permute-start.2 = (bf16[64,1024]{1,0:T(8,128)(2,1)S(1)}, bf16[64,1024]{1,0:T(8,128)(2,1)S(1)}, u32[]{:S(2)}, u32[]{:S(2)}) collective-permute-start(bf16[64,1024]{1,0:T(8,128)(2,1)S(1)} %shard_map.40.refs_3_.refs_0_), channel_id=1, source_target_pairs={{0,4},{1,5},{2,6},{3,7},{4,0},{5,1},{6,2},{7,3},{8,12},{9,13},{10,... | collective-permute-start | bytes 393224 | tf_op jit(solution)/shard_map/ppermute | solution.py:314
  39.9 1.2 %collective-permute-done.3.refs_2_ = bf16[32,1024]{1,0:T(8,128)(2,1)S(1)} collective-permute-done((bf16[32,1024]{1,0:T(8,128)(2,1)S(1)}, bf16[32,1024]{1,0:T(8,128)(2,1)S(1)}, u32[]{:S(2)}, u32[]{:S(2)}) %collective-permute-start.3) | collective-permute-done | bytes 65568 | tf_op jit(solution)/shard_map/ppermute | solution.py:314
  41.2 2.2 %all_gather.7.refs_0_.refs_8_ = bf16[256,1024]{1,0:T(8,128)(2,1)S(1)} all-gather(bf16[128,1024]{1,0:T(8,128)(2,1)S(1)} %shard_map.41), channel_id=1, replica_groups={{0,1},{2,3},{4,5},{6,7},{8,9},{10,11},{12,13},{14,15},{16,17},{18,19},{..., dimensions={0}, use_global_device_ids=true | all-gather | bytes 786432 | tf_op jit(solution)/shard_map/all_gather | solution.py:333
  43.4 2.4 %collective-permute-start.4 = (bf16[64,1024]{1,0:T(8,128)(2,1)S(1)}, bf16[64,1024]{1,0:T(8,128)(2,1)S(1)}, u32[]{:S(2)}, u32[]{:S(2)}) collective-permute-start(bf16[64,1024]{1,0:T(8,128)(2,1)S(1)} %shard_map.42.refs_2_.refs_0_), channel_id=1, source_target_pairs={{0,128},{1,129},{2,130},{3,131},{4,132},{5,133},{6,134},{7,135},{8... | collective-permute-start | bytes 393224 | tf_op jit(solution)/shard_map/ppermute | solution.py:314
  45.8 0.1 collective-permute-done.2.refs_1_.refs_7_
  45.9 0.2 shard_map.43.refs_2_
  46.1 3.5 %collective-permute-start.5 = (bf16[64,1024]{1,0:T(8,128)(2,1)S(1)}, bf16[64,1024]{1,0:T(8,128)(2,1)S(1)}, u32[]{:S(2)}, u32[]{:S(2)}) collective-permute-start(bf16[64,1024]{1,0:T(8,128)(2,1)S(1)} %shard_map.43.refs_2_), channel_id=1, source_target_pairs={{0,12},{1,13},{2,14},{3,15},{4,8},{5,9},{6,10},{7,11},{8,4},{9,5},... | collective-permute-start | bytes 393224 | tf_op jit(solution)/shard_map/ppermute | solution.py:314
  49.6 1.2 %collective-permute-done.4.refs_1_.refs_9_ = bf16[64,1024]{1,0:T(8,128)(2,1)S(1)} collective-permute-done((bf16[64,1024]{1,0:T(8,128)(2,1)S(1)}, bf16[64,1024]{1,0:T(8,128)(2,1)S(1)}, u32[]{:S(2)}, u32[]{:S(2)}) %collective-permute-start.4) | collective-permute-done | bytes 131104 | tf_op jit(solution)/shard_map/ppermute | solution.py:314
  50.8 0.2 shard_map.44.refs_10_
  51.0 1.9 %collective-permute-start.6 = (bf16[64,1024]{1,0:T(8,128)(2,1)S(1)}, bf16[64,1024]{1,0:T(8,128)(2,1)S(1)}, u32[]{:S(2)}, u32[]{:S(2)}) collective-permute-start(bf16[64,1024]{1,0:T(8,128)(2,1)S(1)} %shard_map.44.refs_10_), channel_id=1, source_target_pairs={{0,384},{1,385},{2,386},{3,387},{4,388},{5,389},{6,390},{7,391},{8... | collective-permute-start | bytes 393224 | tf_op jit(solution)/shard_map/ppermute | solution.py:314
  52.9 3.4 %shard_map.45 = (bf16[256,512]{1,0:T(8,128)(2,1)S(1)}, f32[256,512]{1,0:T(8,128)S(1)}, f32[256,512]{1,0:T(8,128)S(1)}) custom-call(s32[1]{0:T(128)} %bitcast.refs_0_, bf16[256,512]{1,0:T(8,128)(2,1)S(1)} %copy-done, bf16[512,1536]{1,0:T(8,128)(2,1)} %refs_2_.3, bf16[256,1024]{1,0:T(8,128)(2,1)S(1)} %get-tuple-element.15.refs_3_, ...), custom_call_target="tpu_custom_call" | custom-call | flops 1000000000 | bytes 1048576 | tf_op jit(solution)/shard_map/pallas_call | solution.py:45
  56.3 2.8 %collective-permute-done.6.refs_4_ = bf16[64,1024]{1,0:T(8,128)(2,1)S(1)} collective-permute-done((bf16[64,1024]{1,0:T(8,128)(2,1)S(1)}, bf16[64,1024]{1,0:T(8,128)(2,1)S(1)}, u32[]{:S(2)}, u32[]{:S(2)}) %collective-permute-start.6) | collective-permute-done | bytes 131104 | tf_op jit(solution)/shard_map/ppermute | solution.py:314
  59.1 2.1 %shard_map.46 = bf16[256,512]{1,0:T(8,128)(2,1)} custom-call(bf16[256,512]{1,0:T(8,128)(2,1)S(1)} %get-tuple-element.22.refs_0_, f32[256,512]{1,0:T(8,128)S(1)} %get-tuple-element.23.refs_1_, f32[256,512]{1,0:T(8,128)S(1)} %get-tuple-element.24.refs_2_, bf16[64,1024]{1,0:T(8,128)(2,1)S(1)} %collective-permute-done.5.refs_3_, ...), custom_call_target="tpu_custom_call" | custom-call | flops 1000000000 | bytes 1048576 | tf_op jit(solution)/shard_map/pallas_call | solution.py:45
  (6 shorter events, 0.1 us)
Async XLA Ops:
  2.9 29.4 %all-to-all-start = ((bf16[32,32,128]{2,1,0:T(8,128)(2,1)}), bf16[32,32,128]{2,1,0:T(8,128)(2,1)S(1)}, u32[]{:S(2)}, u32[]{:S(2)}) async-start(bf16[32,32,128]{2,1,0:T(8,128)(2,1)} %bitcast.1), calls=%async_computation | async-start | bytes 524288 | tf_op jit(solution)/shard_map/all_to_all | solution.py:324
  16.6 9.9 %collective-permute-start = (bf16[128,1024]{1,0:T(8,128)(2,1)S(1)}, bf16[128,1024]{1,0:T(8,128)(2,1)S(1)}, u32[]{:S(2)}, u32[]{:S(2)}) collective-permute-start(bf16[128,1024]{1,0:T(8,128)(2,1)S(1)} %get-tuple-element.16), channel_id=1, source_target_pairs={{0,1},{1,0},{2,3},{3,2},{4,5},{5,4},{6,7},{7,6},{8,9},{9,8},{10,11... | collective-permute-start | bytes 786440 | tf_op jit(solution)/shard_map/ppermute | solution.py:314
  18.6 13.7 %collective-permute-start.1 = (bf16[64,1024]{1,0:T(8,128)(2,1)S(1)}, bf16[64,1024]{1,0:T(8,128)(2,1)S(1)}, u32[]{:S(2)}, u32[]{:S(2)}) collective-permute-start(bf16[64,1024]{1,0:T(8,128)(2,1)S(1)} %get-tuple-element.17), channel_id=1, source_target_pairs={{1,2},{3,4},{5,6},{7,8},{9,10},{11,12},{13,14},{15,16},{17,18},{19... | collective-permute-start | bytes 393224 | tf_op jit(solution)/shard_map/ppermute | solution.py:329
  32.9 8.3 %collective-permute-start.3 = (bf16[32,1024]{1,0:T(8,128)(2,1)S(1)}, bf16[32,1024]{1,0:T(8,128)(2,1)S(1)}, u32[]{:S(2)}, u32[]{:S(2)}) collective-permute-start(bf16[32,1024]{1,0:T(8,128)(2,1)S(1)} %get-tuple-element.21.refs_1_), channel_id=1, source_target_pairs={{0,96},{1,97},{2,98},{3,99},{4,100},{5,101},{6,102},{7,103},{8,104... | collective-permute-start | bytes 196616 | tf_op jit(solution)/shard_map/ppermute | solution.py:314
  35.2 17.7 %copy-start = (bf16[256,512]{1,0:T(8,128)(2,1)S(1)}, bf16[256,512]{1,0:T(8,128)(2,1)}, u32[]{:S(2)}) copy-start(bf16[256,512]{1,0:T(8,128)(2,1)} %refs_1_.3) | copy-start | bytes 786436
  35.2 10.7 %collective-permute-start.2 = (bf16[64,1024]{1,0:T(8,128)(2,1)S(1)}, bf16[64,1024]{1,0:T(8,128)(2,1)S(1)}, u32[]{:S(2)}, u32[]{:S(2)}) collective-permute-start(bf16[64,1024]{1,0:T(8,128)(2,1)S(1)} %shard_map.40.refs_3_.refs_0_), channel_id=1, source_target_pairs={{0,4},{1,5},{2,6},{3,7},{4,0},{5,1},{6,2},{7,3},{8,12},{9,13},{10,... | collective-permute-start | bytes 393224 | tf_op jit(solution)/shard_map/ppermute | solution.py:314
  43.4 7.4 %collective-permute-start.4 = (bf16[64,1024]{1,0:T(8,128)(2,1)S(1)}, bf16[64,1024]{1,0:T(8,128)(2,1)S(1)}, u32[]{:S(2)}, u32[]{:S(2)}) collective-permute-start(bf16[64,1024]{1,0:T(8,128)(2,1)S(1)} %shard_map.42.refs_2_.refs_0_), channel_id=1, source_target_pairs={{0,128},{1,129},{2,130},{3,131},{4,132},{5,133},{6,134},{7,135},{8... | collective-permute-start | bytes 393224 | tf_op jit(solution)/shard_map/ppermute | solution.py:314
  46.1 10.2 %collective-permute-start.5 = (bf16[64,1024]{1,0:T(8,128)(2,1)S(1)}, bf16[64,1024]{1,0:T(8,128)(2,1)S(1)}, u32[]{:S(2)}, u32[]{:S(2)}) collective-permute-start(bf16[64,1024]{1,0:T(8,128)(2,1)S(1)} %shard_map.43.refs_2_), channel_id=1, source_target_pairs={{0,12},{1,13},{2,14},{3,15},{4,8},{5,9},{6,10},{7,11},{8,4},{9,5},... | collective-permute-start | bytes 393224 | tf_op jit(solution)/shard_map/ppermute | solution.py:314
  51.0 8.1 %collective-permute-start.6 = (bf16[64,1024]{1,0:T(8,128)(2,1)S(1)}, bf16[64,1024]{1,0:T(8,128)(2,1)S(1)}, u32[]{:S(2)}, u32[]{:S(2)}) collective-permute-start(bf16[64,1024]{1,0:T(8,128)(2,1)S(1)} %shard_map.44.refs_10_), channel_id=1, source_target_pairs={{0,384},{1,385},{2,386},{3,387},{4,388},{5,389},{6,390},{7,391},{8... | collective-permute-start | bytes 393224 | tf_op jit(solution)/shard_map/ppermute | solution.py:314
